TPU v7x, 768 devices: a whole 4x8x12 slice. The times are simulated.
768 devices in a mesh: blk: 192 (over y, z, x_lo), col: 4 (over x_hi, core).
Axes of the slice: x: 4 (x_hi: 2, x_lo: 2; x = x_hi * 2 + x_lo), y: 8, z: 12, core: 2. Of those that a mesh axis runs over, the one named last changes fastest.
Arguments:
- node_feats: bfloat16 [98304, 512], P('blk', 'col'), may hold values from -6 to 6
- weight: bfloat16 [512, 512], replicated, may hold values from -0.25 to 0.25
- layer_bias: bfloat16 [512], P('col'), may hold values from -4 to 4
- cotangent: bfloat16 [98304, 512], P('blk', 'col'), may hold values from -6 to 6
- adj_tiles: bfloat16 [192, 9, 16, 128, 128], P('blk'), may hold values from -0.1796875 to 0.1796875
- tile_row: int32 [192, 9, 16], P('blk'), may hold values from 0 to 3, as said below
- tile_col: int32 [192, 9, 16], P('blk'), may hold values from 0 to 3
- tile_count: int32 [192, 9], P('blk'), may hold values from 1 to 16, as said below
Outputs:
- activated: bfloat16 [98304, 512], P('blk', 'col')
- grad_nodes: bfloat16 [98304, 512], P('blk', 'col')
- grad_weight: float32 [512, 512], P(None, 'col')
- grad_bias: float32 [512], P('col')
Inputs may be any that keep to these rules, and one draw needn't show every extreme that they name: Within one device and offset, the 16 slots (live or not) name distinct pairs of tile_row and tile_col. `tile_count`: some device and offset has all 16 slots live in every draw.
All inputs are finite; a program needn't handle non-finite values.
Results may differ from a plain program's by a relative error of at most 0.0095.
Values may be sent and summed in bfloat16 or wider, within the bound.
No kernel may reach another device: no remote copies, remote signals or barrier semaphores. Data moves between devices by JAX's collectives and lax.ppermute only.
A program may use at most 32 MiB of HBM per device.

v0:
```python
import jax
import jax.numpy as jnp
from jax import lax
from jax.sharding import PartitionSpec as P


def passed_along(block, axis, distance):
    devices = range(lax.axis_size(axis))
    route = [((i - distance) % len(devices), i) for i in devices]
    return lax.ppermute(block, axis, route)


def rotate_features(moving, hops):
    return passed_along(moving, "blk", hops)


def send_term(moving, hops):
    return passed_along(moving, "blk", hops)


def on_device(node_feats, weight, layer_bias, cotangent, adj_tiles, tile_row, tile_col, tile_count):
    row_count = node_feats.shape[0]
    col_width = node_feats.shape[1]
    tile_size = adj_tiles.shape[-1]
    row_blocks = row_count // tile_size
    offsets = adj_tiles.shape[1]
    reach_span = (offsets - 1) // 2
    tile_slab = adj_tiles[0]
    row_lists = tile_row[0]
    col_lists = tile_col[0]
    counts = tile_count[0]
    capacity = tile_slab.shape[1]
    slot_ids = jnp.arange(capacity, dtype=jnp.int32)
    block_ids = jnp.arange(row_blocks, dtype=jnp.int32)
    column = lax.axis_index("col")
    weight_mine = lax.dynamic_slice_in_dim(weight, column * col_width, col_width, 1)
    gathered = lax.all_gather(node_feats, "col", axis=1, tiled=True)
    projected = jnp.dot(gathered, weight_mine, preferred_element_type=jnp.float32).astype(
        jnp.bfloat16
    )

    def placement_matrix(targets, offset):
        live_slots = slot_ids < counts[offset]
        return ((targets[None, :] == block_ids[:, None]) & live_slots[None, :]).astype(jnp.float32)

    def forward_terms(offset, source):
        blocks = source.reshape(row_blocks, tile_size, col_width)
        picked = jnp.take(blocks, col_lists[offset], axis=0)
        products = jnp.einsum(
            "kab,kbh->kah", tile_slab[offset], picked, preferred_element_type=jnp.float32
        )
        placing = placement_matrix(row_lists[offset], offset)
        added = jnp.einsum("rk,kah->rah", placing, products, precision=lax.Precision.HIGHEST)
        return added.reshape(row_count, col_width)

    def backward_terms(offset, grad_rows):
        blocks = grad_rows.reshape(row_blocks, tile_size, col_width)
        picked = jnp.take(blocks, row_lists[offset], axis=0)
        products = jnp.einsum(
            "kba,kbh->kah", tile_slab[offset], picked, preferred_element_type=jnp.float32
        )
        placing = placement_matrix(col_lists[offset], offset)
        added = jnp.einsum("rk,kah->rah", placing, products, precision=lax.Precision.HIGHEST)
        return added.reshape(row_count, col_width).astype(jnp.bfloat16)

    empty = jnp.zeros((row_count, col_width), jnp.float32)

    def forward_turn(turn, carried):
        summed, incoming = carried
        summed = summed + forward_terms(2 * reach_span - turn, incoming)
        return (summed, rotate_features(incoming, 1))

    incoming = rotate_features(projected, -reach_span)
    summed, incoming = lax.fori_loop(0, 2 * reach_span, forward_turn, (empty, incoming))
    summed = summed + forward_terms(0, incoming)
    preact = summed + layer_bias.astype(jnp.float32)[None, :]
    sigmoid_val = jax.nn.sigmoid(preact)
    activated = (preact * sigmoid_val).astype(jnp.bfloat16)
    grad_pre = (
        cotangent.astype(jnp.float32) * sigmoid_val * (1.0 + preact * (1.0 - sigmoid_val))
    ).astype(jnp.bfloat16)
    returned = backward_terms(reach_span, grad_pre).astype(jnp.float32)
    for offset in range(offsets):
        if offset != reach_span:
            arrived = send_term(backward_terms(offset, grad_pre), offset - reach_span)
            returned = returned + arrived.astype(jnp.float32)
    grad_proj = returned.astype(jnp.bfloat16)
    weight_part = lax.dot_general(
        gathered, grad_proj, (((0,), (0,)), ((), ())), preferred_element_type=jnp.float32
    )
    bias_part = jnp.sum(grad_pre.astype(jnp.float32), axis=0)
    weight_total, bias_total = lax.psum((weight_part, bias_part), "blk")
    node_total = row_count * lax.axis_size("blk")
    grad_scale = 1.0 / jnp.sqrt(jnp.float32(node_total))
    grad_weight = weight_total * grad_scale
    grad_bias = bias_total * grad_scale
    partial_value = lax.dot_general(
        grad_proj, weight_mine, (((1,), (1,)), ((), ())), preferred_element_type=jnp.float32
    )
    grad_nodes = lax.psum_scatter(partial_value, "col", scatter_dimension=1, tiled=True).astype(
        jnp.bfloat16
    )
    return (activated, grad_nodes, grad_weight, grad_bias)


def solution(mesh):
    placed = (
        P("blk", "col"),
        P(),
        P("col"),
        P("blk", "col"),
        P("blk", None, None, None, None),
        P("blk", None, None),
        P("blk", None, None),
        P("blk", None),
    )
    return jax.shard_map(
        on_device,
        mesh=mesh,
        in_specs=placed,
        out_specs=(P("blk", "col"), P("blk", "col"), P(None, "col"), P("col")),
        check_vma=False,
    )
```

profile of v0, /device:TPU:4, one launch (start us, length us, event | category | flops | bytes accessed | tf_op | source)
XLA Modules:
  0.0 1793.4 jit_solution(3891257812852828957)
XLA Ops:
  8.1 15.5 all_gather.3
  23.9 10.6 collective-permute-start.1
  37.1 1.4 compare_and_fusion.8
  38.6 1.4 slice_bitcast_fusion.8
  40.0 1.7 fusion.168
  55.6 89.3 %while.18 = (s32[]{:T(128)}, f32[512,128]{1,0:T(8,128)S(1)}, bf16[512,128]{1,0:T(8,128)(2,1)S(1)}, s32[9,16]{1,0:T(8,128)S(1)}, s32[9]{0:T(128)}, /*index=5*/bf1...) while((s32[]{:T(128)}, f32[512,128]{1,0:T(8,128)S(1)}, ...), condition=%wide.region_1.3_spmd.clone, body=%wide.region_0.2_spmd.clone.sunk | while | flops 80086264 | bytes 6558441 | solution.py:74
  55.6 3.1 collective-permute-start
  58.8 1.3 dynamic_slice.70
  61.4 1.4 fusion.184
  64.0 3.2 collective-permute-done
  67.2 1.9 collective-permute-start
  69.2 1.3 dynamic_slice.70
  71.8 1.4 fusion.184
  74.4 3.9 collective-permute-done
  78.3 1.9 collective-permute-start
  80.3 1.3 dynamic_slice.70
  82.9 1.4 fusion.184
  85.5 3.9 collective-permute-done
  89.4 1.9 collective-permute-start
  91.4 1.3 dynamic_slice.70
  94.0 1.4 fusion.184
  96.6 3.9 collective-permute-done
  100.5 1.9 collective-permute-start
  102.5 1.3 dynamic_slice.70
  105.1 1.4 fusion.184
  107.7 3.9 collective-permute-done
  111.6 1.9 collective-permute-start
  116.2 1.4 fusion.184
  118.8 3.9 collective-permute-done
  122.7 1.9 collective-permute-start
  127.3 1.4 fusion.184
  129.9 3.9 collective-permute-done
  133.8 1.9 collective-permute-start
  135.8 1.3 dynamic_slice.70
  138.4 1.4 fusion.184
  141.0 3.9 collective-permute-done
  145.5 1.7 fusion.52
  149.0 2.3 convert_reduce_fusion
  152.0 1.5 fusion.50
  155.2 1.9 collective-permute-start.2
  157.9 1.5 fusion.46
  160.4 1.9 collective-permute-start.3
  163.1 1.5 fusion.44
  166.9 1.9 collective-permute-start.4
  169.6 1.5 fusion.42
  173.4 4.4 collective-permute-start.5
  178.6 1.5 fusion.40
  182.4 2.5 collective-permute-start.6
  185.5 1.5 fusion.38
  189.9 1.5 fusion.36
  194.4 1.5 fusion.34
  195.9 1.4 copy.37
  198.0 1.5 fusion.48
  199.5 1.7 convolution_convert_fusion.1
  202.4 4.8 collective-permute-start.7
  207.3 4.8 collective-permute-start.8
  212.1 5.2 collective-permute-start.9
  217.8 1.7 collective-permute-done.8
  219.5 5.3 collective-permute-done.9
  224.9 1.3 fusion.91
  227.2 1.3 fusion.103
  228.6 456.0 %psum.15 = f32[128]{0:T(128)S(1)} all-reduce(f32[128]{0:T(128)S(1)} %copy-done.8), channel_id=1, replica_groups=mesh['blk'=192,'col'=4] {'blk'}, use_global_device_ids=true, to_apply=%region_5.7 | all-reduce | flops 128 | bytes 1024 | tf_op jit(solution)/shard_map/psum | solution.py:92
  685.1 1097.4 %all-reduce.2.cloned.1.call-done = f32[512,128]{0,1:T(8,128)} async-done(((f32[512,128]{0,1:T(8,128)}), f32[512,128]{0,1:T(8,128)}) %all-reduce.2.cloned.1.call-update) | async-done | bytes 262160 | tf_op jit(solution)/shard_map/psum | solution.py:92
  1784.3 1.6 convert_element_type.156
  (170 shorter events, 67.1 us)
Async XLA Ops:
  8.0 15.6 copy-start
  8.0 1774.5 %all-reduce.2.cloned.1.call-start = ((), (), s32[]{:S(2)}) async-start(), calls=%async_computation.2 | async-start | bytes 524288 | tf_op jit(solution)/shard_map/psum | solution.py:92
  23.9 31.5 %collective-permute-start.1 = (bf16[512,128]{0,1:T(8,128)(2,1)S(1)}, bf16[512,128]{0,1:T(8,128)(2,1)S(1)}, u32[]{:S(2)}, u32[]{:S(2)}) collective-permute-start(bf16[512,128]{0,1:T(8,128)(2,1)S(1)} %fusion.22), channel_id=1, source_target_pairs={{16,0},{20,4},{24,8},{28,12},{32,16},{36,20},{40,24},{44,28},{48,3... | collective-permute-start | bytes 393224 | tf_op jit(solution)/shard_map/ppermute | solution.py:10
  55.6 11.6 collective-permute-start
  67.2 11.1 collective-permute-start
  78.3 11.1 collective-permute-start
  89.4 11.1 collective-permute-start
  100.5 11.1 collective-permute-start
  111.6 11.1 collective-permute-start
  122.7 11.1 collective-permute-start
  133.8 11.1 collective-permute-start
  148.9 9.0 copy-start.4
  153.5 6.4 copy-start.6
  153.5 6.4 copy-start.9
  155.2 47.2 %collective-permute-start.2 = (bf16[512,128]{1,0:T(8,128)(2,1)S(1)}, bf16[512,128]{1,0:T(8,128)(2,1)}, u32[]{:S(2)}, u32[]{:S(2)}) collective-permute-start(bf16[512,128]{1,0:T(8,128)(2,1)S(1)} %bitcast.250), channel_id=1, source_target_pairs={{16,0},{20,4},{24,8},{28,12},{32,16},{36,20},{40,24},{44,28},{48,3... | collective-permute-start | bytes 393224 | tf_op jit(solution)/shard_map/ppermute | solution.py:10
  160.4 46.8 %collective-permute-start.3 = (bf16[512,128]{1,0:T(8,128)(2,1)S(1)}, bf16[512,128]{1,0:T(8,128)(2,1)}, u32[]{:S(2)}, u32[]{:S(2)}) collective-permute-start(bf16[512,128]{1,0:T(8,128)(2,1)S(1)} %bitcast.251), channel_id=1, source_target_pairs={{12,0},{16,4},{20,8},{24,12},{28,16},{32,20},{36,24},{40,28},{44,3... | collective-permute-start | bytes 393224 | tf_op jit(solution)/shard_map/ppermute | solution.py:10
  166.9 45.2 %collective-permute-start.4 = (bf16[512,128]{1,0:T(8,128)(2,1)}, bf16[512,128]{1,0:T(8,128)(2,1)}, u32[]{:S(2)}, u32[]{:S(2)}) collective-permute-start(bf16[512,128]{1,0:T(8,128)(2,1)} %bitcast.35), channel_id=1, source_target_pairs={{8,0},{12,4},{16,8},{20,12},{24,16},{28,20},{32,24},{36,28},{40,32... | collective-permute-start | bytes 393224 | tf_op jit(solution)/shard_map/ppermute | solution.py:10
  173.4 44.4 %collective-permute-start.5 = (bf16[512,128]{1,0:T(8,128)(2,1)}, bf16[512,128]{1,0:T(8,128)(2,1)}, u32[]{:S(2)}, u32[]{:S(2)}) collective-permute-start(bf16[512,128]{1,0:T(8,128)(2,1)} %bitcast.42), channel_id=1, source_target_pairs={{4,0},{8,4},{12,8},{16,12},{20,16},{24,20},{28,24},{32,28},{36,32}... | collective-permute-start | bytes 393224 | tf_op jit(solution)/shard_map/ppermute | solution.py:10
  182.4 35.4 %collective-permute-start.6 = (bf16[512,128]{1,0:T(8,128)(2,1)}, bf16[512,128]{1,0:T(8,128)(2,1)}, u32[]{:S(2)}, u32[]{:S(2)}) collective-permute-start(bf16[512,128]{1,0:T(8,128)(2,1)} %bitcast.49), channel_id=1, source_target_pairs={{764,0},{0,4},{4,8},{8,12},{12,16},{16,20},{20,24},{24,28},{28,32}... | collective-permute-start | bytes 393224 | tf_op jit(solution)/shard_map/ppermute | solution.py:10
  187.5 7.0 copy-start.3
  191.4 6.6 copy-start.2
  195.9 6.5 copy-start.1
  195.9 21.3 %copy-start.5 = (s32[16]{0:T(128)S(1)}, s32[16]{0:T(128)}, u32[]{:S(2)}) copy-start(s32[16]{0:T(128)} %get-tuple-element.323) | copy-start | bytes 196
  195.9 21.3 %copy-start.7 = (pred[16]{0:T(512)(128)(4,1)S(1)}, pred[16]{0:T(512)(128)(4,1)}, u32[]{:S(2)}) copy-start(pred[16]{0:T(512)(128)(4,1)} %iota_compare_fusion.19) | copy-start | bytes 52
  201.2 27.4 %copy-start.8 = (f32[128]{0:T(128)S(1)}, f32[128]{0:T(128)}, u32[]{:S(2)}) copy-start(f32[128]{0:T(128)} %get-tuple-element.294) | copy-start | bytes 1540
  202.4 15.4 collective-permute-start.7
  207.3 12.3 collective-permute-start.8
  212.1 12.7 collective-permute-start.9
  227.2 1557.2 %reduce-scatter.2.cloned.1.call-start = ((), (), s32[]{:S(2)}) async-start(), calls=%async_computation.1 | async-start | bytes 1310720 | tf_op jit(solution)/shard_map/reduce_scatter | solution.py:100
Sparse Core Ops, SparseCore 0:
  227.3 1555.1 all-reduce.1
Sparse Core Ops, SparseCore 1:
  231.0 37.8 reduce-scatter.1
where the time goes:
time: 1800 us; the launch traced here: 1790 us
  waiting for transfers between devices  1140 us (63%)
  blocking collectives  472 us (26%)
  starting transfers between devices  54.7 us (3%)
  matrix products  47.8 us (3%)
  local copies, waits for them, and re-layouts  39.2 us (2%)
  other arithmetic  28.3 us (2%)
    psum x1, waiting for transfers between devices, on_device(): weight_total, bias_total = lax.psum((weight_part, bias_part), 'blk')  1100 us
    psum x1, blocking collectives, on_device(): weight_total, bias_total = lax.psum((weight_part, bias_part), 'blk')  456 us
    ppermute x17, starting transfers between devices, passed_along(): return lax.ppermute(block, axis, route)  54.6 us
    ppermute x17, waiting for transfers between devices, passed_along(): return lax.ppermute(block, axis, route)  37.7 us
  transfers between devices with their start and end apart: 19, of which 11 were waited for; matrix products, arithmetic and copies ran while one was open for 6% of the time, Pallas kernels for 0%

commit v1 on v0

v1 whole, which is shorter than its diff:
```python
import jax
import jax.numpy as jnp
import numpy as np
from jax import lax
from jax.experimental import pallas as pl
from jax.experimental.pallas import tpu as pltpu
from jax.sharding import Mesh
from jax.sharding import PartitionSpec as P

NODES = 98304
TILE = 128
BLOCKS = 4
ROWS = TILE * BLOCKS
WIDTH = 128
COLS = 4
HIDDEN = WIDTH * COLS
OFFSETS = 9
SLOTS = 16
REACH = 4
WINDOW = OFFSETS + 1
N_Y, N_Z, N_XL = 8, 12, 2
PAIRS = N_Y * N_Z
PACK_ROWS = ROWS + 16
RING = N_Z * N_XL
SHARE = 24
BLK = ("y", "z", "xl")
COL = ("xh", "core")
BF16 = jnp.bfloat16
F32 = jnp.float32
VMEM = pl.BlockSpec(memory_space=pltpu.VMEM)
SMEM = pl.BlockSpec(memory_space=pltpu.SMEM)


def params(**more):
    return pltpu.CompilerParams(vmem_limit_bytes=32 * 1024 * 1024, **more)


def dense_kernel(side, rows, cols, counts, slab, dense):
    place = pl.program_id(0)
    offset = place - side[0]
    inside = (offset >= 0) & (offset < OFFSETS)

    @pl.when(inside)
    def _():
        live = counts[offset]
        for slot in range(SLOTS):
            at = offset * SLOTS + slot
            row = pl.multiple_of(rows[at] * TILE, TILE)
            col = pl.multiple_of(cols[at] * TILE, TILE)
            tile = slab[0, slot]
            dense[0, pl.ds(row, TILE), pl.ds(col, TILE)] = jnp.where(
                slot < live, tile, jnp.zeros_like(tile)
            )

    @pl.when(jnp.logical_not(inside))
    def _():
        dense[...] = jnp.zeros_like(dense)


def make_dense(side, rows, cols, counts, slab):
    return pl.pallas_call(
        dense_kernel,
        grid_spec=pltpu.PrefetchScalarGridSpec(
            num_scalar_prefetch=4,
            grid=(WINDOW,),
            in_specs=[
                pl.BlockSpec(
                    (1, SLOTS, TILE, TILE),
                    lambda j, side, *_: (jnp.clip(j - side[0], 0, OFFSETS - 1), 0, 0, 0),
                )
            ],
            out_specs=pl.BlockSpec((1, ROWS, ROWS), lambda j, *_: (j, 0, 0)),
        ),
        out_shape=jax.ShapeDtypeStruct((WINDOW, ROWS, ROWS), BF16),
        compiler_params=params(),
        cost_estimate=pl.CostEstimate(flops=0, bytes_accessed=10 << 20, transcendentals=0),
        name="dense_tiles",
    )(side, rows, cols, counts, slab)


def gather_kernel(dense, xa, xb, xc, xd, xe, out):
    total = jnp.zeros((ROWS, WIDTH), F32)
    for k, pair in enumerate((xa, xb, xc, xd, xe)):
        for s in range(2):
            total += jnp.dot(dense[2 * k + s], pair[s], preferred_element_type=F32)
    out[...] = total.astype(BF16)


def gather_rows(dense, pairs):
    return pl.pallas_call(
        gather_kernel,
        in_specs=[VMEM] * 6,
        out_specs=VMEM,
        out_shape=jax.ShapeDtypeStruct((ROWS, WIDTH), BF16),
        compiler_params=params(),
        cost_estimate=pl.CostEstimate(
            flops=2 * WINDOW * ROWS * ROWS * WIDTH, bytes_accessed=8 << 20, transcendentals=0
        ),
        name="aggregate_features",
    )(dense, *pairs)


def middle_kernel(column, mixed, packed, weight, dense, act, part, ta, tb, tc, td, te, act_all, grad_all, feats):
    mine = pl.multiple_of(column[0] * WIDTH, WIDTH)
    bias = jnp.concatenate(
        [packed[c, ROWS:, :] for c in range(COLS)], axis=1
    )[0:1].astype(F32)
    step = 128
    for i in range(ROWS // step):
        span = slice(i * step, (i + 1) * step)
        own = jnp.concatenate([mixed[c, span, :] for c in range(COLS)], axis=1)
        feats[span, :] = own
        preact = jnp.dot(own, weight[...], preferred_element_type=F32) + bias
        sig = 1.0 / (1.0 + jnp.exp(-preact))
        act_all[span, :] = (preact * sig).astype(BF16)
        cot = jnp.concatenate([packed[c, span, :] for c in range(COLS)], axis=1)
        grad_all[span, :] = (
            cot.astype(F32) * sig * (1.0 + preact * (1.0 - sig))
        ).astype(BF16)
    act[...] = act_all[:, pl.ds(mine, WIDTH)]
    grad_mine = grad_all[:, pl.ds(mine, WIDTH)].astype(F32)
    weight_grad = jnp.dot(
        grad_mine.T.astype(BF16), feats[...], preferred_element_type=F32
    )
    part[0:ROWS, :] = weight_grad.T
    first = lax.broadcasted_iota(jnp.int32, (RING * SHARE - HIDDEN, WIDTH), 0) == 0
    part[ROWS:, :] = jnp.where(first, jnp.sum(grad_mine, axis=0, keepdims=True), 0.0)
    back = lax.dot_general(
        weight[pl.ds(mine, WIDTH), :],
        grad_all[...],
        (((1,), (1,)), ((), ())),
        preferred_element_type=F32,
    ).astype(BF16)
    for k, pair in enumerate((ta, tb, tc, td, te)):
        for s in range(2):
            pair[s] = jnp.dot(back, dense[2 * k + s], preferred_element_type=F32).astype(BF16)


def middle(column, mixed, packed, weight, dense):
    term = jax.ShapeDtypeStruct((2, WIDTH, ROWS), BF16)
    return pl.pallas_call(
        middle_kernel,
        in_specs=[SMEM] + [VMEM] * 4,
        out_specs=[VMEM] * 7,
        out_shape=[
            jax.ShapeDtypeStruct((ROWS, WIDTH), BF16),
            jax.ShapeDtypeStruct((RING * SHARE, WIDTH), F32),
        ]
        + [term] * 5,
        scratch_shapes=[pltpu.VMEM((ROWS, HIDDEN), BF16)] * 3,
        compiler_params=params(),
        cost_estimate=pl.CostEstimate(
            flops=2 * (WINDOW + 9) * ROWS * ROWS * WIDTH, bytes_accessed=10 << 20, transcendentals=ROWS * HIDDEN
        ),
        name="activation_and_terms",
    )(column, mixed, packed, weight, dense)


def split_kernel(side, own, ta, tb, td, te, keep, send):
    for s in range(2):
        total = own[s].astype(F32)
        for arrived in (ta, tb, td, te):
            total += arrived[s].astype(F32)

        @pl.when(side[0] == s)
        def _():
            keep[...] = total

        @pl.when(side[0] != s)
        def _():
            send[...] = total.astype(BF16)


def split_terms(side, own, arrived):
    return pl.pallas_call(
        split_kernel,
        in_specs=[SMEM] + [VMEM] * 5,
        out_specs=[VMEM] * 2,
        out_shape=[
            jax.ShapeDtypeStruct((WIDTH, ROWS), F32),
            jax.ShapeDtypeStruct((WIDTH, ROWS), BF16),
        ],
        compiler_params=params(),
        cost_estimate=pl.CostEstimate(flops=1 << 20, bytes_accessed=2 << 20, transcendentals=0),
        name="pair_sums",
    )(side, own, *arrived)


def last_kernel(keep, arrived, out):
    out[...] = (keep[...] + arrived[...].astype(F32)).T.astype(BF16)


def last_sum(keep, arrived):
    return pl.pallas_call(
        last_kernel,
        in_specs=[VMEM] * 2,
        out_specs=VMEM,
        out_shape=jax.ShapeDtypeStruct((ROWS, WIDTH), BF16),
        compiler_params=params(),
        cost_estimate=pl.CostEstimate(flops=1 << 17, bytes_accessed=1 << 19, transcendentals=0),
        name="node_gradient",
    )(keep, arrived)


def from_pair(block, hops):
    route = [
        (2 * ((p + hops) % PAIRS) + s, 2 * p + s) for p in range(PAIRS) for s in range(2)
    ]
    return lax.ppermute(block, BLK, route)


def on_device(node_feats, weight, layer_bias, cotangent, adj_tiles, tile_row, tile_col, tile_count):
    side = lax.axis_index("xl").astype(jnp.int32).reshape(1)
    column = lax.axis_index(COL).astype(jnp.int32).reshape(1)

    dense = make_dense(
        side, tile_row.reshape(-1), tile_col.reshape(-1), tile_count.reshape(-1), adj_tiles[0]
    )
    with jax.named_scope("feature_halo"):
        pair = lax.all_gather(node_feats, "xl", axis=0, tiled=False)
        pairs = [pair if k == 0 else from_pair(pair, k) for k in (-2, -1, 0, 1, 2)]
    mine = gather_rows(dense, pairs)
    with jax.named_scope("column_gather"):
        packed = jnp.concatenate([cotangent, jnp.broadcast_to(layer_bias[None], (16, WIDTH))], axis=0)
        packed = lax.all_gather(packed, COL, axis=0, tiled=False)
        mixed = lax.all_gather(mine, COL, axis=0, tiled=False)
    act, part, ta, tb, tc, td, te = middle(column, mixed, packed, weight, dense)

    with jax.named_scope("term_halo"):
        arrived = [from_pair(t, -k) for k, t in ((-2, ta), (-1, tb), (1, td), (2, te))]
    keep, send = split_terms(side, tc, arrived)
    with jax.named_scope("term_exchange"):
        swap = [(b ^ 1, b) for b in range(2 * PAIRS)]
        other = lax.ppermute(send, BLK, swap)
    grad_nodes = last_sum(keep, other)

    with jax.named_scope("weight_sum"):
        ring = ("z", "xl")
        shares = lax.all_to_all(part.reshape(RING, SHARE, WIDTH), ring, 0, 0, tiled=True)
        share = jnp.sum(shares, axis=0)
        shares = lax.all_to_all(
            jnp.broadcast_to(share[None], (N_Y, SHARE, WIDTH)), "y", 0, 0, tiled=True
        )
        share = jnp.sum(shares, axis=0) * (1.0 / jnp.sqrt(F32(NODES)))
        whole = lax.all_to_all(
            jnp.broadcast_to(share[None], (RING, SHARE, WIDTH)), ring, 0, 0, tiled=True
        ).reshape(RING * SHARE, WIDTH)
    return act, grad_nodes, whole[:HIDDEN], whole[HIDDEN]


def solution(mesh):
    fine = Mesh(
        np.asarray(mesh.devices).reshape(N_Y, N_Z, N_XL, 2, 2), ("y", "z", "xl", "xh", "core")
    )
    placed = (
        P(BLK, COL),
        P(),
        P(COL),
        P(BLK, COL),
        P(BLK, None, None, None, None),
        P(BLK, None, None),
        P(BLK, None, None),
        P(BLK, None),
    )
    return jax.shard_map(
        on_device,
        mesh=fine,
        in_specs=placed,
        out_specs=(P(BLK, COL), P(BLK, COL), P(None, COL), P(COL)),
        check_vma=False,
    )
```

time: 1800 us -> 141 us (0.08)
  the two profiles are of different devices: /device:TPU:4 before, /device:TPU:64 now
where the time goes in v1:
time: 141 us
  blocking collectives  57 us (40%)
  starting transfers between devices  48.4 us (34%)
  waiting for transfers between devices  21.2 us (15%)
  Pallas kernels  6.75 us (5%)
  local copies, waits for them, and re-layouts  5.14 us (4%)
  other arithmetic  1.48 us (1%)
    ppermute x8, starting transfers between devices, from_pair(): return lax.ppermute(block, BLK, route)  38.1 us
    all_to_all x1, blocking collectives, on_device(): lax.all_to_all(part.reshape(RING, SHARE, WIDTH), ring, 0, 0, tiled=True)  18.4 us
    ppermute x8, waiting for transfers between devices, from_pair(): return lax.ppermute(block, BLK, route)  17.7 us
    all_to_all x1, blocking collectives, on_device(): lax.all_to_all(jnp.broadcast_to(share[None], (N_Y, SHARE, WIDTH)), 'y', 0...  14.7 us
    all_gather x1, blocking collectives, on_device(): packed = lax.all_gather(packed, COL, axis=0, tiled=False)  8.93 us
    all_gather x1, blocking collectives, on_device(): mixed = lax.all_gather(mine, COL, axis=0, tiled=False)  8.7 us
    all_to_all x1, starting transfers between devices, on_device(): lax.all_to_all(jnp.broadcast_to(share[None], (RING, SHARE, WIDTH)), ring,...  6.93 us
    all_gather x1, blocking collectives, on_device(): pair = lax.all_gather(node_feats, 'xl', axis=0, tiled=False)  6.26 us
  transfers between devices with their start and end apart: 10, of which 5 were waited for; matrix products, arithmetic and copies ran while one was open for 1% of the time, Pallas kernels for 2%

profile of v1, /device:TPU:64, one launch (start us, length us, event | category | flops | bytes accessed | tf_op | source)
XLA Modules:
  0.0 140.8 jit_solution(1660622040419300851)
XLA Ops:
  0.6 0.0 copy-start.3
  0.6 0.0 copy-start.4
  0.7 6.3 %all-gather = bf16[1024,128]{1,0:T(8,128)(2,1)S(1)} all-gather(bf16[512,128]{1,0:T(8,128)(2,1)} %param.8), channel_id=2, replica_groups=mesh['y'=8,'z'=12,'xl'=2,'xh'=2,'core'=2] {'xl'}, dimensions={0}, use_global_device_ids=true | all-gather | bytes 393216 | tf_op jit(solution)/shard_map/feature_halo/all_gather | solution.py:220
  6.9 16.6 %collective-permute-start.3 = (bf16[2,512,128]{2,1,0:T(8,128)(2,1)S(1)}, bf16[2,512,128]{2,1,0:T(8,128)(2,1)S(1)}, u32[]{:S(2)}, u32[]{:S(2)}) collective-permute-start(bf16[2,512,128]{2,1,0:T(8,128)(2,1)S(1)} %bitcast.14), channel_id=1, source_target_pairs={{16,0},{20,4},{24,8},{28,12},{32,16},{36,20},{40,24},{44,28},{48,3... | collective-permute-start | bytes 786440 | tf_op jit(solution)/shard_map/feature_halo/ppermute | solution.py:209
  23.5 2.5 %collective-permute-start.2 = (bf16[2,512,128]{2,1,0:T(8,128)(2,1)S(1)}, bf16[2,512,128]{2,1,0:T(8,128)(2,1)S(1)}, u32[]{:S(2)}, u32[]{:S(2)}) collective-permute-start(bf16[2,512,128]{2,1,0:T(8,128)(2,1)S(1)} %bitcast.15), channel_id=1, source_target_pairs={{8,0},{12,4},{16,8},{20,12},{24,16},{28,20},{32,24},{36,28},{40,32... | collective-permute-start | bytes 786440 | tf_op jit(solution)/shard_map/feature_halo/ppermute | solution.py:209
  26.0 3.4 %collective-permute-start.1 = (bf16[2,512,128]{2,1,0:T(8,128)(2,1)S(1)}, bf16[2,512,128]{2,1,0:T(8,128)(2,1)S(1)}, u32[]{:S(2)}, u32[]{:S(2)}) collective-permute-start(bf16[2,512,128]{2,1,0:T(8,128)(2,1)S(1)} %bitcast.16), channel_id=1, source_target_pairs={{760,0},{764,4},{0,8},{4,12},{8,16},{12,20},{16,24},{20,28},{24,32... | collective-permute-start | bytes 786440 | tf_op jit(solution)/shard_map/feature_halo/ppermute | solution.py:209
  29.3 1.9 %collective-permute-start = (bf16[2,512,128]{2,1,0:T(8,128)(2,1)S(1)}, bf16[2,512,128]{2,1,0:T(8,128)(2,1)S(1)}, u32[]{:S(2)}, u32[]{:S(2)}) collective-permute-start(bf16[2,512,128]{2,1,0:T(8,128)(2,1)S(1)} %bitcast.17), channel_id=1, source_target_pairs={{752,0},{756,4},{760,8},{764,12},{0,16},{4,20},{8,24},{12,28},{16,... | collective-permute-start | bytes 786440 | tf_op jit(solution)/shard_map/feature_halo/ppermute | solution.py:209
  31.3 0.7 reduce
  32.0 0.1 reshape.36.rows
  32.1 0.7 reduce.1
  32.8 0.1 reshape.37.cols
  32.9 0.0 copy-start
  32.9 2.3 %copy-done = bf16[1,9,16,128,128]{4,3,2,1,0:T(8,128)(2,1)S(1)} copy-done((bf16[1,9,16,128,128]{4,3,2,1,0:T(8,128)(2,1)S(1)}, bf16[1,9,16,128,128]{4,3,2,1,0:T(8,128)(2,1)}, u32[]{:S(2)}) %copy-start) | copy-done | bytes 4718616
  35.2 0.0 copy-start.2
  35.2 0.7 copy-done.2
  35.9 2.2 %dense_tiles.1.dense = bf16[10,512,512]{2,1,0:T(8,128)(2,1)S(1)} custom-call(s32[1]{0:T(128)} %bitcast.1.side, s32[144]{0:T(256)S(1)} %reshape.36.rows, s32[144]{0:T(256)S(1)} %reshape.37.cols, s32[9]{0:T(128)S(1)} %bitcast.20, bf16[9,16,128,128]{3,2,1,0:T(8,128)(2,1)S(1)} %bitcast.11), custom_call_target="tpu_custom_call" | custom-call | bytes 10485760 | tf_op jit(solution)/shard_map/dense_tiles/pallas_call | solution.py:61
  38.1 0.0 copy-done.4
  38.1 0.0 copy-start.1
  38.1 0.0 copy-done.3
  38.2 8.9 %all-gather.2 = bf16[2112,128]{1,0:T(8,128)(2,1)S(1)} all-gather(bf16[528,128]{1,0:T(8,128)(2,1)S(1)} %pad_maximum_fusion), channel_id=4, replica_groups=mesh['y'=8,'z'=12,'xl'=2,'xh'=2,'core'=2] {'xh','core'}, dimensions={0}, use_global_device_ids=true | all-gather | bytes 675840 | tf_op jit(solution)/shard_map/column_gather/all_gather | solution.py:225
  47.1 0.0 collective-permute-done.3.xe
  47.1 0.0 collective-permute-done.2.xd
  47.1 0.0 collective-permute-done.1.xb
  47.1 1.9 %collective-permute-done.xa = bf16[2,512,128]{2,1,0:T(8,128)(2,1)S(1)} collective-permute-done((bf16[2,512,128]{2,1,0:T(8,128)(2,1)S(1)}, bf16[2,512,128]{2,1,0:T(8,128)(2,1)S(1)}, u32[]{:S(2)}, u32[]{:S(2)}) %collective-permute-start) | collective-permute-done | bytes 262176 | tf_op jit(solution)/shard_map/feature_halo/ppermute | solution.py:209
  49.0 1.5 %aggregate_features.1 = bf16[512,128]{1,0:T(8,128)(2,1)S(1)} custom-call(bf16[10,512,512]{2,1,0:T(8,128)(2,1)S(1)} %dense_tiles.1.dense, bf16[2,512,128]{2,1,0:T(8,128)(2,1)S(1)} %collective-permute-done.xa, bf16[2,512,128]{2,1,0:T(8,128)(2,1)S(1)} %collective-permute-done.1.xb, bf16[2,512,128]{2,1,0:T(8,128)(2,1)S(1)} %bitcast.18, ...), custom_call_target="tpu_custom_call" | custom-call | flops 671088640 | bytes 8388608 | tf_op jit(solution)/shard_map/aggregate_features/pallas_call | solution.py:90
  50.5 8.7 %all-gather.1 = bf16[2048,128]{1,0:T(8,128)(2,1)S(1)} all-gather(bf16[512,128]{1,0:T(8,128)(2,1)S(1)} %aggregate_features.1), channel_id=3, replica_groups=mesh['y'=8,'z'=12,'xl'=2,'xh'=2,'core'=2] {'xh','core'}, dimensions={0}, use_global_device_ids=true | all-gather | bytes 655360 | tf_op jit(solution)/shard_map/column_gather/all_gather | solution.py:226
  59.2 0.0 copy-done.1
  59.2 2.0 %activation_and_terms.1 = (bf16[512,128]{1,0:T(8,128)(2,1)}, f32[576,128]{1,0:T(8,128)S(1)}, bf16[2,128,512]{2,1,0:T(8,128)(2,1)S(1)}, bf16[2,128,512]{2,1,0:T(8...) custom-call(s32[1]{0:T(128)} %bitcast.column, ...), custom_call_target="tpu_custom_call" | custom-call | flops 1275068416 | bytes 10485760 | tf_op jit(solution)/shard_map/activation_and_terms/pallas_call | solution.py:141
  61.2 18.4 %all_to_all.15 = f32[24,24,128]{2,1,0:T(8,128)S(1)} all-to-all(f32[24,24,128]{2,1,0:T(8,128)S(1)} %bitcast.19), channel_id=1, replica_groups=mesh['y'=8,'z'=12,'xl'=2,'xh'=2,'core'=2] {'z','xl'}, dimensions={0} | all-to-all | bytes 589824 | tf_op jit(solution)/shard_map/weight_sum/all_to_all | solution.py:239
  79.7 14.7 %all_to_all.16 = f32[8,24,128]{2,1,0:T(8,128)S(1)} all-to-all(f32[8,24,128]{2,1,0:T(8,128)S(1)} %broadcast_in_dim.7), channel_id=1, replica_groups=mesh['y'=8,'z'=12,'xl'=2,'xh'=2,'core'=2] {'y'}, dimensions={0} | all-to-all | bytes 196608 | tf_op jit(solution)/shard_map/weight_sum/all_to_all | solution.py:241
  94.4 0.7 broadcast_in_dim.8
  95.1 6.9 %all-to-all-start.2 = ((f32[24,24,128]{2,1,0:T(8,128)}), f32[24,24,128]{2,1,0:T(8,128)S(1)}, u32[]{:S(2)}, u32[]{:S(2)}) async-start(f32[24,24,128]{2,1,0:T(8,128)} %broadcast_in_dim.8), calls=%async_computation.2 | async-start | bytes 589824 | tf_op jit(solution)/shard_map/weight_sum/all_to_all | solution.py:245
  102.1 4.5 %collective-permute-start.4 = (bf16[2,128,512]{2,1,0:T(8,128)(2,1)S(1)}, bf16[2,128,512]{2,1,0:T(8,128)(2,1)S(1)}, u32[]{:S(2)}, u32[]{:S(2)}) collective-permute-start(bf16[2,128,512]{2,1,0:T(8,128)(2,1)S(1)} %get-tuple-element.15), channel_id=1, source_target_pairs={{16,0},{20,4},{24,8},{28,12},{32,16},{36,20},{40,24},{44,28},{48,3... | collective-permute-start | bytes 786440 | tf_op jit(solution)/shard_map/term_halo/ppermute | solution.py:209
  106.6 3.4 %collective-permute-start.5 = (bf16[2,128,512]{2,1,0:T(8,128)(2,1)S(1)}, bf16[2,128,512]{2,1,0:T(8,128)(2,1)S(1)}, u32[]{:S(2)}, u32[]{:S(2)}) collective-permute-start(bf16[2,128,512]{2,1,0:T(8,128)(2,1)S(1)} %get-tuple-element.16), channel_id=1, source_target_pairs={{8,0},{12,4},{16,8},{20,12},{24,16},{28,20},{32,24},{36,28},{40,32... | collective-permute-start | bytes 786440 | tf_op jit(solution)/shard_map/term_halo/ppermute | solution.py:209
  110.0 2.5 %collective-permute-start.6 = (bf16[2,128,512]{2,1,0:T(8,128)(2,1)S(1)}, bf16[2,128,512]{2,1,0:T(8,128)(2,1)S(1)}, u32[]{:S(2)}, u32[]{:S(2)}) collective-permute-start(bf16[2,128,512]{2,1,0:T(8,128)(2,1)S(1)} %get-tuple-element.17), channel_id=1, source_target_pairs={{760,0},{764,4},{0,8},{4,12},{8,16},{12,20},{16,24},{20,28},{24,32... | collective-permute-start | bytes 786440 | tf_op jit(solution)/shard_map/term_halo/ppermute | solution.py:209
  112.5 3.4 %collective-permute-start.7 = (bf16[2,128,512]{2,1,0:T(8,128)(2,1)S(1)}, bf16[2,128,512]{2,1,0:T(8,128)(2,1)S(1)}, u32[]{:S(2)}, u32[]{:S(2)}) collective-permute-start(bf16[2,128,512]{2,1,0:T(8,128)(2,1)S(1)} %get-tuple-element.18), channel_id=1, source_target_pairs={{752,0},{756,4},{760,8},{764,12},{0,16},{4,20},{8,24},{12,28},{16,... | collective-permute-start | bytes 786440 | tf_op jit(solution)/shard_map/term_halo/ppermute | solution.py:209
  115.9 9.8 %collective-permute-done.4.ta = bf16[2,128,512]{2,1,0:T(8,128)(2,1)S(1)} collective-permute-done((bf16[2,128,512]{2,1,0:T(8,128)(2,1)S(1)}, bf16[2,128,512]{2,1,0:T(8,128)(2,1)S(1)}, u32[]{:S(2)}, u32[]{:S(2)}) %collective-permute-start.4) | collective-permute-done | bytes 262176 | tf_op jit(solution)/shard_map/term_halo/ppermute | solution.py:209
  125.7 2.2 %collective-permute-done.5.tb = bf16[2,128,512]{2,1,0:T(8,128)(2,1)S(1)} collective-permute-done((bf16[2,128,512]{2,1,0:T(8,128)(2,1)S(1)}, bf16[2,128,512]{2,1,0:T(8,128)(2,1)S(1)}, u32[]{:S(2)}, u32[]{:S(2)}) %collective-permute-start.5) | collective-permute-done | bytes 262176 | tf_op jit(solution)/shard_map/term_halo/ppermute | solution.py:209
  127.9 0.0 collective-permute-done.6.td
  127.9 3.8 %collective-permute-done.7.te = bf16[2,128,512]{2,1,0:T(8,128)(2,1)S(1)} collective-permute-done((bf16[2,128,512]{2,1,0:T(8,128)(2,1)S(1)}, bf16[2,128,512]{2,1,0:T(8,128)(2,1)S(1)}, u32[]{:S(2)}, u32[]{:S(2)}) %collective-permute-start.7) | collective-permute-done | bytes 262176 | tf_op jit(solution)/shard_map/term_halo/ppermute | solution.py:209
  131.7 0.2 pair_sums.1
  132.0 3.4 %collective-permute-start.8 = (bf16[128,512]{1,0:T(8,128)(2,1)S(1)}, bf16[128,512]{1,0:T(8,128)(2,1)S(1)}, u32[]{:S(2)}, u32[]{:S(2)}) collective-permute-start(bf16[128,512]{1,0:T(8,128)(2,1)S(1)} %get-tuple-element.20), channel_id=1, source_target_pairs={{4,0},{0,4},{12,8},{8,12},{20,16},{16,20},{28,24},{24,28},{36,32},... | collective-permute-start | bytes 393224 | tf_op jit(solution)/shard_map/term_exchange/ppermute | solution.py:234
  135.3 3.5 %collective-permute-done.8.arrived = bf16[128,512]{1,0:T(8,128)(2,1)S(1)} collective-permute-done((bf16[128,512]{1,0:T(8,128)(2,1)S(1)}, bf16[128,512]{1,0:T(8,128)(2,1)S(1)}, u32[]{:S(2)}, u32[]{:S(2)}) %collective-permute-start.8) | collective-permute-done | bytes 131104 | tf_op jit(solution)/shard_map/term_exchange/ppermute | solution.py:234
  138.8 0.8 node_gradient.1
  139.6 0.0 all-to-all-done.2
  139.6 0.5 slice_bitcast_fusion
  140.1 0.7 slice.8
  (6 shorter events, 0.1 us)
Async XLA Ops:
  0.6 37.5 %copy-start.3 = (bf16[512,128]{1,0:T(8,128)(2,1)S(1)}, bf16[512,128]{1,0:T(8,128)(2,1)}, u32[]{:S(2)}) copy-start(bf16[512,128]{1,0:T(8,128)(2,1)} %param.11) | copy-start | bytes 393220
  0.6 37.5 %copy-start.4 = (bf16[128]{0:T(256)(128)(2,1)S(1)}, bf16[128]{0:T(256)(128)(2,1)}, u32[]{:S(2)}) copy-start(bf16[128]{0:T(256)(128)(2,1)} %param.10) | copy-start | bytes 772
  6.9 40.2 %collective-permute-start.3 = (bf16[2,512,128]{2,1,0:T(8,128)(2,1)S(1)}, bf16[2,512,128]{2,1,0:T(8,128)(2,1)S(1)}, u32[]{:S(2)}, u32[]{:S(2)}) collective-permute-start(bf16[2,512,128]{2,1,0:T(8,128)(2,1)S(1)} %bitcast.14), channel_id=1, source_target_pairs={{16,0},{20,4},{24,8},{28,12},{32,16},{36,20},{40,24},{44,28},{48,3... | collective-permute-start | bytes 786440 | tf_op jit(solution)/shard_map/feature_halo/ppermute | solution.py:209
  23.5 23.6 %collective-permute-start.2 = (bf16[2,512,128]{2,1,0:T(8,128)(2,1)S(1)}, bf16[2,512,128]{2,1,0:T(8,128)(2,1)S(1)}, u32[]{:S(2)}, u32[]{:S(2)}) collective-permute-start(bf16[2,512,128]{2,1,0:T(8,128)(2,1)S(1)} %bitcast.15), channel_id=1, source_target_pairs={{8,0},{12,4},{16,8},{20,12},{24,16},{28,20},{32,24},{36,28},{40,32... | collective-permute-start | bytes 786440 | tf_op jit(solution)/shard_map/feature_halo/ppermute | solution.py:209
  26.0 21.2 %collective-permute-start.1 = (bf16[2,512,128]{2,1,0:T(8,128)(2,1)S(1)}, bf16[2,512,128]{2,1,0:T(8,128)(2,1)S(1)}, u32[]{:S(2)}, u32[]{:S(2)}) collective-permute-start(bf16[2,512,128]{2,1,0:T(8,128)(2,1)S(1)} %bitcast.16), channel_id=1, source_target_pairs={{760,0},{764,4},{0,8},{4,12},{8,16},{12,20},{16,24},{20,28},{24,32... | collective-permute-start | bytes 786440 | tf_op jit(solution)/shard_map/feature_halo/ppermute | solution.py:209
  29.3 19.7 %collective-permute-start = (bf16[2,512,128]{2,1,0:T(8,128)(2,1)S(1)}, bf16[2,512,128]{2,1,0:T(8,128)(2,1)S(1)}, u32[]{:S(2)}, u32[]{:S(2)}) collective-permute-start(bf16[2,512,128]{2,1,0:T(8,128)(2,1)S(1)} %bitcast.17), channel_id=1, source_target_pairs={{752,0},{756,4},{760,8},{764,12},{0,16},{4,20},{8,24},{12,28},{16,... | collective-permute-start | bytes 786440 | tf_op jit(solution)/shard_map/feature_halo/ppermute | solution.py:209
  32.9 2.3 %copy-start = (bf16[1,9,16,128,128]{4,3,2,1,0:T(8,128)(2,1)S(1)}, bf16[1,9,16,128,128]{4,3,2,1,0:T(8,128)(2,1)}, u32[]{:S(2)}) copy-start(bf16[1,9,16,128,128]{4,3,2,1,0:T(8,128)(2,1)} %param.12) | copy-start | bytes 14155780
  35.2 0.7 copy-start.2
  38.1 21.1 %copy-start.1 = (bf16[512,512]{1,0:T(8,128)(2,1)S(1)}, bf16[512,512]{1,0:T(8,128)(2,1)}, u32[]{:S(2)}) copy-start(bf16[512,512]{1,0:T(8,128)(2,1)} %weight.1) | copy-start | bytes 1572868
  95.1 44.5 %all-to-all-start.2 = ((f32[24,24,128]{2,1,0:T(8,128)}), f32[24,24,128]{2,1,0:T(8,128)S(1)}, u32[]{:S(2)}, u32[]{:S(2)}) async-start(f32[24,24,128]{2,1,0:T(8,128)} %broadcast_in_dim.8), calls=%async_computation.2 | async-start | bytes 589824 | tf_op jit(solution)/shard_map/weight_sum/all_to_all | solution.py:245
  102.1 23.6 %collective-permute-start.4 = (bf16[2,128,512]{2,1,0:T(8,128)(2,1)S(1)}, bf16[2,128,512]{2,1,0:T(8,128)(2,1)S(1)}, u32[]{:S(2)}, u32[]{:S(2)}) collective-permute-start(bf16[2,128,512]{2,1,0:T(8,128)(2,1)S(1)} %get-tuple-element.15), channel_id=1, source_target_pairs={{16,0},{20,4},{24,8},{28,12},{32,16},{36,20},{40,24},{44,28},{48,3... | collective-permute-start | bytes 786440 | tf_op jit(solution)/shard_map/term_halo/ppermute | solution.py:209
  106.6 21.3 %collective-permute-start.5 = (bf16[2,128,512]{2,1,0:T(8,128)(2,1)S(1)}, bf16[2,128,512]{2,1,0:T(8,128)(2,1)S(1)}, u32[]{:S(2)}, u32[]{:S(2)}) collective-permute-start(bf16[2,128,512]{2,1,0:T(8,128)(2,1)S(1)} %get-tuple-element.16), channel_id=1, source_target_pairs={{8,0},{12,4},{16,8},{20,12},{24,16},{28,20},{32,24},{36,28},{40,32... | collective-permute-start | bytes 786440 | tf_op jit(solution)/shard_map/term_halo/ppermute | solution.py:209
  110.0 17.9 %collective-permute-start.6 = (bf16[2,128,512]{2,1,0:T(8,128)(2,1)S(1)}, bf16[2,128,512]{2,1,0:T(8,128)(2,1)S(1)}, u32[]{:S(2)}, u32[]{:S(2)}) collective-permute-start(bf16[2,128,512]{2,1,0:T(8,128)(2,1)S(1)} %get-tuple-element.17), channel_id=1, source_target_pairs={{760,0},{764,4},{0,8},{4,12},{8,16},{12,20},{16,24},{20,28},{24,32... | collective-permute-start | bytes 786440 | tf_op jit(solution)/shard_map/term_halo/ppermute | solution.py:209
  112.5 19.2 %collective-permute-start.7 = (bf16[2,128,512]{2,1,0:T(8,128)(2,1)S(1)}, bf16[2,128,512]{2,1,0:T(8,128)(2,1)S(1)}, u32[]{:S(2)}, u32[]{:S(2)}) collective-permute-start(bf16[2,128,512]{2,1,0:T(8,128)(2,1)S(1)} %get-tuple-element.18), channel_id=1, source_target_pairs={{752,0},{756,4},{760,8},{764,12},{0,16},{4,20},{8,24},{12,28},{16,... | collective-permute-start | bytes 786440 | tf_op jit(solution)/shard_map/term_halo/ppermute | solution.py:209
  132.0 6.9 %collective-permute-start.8 = (bf16[128,512]{1,0:T(8,128)(2,1)S(1)}, bf16[128,512]{1,0:T(8,128)(2,1)S(1)}, u32[]{:S(2)}, u32[]{:S(2)}) collective-permute-start(bf16[128,512]{1,0:T(8,128)(2,1)S(1)} %get-tuple-element.20), channel_id=1, source_target_pairs={{4,0},{0,4},{12,8},{8,12},{20,16},{16,20},{28,24},{24,28},{36,32},... | collective-permute-start | bytes 393224 | tf_op jit(solution)/shard_map/term_exchange/ppermute | solution.py:234

commit v2 on v1

--- a/solution.py
+++ b/solution.py
@@ -31,8 +31,8 @@
 SMEM = pl.BlockSpec(memory_space=pltpu.SMEM)
 
 
-def params(**more):
-    return pltpu.CompilerParams(vmem_limit_bytes=32 * 1024 * 1024, **more)
+def params(mib=32):
+    return pltpu.CompilerParams(vmem_limit_bytes=mib * 1024 * 1024)
 
 
 def dense_kernel(side, rows, cols, counts, slab, dense):
@@ -42,12 +42,11 @@
 
     @pl.when(inside)
     def _():
-        live = counts[offset]
+        live = counts[0, offset]
         for slot in range(SLOTS):
-            at = offset * SLOTS + slot
-            row = pl.multiple_of(rows[at] * TILE, TILE)
-            col = pl.multiple_of(cols[at] * TILE, TILE)
-            tile = slab[0, slot]
+            row = pl.multiple_of(rows[0, offset, slot] * TILE, TILE)
+            col = pl.multiple_of(cols[0, offset, slot] * TILE, TILE)
+            tile = slab[0, 0, slot]
             dense[0, pl.ds(row, TILE), pl.ds(col, TILE)] = jnp.where(
                 slot < live, tile, jnp.zeros_like(tile)
             )
@@ -65,8 +64,8 @@
             grid=(WINDOW,),
             in_specs=[
                 pl.BlockSpec(
-                    (1, SLOTS, TILE, TILE),
-                    lambda j, side, *_: (jnp.clip(j - side[0], 0, OFFSETS - 1), 0, 0, 0),
+                    (1, 1, SLOTS, TILE, TILE),
+                    lambda j, side, *_: (0, jnp.clip(j - side[0], 0, OFFSETS - 1), 0, 0, 0),
                 )
             ],
             out_specs=pl.BlockSpec((1, ROWS, ROWS), lambda j, *_: (j, 0, 0)),
@@ -156,7 +155,7 @@
     )(column, mixed, packed, weight, dense)
 
 
-def split_kernel(side, own, ta, tb, td, te, keep, send):
+def split_kernel(side, own, ta, tb, td, te, shares, keep, send, spread):
     for s in range(2):
         total = own[s].astype(F32)
         for arrived in (ta, tb, td, te):
@@ -170,36 +169,44 @@
         def _():
             send[...] = total.astype(BF16)
 
-
-def split_terms(side, own, arrived):
+    spread[...] = jnp.broadcast_to(jnp.sum(shares[...], axis=0)[None], spread.shape)
+
+
+def split_terms(side, own, arrived, shares):
     return pl.pallas_call(
         split_kernel,
-        in_specs=[SMEM] + [VMEM] * 5,
-        out_specs=[VMEM] * 2,
+        in_specs=[SMEM] + [VMEM] * 6,
+        out_specs=[VMEM] * 3,
         out_shape=[
             jax.ShapeDtypeStruct((WIDTH, ROWS), F32),
             jax.ShapeDtypeStruct((WIDTH, ROWS), BF16),
+            jax.ShapeDtypeStruct((N_Y, SHARE, WIDTH), F32),
         ],
         compiler_params=params(),
         cost_estimate=pl.CostEstimate(flops=1 << 20, bytes_accessed=2 << 20, transcendentals=0),
         name="pair_sums",
-    )(side, own, *arrived)
-
-
-def last_kernel(keep, arrived, out):
+    )(side, own, *arrived, shares)
+
+
+def last_kernel(keep, arrived, shares, out, spread):
     out[...] = (keep[...] + arrived[...].astype(F32)).T.astype(BF16)
-
-
-def last_sum(keep, arrived):
+    total = jnp.sum(shares[...], axis=0) * (1.0 / jnp.sqrt(F32(NODES)))
+    spread[...] = jnp.broadcast_to(total.astype(BF16)[None], spread.shape)
+
+
+def last_sum(keep, arrived, shares):
     return pl.pallas_call(
         last_kernel,
-        in_specs=[VMEM] * 2,
-        out_specs=VMEM,
-        out_shape=jax.ShapeDtypeStruct((ROWS, WIDTH), BF16),
+        in_specs=[VMEM] * 3,
+        out_specs=[VMEM] * 2,
+        out_shape=[
+            jax.ShapeDtypeStruct((ROWS, WIDTH), BF16),
+            jax.ShapeDtypeStruct((RING, SHARE, WIDTH), BF16),
+        ],
         compiler_params=params(),
         cost_estimate=pl.CostEstimate(flops=1 << 17, bytes_accessed=1 << 19, transcendentals=0),
         name="node_gradient",
-    )(keep, arrived)
+    )(keep, arrived, shares)
 
 
 def from_pair(block, hops):
@@ -213,39 +220,33 @@
     side = lax.axis_index("xl").astype(jnp.int32).reshape(1)
     column = lax.axis_index(COL).astype(jnp.int32).reshape(1)
 
-    dense = make_dense(
-        side, tile_row.reshape(-1), tile_col.reshape(-1), tile_count.reshape(-1), adj_tiles[0]
-    )
+    dense = make_dense(side, tile_row, tile_col, tile_count, adj_tiles)
     with jax.named_scope("feature_halo"):
         pair = lax.all_gather(node_feats, "xl", axis=0, tiled=False)
         pairs = [pair if k == 0 else from_pair(pair, k) for k in (-2, -1, 0, 1, 2)]
     mine = gather_rows(dense, pairs)
     with jax.named_scope("column_gather"):
         packed = jnp.concatenate([cotangent, jnp.broadcast_to(layer_bias[None], (16, WIDTH))], axis=0)
-        packed = lax.all_gather(packed, COL, axis=0, tiled=False)
+        packed = jnp.broadcast_to(packed[None], (COLS, PACK_ROWS, WIDTH))
+        packed = lax.all_to_all(packed, COL, 0, 0, tiled=True)
         mixed = lax.all_gather(mine, COL, axis=0, tiled=False)
     act, part, ta, tb, tc, td, te = middle(column, mixed, packed, weight, dense)
 
+    ring = ("z", "xl")
+    with jax.named_scope("weight_scatter"):
+        shares = lax.all_to_all(part.reshape(RING, SHARE, WIDTH), ring, 0, 0, tiled=True)
     with jax.named_scope("term_halo"):
         arrived = [from_pair(t, -k) for k, t in ((-2, ta), (-1, tb), (1, td), (2, te))]
-    keep, send = split_terms(side, tc, arrived)
+    keep, send, spread = split_terms(side, tc, arrived, shares)
+    with jax.named_scope("weight_rows"):
+        shares = lax.all_to_all(spread, "y", 0, 0, tiled=True)
     with jax.named_scope("term_exchange"):
         swap = [(b ^ 1, b) for b in range(2 * PAIRS)]
         other = lax.ppermute(send, BLK, swap)
-    grad_nodes = last_sum(keep, other)
-
-    with jax.named_scope("weight_sum"):
-        ring = ("z", "xl")
-        shares = lax.all_to_all(part.reshape(RING, SHARE, WIDTH), ring, 0, 0, tiled=True)
-        share = jnp.sum(shares, axis=0)
-        shares = lax.all_to_all(
-            jnp.broadcast_to(share[None], (N_Y, SHARE, WIDTH)), "y", 0, 0, tiled=True
-        )
-        share = jnp.sum(shares, axis=0) * (1.0 / jnp.sqrt(F32(NODES)))
-        whole = lax.all_to_all(
-            jnp.broadcast_to(share[None], (RING, SHARE, WIDTH)), ring, 0, 0, tiled=True
-        ).reshape(RING * SHARE, WIDTH)
-    return act, grad_nodes, whole[:HIDDEN], whole[HIDDEN]
+    grad_nodes, spread = last_sum(keep, other, shares)
+    with jax.named_scope("weight_gather"):
+        whole = lax.all_to_all(spread, ring, 0, 0, tiled=True).reshape(RING * SHARE, WIDTH)
+    return act, grad_nodes, whole[:HIDDEN].astype(F32), whole[HIDDEN].astype(F32)
 
 
 def solution(mesh):

time: 141 us -> 138 us (0.979)
  the two profiles are of different devices: /device:TPU:64 before, /device:TPU:4 now
where the time goes in v2:
time: 138 us; the launch traced here: 137 us
  starting transfers between devices  59 us (43%)
  blocking collectives  34.2 us (25%)
  waiting for transfers between devices  22.2 us (16%)
  local copies, waits for them, and re-layouts  10.7 us (8%)
  Pallas kernels  8.28 us (6%)
  other arithmetic  2.15 us (2%)
    ppermute x8, starting transfers between devices, from_pair(): return lax.ppermute(block, BLK, route)  41.6 us
    all_to_all x1, blocking collectives, on_device(): lax.all_to_all(spread, ring, 0, 0, tiled=True).reshape(RING * SHARE, WIDTH)  20.1 us
    ppermute x8, waiting for transfers between devices, from_pair(): return lax.ppermute(block, BLK, route)  16.8 us
    unnamed x12, local copies, waits for them, and re-layouts  9.18 us
    all_gather x1, blocking collectives, on_device(): mixed = lax.all_gather(mine, COL, axis=0, tiled=False)  8 us
    all_gather x1, blocking collectives, on_device(): pair = lax.all_gather(node_feats, 'xl', axis=0, tiled=False)  6.13 us
    all_to_all x1, starting transfers between devices, on_device(): lax.all_to_all(part.reshape(RING, SHARE, WIDTH), ring, 0, 0, tiled=True)  5.13 us
    all_to_all x1, starting transfers between devices, on_device(): packed = lax.all_to_all(packed, COL, 0, 0, tiled=True)  4.8 us
  transfers between devices with their start and end apart: 12, of which 6 were waited for; matrix products, arithmetic and copies ran while one was open for 3% of the time, Pallas kernels for 3%

profile of v2, /device:TPU:4, one launch (start us, length us, event | category | flops | bytes accessed | tf_op | source)
XLA Modules:
  0.0 137.3 jit_solution(944238471913302770)
XLA Ops:
  0.6 6.1 %all-gather = bf16[1024,128]{1,0:T(8,128)(2,1)S(1)} all-gather(bf16[512,128]{1,0:T(8,128)(2,1)} %param.8), channel_id=2, replica_groups=mesh['y'=8,'z'=12,'xl'=2,'xh'=2,'core'=2] {'xl'}, dimensions={0}, use_global_device_ids=true | all-gather | bytes 393216 | tf_op jit(solution)/shard_map/feature_halo/all_gather | solution.py:225
  6.8 17.5 %collective-permute-start.3 = (bf16[2,512,128]{2,1,0:T(8,128)(2,1)S(1)}, bf16[2,512,128]{2,1,0:T(8,128)(2,1)S(1)}, u32[]{:S(2)}, u32[]{:S(2)}) collective-permute-start(bf16[2,512,128]{2,1,0:T(8,128)(2,1)S(1)} %bitcast.12), channel_id=1, source_target_pairs={{16,0},{20,4},{24,8},{28,12},{32,16},{36,20},{40,24},{44,28},{48,3... | collective-permute-start | bytes 786440 | tf_op jit(solution)/shard_map/feature_halo/ppermute | solution.py:216
  24.2 2.5 %collective-permute-start.2 = (bf16[2,512,128]{2,1,0:T(8,128)(2,1)S(1)}, bf16[2,512,128]{2,1,0:T(8,128)(2,1)S(1)}, u32[]{:S(2)}, u32[]{:S(2)}) collective-permute-start(bf16[2,512,128]{2,1,0:T(8,128)(2,1)S(1)} %bitcast.13), channel_id=1, source_target_pairs={{8,0},{12,4},{16,8},{20,12},{24,16},{28,20},{32,24},{36,28},{40,32... | collective-permute-start | bytes 786440 | tf_op jit(solution)/shard_map/feature_halo/ppermute | solution.py:216
  26.7 3.4 %collective-permute-start.1 = (bf16[2,512,128]{2,1,0:T(8,128)(2,1)S(1)}, bf16[2,512,128]{2,1,0:T(8,128)(2,1)S(1)}, u32[]{:S(2)}, u32[]{:S(2)}) collective-permute-start(bf16[2,512,128]{2,1,0:T(8,128)(2,1)S(1)} %bitcast.14), channel_id=1, source_target_pairs={{760,0},{764,4},{0,8},{4,12},{8,16},{12,20},{16,24},{20,28},{24,32... | collective-permute-start | bytes 786440 | tf_op jit(solution)/shard_map/feature_halo/ppermute | solution.py:216
  30.1 2.8 %collective-permute-start = (bf16[2,512,128]{2,1,0:T(8,128)(2,1)S(1)}, bf16[2,512,128]{2,1,0:T(8,128)(2,1)S(1)}, u32[]{:S(2)}, u32[]{:S(2)}) collective-permute-start(bf16[2,512,128]{2,1,0:T(8,128)(2,1)S(1)} %bitcast.15), channel_id=1, source_target_pairs={{752,0},{756,4},{760,8},{764,12},{0,16},{4,20},{8,24},{12,28},{16,... | collective-permute-start | bytes 786440 | tf_op jit(solution)/shard_map/feature_halo/ppermute | solution.py:216
  32.9 0.7 broadcast_in_dim.4
  33.6 0.9 pad_maximum_fusion
  34.5 0.9 broadcast_in_dim.5
  35.4 4.8 %all-to-all-start = ((bf16[4,528,128]{2,1,0:T(8,128)(2,1)}), bf16[4,528,128]{2,1,0:T(8,128)(2,1)S(1)}, u32[]{:S(2)}, u32[]{:S(2)}) async-start(bf16[4,528,128]{2,1,0:T(8,128)(2,1)} %broadcast_in_dim.5), calls=%async_computation | async-start | bytes 1081344 | tf_op jit(solution)/shard_map/column_gather/all_to_all | solution.py:231
  40.2 0.7 copy.12.rows
  40.9 0.7 copy.13.cols
  41.5 0.0 copy-start.2
  41.6 2.3 %copy-done.2 = bf16[1,9,16,128,128]{4,3,2,1,0:T(8,128)(2,1)S(1)} copy-done((bf16[1,9,16,128,128]{4,3,2,1,0:T(8,128)(2,1)S(1)}, bf16[1,9,16,128,128]{4,3,2,1,0:T(8,128)(2,1)}, u32[]{:S(2)}) %copy-start.2) | copy-done | bytes 4718616
  43.9 0.0 copy-start.4
  43.9 0.7 copy-done.4
  44.5 2.5 %dense_tiles.1.dense = bf16[10,512,512]{2,1,0:T(8,128)(2,1)S(1)} custom-call(s32[1]{0:T(128)} %bitcast.1.side, s32[1,9,16]{2,1,0:T(8,128)S(1)} %copy.12.rows, s32[1,9,16]{2,1,0:T(8,128)S(1)} %copy.13.cols, s32[1,9]{1,0:T(1,128)S(1)} %copy-done.4, bf16[1,9,16,128,128]{4,3,2,1,0:T(8,128)(2,1)S(1)} %copy-done.2), custom_call_target="tpu_custom_call" | custom-call | bytes 10485760 | tf_op jit(solution)/shard_map/dense_tiles/pallas_call | solution.py:60
  47.0 0.0 copy-start.3
  47.0 0.0 collective-permute-done.3.xe
  47.1 0.0 collective-permute-done.2.xd
  47.1 0.0 collective-permute-done.1.xb
  47.1 1.2 collective-permute-done.xa
  48.3 1.5 %aggregate_features.1 = bf16[512,128]{1,0:T(8,128)(2,1)S(1)} custom-call(bf16[10,512,512]{2,1,0:T(8,128)(2,1)S(1)} %dense_tiles.1.dense, bf16[2,512,128]{2,1,0:T(8,128)(2,1)S(1)} %collective-permute-done.xa, bf16[2,512,128]{2,1,0:T(8,128)(2,1)S(1)} %collective-permute-done.1.xb, bf16[2,512,128]{2,1,0:T(8,128)(2,1)S(1)} %bitcast.16, ...), custom_call_target="tpu_custom_call" | custom-call | flops 671088640 | bytes 8388608 | tf_op jit(solution)/shard_map/aggregate_features/pallas_call | solution.py:89
  49.8 0.0 copy-start
  49.8 2.3 %copy-done = bf16[10,512,512]{2,1,0:T(8,128)(2,1)} copy-done((bf16[10,512,512]{2,1,0:T(8,128)(2,1)}, bf16[10,512,512]{2,1,0:T(8,128)(2,1)S(1)}, u32[]{:S(2)}) %copy-start) | copy-done | bytes 5242904
  52.1 8.0 %all-gather.1 = bf16[2048,128]{1,0:T(8,128)(2,1)S(1)} all-gather(bf16[512,128]{1,0:T(8,128)(2,1)S(1)} %aggregate_features.1), channel_id=3, replica_groups=mesh['y'=8,'z'=12,'xl'=2,'xh'=2,'core'=2] {'xh','core'}, dimensions={0}, use_global_device_ids=true | all-gather | bytes 655360 | tf_op jit(solution)/shard_map/column_gather/all_gather | solution.py:232
  60.1 0.0 all-to-all-done.packed
  60.1 0.0 copy-done.3
  60.1 0.0 copy-start.1
  60.1 2.5 %copy-done.1 = bf16[10,512,512]{2,1,0:T(8,128)(2,1)S(1)} copy-done((bf16[10,512,512]{2,1,0:T(8,128)(2,1)S(1)}, bf16[10,512,512]{2,1,0:T(8,128)(2,1)}, u32[]{:S(2)}) %copy-start.1) | copy-done | bytes 5242904
  62.6 2.6 %activation_and_terms.1 = (bf16[512,128]{1,0:T(8,128)(2,1)}, f32[576,128]{1,0:T(8,128)}, bf16[2,128,512]{2,1,0:T(8,128)(2,1)S(1)}, bf16[2,128,512]{2,1,0:T(8,128...) custom-call(s32[1]{0:T(128)} %bitcast.column, ...), custom_call_target="tpu_custom_call" | custom-call | flops 1275068416 | bytes 10485760 | tf_op jit(solution)/shard_map/activation_and_terms/pallas_call | solution.py:140
  65.2 5.1 %all-to-all-start.1 = ((f32[24,24,128]{2,1,0:T(8,128)}), f32[24,24,128]{2,1,0:T(8,128)S(1)}, u32[]{:S(2)}, u32[]{:S(2)}) async-start(f32[24,24,128]{2,1,0:T(8,128)} %bitcast.4), calls=%async_computation.1 | async-start | bytes 589824 | tf_op jit(solution)/shard_map/weight_scatter/all_to_all | solution.py:237
  70.4 7.7 %collective-permute-start.4 = (bf16[2,128,512]{2,1,0:T(8,128)(2,1)S(1)}, bf16[2,128,512]{2,1,0:T(8,128)(2,1)S(1)}, u32[]{:S(2)}, u32[]{:S(2)}) collective-permute-start(bf16[2,128,512]{2,1,0:T(8,128)(2,1)S(1)} %get-tuple-element.18), channel_id=1, source_target_pairs={{16,0},{20,4},{24,8},{28,12},{32,16},{36,20},{40,24},{44,28},{48,3... | collective-permute-start | bytes 786440 | tf_op jit(solution)/shard_map/term_halo/ppermute | solution.py:216
  78.1 3.4 %collective-permute-start.5 = (bf16[2,128,512]{2,1,0:T(8,128)(2,1)S(1)}, bf16[2,128,512]{2,1,0:T(8,128)(2,1)S(1)}, u32[]{:S(2)}, u32[]{:S(2)}) collective-permute-start(bf16[2,128,512]{2,1,0:T(8,128)(2,1)S(1)} %get-tuple-element.19), channel_id=1, source_target_pairs={{8,0},{12,4},{16,8},{20,12},{24,16},{28,20},{32,24},{36,28},{40,32... | collective-permute-start | bytes 786440 | tf_op jit(solution)/shard_map/term_halo/ppermute | solution.py:216
  81.4 2.5 %collective-permute-start.6 = (bf16[2,128,512]{2,1,0:T(8,128)(2,1)S(1)}, bf16[2,128,512]{2,1,0:T(8,128)(2,1)S(1)}, u32[]{:S(2)}, u32[]{:S(2)}) collective-permute-start(bf16[2,128,512]{2,1,0:T(8,128)(2,1)S(1)} %get-tuple-element.20), channel_id=1, source_target_pairs={{760,0},{764,4},{0,8},{4,12},{8,16},{12,20},{16,24},{20,28},{24,32... | collective-permute-start | bytes 786440 | tf_op jit(solution)/shard_map/term_halo/ppermute | solution.py:216
  83.9 1.9 %collective-permute-start.7 = (bf16[2,128,512]{2,1,0:T(8,128)(2,1)S(1)}, bf16[2,128,512]{2,1,0:T(8,128)(2,1)S(1)}, u32[]{:S(2)}, u32[]{:S(2)}) collective-permute-start(bf16[2,128,512]{2,1,0:T(8,128)(2,1)S(1)} %get-tuple-element.21), channel_id=1, source_target_pairs={{752,0},{756,4},{760,8},{764,12},{0,16},{4,20},{8,24},{12,28},{16,... | collective-permute-start | bytes 786440 | tf_op jit(solution)/shard_map/term_halo/ppermute | solution.py:216
  85.9 9.6 %collective-permute-done.4.ta = bf16[2,128,512]{2,1,0:T(8,128)(2,1)S(1)} collective-permute-done((bf16[2,128,512]{2,1,0:T(8,128)(2,1)S(1)}, bf16[2,128,512]{2,1,0:T(8,128)(2,1)S(1)}, u32[]{:S(2)}, u32[]{:S(2)}) %collective-permute-start.4) | collective-permute-done | bytes 262176 | tf_op jit(solution)/shard_map/term_halo/ppermute | solution.py:216
  95.5 3.9 %collective-permute-done.5.tb = bf16[2,128,512]{2,1,0:T(8,128)(2,1)S(1)} collective-permute-done((bf16[2,128,512]{2,1,0:T(8,128)(2,1)S(1)}, bf16[2,128,512]{2,1,0:T(8,128)(2,1)S(1)}, u32[]{:S(2)}, u32[]{:S(2)}) %collective-permute-start.5) | collective-permute-done | bytes 262176 | tf_op jit(solution)/shard_map/term_halo/ppermute | solution.py:216
  99.5 2.1 %collective-permute-done.6.td = bf16[2,128,512]{2,1,0:T(8,128)(2,1)S(1)} collective-permute-done((bf16[2,128,512]{2,1,0:T(8,128)(2,1)S(1)}, bf16[2,128,512]{2,1,0:T(8,128)(2,1)S(1)}, u32[]{:S(2)}, u32[]{:S(2)}) %collective-permute-start.6) | collective-permute-done | bytes 262176 | tf_op jit(solution)/shard_map/term_halo/ppermute | solution.py:216
  101.5 0.0 collective-permute-done.7.te
  101.5 0.0 all-to-all-done.1.shares
  101.5 0.9 pair_sums.1
  102.4 4.1 %all-to-all-start.2 = ((f32[8,24,128]{2,1,0:T(8,128)}), f32[8,24,128]{2,1,0:T(8,128)S(1)}, u32[]{:S(2)}, u32[]{:S(2)}) async-start(f32[8,24,128]{2,1,0:T(8,128)} %get-tuple-element.25), calls=%async_computation.2 | async-start | bytes 196608 | tf_op jit(solution)/shard_map/weight_rows/all_to_all | solution.py:242
  106.5 3.4 %collective-permute-start.8 = (bf16[128,512]{1,0:T(8,128)(2,1)S(1)}, bf16[128,512]{1,0:T(8,128)(2,1)S(1)}, u32[]{:S(2)}, u32[]{:S(2)}) collective-permute-start(bf16[128,512]{1,0:T(8,128)(2,1)S(1)} %get-tuple-element.24), channel_id=1, source_target_pairs={{4,0},{0,4},{12,8},{8,12},{20,16},{16,20},{28,24},{24,28},{36,32},... | collective-permute-start | bytes 393224 | tf_op jit(solution)/shard_map/term_exchange/ppermute | solution.py:245
  109.9 3.5 %collective-permute-done.8.arrived = bf16[128,512]{1,0:T(8,128)(2,1)S(1)} collective-permute-done((bf16[128,512]{1,0:T(8,128)(2,1)S(1)}, bf16[128,512]{1,0:T(8,128)(2,1)S(1)}, u32[]{:S(2)}, u32[]{:S(2)}) %collective-permute-start.8) | collective-permute-done | bytes 131104 | tf_op jit(solution)/shard_map/term_exchange/ppermute | solution.py:245
  113.4 1.9 %all-to-all-done.2.shares = f32[8,24,128]{2,1,0:T(8,128)S(1)} async-done(((f32[8,24,128]{2,1,0:T(8,128)}), f32[8,24,128]{2,1,0:T(8,128)S(1)}, u32[]{:S(2)}, u32[]{:S(2)}) %all-to-all-start.2) | async-done | bytes 98336 | tf_op jit(solution)/shard_map/weight_rows/all_to_all | solution.py:242
  115.2 0.8 node_gradient.1
  116.0 20.1 %all_to_all.20 = bf16[24,24,128]{2,1,0:T(8,128)(2,1)S(1)} all-to-all(bf16[24,24,128]{2,1,0:T(8,128)(2,1)S(1)} %get-tuple-element.27), channel_id=1, replica_groups=mesh['y'=8,'z'=12,'xl'=2,'xh'=2,'core'=2] {'z','xl'}, dimensions={0} | all-to-all | bytes 294912 | tf_op jit(solution)/shard_map/weight_gather/all_to_all | solution.py:248
  136.1 0.5 fusion
  136.6 0.7 slice_convert_fusion
Async XLA Ops:
  6.8 40.3 %collective-permute-start.3 = (bf16[2,512,128]{2,1,0:T(8,128)(2,1)S(1)}, bf16[2,512,128]{2,1,0:T(8,128)(2,1)S(1)}, u32[]{:S(2)}, u32[]{:S(2)}) collective-permute-start(bf16[2,512,128]{2,1,0:T(8,128)(2,1)S(1)} %bitcast.12), channel_id=1, source_target_pairs={{16,0},{20,4},{24,8},{28,12},{32,16},{36,20},{40,24},{44,28},{48,3... | collective-permute-start | bytes 786440 | tf_op jit(solution)/shard_map/feature_halo/ppermute | solution.py:216
  24.2 22.8 %collective-permute-start.2 = (bf16[2,512,128]{2,1,0:T(8,128)(2,1)S(1)}, bf16[2,512,128]{2,1,0:T(8,128)(2,1)S(1)}, u32[]{:S(2)}, u32[]{:S(2)}) collective-permute-start(bf16[2,512,128]{2,1,0:T(8,128)(2,1)S(1)} %bitcast.13), channel_id=1, source_target_pairs={{8,0},{12,4},{16,8},{20,12},{24,16},{28,20},{32,24},{36,28},{40,32... | collective-permute-start | bytes 786440 | tf_op jit(solution)/shard_map/feature_halo/ppermute | solution.py:216
  26.7 20.4 %collective-permute-start.1 = (bf16[2,512,128]{2,1,0:T(8,128)(2,1)S(1)}, bf16[2,512,128]{2,1,0:T(8,128)(2,1)S(1)}, u32[]{:S(2)}, u32[]{:S(2)}) collective-permute-start(bf16[2,512,128]{2,1,0:T(8,128)(2,1)S(1)} %bitcast.14), channel_id=1, source_target_pairs={{760,0},{764,4},{0,8},{4,12},{8,16},{12,20},{16,24},{20,28},{24,32... | collective-permute-start | bytes 786440 | tf_op jit(solution)/shard_map/feature_halo/ppermute | solution.py:216
  30.1 18.2 %collective-permute-start = (bf16[2,512,128]{2,1,0:T(8,128)(2,1)S(1)}, bf16[2,512,128]{2,1,0:T(8,128)(2,1)S(1)}, u32[]{:S(2)}, u32[]{:S(2)}) collective-permute-start(bf16[2,512,128]{2,1,0:T(8,128)(2,1)S(1)} %bitcast.15), channel_id=1, source_target_pairs={{752,0},{756,4},{760,8},{764,12},{0,16},{4,20},{8,24},{12,28},{16,... | collective-permute-start | bytes 786440 | tf_op jit(solution)/shard_map/feature_halo/ppermute | solution.py:216
  35.4 24.7 %all-to-all-start = ((bf16[4,528,128]{2,1,0:T(8,128)(2,1)}), bf16[4,528,128]{2,1,0:T(8,128)(2,1)S(1)}, u32[]{:S(2)}, u32[]{:S(2)}) async-start(bf16[4,528,128]{2,1,0:T(8,128)(2,1)} %broadcast_in_dim.5), calls=%async_computation | async-start | bytes 1081344 | tf_op jit(solution)/shard_map/column_gather/all_to_all | solution.py:231
  41.5 2.3 %copy-start.2 = (bf16[1,9,16,128,128]{4,3,2,1,0:T(8,128)(2,1)S(1)}, bf16[1,9,16,128,128]{4,3,2,1,0:T(8,128)(2,1)}, u32[]{:S(2)}) copy-start(bf16[1,9,16,128,128]{4,3,2,1,0:T(8,128)(2,1)} %slab.1) | copy-start | bytes 14155780
  43.9 0.7 copy-start.4
  47.0 13.1 %copy-start.3 = (bf16[512,512]{1,0:T(8,128)(2,1)S(1)}, bf16[512,512]{1,0:T(8,128)(2,1)}, u32[]{:S(2)}) copy-start(bf16[512,512]{1,0:T(8,128)(2,1)} %weight.1) | copy-start | bytes 1572868
  49.8 2.3 %copy-start = (bf16[10,512,512]{2,1,0:T(8,128)(2,1)}, bf16[10,512,512]{2,1,0:T(8,128)(2,1)S(1)}, u32[]{:S(2)}) copy-start(bf16[10,512,512]{2,1,0:T(8,128)(2,1)S(1)} %dense_tiles.1.dense) | copy-start | bytes 15728644
  60.1 2.5 %copy-start.1 = (bf16[10,512,512]{2,1,0:T(8,128)(2,1)S(1)}, bf16[10,512,512]{2,1,0:T(8,128)(2,1)}, u32[]{:S(2)}) copy-start(bf16[10,512,512]{2,1,0:T(8,128)(2,1)} %copy-done) | copy-start | bytes 15728644
  65.2 36.3 %all-to-all-start.1 = ((f32[24,24,128]{2,1,0:T(8,128)}), f32[24,24,128]{2,1,0:T(8,128)S(1)}, u32[]{:S(2)}, u32[]{:S(2)}) async-start(f32[24,24,128]{2,1,0:T(8,128)} %bitcast.4), calls=%async_computation.1 | async-start | bytes 589824 | tf_op jit(solution)/shard_map/weight_scatter/all_to_all | solution.py:237
  70.4 25.1 %collective-permute-start.4 = (bf16[2,128,512]{2,1,0:T(8,128)(2,1)S(1)}, bf16[2,128,512]{2,1,0:T(8,128)(2,1)S(1)}, u32[]{:S(2)}, u32[]{:S(2)}) collective-permute-start(bf16[2,128,512]{2,1,0:T(8,128)(2,1)S(1)} %get-tuple-element.18), channel_id=1, source_target_pairs={{16,0},{20,4},{24,8},{28,12},{32,16},{36,20},{40,24},{44,28},{48,3... | collective-permute-start | bytes 786440 | tf_op jit(solution)/shard_map/term_halo/ppermute | solution.py:216
  78.1 21.4 %collective-permute-start.5 = (bf16[2,128,512]{2,1,0:T(8,128)(2,1)S(1)}, bf16[2,128,512]{2,1,0:T(8,128)(2,1)S(1)}, u32[]{:S(2)}, u32[]{:S(2)}) collective-permute-start(bf16[2,128,512]{2,1,0:T(8,128)(2,1)S(1)} %get-tuple-element.19), channel_id=1, source_target_pairs={{8,0},{12,4},{16,8},{20,12},{24,16},{28,20},{32,24},{36,28},{40,32... | collective-permute-start | bytes 786440 | tf_op jit(solution)/shard_map/term_halo/ppermute | solution.py:216
  81.4 20.1 %collective-permute-start.6 = (bf16[2,128,512]{2,1,0:T(8,128)(2,1)S(1)}, bf16[2,128,512]{2,1,0:T(8,128)(2,1)S(1)}, u32[]{:S(2)}, u32[]{:S(2)}) collective-permute-start(bf16[2,128,512]{2,1,0:T(8,128)(2,1)S(1)} %get-tuple-element.20), channel_id=1, source_target_pairs={{760,0},{764,4},{0,8},{4,12},{8,16},{12,20},{16,24},{20,28},{24,32... | collective-permute-start | bytes 786440 | tf_op jit(solution)/shard_map/term_halo/ppermute | solution.py:216
  83.9 17.6 %collective-permute-start.7 = (bf16[2,128,512]{2,1,0:T(8,128)(2,1)S(1)}, bf16[2,128,512]{2,1,0:T(8,128)(2,1)S(1)}, u32[]{:S(2)}, u32[]{:S(2)}) collective-permute-start(bf16[2,128,512]{2,1,0:T(8,128)(2,1)S(1)} %get-tuple-element.21), channel_id=1, source_target_pairs={{752,0},{756,4},{760,8},{764,12},{0,16},{4,20},{8,24},{12,28},{16,... | collective-permute-start | bytes 786440 | tf_op jit(solution)/shard_map/term_halo/ppermute | solution.py:216
  102.4 12.8 %all-to-all-start.2 = ((f32[8,24,128]{2,1,0:T(8,128)}), f32[8,24,128]{2,1,0:T(8,128)S(1)}, u32[]{:S(2)}, u32[]{:S(2)}) async-start(f32[8,24,128]{2,1,0:T(8,128)} %get-tuple-element.25), calls=%async_computation.2 | async-start | bytes 196608 | tf_op jit(solution)/shard_map/weight_rows/all_to_all | solution.py:242
  106.5 6.8 %collective-permute-start.8 = (bf16[128,512]{1,0:T(8,128)(2,1)S(1)}, bf16[128,512]{1,0:T(8,128)(2,1)S(1)}, u32[]{:S(2)}, u32[]{:S(2)}) collective-permute-start(bf16[128,512]{1,0:T(8,128)(2,1)S(1)} %get-tuple-element.24), channel_id=1, source_target_pairs={{4,0},{0,4},{12,8},{8,12},{20,16},{16,20},{28,24},{24,28},{36,32},... | collective-permute-start | bytes 393224 | tf_op jit(solution)/shard_map/term_exchange/ppermute | solution.py:245

commit v3 on v2

v3 whole, which is shorter than its diff:
```python
import jax
import jax.numpy as jnp
import numpy as np
from jax import lax
from jax.experimental import pallas as pl
from jax.experimental.pallas import tpu as pltpu
from jax.sharding import Mesh
from jax.sharding import PartitionSpec as P

NODES = 98304
TILE = 128
BLOCKS = 4
ROWS = TILE * BLOCKS
WIDTH = 128
COLS = 4
HIDDEN = WIDTH * COLS
OFFSETS = 9
SLOTS = 16
REACH = 4
N_Y, N_Z, N_XL = 8, 12, 2
PAIRS = N_Y * N_Z
PACK_ROWS = ROWS + 16
RING = N_Z * N_XL
SHARE = 24
BLK = ("y", "z", "xl")
COL = ("xh", "core")
BF16 = jnp.bfloat16
F32 = jnp.float32
VMEM = pl.BlockSpec(memory_space=pltpu.VMEM)
SMEM = pl.BlockSpec(memory_space=pltpu.SMEM)


def params(mib=16):
    return pltpu.CompilerParams(vmem_limit_bytes=mib * 1024 * 1024)


def dense_kernel(codes, slab, dense):
    offset = pl.program_id(0)
    for slot in range(SLOTS):
        code = codes[offset, slot]
        row = pl.multiple_of(((code // BLOCKS) % BLOCKS) * TILE, TILE)
        col = pl.multiple_of((code % BLOCKS) * TILE, TILE)
        tile = slab[0, 0, slot]
        dense[0, pl.ds(row, TILE), pl.ds(col, TILE)] = jnp.where(
            code < BLOCKS * BLOCKS, tile, jnp.zeros_like(tile)
        )


def make_dense(codes, slab):
    return pl.pallas_call(
        dense_kernel,
        grid_spec=pltpu.PrefetchScalarGridSpec(
            num_scalar_prefetch=1,
            grid=(OFFSETS,),
            in_specs=[pl.BlockSpec((1, 1, SLOTS, TILE, TILE), lambda o, _: (0, o, 0, 0, 0))],
            out_specs=pl.BlockSpec((1, ROWS, ROWS), lambda o, _: (o, 0, 0)),
        ),
        out_shape=jax.ShapeDtypeStruct((OFFSETS, ROWS, ROWS), BF16),
        compiler_params=params(),
        cost_estimate=pl.CostEstimate(flops=0, bytes_accessed=10 << 20, transcendentals=0),
        name="dense_tiles",
    )(codes, slab)


def stack_kernel(before, x, after, cots, out):
    del cots
    for i, block in enumerate((before, x, after)):
        out[i] = block[...]


def stack_blocks(before, x, after, cots):
    return pl.pallas_call(
        stack_kernel,
        in_specs=[VMEM] * 3 + [pl.BlockSpec(memory_space=pl.ANY)],
        out_specs=VMEM,
        out_shape=jax.ShapeDtypeStruct((3, ROWS, WIDTH), BF16),
        compiler_params=params(),
        cost_estimate=pl.CostEstimate(flops=0, bytes_accessed=1 << 20, transcendentals=0),
        name="near_blocks",
    )(before, x, after, cots)


def gather_kernel(side, dense, xa, xb, xc, xd, xe, near, far, bias, out):
    total = jnp.zeros((ROWS, WIDTH), F32)
    for k, block in enumerate((xa, xb, xc, xd, xe)):
        total += jnp.dot(dense[2 * k], block[...], preferred_element_type=F32)
    for i in range(3):
        total += jnp.dot(dense[3 + 2 * i - 2 * side[0]], near[i], preferred_element_type=F32)
    total += jnp.dot(dense[1 + 6 * side[0]], far[...], preferred_element_type=F32)
    out[0:ROWS, :] = total.astype(BF16)
    out[ROWS:, :] = jnp.broadcast_to(bias[...], (16, WIDTH))


def gather_rows(side, dense, plane, near, far, bias):
    return pl.pallas_call(
        gather_kernel,
        in_specs=[SMEM] + [VMEM] * 9,
        out_specs=VMEM,
        out_shape=jax.ShapeDtypeStruct((PACK_ROWS, WIDTH), BF16),
        compiler_params=params(),
        cost_estimate=pl.CostEstimate(
            flops=2 * OFFSETS * ROWS * ROWS * WIDTH, bytes_accessed=8 << 20, transcendentals=0
        ),
        name="aggregate_features",
    )(side, dense, *plane, near, far, bias)


def middle_kernel(
    place, mixed, cots, weight, dense,
    act, part, near, far, ta, tb, tc, td, te,
    act_all, grad_all, feats,
):
    side = place[0]
    mine = pl.multiple_of(place[1] * WIDTH, WIDTH)
    bias = jnp.concatenate([mixed[c, ROWS:, :] for c in range(COLS)], axis=1)[0:1].astype(F32)
    step = 128
    for i in range(ROWS // step):
        span = slice(i * step, (i + 1) * step)
        own = jnp.concatenate([mixed[c, span, :] for c in range(COLS)], axis=1)
        feats[span, :] = own
        preact = jnp.dot(own, weight[...], preferred_element_type=F32) + bias
        sig = 1.0 / (1.0 + jnp.exp(-preact))
        act_all[span, :] = (preact * sig).astype(BF16)
        cot = jnp.concatenate([cots[c, span, :] for c in range(COLS)], axis=1)
        grad_all[span, :] = (
            cot.astype(F32) * sig * (1.0 + preact * (1.0 - sig))
        ).astype(BF16)
    act[...] = act_all[:, pl.ds(mine, WIDTH)]
    grad_mine = grad_all[:, pl.ds(mine, WIDTH)].astype(F32)
    weight_grad = jnp.dot(
        grad_mine.T.astype(BF16), feats[...], preferred_element_type=F32
    )
    part[0:ROWS, :] = weight_grad.T
    first = lax.broadcasted_iota(jnp.int32, (RING * SHARE - HIDDEN, WIDTH), 0) == 0
    part[ROWS:, :] = jnp.where(first, jnp.sum(grad_mine, axis=0, keepdims=True), 0.0)
    back = lax.dot_general(
        weight[pl.ds(mine, WIDTH), :],
        grad_all[...],
        (((1,), (1,)), ((), ())),
        preferred_element_type=F32,
    ).astype(BF16)
    for k, term in enumerate((ta, tb, tc, td, te)):
        term[...] = jnp.dot(back, dense[2 * k], preferred_element_type=F32).astype(BF16)
    for i in range(3):
        near[i] = jnp.dot(
            back, dense[3 + 2 * i - 2 * side], preferred_element_type=F32
        ).astype(BF16)
    far[...] = jnp.dot(back, dense[1 + 6 * side], preferred_element_type=F32).astype(BF16)


def middle(place, mixed, cots, weight, dense):
    term = jax.ShapeDtypeStruct((WIDTH, ROWS), BF16)
    return pl.pallas_call(
        middle_kernel,
        in_specs=[SMEM] + [VMEM] * 4,
        out_specs=[VMEM] * 9,
        out_shape=[
            jax.ShapeDtypeStruct((ROWS, WIDTH), BF16),
            jax.ShapeDtypeStruct((RING * SHARE, WIDTH), F32),
            jax.ShapeDtypeStruct((3, WIDTH, ROWS), BF16),
        ]
        + [term] * 6,
        scratch_shapes=[pltpu.VMEM((ROWS, HIDDEN), BF16)] * 3,
        compiler_params=params(),
        cost_estimate=pl.CostEstimate(
            flops=2 * (OFFSETS + 9) * ROWS * ROWS * WIDTH, bytes_accessed=10 << 20, transcendentals=ROWS * HIDDEN
        ),
        name="activation_and_terms",
    )(place, mixed, cots, weight, dense)


def near_kernel(tb, tc, td, near, ra, re, rf, shares, before, keep, after, spread):
    before[...] = (tb[...].astype(F32) + near[0].astype(F32)).astype(BF16)
    total = tc[...].astype(F32) + near[1].astype(F32)
    for arrived in (ra, re, rf):
        total += arrived[...].astype(F32)
    keep[...] = total
    after[...] = (td[...].astype(F32) + near[2].astype(F32)).astype(BF16)
    spread[...] = jnp.broadcast_to(jnp.sum(shares[...], axis=0)[None], spread.shape)


def near_sums(tb, tc, td, near, arrived, shares):
    term = jax.ShapeDtypeStruct((WIDTH, ROWS), BF16)
    return pl.pallas_call(
        near_kernel,
        in_specs=[VMEM] * 8,
        out_specs=[VMEM] * 4,
        out_shape=[
            term,
            jax.ShapeDtypeStruct((WIDTH, ROWS), F32),
            term,
            jax.ShapeDtypeStruct((N_Y, SHARE, WIDTH), F32),
        ],
        compiler_params=params(),
        cost_estimate=pl.CostEstimate(flops=1 << 20, bytes_accessed=2 << 20, transcendentals=0),
        name="near_sums",
    )(tb, tc, td, near, *arrived, shares)


def last_kernel(keep, rb, rd, shares, out, spread):
    total = keep[...] + rb[...].astype(F32) + rd[...].astype(F32)
    out[...] = total.T.astype(BF16)
    share = jnp.sum(shares[...], axis=0) * (1.0 / jnp.sqrt(F32(NODES)))
    spread[...] = jnp.broadcast_to(share.astype(BF16)[None], spread.shape)


def last_sum(keep, arrived, shares):
    return pl.pallas_call(
        last_kernel,
        in_specs=[VMEM] * 4,
        out_specs=[VMEM] * 2,
        out_shape=[
            jax.ShapeDtypeStruct((ROWS, WIDTH), BF16),
            jax.ShapeDtypeStruct((RING, SHARE, WIDTH), BF16),
        ],
        compiler_params=params(),
        cost_estimate=pl.CostEstimate(flops=1 << 17, bytes_accessed=1 << 19, transcendentals=0),
        name="node_gradient",
    )(keep, *arrived, shares)


def widen_kernel(whole, weight_grad, bias_grad):
    weight_grad[...] = whole[0:HIDDEN, :].astype(F32)
    bias_grad[...] = whole[HIDDEN : HIDDEN + 16, :].astype(F32)[0:1]


def widen(whole):
    return pl.pallas_call(
        widen_kernel,
        in_specs=[VMEM],
        out_specs=[VMEM] * 2,
        out_shape=[
            jax.ShapeDtypeStruct((HIDDEN, WIDTH), F32),
            jax.ShapeDtypeStruct((1, WIDTH), F32),
        ],
        compiler_params=params(),
        name="weight_gradient",
    )(whole)


def from_pair(block, hops):
    route = [
        (2 * ((p + hops) % PAIRS) + s, 2 * p + s) for p in range(PAIRS) for s in range(2)
    ]
    return lax.ppermute(block, BLK, route)


def routed(block, source):
    route = []
    for p in range(PAIRS):
        for s in range(2):
            pair, other = source(p, s)
            route.append((2 * (pair % PAIRS) + other, 2 * p + s))
    return lax.ppermute(block, BLK, route)


def on_device(node_feats, weight, layer_bias, cotangent, adj_tiles, tile_row, tile_col, tile_count):
    side = lax.axis_index("xl").astype(jnp.int32)
    column = lax.axis_index(COL).astype(jnp.int32)
    slots = jnp.arange(SLOTS, dtype=jnp.int32)[None, :]
    dead = slots >= tile_count[0][:, None]
    codes = tile_row[0] * BLOCKS + tile_col[0] + BLOCKS * BLOCKS * dead.astype(jnp.int32)

    with jax.named_scope("column_gather"):
        cots = lax.all_gather(cotangent, COL, axis=0, tiled=False)
    with jax.named_scope("feature_halo"):
        x = node_feats
        before, after = from_pair(x, -1), from_pair(x, 1)
        far_before, far_after = from_pair(x, -2), from_pair(x, 2)
        far = routed(x, lambda p, s: (p - 2 + 4 * s, 1 - s))
        near = stack_blocks(before, x, after, cots)
        near = routed(near, lambda p, s: (p, 1 - s))
    dense = make_dense(codes, adj_tiles)
    plane = (far_before, before, x, after, far_after)
    mine = gather_rows(side.reshape(1), dense, plane, near, far, layer_bias.reshape(1, WIDTH))
    with jax.named_scope("column_gather"):
        mixed = lax.all_gather(mine, COL, axis=0, tiled=False)
    act, part, near, far, ta, tb, tc, td, te = middle(
        jnp.stack([side, column]), mixed, cots, weight, dense
    )

    ring = ("z", "xl")
    with jax.named_scope("weight_scatter"):
        shares = lax.all_to_all(part.reshape(RING, SHARE, WIDTH), ring, 0, 0, tiled=True)
    with jax.named_scope("term_halo"):
        near = routed(near, lambda p, s: (p, 1 - s))
        ra, re = from_pair(ta, 2), from_pair(te, -2)
        rf = routed(far, lambda p, s: (p - 2 + 4 * s, 1 - s))
    before, keep, after, spread = near_sums(tb, tc, td, near, (ra, re, rf), shares)
    with jax.named_scope("weight_rows"):
        shares = lax.all_to_all(spread, "y", 0, 0, tiled=True)
    with jax.named_scope("term_halo"):
        rb, rd = from_pair(before, 1), from_pair(after, -1)
    grad_nodes, spread = last_sum(keep, (rb, rd), shares)
    with jax.named_scope("weight_gather"):
        whole = lax.all_to_all(spread, ring, 0, 0, tiled=True).reshape(RING * SHARE, WIDTH)
    weight_grad, bias_grad = widen(whole)
    return act, grad_nodes, weight_grad, bias_grad.reshape(WIDTH)


def solution(mesh):
    fine = Mesh(
        np.asarray(mesh.devices).reshape(N_Y, N_Z, N_XL, 2, 2), ("y", "z", "xl", "xh", "core")
    )
    placed = (
        P(BLK, COL),
        P(),
        P(COL),
        P(BLK, COL),
        P(BLK, None, None, None, None),
        P(BLK, None, None),
        P(BLK, None, None),
        P(BLK, None),
    )
    return jax.shard_map(
        on_device,
        mesh=fine,
        in_specs=placed,
        out_specs=(P(BLK, COL), P(BLK, COL), P(None, COL), P(COL)),
        check_vma=False,
    )
```

time: 138 us -> 142 us (1.029)
  the two profiles are of different devices: /device:TPU:4 before, /device:TPU:2 now
where the time goes in v3:
time: 142 us; the launch traced here: 141 us
  starting transfers between devices  73.2 us (52%)
  blocking collectives  32.6 us (23%)
  waiting for transfers between devices  19.4 us (14%)
  Pallas kernels  11.7 us (8%)
  local copies, waits for them, and re-layouts  2.35 us (2%)
    ppermute x8, starting transfers between devices, from_pair(): return lax.ppermute(block, BLK, route)  42.6 us
    ppermute x8, waiting for transfers between devices, from_pair(): return lax.ppermute(block, BLK, route)  18.5 us
    all_to_all x1, blocking collectives, on_device(): lax.all_to_all(spread, ring, 0, 0, tiled=True).reshape(RING * SHARE, WIDTH)  16 us
    ppermute x4, starting transfers between devices, routed(): return lax.ppermute(block, BLK, route)  13.8 us
    all_to_all x1, starting transfers between devices, on_device(): lax.all_to_all(part.reshape(RING, SHARE, WIDTH), ring, 0, 0, tiled=True)  12.6 us
    all_gather x1, blocking collectives, on_device(): mixed = lax.all_gather(mine, COL, axis=0, tiled=False)  8.41 us
    all_gather x1, blocking collectives, on_device(): cots = lax.all_gather(cotangent, COL, axis=0, tiled=False)  8.23 us
    all_to_all x1, starting transfers between devices, on_device(): shares = lax.all_to_all(spread, 'y', 0, 0, tiled=True)  4.08 us
  transfers between devices with their start and end apart: 14, of which 7 were waited for; matrix products, arithmetic and copies ran while one was open for 1% of the time, Pallas kernels for 2%

profile of v3, /device:TPU:2, one launch (start us, length us, event | category | flops | bytes accessed | tf_op | source)
XLA Modules:
  0.0 140.8 jit_solution(17461259813824240477)
XLA Ops:
  0.6 17.5 %collective-permute-start.2 = (bf16[512,128]{1,0:T(8,128)(2,1)}, bf16[512,128]{1,0:T(8,128)(2,1)S(1)}, u32[]{:S(2)}, u32[]{:S(2)}) collective-permute-start(bf16[512,128]{1,0:T(8,128)(2,1)} %xc.1), channel_id=1, source_target_pairs={{8,0},{12,4},{16,8},{20,12},{24,16},{28,20},{32,24},{36,28},{40,32... | collective-permute-start | bytes 393224 | tf_op jit(solution)/shard_map/feature_halo/ppermute | solution.py:245
  18.1 1.9 %collective-permute-start.1 = (bf16[512,128]{1,0:T(8,128)(2,1)}, bf16[512,128]{1,0:T(8,128)(2,1)S(1)}, u32[]{:S(2)}, u32[]{:S(2)}) collective-permute-start(bf16[512,128]{1,0:T(8,128)(2,1)} %xc.1), channel_id=1, source_target_pairs={{760,0},{764,4},{0,8},{4,12},{8,16},{12,20},{16,24},{20,28},{24,32... | collective-permute-start | bytes 393224 | tf_op jit(solution)/shard_map/feature_halo/ppermute | solution.py:245
  20.1 8.2 %all-gather = bf16[2048,128]{1,0:T(8,128)(2,1)S(1)} all-gather(bf16[512,128]{1,0:T(8,128)(2,1)} %param.11), channel_id=2, replica_groups=mesh['y'=8,'z'=12,'xl'=2,'xh'=2,'core'=2] {'xh','core'}, dimensions={0}, use_global_device_ids=true | all-gather | bytes 655360 | tf_op jit(solution)/shard_map/column_gather/all_gather | solution.py:265
  28.3 0.0 collective-permute-done.2.after.xd
  28.3 0.2 collective-permute-done.1.before.xb
  28.5 0.9 near_blocks.1
  29.5 2.9 %collective-permute-start.4 = (bf16[3,512,128]{2,1,0:T(8,128)(2,1)S(1)}, bf16[3,512,128]{2,1,0:T(8,128)(2,1)S(1)}, u32[]{:S(2)}, u32[]{:S(2)}) collective-permute-start(bf16[3,512,128]{2,1,0:T(8,128)(2,1)S(1)} %near_blocks.1), channel_id=1, source_target_pairs={{4,0},{0,4},{12,8},{8,12},{20,16},{16,20},{28,24},{24,28},{36,32},... | collective-permute-start | bytes 1179656 | tf_op jit(solution)/shard_map/feature_halo/ppermute | solution.py:254
  32.4 3.9 %collective-permute-start.3 = (bf16[512,128]{1,0:T(8,128)(2,1)}, bf16[512,128]{1,0:T(8,128)(2,1)S(1)}, u32[]{:S(2)}, u32[]{:S(2)}) collective-permute-start(bf16[512,128]{1,0:T(8,128)(2,1)} %xc.1), channel_id=1, source_target_pairs={{16,0},{20,4},{24,8},{28,12},{32,16},{36,20},{40,24},{44,28},{48,3... | collective-permute-start | bytes 393224 | tf_op jit(solution)/shard_map/feature_halo/ppermute | solution.py:245
  36.3 2.8 %collective-permute-start = (bf16[512,128]{1,0:T(8,128)(2,1)}, bf16[512,128]{1,0:T(8,128)(2,1)S(1)}, u32[]{:S(2)}, u32[]{:S(2)}) collective-permute-start(bf16[512,128]{1,0:T(8,128)(2,1)} %xc.1), channel_id=1, source_target_pairs={{752,0},{756,4},{760,8},{764,12},{0,16},{4,20},{8,24},{12,28},{16,... | collective-permute-start | bytes 393224 | tf_op jit(solution)/shard_map/feature_halo/ppermute | solution.py:245
  39.1 2.4 %collective-permute-start.5 = (bf16[512,128]{1,0:T(8,128)(2,1)}, bf16[512,128]{1,0:T(8,128)(2,1)S(1)}, u32[]{:S(2)}, u32[]{:S(2)}) collective-permute-start(bf16[512,128]{1,0:T(8,128)(2,1)} %xc.1), channel_id=1, source_target_pairs={{756,0},{16,4},{764,8},{24,12},{4,16},{32,20},{12,24},{40,28},{20,... | collective-permute-start | bytes 393224 | tf_op jit(solution)/shard_map/feature_halo/ppermute | solution.py:254
  41.5 0.8 bitcast_add_fusion.codes
  42.3 0.0 copy-start
  42.3 2.3 %copy-done = bf16[1,9,16,128,128]{4,3,2,1,0:T(8,128)(2,1)S(1)} copy-done((bf16[1,9,16,128,128]{4,3,2,1,0:T(8,128)(2,1)S(1)}, bf16[1,9,16,128,128]{4,3,2,1,0:T(8,128)(2,1)}, u32[]{:S(2)}) %copy-start) | copy-done | bytes 4718616
  44.6 0.0 copy-start.2
  44.7 3.1 %dense_tiles.1.dense = bf16[9,512,512]{2,1,0:T(8,128)(2,1)S(1)} custom-call(s32[9,16]{1,0:T(8,128)S(1)} %bitcast_add_fusion.codes, bf16[1,9,16,128,128]{4,3,2,1,0:T(8,128)(2,1)S(1)} %copy-done), custom_call_target="tpu_custom_call" | custom-call | bytes 10485760 | tf_op jit(solution)/shard_map/dense_tiles/pallas_call | solution.py:50
  47.8 0.0 copy-start.1
  47.8 0.1 pad_add_fusion.place
  47.9 0.0 collective-permute-done.3.xe
  47.9 2.7 %collective-permute-done.xa = bf16[512,128]{1,0:T(8,128)(2,1)S(1)} collective-permute-done((bf16[512,128]{1,0:T(8,128)(2,1)}, bf16[512,128]{1,0:T(8,128)(2,1)S(1)}, u32[]{:S(2)}, u32[]{:S(2)}) %collective-permute-start) | collective-permute-done | bytes 131104 | tf_op jit(solution)/shard_map/feature_halo/ppermute | solution.py:245
  50.5 0.0 collective-permute-done.5.far
  50.6 0.0 collective-permute-done.4.near
  50.6 0.0 copy-done.2
  50.6 2.3 %aggregate_features.1 = bf16[528,128]{1,0:T(8,128)(2,1)S(1)} custom-call(s32[1]{0:T(128)} %bitcast.side, bf16[9,512,512]{2,1,0:T(8,128)(2,1)S(1)} %dense_tiles.1.dense, bf16[512,128]{1,0:T(8,128)(2,1)S(1)} %collective-permute-done.xa, bf16[512,128]{1,0:T(8,128)(2,1)S(1)} %collective-permute-done.1.before.xb, bf16[512,128]{1,0:T(8,128)(2,1)} %xc.1, ...), custom_call_target="tpu_custom_call" | custom-call | flops 603979776 | bytes 8388608 | tf_op jit(solution)/shard_map/aggregate_features/pallas_call | solution.py:95
  52.9 8.4 %all-gather.1 = bf16[2112,128]{1,0:T(8,128)(2,1)S(1)} all-gather(bf16[528,128]{1,0:T(8,128)(2,1)S(1)} %aggregate_features.1), channel_id=3, replica_groups=mesh['y'=8,'z'=12,'xl'=2,'xh'=2,'core'=2] {'xh','core'}, dimensions={0}, use_global_device_ids=true | all-gather | bytes 675840 | tf_op jit(solution)/shard_map/column_gather/all_gather | solution.py:277
  61.3 0.0 copy-done.1
  61.3 3.1 %activation_and_terms.1 = (bf16[512,128]{1,0:T(8,128)(2,1)}, f32[576,128]{1,0:T(8,128)}, bf16[3,128,512]{2,1,0:T(8,128)(2,1)S(1)}, bf16[128,512]{1,0:T(8,128)(2,...) custom-call(s32[2]{0:T(128)S(1)} %pad_add_fusion.place, ...), custom_call_target="tpu_custom_call" | custom-call | flops 1207959552 | bytes 10485760 | tf_op jit(solution)/shard_map/activation_and_terms/pallas_call | solution.py:153
  64.4 12.6 %all-to-all-start = ((f32[24,24,128]{2,1,0:T(8,128)}), f32[24,24,128]{2,1,0:T(8,128)S(1)}, u32[]{:S(2)}, u32[]{:S(2)}) async-start(f32[24,24,128]{2,1,0:T(8,128)} %bitcast.7), calls=%async_computation | async-start | bytes 589824 | tf_op jit(solution)/shard_map/weight_scatter/all_to_all | solution.py:284
  77.0 2.1 %collective-permute-start.6 = (bf16[3,128,512]{2,1,0:T(8,128)(2,1)S(1)}, bf16[3,128,512]{2,1,0:T(8,128)(2,1)S(1)}, u32[]{:S(2)}, u32[]{:S(2)}) collective-permute-start(bf16[3,128,512]{2,1,0:T(8,128)(2,1)S(1)} %get-tuple-element.25), channel_id=1, source_target_pairs={{4,0},{0,4},{12,8},{8,12},{20,16},{16,20},{28,24},{24,28},{36,32},... | collective-permute-start | bytes 1179656 | tf_op jit(solution)/shard_map/term_halo/ppermute | solution.py:254
  79.1 5.1 %collective-permute-start.7 = (bf16[128,512]{1,0:T(8,128)(2,1)S(1)}, bf16[128,512]{1,0:T(8,128)(2,1)S(1)}, u32[]{:S(2)}, u32[]{:S(2)}) collective-permute-start(bf16[128,512]{1,0:T(8,128)(2,1)S(1)} %get-tuple-element.26), channel_id=1, source_target_pairs={{16,0},{20,4},{24,8},{28,12},{32,16},{36,20},{40,24},{44,28},{48,3... | collective-permute-start | bytes 393224 | tf_op jit(solution)/shard_map/term_halo/ppermute | solution.py:245
  84.3 1.9 %collective-permute-start.8 = (bf16[128,512]{1,0:T(8,128)(2,1)S(1)}, bf16[128,512]{1,0:T(8,128)(2,1)S(1)}, u32[]{:S(2)}, u32[]{:S(2)}) collective-permute-start(bf16[128,512]{1,0:T(8,128)(2,1)S(1)} %get-tuple-element.27), channel_id=1, source_target_pairs={{752,0},{756,4},{760,8},{764,12},{0,16},{4,20},{8,24},{12,28},{16,... | collective-permute-start | bytes 393224 | tf_op jit(solution)/shard_map/term_halo/ppermute | solution.py:245
  86.2 6.5 %collective-permute-start.9 = (bf16[128,512]{1,0:T(8,128)(2,1)S(1)}, bf16[128,512]{1,0:T(8,128)(2,1)S(1)}, u32[]{:S(2)}, u32[]{:S(2)}) collective-permute-start(bf16[128,512]{1,0:T(8,128)(2,1)S(1)} %get-tuple-element.28), channel_id=1, source_target_pairs={{756,0},{16,4},{764,8},{24,12},{4,16},{32,20},{12,24},{40,28},{20,... | collective-permute-start | bytes 393224 | tf_op jit(solution)/shard_map/term_halo/ppermute | solution.py:254
  92.7 2.5 %collective-permute-done.7.ra = bf16[128,512]{1,0:T(8,128)(2,1)S(1)} collective-permute-done((bf16[128,512]{1,0:T(8,128)(2,1)S(1)}, bf16[128,512]{1,0:T(8,128)(2,1)S(1)}, u32[]{:S(2)}, u32[]{:S(2)}) %collective-permute-start.7) | collective-permute-done | bytes 131104 | tf_op jit(solution)/shard_map/term_halo/ppermute | solution.py:245
  95.1 4.9 %collective-permute-done.8.re = bf16[128,512]{1,0:T(8,128)(2,1)S(1)} collective-permute-done((bf16[128,512]{1,0:T(8,128)(2,1)S(1)}, bf16[128,512]{1,0:T(8,128)(2,1)S(1)}, u32[]{:S(2)}, u32[]{:S(2)}) %collective-permute-start.8) | collective-permute-done | bytes 131104 | tf_op jit(solution)/shard_map/term_halo/ppermute | solution.py:245
  100.0 0.9 collective-permute-done.9.rf
  100.9 0.0 collective-permute-done.6.near
  100.9 0.0 all-to-all-done.shares
  100.9 0.7 near_sums.1
  101.6 4.1 %all-to-all-start.1 = ((f32[8,24,128]{2,1,0:T(8,128)}), f32[8,24,128]{2,1,0:T(8,128)S(1)}, u32[]{:S(2)}, u32[]{:S(2)}) async-start(f32[8,24,128]{2,1,0:T(8,128)} %get-tuple-element.33), calls=%async_computation.1 | async-start | bytes 196608 | tf_op jit(solution)/shard_map/weight_rows/all_to_all | solution.py:291
  105.7 7.5 %collective-permute-start.10 = (bf16[128,512]{1,0:T(8,128)(2,1)S(1)}, bf16[128,512]{1,0:T(8,128)(2,1)S(1)}, u32[]{:S(2)}, u32[]{:S(2)}) collective-permute-start(bf16[128,512]{1,0:T(8,128)(2,1)S(1)} %get-tuple-element.31), channel_id=1, source_target_pairs={{8,0},{12,4},{16,8},{20,12},{24,16},{28,20},{32,24},{36,28},{40,32... | collective-permute-start | bytes 393224 | tf_op jit(solution)/shard_map/term_halo/ppermute | solution.py:245
  113.2 1.9 %collective-permute-start.11 = (bf16[128,512]{1,0:T(8,128)(2,1)S(1)}, bf16[128,512]{1,0:T(8,128)(2,1)S(1)}, u32[]{:S(2)}, u32[]{:S(2)}) collective-permute-start(bf16[128,512]{1,0:T(8,128)(2,1)S(1)} %get-tuple-element.32), channel_id=1, source_target_pairs={{760,0},{764,4},{0,8},{4,12},{8,16},{12,20},{16,24},{20,28},{24,32... | collective-permute-start | bytes 393224 | tf_op jit(solution)/shard_map/term_halo/ppermute | solution.py:245
  115.1 0.6 collective-permute-done.10.rb
  115.7 7.7 %collective-permute-done.11.rd = bf16[128,512]{1,0:T(8,128)(2,1)S(1)} collective-permute-done((bf16[128,512]{1,0:T(8,128)(2,1)S(1)}, bf16[128,512]{1,0:T(8,128)(2,1)S(1)}, u32[]{:S(2)}, u32[]{:S(2)}) %collective-permute-start.11) | collective-permute-done | bytes 131104 | tf_op jit(solution)/shard_map/term_halo/ppermute | solution.py:245
  123.4 0.0 all-to-all-done.1.shares
  123.4 0.8 node_gradient.1
  124.1 16.0 %all_to_all.15 = bf16[24,24,128]{2,1,0:T(8,128)(2,1)S(1)} all-to-all(bf16[24,24,128]{2,1,0:T(8,128)(2,1)S(1)} %get-tuple-element.35), channel_id=1, replica_groups=mesh['y'=8,'z'=12,'xl'=2,'xh'=2,'core'=2] {'z','xl'}, dimensions={0} | all-to-all | bytes 294912 | tf_op jit(solution)/shard_map/weight_gather/all_to_all | solution.py:296
  140.1 0.7 weight_gradient.1
Async XLA Ops:
  0.6 27.7 %collective-permute-start.2 = (bf16[512,128]{1,0:T(8,128)(2,1)}, bf16[512,128]{1,0:T(8,128)(2,1)S(1)}, u32[]{:S(2)}, u32[]{:S(2)}) collective-permute-start(bf16[512,128]{1,0:T(8,128)(2,1)} %xc.1), channel_id=1, source_target_pairs={{8,0},{12,4},{16,8},{20,12},{24,16},{28,20},{32,24},{36,28},{40,32... | collective-permute-start | bytes 393224 | tf_op jit(solution)/shard_map/feature_halo/ppermute | solution.py:245
  18.1 10.4 %collective-permute-start.1 = (bf16[512,128]{1,0:T(8,128)(2,1)}, bf16[512,128]{1,0:T(8,128)(2,1)S(1)}, u32[]{:S(2)}, u32[]{:S(2)}) collective-permute-start(bf16[512,128]{1,0:T(8,128)(2,1)} %xc.1), channel_id=1, source_target_pairs={{760,0},{764,4},{0,8},{4,12},{8,16},{12,20},{16,24},{20,28},{24,32... | collective-permute-start | bytes 393224 | tf_op jit(solution)/shard_map/feature_halo/ppermute | solution.py:245
  29.5 21.1 %collective-permute-start.4 = (bf16[3,512,128]{2,1,0:T(8,128)(2,1)S(1)}, bf16[3,512,128]{2,1,0:T(8,128)(2,1)S(1)}, u32[]{:S(2)}, u32[]{:S(2)}) collective-permute-start(bf16[3,512,128]{2,1,0:T(8,128)(2,1)S(1)} %near_blocks.1), channel_id=1, source_target_pairs={{4,0},{0,4},{12,8},{8,12},{20,16},{16,20},{28,24},{24,28},{36,32},... | collective-permute-start | bytes 1179656 | tf_op jit(solution)/shard_map/feature_halo/ppermute | solution.py:254
  32.4 15.5 %collective-permute-start.3 = (bf16[512,128]{1,0:T(8,128)(2,1)}, bf16[512,128]{1,0:T(8,128)(2,1)S(1)}, u32[]{:S(2)}, u32[]{:S(2)}) collective-permute-start(bf16[512,128]{1,0:T(8,128)(2,1)} %xc.1), channel_id=1, source_target_pairs={{16,0},{20,4},{24,8},{28,12},{32,16},{36,20},{40,24},{44,28},{48,3... | collective-permute-start | bytes 393224 | tf_op jit(solution)/shard_map/feature_halo/ppermute | solution.py:245
  36.3 14.3 %collective-permute-start = (bf16[512,128]{1,0:T(8,128)(2,1)}, bf16[512,128]{1,0:T(8,128)(2,1)S(1)}, u32[]{:S(2)}, u32[]{:S(2)}) collective-permute-start(bf16[512,128]{1,0:T(8,128)(2,1)} %xc.1), channel_id=1, source_target_pairs={{752,0},{756,4},{760,8},{764,12},{0,16},{4,20},{8,24},{12,28},{16,... | collective-permute-start | bytes 393224 | tf_op jit(solution)/shard_map/feature_halo/ppermute | solution.py:245
  39.1 11.4 %collective-permute-start.5 = (bf16[512,128]{1,0:T(8,128)(2,1)}, bf16[512,128]{1,0:T(8,128)(2,1)S(1)}, u32[]{:S(2)}, u32[]{:S(2)}) collective-permute-start(bf16[512,128]{1,0:T(8,128)(2,1)} %xc.1), channel_id=1, source_target_pairs={{756,0},{16,4},{764,8},{24,12},{4,16},{32,20},{12,24},{40,28},{20,... | collective-permute-start | bytes 393224 | tf_op jit(solution)/shard_map/feature_halo/ppermute | solution.py:254
  42.3 2.3 %copy-start = (bf16[1,9,16,128,128]{4,3,2,1,0:T(8,128)(2,1)S(1)}, bf16[1,9,16,128,128]{4,3,2,1,0:T(8,128)(2,1)}, u32[]{:S(2)}) copy-start(bf16[1,9,16,128,128]{4,3,2,1,0:T(8,128)(2,1)} %slab.1) | copy-start | bytes 14155780
  44.6 5.9 %copy-start.2 = (bf16[128]{0:T(256)(128)(2,1)S(1)}, bf16[128]{0:T(256)(128)(2,1)}, u32[]{:S(2)}) copy-start(bf16[128]{0:T(256)(128)(2,1)} %param.10) | copy-start | bytes 772
  47.8 13.5 %copy-start.1 = (bf16[512,512]{1,0:T(8,128)(2,1)S(1)}, bf16[512,512]{1,0:T(8,128)(2,1)}, u32[]{:S(2)}) copy-start(bf16[512,512]{1,0:T(8,128)(2,1)} %weight.1) | copy-start | bytes 1572868
  64.4 36.5 %all-to-all-start = ((f32[24,24,128]{2,1,0:T(8,128)}), f32[24,24,128]{2,1,0:T(8,128)S(1)}, u32[]{:S(2)}, u32[]{:S(2)}) async-start(f32[24,24,128]{2,1,0:T(8,128)} %bitcast.7), calls=%async_computation | async-start | bytes 589824 | tf_op jit(solution)/shard_map/weight_scatter/all_to_all | solution.py:284
  77.0 23.9 %collective-permute-start.6 = (bf16[3,128,512]{2,1,0:T(8,128)(2,1)S(1)}, bf16[3,128,512]{2,1,0:T(8,128)(2,1)S(1)}, u32[]{:S(2)}, u32[]{:S(2)}) collective-permute-start(bf16[3,128,512]{2,1,0:T(8,128)(2,1)S(1)} %get-tuple-element.25), channel_id=1, source_target_pairs={{4,0},{0,4},{12,8},{8,12},{20,16},{16,20},{28,24},{24,28},{36,32},... | collective-permute-start | bytes 1179656 | tf_op jit(solution)/shard_map/term_halo/ppermute | solution.py:254
  79.1 16.0 %collective-permute-start.7 = (bf16[128,512]{1,0:T(8,128)(2,1)S(1)}, bf16[128,512]{1,0:T(8,128)(2,1)S(1)}, u32[]{:S(2)}, u32[]{:S(2)}) collective-permute-start(bf16[128,512]{1,0:T(8,128)(2,1)S(1)} %get-tuple-element.26), channel_id=1, source_target_pairs={{16,0},{20,4},{24,8},{28,12},{32,16},{36,20},{40,24},{44,28},{48,3... | collective-permute-start | bytes 393224 | tf_op jit(solution)/shard_map/term_halo/ppermute | solution.py:245
  84.3 15.7 %collective-permute-start.8 = (bf16[128,512]{1,0:T(8,128)(2,1)S(1)}, bf16[128,512]{1,0:T(8,128)(2,1)S(1)}, u32[]{:S(2)}, u32[]{:S(2)}) collective-permute-start(bf16[128,512]{1,0:T(8,128)(2,1)S(1)} %get-tuple-element.27), channel_id=1, source_target_pairs={{752,0},{756,4},{760,8},{764,12},{0,16},{4,20},{8,24},{12,28},{16,... | collective-permute-start | bytes 393224 | tf_op jit(solution)/shard_map/term_halo/ppermute | solution.py:245
  86.2 14.7 %collective-permute-start.9 = (bf16[128,512]{1,0:T(8,128)(2,1)S(1)}, bf16[128,512]{1,0:T(8,128)(2,1)S(1)}, u32[]{:S(2)}, u32[]{:S(2)}) collective-permute-start(bf16[128,512]{1,0:T(8,128)(2,1)S(1)} %get-tuple-element.28), channel_id=1, source_target_pairs={{756,0},{16,4},{764,8},{24,12},{4,16},{32,20},{12,24},{40,28},{20,... | collective-permute-start | bytes 393224 | tf_op jit(solution)/shard_map/term_halo/ppermute | solution.py:254
  101.6 21.8 %all-to-all-start.1 = ((f32[8,24,128]{2,1,0:T(8,128)}), f32[8,24,128]{2,1,0:T(8,128)S(1)}, u32[]{:S(2)}, u32[]{:S(2)}) async-start(f32[8,24,128]{2,1,0:T(8,128)} %get-tuple-element.33), calls=%async_computation.1 | async-start | bytes 196608 | tf_op jit(solution)/shard_map/weight_rows/all_to_all | solution.py:291
  105.7 10.0 %collective-permute-start.10 = (bf16[128,512]{1,0:T(8,128)(2,1)S(1)}, bf16[128,512]{1,0:T(8,128)(2,1)S(1)}, u32[]{:S(2)}, u32[]{:S(2)}) collective-permute-start(bf16[128,512]{1,0:T(8,128)(2,1)S(1)} %get-tuple-element.31), channel_id=1, source_target_pairs={{8,0},{12,4},{16,8},{20,12},{24,16},{28,20},{32,24},{36,28},{40,32... | collective-permute-start | bytes 393224 | tf_op jit(solution)/shard_map/term_halo/ppermute | solution.py:245
  113.2 10.2 %collective-permute-start.11 = (bf16[128,512]{1,0:T(8,128)(2,1)S(1)}, bf16[128,512]{1,0:T(8,128)(2,1)S(1)}, u32[]{:S(2)}, u32[]{:S(2)}) collective-permute-start(bf16[128,512]{1,0:T(8,128)(2,1)S(1)} %get-tuple-element.32), channel_id=1, source_target_pairs={{760,0},{764,4},{0,8},{4,12},{8,16},{12,20},{16,24},{20,28},{24,32... | collective-permute-start | bytes 393224 | tf_op jit(solution)/shard_map/term_halo/ppermute | solution.py:245

commit v4 on v2

v4 whole, which is shorter than its diff:
```python
import jax
import jax.numpy as jnp
import numpy as np
from jax import lax
from jax.experimental import pallas as pl
from jax.experimental.pallas import tpu as pltpu
from jax.sharding import Mesh
from jax.sharding import PartitionSpec as P

NODES = 98304
TILE = 128
BLOCKS = 4
ROWS = TILE * BLOCKS
WIDTH = 128
COLS = 4
HIDDEN = WIDTH * COLS
OFFSETS = 9
SLOTS = 16
REACH = 4
WINDOW = OFFSETS + 1
N_Y, N_Z, N_XL = 8, 12, 2
PAIRS = N_Y * N_Z
PACK_ROWS = ROWS + 16
RING = N_Z * N_XL
SHARE = 24
BLK = ("y", "z", "xl")
COL = ("xh", "core")
BF16 = jnp.bfloat16
F32 = jnp.float32
VMEM = pl.BlockSpec(memory_space=pltpu.VMEM)
SMEM = pl.BlockSpec(memory_space=pltpu.SMEM)


def params(mib=16):
    return pltpu.CompilerParams(vmem_limit_bytes=mib * 1024 * 1024)


def dense_kernel(side, codes, slab, cots, dense):
    del cots
    left_over = (1 - side[0]) * OFFSETS
    dense[left_over] = jnp.zeros((ROWS, ROWS), BF16)

    @pl.loop(0, OFFSETS)
    def _(offset):
        for slot in range(SLOTS):
            code = codes[offset, slot]
            row = pl.multiple_of(((code >> 2) & 3) * TILE, TILE)
            col = pl.multiple_of((code & 3) * TILE, TILE)
            tile = slab[0, offset, slot]
            dense[offset + side[0], pl.ds(row, TILE), pl.ds(col, TILE)] = jnp.where(
                code < BLOCKS * BLOCKS, tile, jnp.zeros_like(tile)
            )


def make_dense(side, codes, slab, cots):
    return pl.pallas_call(
        dense_kernel,
        in_specs=[SMEM, SMEM, VMEM, pl.BlockSpec(memory_space=pl.ANY)],
        out_specs=VMEM,
        out_shape=jax.ShapeDtypeStruct((WINDOW, ROWS, ROWS), BF16),
        compiler_params=params(),
        cost_estimate=pl.CostEstimate(flops=0, bytes_accessed=10 << 20, transcendentals=0),
        name="dense_tiles",
    )(side, codes, slab, cots)


def gather_kernel(dense, xa, xb, xc, xd, xe, bias, out):
    total = jnp.zeros((ROWS, WIDTH), F32)
    for k, pair in enumerate((xa, xb, xc, xd, xe)):
        for s in range(2):
            total += jnp.dot(dense[2 * k + s], pair[s], preferred_element_type=F32)
    out[0:ROWS, :] = total.astype(BF16)
    out[ROWS:, :] = jnp.broadcast_to(bias[...], (16, WIDTH))


def gather_rows(dense, pairs, bias):
    return pl.pallas_call(
        gather_kernel,
        in_specs=[VMEM] * 7,
        out_specs=VMEM,
        out_shape=jax.ShapeDtypeStruct((PACK_ROWS, WIDTH), BF16),
        compiler_params=params(),
        cost_estimate=pl.CostEstimate(
            flops=2 * WINDOW * ROWS * ROWS * WIDTH, bytes_accessed=8 << 20, transcendentals=0
        ),
        name="aggregate_features",
    )(dense, *pairs, bias)


def middle_kernel(column, mixed, cots, weight, dense, act, part, ta, tb, tc, td, te, act_all, grad_all, feats):
    mine = pl.multiple_of(column[0] * WIDTH, WIDTH)
    bias = jnp.concatenate([mixed[c, ROWS:, :] for c in range(COLS)], axis=1)[0:1].astype(F32)
    step = 128
    for i in range(ROWS // step):
        span = slice(i * step, (i + 1) * step)
        own = jnp.concatenate([mixed[c, span, :] for c in range(COLS)], axis=1)
        feats[span, :] = own
        preact = jnp.dot(own, weight[...], preferred_element_type=F32) + bias
        sig = 1.0 / (1.0 + jnp.exp(-preact))
        act_all[span, :] = (preact * sig).astype(BF16)
        cot = jnp.concatenate([cots[c, span, :] for c in range(COLS)], axis=1)
        grad_all[span, :] = (
            cot.astype(F32) * sig * (1.0 + preact * (1.0 - sig))
        ).astype(BF16)
    act[...] = act_all[:, pl.ds(mine, WIDTH)]
    grad_mine = grad_all[:, pl.ds(mine, WIDTH)].astype(F32)
    weight_grad = jnp.dot(
        grad_mine.T.astype(BF16), feats[...], preferred_element_type=F32
    )
    part[0:ROWS, :] = weight_grad.T
    first = lax.broadcasted_iota(jnp.int32, (RING * SHARE - HIDDEN, WIDTH), 0) == 0
    part[ROWS:, :] = jnp.where(first, jnp.sum(grad_mine, axis=0, keepdims=True), 0.0)
    back = lax.dot_general(
        weight[pl.ds(mine, WIDTH), :],
        grad_all[...],
        (((1,), (1,)), ((), ())),
        preferred_element_type=F32,
    ).astype(BF16)
    for k, pair in enumerate((ta, tb, tc, td, te)):
        for s in range(2):
            pair[s] = jnp.dot(back, dense[2 * k + s], preferred_element_type=F32).astype(BF16)


def middle(column, mixed, cots, weight, dense):
    term = jax.ShapeDtypeStruct((2, WIDTH, ROWS), BF16)
    return pl.pallas_call(
        middle_kernel,
        in_specs=[SMEM] + [VMEM] * 4,
        out_specs=[VMEM] * 7,
        out_shape=[
            jax.ShapeDtypeStruct((ROWS, WIDTH), BF16),
            jax.ShapeDtypeStruct((RING * SHARE, WIDTH), F32),
        ]
        + [term] * 5,
        scratch_shapes=[pltpu.VMEM((ROWS, HIDDEN), BF16)] * 3,
        compiler_params=params(),
        cost_estimate=pl.CostEstimate(
            flops=2 * (WINDOW + 9) * ROWS * ROWS * WIDTH, bytes_accessed=10 << 20, transcendentals=ROWS * HIDDEN
        ),
        name="activation_and_terms",
    )(column, mixed, cots, weight, dense)


def share_kernel(scale, shares, *rest):
    spread = rest[-1]
    total = jnp.sum(shares[...], axis=0) * scale
    spread[...] = jnp.broadcast_to(total.astype(spread.dtype)[None], spread.shape)


def spread_sum(shares, behind, copies, scale, dtype):
    return pl.pallas_call(
        lambda *refs: share_kernel(scale, *refs),
        in_specs=[VMEM] + [pl.BlockSpec(memory_space=pl.ANY)] * len(behind),
        out_specs=VMEM,
        out_shape=jax.ShapeDtypeStruct((copies, SHARE, WIDTH), dtype),
        compiler_params=params(),
        cost_estimate=pl.CostEstimate(flops=1 << 16, bytes_accessed=1 << 19, transcendentals=0),
        name="spread_sum",
    )(shares, *behind)


def split_kernel(side, own, ta, tb, td, te, first, keep, send):
    del first
    for s in range(2):
        total = own[s].astype(F32)
        for arrived in (ta, tb, td, te):
            total += arrived[s].astype(F32)

        @pl.when(side[0] == s)
        def _():
            keep[...] = total

        @pl.when(side[0] != s)
        def _():
            send[...] = total.astype(BF16)


def split_terms(side, own, arrived, first):
    return pl.pallas_call(
        split_kernel,
        in_specs=[SMEM] + [VMEM] * 5 + [pl.BlockSpec(memory_space=pl.ANY)],
        out_specs=[VMEM] * 2,
        out_shape=[
            jax.ShapeDtypeStruct((WIDTH, ROWS), F32),
            jax.ShapeDtypeStruct((WIDTH, ROWS), BF16),
        ],
        compiler_params=params(),
        cost_estimate=pl.CostEstimate(flops=1 << 20, bytes_accessed=2 << 20, transcendentals=0),
        name="pair_sums",
    )(side, own, *arrived, first)


def last_kernel(keep, arrived, first, out):
    del first
    out[...] = (keep[...] + arrived[...].astype(F32)).T.astype(BF16)


def last_sum(keep, arrived, first):
    return pl.pallas_call(
        last_kernel,
        in_specs=[VMEM] * 2 + [pl.BlockSpec(memory_space=pl.ANY)],
        out_specs=VMEM,
        out_shape=jax.ShapeDtypeStruct((ROWS, WIDTH), BF16),
        compiler_params=params(),
        cost_estimate=pl.CostEstimate(flops=1 << 17, bytes_accessed=1 << 19, transcendentals=0),
        name="node_gradient",
    )(keep, arrived, first)


def widen_kernel(whole, weight_grad, bias_grad):
    weight_grad[...] = whole[0:HIDDEN, :].astype(F32)
    bias_grad[...] = whole[HIDDEN : HIDDEN + 16, :].astype(F32)[0:1]


def widen(whole):
    return pl.pallas_call(
        widen_kernel,
        in_specs=[VMEM],
        out_specs=[VMEM] * 2,
        out_shape=[
            jax.ShapeDtypeStruct((HIDDEN, WIDTH), F32),
            jax.ShapeDtypeStruct((1, WIDTH), F32),
        ],
        compiler_params=params(),
        name="weight_gradient",
    )(whole)


def from_pair(block, hops):
    route = [
        (2 * ((p + hops) % PAIRS) + s, 2 * p + s) for p in range(PAIRS) for s in range(2)
    ]
    return lax.ppermute(block, BLK, route)


def on_device(node_feats, weight, layer_bias, cotangent, adj_tiles, tile_row, tile_col, tile_count):
    side = lax.axis_index("xl").astype(jnp.int32).reshape(1)
    column = lax.axis_index(COL).astype(jnp.int32).reshape(1)
    slots = jnp.arange(SLOTS, dtype=jnp.int32)[None, :]
    dead = slots >= tile_count[0][:, None]
    codes = tile_row[0] * BLOCKS + tile_col[0] + BLOCKS * BLOCKS * dead.astype(jnp.int32)

    with jax.named_scope("feature_halo"):
        pair = lax.all_gather(node_feats, "xl", axis=0, tiled=False)
        pairs = [pair if k == 0 else from_pair(pair, k) for k in (-2, -1, 0, 1, 2)]
    with jax.named_scope("column_gather"):
        cots = lax.all_gather(cotangent, COL, axis=0, tiled=False)
    dense = make_dense(side, codes, adj_tiles, cots)
    mine = gather_rows(dense, pairs, layer_bias.reshape(1, WIDTH))
    with jax.named_scope("column_gather"):
        mixed = lax.all_gather(mine, COL, axis=0, tiled=False)
    act, part, ta, tb, tc, td, te = middle(column, mixed, cots, weight, dense)

    ring = ("z", "xl")
    with jax.named_scope("weight_scatter"):
        shares = lax.all_to_all(part.reshape(RING, SHARE, WIDTH), ring, 0, 0, tiled=True)
    with jax.named_scope("term_halo"):
        arrived = [from_pair(t, -k) for k, t in ((-2, ta), (-1, tb), (1, td), (2, te))]
    spread = spread_sum(shares, arrived[1:3], N_Y, 1.0, F32)
    keep, send = split_terms(side, tc, arrived, spread)
    with jax.named_scope("weight_rows"):
        shares = lax.all_to_all(spread, "y", 0, 0, tiled=True)
    with jax.named_scope("term_exchange"):
        swap = [(b ^ 1, b) for b in range(2 * PAIRS)]
        other = lax.ppermute(send, BLK, swap)
    spread = spread_sum(shares, [keep], RING, float(NODES) ** -0.5, BF16)
    grad_nodes = last_sum(keep, other, spread)
    with jax.named_scope("weight_gather"):
        whole = lax.all_to_all(spread, ring, 0, 0, tiled=True).reshape(RING * SHARE, WIDTH)
    weight_grad, bias_grad = widen(whole)
    return act, grad_nodes, weight_grad, bias_grad.reshape(WIDTH)


def solution(mesh):
    fine = Mesh(
        np.asarray(mesh.devices).reshape(N_Y, N_Z, N_XL, 2, 2), ("y", "z", "xl", "xh", "core")
    )
    placed = (
        P(BLK, COL),
        P(),
        P(COL),
        P(BLK, COL),
        P(BLK, None, None, None, None),
        P(BLK, None, None),
        P(BLK, None, None),
        P(BLK, None),
    )
    return jax.shard_map(
        on_device,
        mesh=fine,
        in_specs=placed,
        out_specs=(P(BLK, COL), P(BLK, COL), P(None, COL), P(COL)),
        check_vma=False,
    )
```

time: 138 us -> 123 us (0.89)
  the two profiles are of different devices: /device:TPU:4 before, /device:TPU:2 now
where the time goes in v4:
time: 123 us
  starting transfers between devices  55.9 us (45%)
  blocking collectives  29.7 us (24%)
  waiting for transfers between devices  23.8 us (19%)
  Pallas kernels  9.43 us (8%)
  local copies, waits for them, and re-layouts  2.35 us (2%)
    ppermute x8, starting transfers between devices, from_pair(): return lax.ppermute(block, BLK, route)  33.6 us
    all_gather x1, blocking collectives, on_device(): pair = lax.all_gather(node_feats, 'xl', axis=0, tiled=False)  13.4 us
    ppermute x8, waiting for transfers between devices, from_pair(): return lax.ppermute(block, BLK, route)  11.7 us
    all_to_all x1, starting transfers between devices, on_device(): lax.all_to_all(spread, ring, 0, 0, tiled=True).reshape(RING * SHARE, WIDTH)  10.3 us
    all_gather x1, blocking collectives, on_device(): cots = lax.all_gather(cotangent, COL, axis=0, tiled=False)  8.23 us
    all_gather x1, blocking collectives, on_device(): mixed = lax.all_gather(mine, COL, axis=0, tiled=False)  8.06 us
    all_to_all x1, starting transfers between devices, on_device(): lax.all_to_all(part.reshape(RING, SHARE, WIDTH), ring, 0, 0, tiled=True)  5.78 us
    ppermute x1, waiting for transfers between devices, on_device(): other = lax.ppermute(send, BLK, swap)  4.98 us
  transfers between devices with their start and end apart: 12, of which 7 were waited for; matrix products, arithmetic and copies ran while one was open for 1% of the time, Pallas kernels for 3%

profile of v4, /device:TPU:2, one launch (start us, length us, event | category | flops | bytes accessed | tf_op | source)
XLA Modules:
  0.0 122.7 jit_solution(17377621477872936536)
XLA Ops:
  0.6 13.4 %all-gather.1 = bf16[1024,128]{1,0:T(8,128)(2,1)S(1)} all-gather(bf16[512,128]{1,0:T(8,128)(2,1)} %param.8), channel_id=3, replica_groups=mesh['y'=8,'z'=12,'xl'=2,'xh'=2,'core'=2] {'xl'}, dimensions={0}, use_global_device_ids=true | all-gather | bytes 393216 | tf_op jit(solution)/shard_map/feature_halo/all_gather | solution.py:244
  14.1 10.2 %collective-permute-start.3 = (bf16[2,512,128]{2,1,0:T(8,128)(2,1)S(1)}, bf16[2,512,128]{2,1,0:T(8,128)(2,1)S(1)}, u32[]{:S(2)}, u32[]{:S(2)}) collective-permute-start(bf16[2,512,128]{2,1,0:T(8,128)(2,1)S(1)} %bitcast.15), channel_id=1, source_target_pairs={{16,0},{20,4},{24,8},{28,12},{32,16},{36,20},{40,24},{44,28},{48,3... | collective-permute-start | bytes 786440 | tf_op jit(solution)/shard_map/feature_halo/ppermute | solution.py:233
  24.2 2.5 %collective-permute-start.2 = (bf16[2,512,128]{2,1,0:T(8,128)(2,1)S(1)}, bf16[2,512,128]{2,1,0:T(8,128)(2,1)S(1)}, u32[]{:S(2)}, u32[]{:S(2)}) collective-permute-start(bf16[2,512,128]{2,1,0:T(8,128)(2,1)S(1)} %bitcast.16), channel_id=1, source_target_pairs={{8,0},{12,4},{16,8},{20,12},{24,16},{28,20},{32,24},{36,28},{40,32... | collective-permute-start | bytes 786440 | tf_op jit(solution)/shard_map/feature_halo/ppermute | solution.py:233
  26.7 3.4 %collective-permute-start.1 = (bf16[2,512,128]{2,1,0:T(8,128)(2,1)S(1)}, bf16[2,512,128]{2,1,0:T(8,128)(2,1)S(1)}, u32[]{:S(2)}, u32[]{:S(2)}) collective-permute-start(bf16[2,512,128]{2,1,0:T(8,128)(2,1)S(1)} %bitcast.17), channel_id=1, source_target_pairs={{760,0},{764,4},{0,8},{4,12},{8,16},{12,20},{16,24},{20,28},{24,32... | collective-permute-start | bytes 786440 | tf_op jit(solution)/shard_map/feature_halo/ppermute | solution.py:233
  30.1 2.8 %collective-permute-start = (bf16[2,512,128]{2,1,0:T(8,128)(2,1)S(1)}, bf16[2,512,128]{2,1,0:T(8,128)(2,1)S(1)}, u32[]{:S(2)}, u32[]{:S(2)}) collective-permute-start(bf16[2,512,128]{2,1,0:T(8,128)(2,1)S(1)} %bitcast.18), channel_id=1, source_target_pairs={{752,0},{756,4},{760,8},{764,12},{0,16},{4,20},{8,24},{12,28},{16,... | collective-permute-start | bytes 786440 | tf_op jit(solution)/shard_map/feature_halo/ppermute | solution.py:233
  32.9 8.2 %all-gather = bf16[2048,128]{1,0:T(8,128)(2,1)S(1)} all-gather(bf16[512,128]{1,0:T(8,128)(2,1)} %param.11), channel_id=2, replica_groups=mesh['y'=8,'z'=12,'xl'=2,'xh'=2,'core'=2] {'xh','core'}, dimensions={0}, use_global_device_ids=true | all-gather | bytes 655360 | tf_op jit(solution)/shard_map/column_gather/all_gather | solution.py:247
  41.2 0.8 bitcast_add_fusion.codes
  41.9 0.0 copy-start
  41.9 2.3 %copy-done = bf16[1,9,16,128,128]{4,3,2,1,0:T(8,128)(2,1)S(1)} copy-done((bf16[1,9,16,128,128]{4,3,2,1,0:T(8,128)(2,1)S(1)}, bf16[1,9,16,128,128]{4,3,2,1,0:T(8,128)(2,1)}, u32[]{:S(2)}) %copy-start) | copy-done | bytes 4718616
  44.3 0.0 copy-start.2
  44.3 2.2 %dense_tiles.1.dense = bf16[10,512,512]{2,1,0:T(8,128)(2,1)S(1)} custom-call(s32[1]{0:T(128)} %bitcast.1.side, s32[9,16]{1,0:T(8,128)S(1)} %bitcast_add_fusion.codes, bf16[1,9,16,128,128]{4,3,2,1,0:T(8,128)(2,1)S(1)} %copy-done, bf16[4,512,128]{2,1,0:T(8,128)(2,1)S(1)} %bitcast.12), custom_call_target="tpu_custom_call" | custom-call | bytes 10485760 | tf_op jit(solution)/shard_map/dense_tiles/pallas_call | solution.py:56
  46.5 0.0 copy-start.1
  46.5 0.0 collective-permute-done.3.xe
  46.5 0.0 collective-permute-done.2.xd
  46.5 0.0 collective-permute-done.1.xb
  46.5 1.7 %collective-permute-done.xa = bf16[2,512,128]{2,1,0:T(8,128)(2,1)S(1)} collective-permute-done((bf16[2,512,128]{2,1,0:T(8,128)(2,1)S(1)}, bf16[2,512,128]{2,1,0:T(8,128)(2,1)S(1)}, u32[]{:S(2)}, u32[]{:S(2)}) %collective-permute-start) | collective-permute-done | bytes 262176 | tf_op jit(solution)/shard_map/feature_halo/ppermute | solution.py:233
  48.3 0.0 copy-done.2
  48.3 1.5 %aggregate_features.1 = bf16[528,128]{1,0:T(8,128)(2,1)S(1)} custom-call(bf16[10,512,512]{2,1,0:T(8,128)(2,1)S(1)} %dense_tiles.1.dense, bf16[2,512,128]{2,1,0:T(8,128)(2,1)S(1)} %collective-permute-done.xa, bf16[2,512,128]{2,1,0:T(8,128)(2,1)S(1)} %collective-permute-done.1.xb, bf16[2,512,128]{2,1,0:T(8,128)(2,1)S(1)} %bitcast.19, ...), custom_call_target="tpu_custom_call" | custom-call | flops 671088640 | bytes 8388608 | tf_op jit(solution)/shard_map/aggregate_features/pallas_call | solution.py:77
  49.8 8.1 %all-gather.2 = bf16[2112,128]{1,0:T(8,128)(2,1)S(1)} all-gather(bf16[528,128]{1,0:T(8,128)(2,1)S(1)} %aggregate_features.1), channel_id=4, replica_groups=mesh['y'=8,'z'=12,'xl'=2,'xh'=2,'core'=2] {'xh','core'}, dimensions={0}, use_global_device_ids=true | all-gather | bytes 675840 | tf_op jit(solution)/shard_map/column_gather/all_gather | solution.py:251
  57.9 0.0 copy-done.1
  57.9 2.6 %activation_and_terms.1 = (bf16[512,128]{1,0:T(8,128)(2,1)}, f32[576,128]{1,0:T(8,128)}, bf16[2,128,512]{2,1,0:T(8,128)(2,1)S(1)}, bf16[2,128,512]{2,1,0:T(8,128...) custom-call(s32[1]{0:T(128)} %bitcast.column, ...), custom_call_target="tpu_custom_call" | custom-call | flops 1275068416 | bytes 10485760 | tf_op jit(solution)/shard_map/activation_and_terms/pallas_call | solution.py:126
  60.5 5.8 %all-to-all-start = ((f32[24,24,128]{2,1,0:T(8,128)}), f32[24,24,128]{2,1,0:T(8,128)S(1)}, u32[]{:S(2)}, u32[]{:S(2)}) async-start(f32[24,24,128]{2,1,0:T(8,128)} %bitcast.8), calls=%async_computation | async-start | bytes 589824 | tf_op jit(solution)/shard_map/weight_scatter/all_to_all | solution.py:256
  66.3 6.1 %collective-permute-start.5 = (bf16[2,128,512]{2,1,0:T(8,128)(2,1)S(1)}, bf16[2,128,512]{2,1,0:T(8,128)(2,1)S(1)}, u32[]{:S(2)}, u32[]{:S(2)}) collective-permute-start(bf16[2,128,512]{2,1,0:T(8,128)(2,1)S(1)} %get-tuple-element.18), channel_id=1, source_target_pairs={{8,0},{12,4},{16,8},{20,12},{24,16},{28,20},{32,24},{36,28},{40,32... | collective-permute-start | bytes 786440 | tf_op jit(solution)/shard_map/term_halo/ppermute | solution.py:233
  72.4 1.9 %collective-permute-start.6 = (bf16[2,128,512]{2,1,0:T(8,128)(2,1)S(1)}, bf16[2,128,512]{2,1,0:T(8,128)(2,1)S(1)}, u32[]{:S(2)}, u32[]{:S(2)}) collective-permute-start(bf16[2,128,512]{2,1,0:T(8,128)(2,1)S(1)} %get-tuple-element.19), channel_id=1, source_target_pairs={{760,0},{764,4},{0,8},{4,12},{8,16},{12,20},{16,24},{20,28},{24,32... | collective-permute-start | bytes 786440 | tf_op jit(solution)/shard_map/term_halo/ppermute | solution.py:233
  74.3 4.8 %collective-permute-start.4 = (bf16[2,128,512]{2,1,0:T(8,128)(2,1)S(1)}, bf16[2,128,512]{2,1,0:T(8,128)(2,1)S(1)}, u32[]{:S(2)}, u32[]{:S(2)}) collective-permute-start(bf16[2,128,512]{2,1,0:T(8,128)(2,1)S(1)} %get-tuple-element.17), channel_id=1, source_target_pairs={{16,0},{20,4},{24,8},{28,12},{32,16},{36,20},{40,24},{44,28},{48,3... | collective-permute-start | bytes 786440 | tf_op jit(solution)/shard_map/term_halo/ppermute | solution.py:233
  79.1 1.9 %collective-permute-start.7 = (bf16[2,128,512]{2,1,0:T(8,128)(2,1)S(1)}, bf16[2,128,512]{2,1,0:T(8,128)(2,1)S(1)}, u32[]{:S(2)}, u32[]{:S(2)}) collective-permute-start(bf16[2,128,512]{2,1,0:T(8,128)(2,1)S(1)} %get-tuple-element.20), channel_id=1, source_target_pairs={{752,0},{756,4},{760,8},{764,12},{0,16},{4,20},{8,24},{12,28},{16,... | collective-permute-start | bytes 786440 | tf_op jit(solution)/shard_map/term_halo/ppermute | solution.py:233
  81.1 3.8 %collective-permute-done.5.refs_1_.tb = bf16[2,128,512]{2,1,0:T(8,128)(2,1)S(1)} collective-permute-done((bf16[2,128,512]{2,1,0:T(8,128)(2,1)S(1)}, bf16[2,128,512]{2,1,0:T(8,128)(2,1)S(1)}, u32[]{:S(2)}, u32[]{:S(2)}) %collective-permute-start.5) | collective-permute-done | bytes 262176 | tf_op jit(solution)/shard_map/term_halo/ppermute | solution.py:233
  84.9 1.8 %collective-permute-done.6.refs_2_.td = bf16[2,128,512]{2,1,0:T(8,128)(2,1)S(1)} collective-permute-done((bf16[2,128,512]{2,1,0:T(8,128)(2,1)S(1)}, bf16[2,128,512]{2,1,0:T(8,128)(2,1)S(1)}, u32[]{:S(2)}, u32[]{:S(2)}) %collective-permute-start.6) | collective-permute-done | bytes 262176 | tf_op jit(solution)/shard_map/term_halo/ppermute | solution.py:233
  86.8 0.0 all-to-all-done.refs_0_
  86.8 0.7 spread_sum.2.first
  87.4 4.1 %all-to-all-start.1 = ((f32[8,24,128]{2,1,0:T(8,128)}), f32[8,24,128]{2,1,0:T(8,128)S(1)}, u32[]{:S(2)}, u32[]{:S(2)}) async-start(f32[8,24,128]{2,1,0:T(8,128)} %spread_sum.2.first), calls=%async_computation.1 | async-start | bytes 196608 | tf_op jit(solution)/shard_map/weight_rows/all_to_all | solution.py:262
  91.5 4.2 %collective-permute-done.4.ta = bf16[2,128,512]{2,1,0:T(8,128)(2,1)S(1)} collective-permute-done((bf16[2,128,512]{2,1,0:T(8,128)(2,1)S(1)}, bf16[2,128,512]{2,1,0:T(8,128)(2,1)S(1)}, u32[]{:S(2)}, u32[]{:S(2)}) %collective-permute-start.4) | collective-permute-done | bytes 262176 | tf_op jit(solution)/shard_map/term_halo/ppermute | solution.py:233
  95.8 0.0 collective-permute-done.7.te
  95.8 0.2 pair_sums.1
  96.0 4.3 %all-to-all-done.1.refs_0_ = f32[8,24,128]{2,1,0:T(8,128)S(1)} async-done(((f32[8,24,128]{2,1,0:T(8,128)}), f32[8,24,128]{2,1,0:T(8,128)S(1)}, u32[]{:S(2)}, u32[]{:S(2)}) %all-to-all-start.1) | async-done | bytes 98336 | tf_op jit(solution)/shard_map/weight_rows/all_to_all | solution.py:262
  100.3 0.7 spread_sum.3.first
  100.9 10.3 %all-to-all-start.2 = ((bf16[24,24,128]{2,1,0:T(8,128)(2,1)}), bf16[24,24,128]{2,1,0:T(8,128)(2,1)S(1)}, u32[]{:S(2)}, u32[]{:S(2)}) async-start(bf16[24,24,128]{2,1,0:T(8,128)(2,1)} %spread_sum.3.first), calls=%async_computation.2 | async-start | bytes 294912 | tf_op jit(solution)/shard_map/weight_gather/all_to_all | solution.py:269
  111.3 2.1 %collective-permute-start.8 = (bf16[128,512]{1,0:T(8,128)(2,1)S(1)}, bf16[128,512]{1,0:T(8,128)(2,1)S(1)}, u32[]{:S(2)}, u32[]{:S(2)}) collective-permute-start(bf16[128,512]{1,0:T(8,128)(2,1)S(1)} %get-tuple-element.23), channel_id=1, source_target_pairs={{4,0},{0,4},{12,8},{8,12},{20,16},{16,20},{28,24},{24,28},{36,32},... | collective-permute-start | bytes 393224 | tf_op jit(solution)/shard_map/term_exchange/ppermute | solution.py:265
  113.4 5.0 %collective-permute-done.8.arrived = bf16[128,512]{1,0:T(8,128)(2,1)S(1)} collective-permute-done((bf16[128,512]{1,0:T(8,128)(2,1)S(1)}, bf16[128,512]{1,0:T(8,128)(2,1)S(1)}, u32[]{:S(2)}, u32[]{:S(2)}) %collective-permute-start.8) | collective-permute-done | bytes 131104 | tf_op jit(solution)/shard_map/term_exchange/ppermute | solution.py:265
  118.4 0.8 node_gradient.1
  119.1 2.9 %all-to-all-done.2 = bf16[24,24,128]{2,1,0:T(8,128)(2,1)S(1)} async-done(((bf16[24,24,128]{2,1,0:T(8,128)(2,1)}), bf16[24,24,128]{2,1,0:T(8,128)(2,1)S(1)}, u32[]{:S(2)}, u32[]{:S(2)}) %all-to-all-start.2) | async-done | bytes 147488 | tf_op jit(solution)/shard_map/weight_gather/all_to_all | solution.py:269
  122.0 0.7 weight_gradient.1
Async XLA Ops:
  14.1 32.5 %collective-permute-start.3 = (bf16[2,512,128]{2,1,0:T(8,128)(2,1)S(1)}, bf16[2,512,128]{2,1,0:T(8,128)(2,1)S(1)}, u32[]{:S(2)}, u32[]{:S(2)}) collective-permute-start(bf16[2,512,128]{2,1,0:T(8,128)(2,1)S(1)} %bitcast.15), channel_id=1, source_target_pairs={{16,0},{20,4},{24,8},{28,12},{32,16},{36,20},{40,24},{44,28},{48,3... | collective-permute-start | bytes 786440 | tf_op jit(solution)/shard_map/feature_halo/ppermute | solution.py:233
  24.2 22.3 %collective-permute-start.2 = (bf16[2,512,128]{2,1,0:T(8,128)(2,1)S(1)}, bf16[2,512,128]{2,1,0:T(8,128)(2,1)S(1)}, u32[]{:S(2)}, u32[]{:S(2)}) collective-permute-start(bf16[2,512,128]{2,1,0:T(8,128)(2,1)S(1)} %bitcast.16), channel_id=1, source_target_pairs={{8,0},{12,4},{16,8},{20,12},{24,16},{28,20},{32,24},{36,28},{40,32... | collective-permute-start | bytes 786440 | tf_op jit(solution)/shard_map/feature_halo/ppermute | solution.py:233
  26.7 19.8 %collective-permute-start.1 = (bf16[2,512,128]{2,1,0:T(8,128)(2,1)S(1)}, bf16[2,512,128]{2,1,0:T(8,128)(2,1)S(1)}, u32[]{:S(2)}, u32[]{:S(2)}) collective-permute-start(bf16[2,512,128]{2,1,0:T(8,128)(2,1)S(1)} %bitcast.17), channel_id=1, source_target_pairs={{760,0},{764,4},{0,8},{4,12},{8,16},{12,20},{16,24},{20,28},{24,32... | collective-permute-start | bytes 786440 | tf_op jit(solution)/shard_map/feature_halo/ppermute | solution.py:233
  30.1 18.2 %collective-permute-start = (bf16[2,512,128]{2,1,0:T(8,128)(2,1)S(1)}, bf16[2,512,128]{2,1,0:T(8,128)(2,1)S(1)}, u32[]{:S(2)}, u32[]{:S(2)}) collective-permute-start(bf16[2,512,128]{2,1,0:T(8,128)(2,1)S(1)} %bitcast.18), channel_id=1, source_target_pairs={{752,0},{756,4},{760,8},{764,12},{0,16},{4,20},{8,24},{12,28},{16,... | collective-permute-start | bytes 786440 | tf_op jit(solution)/shard_map/feature_halo/ppermute | solution.py:233
  41.9 2.3 %copy-start = (bf16[1,9,16,128,128]{4,3,2,1,0:T(8,128)(2,1)S(1)}, bf16[1,9,16,128,128]{4,3,2,1,0:T(8,128)(2,1)}, u32[]{:S(2)}) copy-start(bf16[1,9,16,128,128]{4,3,2,1,0:T(8,128)(2,1)} %slab.1) | copy-start | bytes 14155780
  44.3 4.0 %copy-start.2 = (bf16[128]{0:T(256)(128)(2,1)S(1)}, bf16[128]{0:T(256)(128)(2,1)}, u32[]{:S(2)}) copy-start(bf16[128]{0:T(256)(128)(2,1)} %param.10) | copy-start | bytes 772
  46.5 11.4 %copy-start.1 = (bf16[512,512]{1,0:T(8,128)(2,1)S(1)}, bf16[512,512]{1,0:T(8,128)(2,1)}, u32[]{:S(2)}) copy-start(bf16[512,512]{1,0:T(8,128)(2,1)} %weight.1) | copy-start | bytes 1572868
  60.5 26.3 %all-to-all-start = ((f32[24,24,128]{2,1,0:T(8,128)}), f32[24,24,128]{2,1,0:T(8,128)S(1)}, u32[]{:S(2)}, u32[]{:S(2)}) async-start(f32[24,24,128]{2,1,0:T(8,128)} %bitcast.8), calls=%async_computation | async-start | bytes 589824 | tf_op jit(solution)/shard_map/weight_scatter/all_to_all | solution.py:256
  66.3 18.6 %collective-permute-start.5 = (bf16[2,128,512]{2,1,0:T(8,128)(2,1)S(1)}, bf16[2,128,512]{2,1,0:T(8,128)(2,1)S(1)}, u32[]{:S(2)}, u32[]{:S(2)}) collective-permute-start(bf16[2,128,512]{2,1,0:T(8,128)(2,1)S(1)} %get-tuple-element.18), channel_id=1, source_target_pairs={{8,0},{12,4},{16,8},{20,12},{24,16},{28,20},{32,24},{36,28},{40,32... | collective-permute-start | bytes 786440 | tf_op jit(solution)/shard_map/term_halo/ppermute | solution.py:233
  72.4 14.4 %collective-permute-start.6 = (bf16[2,128,512]{2,1,0:T(8,128)(2,1)S(1)}, bf16[2,128,512]{2,1,0:T(8,128)(2,1)S(1)}, u32[]{:S(2)}, u32[]{:S(2)}) collective-permute-start(bf16[2,128,512]{2,1,0:T(8,128)(2,1)S(1)} %get-tuple-element.19), channel_id=1, source_target_pairs={{760,0},{764,4},{0,8},{4,12},{8,16},{12,20},{16,24},{20,28},{24,32... | collective-permute-start | bytes 786440 | tf_op jit(solution)/shard_map/term_halo/ppermute | solution.py:233
  74.3 21.4 %collective-permute-start.4 = (bf16[2,128,512]{2,1,0:T(8,128)(2,1)S(1)}, bf16[2,128,512]{2,1,0:T(8,128)(2,1)S(1)}, u32[]{:S(2)}, u32[]{:S(2)}) collective-permute-start(bf16[2,128,512]{2,1,0:T(8,128)(2,1)S(1)} %get-tuple-element.17), channel_id=1, source_target_pairs={{16,0},{20,4},{24,8},{28,12},{32,16},{36,20},{40,24},{44,28},{48,3... | collective-permute-start | bytes 786440 | tf_op jit(solution)/shard_map/term_halo/ppermute | solution.py:233
  79.1 16.6 %collective-permute-start.7 = (bf16[2,128,512]{2,1,0:T(8,128)(2,1)S(1)}, bf16[2,128,512]{2,1,0:T(8,128)(2,1)S(1)}, u32[]{:S(2)}, u32[]{:S(2)}) collective-permute-start(bf16[2,128,512]{2,1,0:T(8,128)(2,1)S(1)} %get-tuple-element.20), channel_id=1, source_target_pairs={{752,0},{756,4},{760,8},{764,12},{0,16},{4,20},{8,24},{12,28},{16,... | collective-permute-start | bytes 786440 | tf_op jit(solution)/shard_map/term_halo/ppermute | solution.py:233
  87.4 12.8 %all-to-all-start.1 = ((f32[8,24,128]{2,1,0:T(8,128)}), f32[8,24,128]{2,1,0:T(8,128)S(1)}, u32[]{:S(2)}, u32[]{:S(2)}) async-start(f32[8,24,128]{2,1,0:T(8,128)} %spread_sum.2.first), calls=%async_computation.1 | async-start | bytes 196608 | tf_op jit(solution)/shard_map/weight_rows/all_to_all | solution.py:262
  100.9 21.1 %all-to-all-start.2 = ((bf16[24,24,128]{2,1,0:T(8,128)(2,1)}), bf16[24,24,128]{2,1,0:T(8,128)(2,1)S(1)}, u32[]{:S(2)}, u32[]{:S(2)}) async-start(bf16[24,24,128]{2,1,0:T(8,128)(2,1)} %spread_sum.3.first), calls=%async_computation.2 | async-start | bytes 294912 | tf_op jit(solution)/shard_map/weight_gather/all_to_all | solution.py:269
  111.3 7.1 %collective-permute-start.8 = (bf16[128,512]{1,0:T(8,128)(2,1)S(1)}, bf16[128,512]{1,0:T(8,128)(2,1)S(1)}, u32[]{:S(2)}, u32[]{:S(2)}) collective-permute-start(bf16[128,512]{1,0:T(8,128)(2,1)S(1)} %get-tuple-element.23), channel_id=1, source_target_pairs={{4,0},{0,4},{12,8},{8,12},{20,16},{16,20},{28,24},{24,28},{36,32},... | collective-permute-start | bytes 393224 | tf_op jit(solution)/shard_map/term_exchange/ppermute | solution.py:265

commit v5 on v4

--- a/solution.py
+++ b/solution.py
@@ -17,7 +17,6 @@
 OFFSETS = 9
 SLOTS = 16
 REACH = 4
-WINDOW = OFFSETS + 1
 N_Y, N_Z, N_XL = 8, 12, 2
 PAIRS = N_Y * N_Z
 PACK_ROWS = ROWS + 16
@@ -35,67 +34,78 @@
     return pltpu.CompilerParams(vmem_limit_bytes=mib * 1024 * 1024)
 
 
-def dense_kernel(side, codes, slab, cots, dense):
-    del cots
-    left_over = (1 - side[0]) * OFFSETS
-    dense[left_over] = jnp.zeros((ROWS, ROWS), BF16)
-
-    @pl.loop(0, OFFSETS)
-    def _(offset):
+def dense_kernel(codes, slab, dense, held, sems):
+    copies = [
+        pltpu.make_async_copy(slab.at[0, o], held.at[o], sems.at[o]) for o in range(OFFSETS)
+    ]
+    for copy in copies:
+        copy.start()
+    for offset, copy in enumerate(copies):
+        copy.wait()
         for slot in range(SLOTS):
             code = codes[offset, slot]
             row = pl.multiple_of(((code >> 2) & 3) * TILE, TILE)
             col = pl.multiple_of((code & 3) * TILE, TILE)
-            tile = slab[0, offset, slot]
-            dense[offset + side[0], pl.ds(row, TILE), pl.ds(col, TILE)] = jnp.where(
+            tile = held[offset, slot]
+            dense[offset, pl.ds(row, TILE), pl.ds(col, TILE)] = jnp.where(
                 code < BLOCKS * BLOCKS, tile, jnp.zeros_like(tile)
             )
 
 
-def make_dense(side, codes, slab, cots):
+def make_dense(codes, slab):
     return pl.pallas_call(
         dense_kernel,
-        in_specs=[SMEM, SMEM, VMEM, pl.BlockSpec(memory_space=pl.ANY)],
+        in_specs=[SMEM, pl.BlockSpec(memory_space=pltpu.HBM)],
         out_specs=VMEM,
-        out_shape=jax.ShapeDtypeStruct((WINDOW, ROWS, ROWS), BF16),
+        out_shape=jax.ShapeDtypeStruct((OFFSETS, ROWS, ROWS), BF16),
+        scratch_shapes=[
+            pltpu.VMEM((OFFSETS, SLOTS, TILE, TILE), BF16),
+            pltpu.SemaphoreType.DMA((OFFSETS,)),
+        ],
         compiler_params=params(),
         cost_estimate=pl.CostEstimate(flops=0, bytes_accessed=10 << 20, transcendentals=0),
         name="dense_tiles",
-    )(side, codes, slab, cots)
-
-
-def gather_kernel(dense, xa, xb, xc, xd, xe, bias, out):
-    total = jnp.zeros((ROWS, WIDTH), F32)
-    for k, pair in enumerate((xa, xb, xc, xd, xe)):
-        for s in range(2):
-            total += jnp.dot(dense[2 * k + s], pair[s], preferred_element_type=F32)
+    )(codes, pltpu.with_memory_space_constraint(slab, pltpu.HBM))
+
+
+def gather_kernel(side, dense, before, own, after, far, lone, bias, out):
+    s = side[0]
+    total = jnp.dot(dense[8 - 8 * s], lone[...], preferred_element_type=F32)
+    for first, pair in ((2 - s, before), (4 - s, own), (6 - s, after), (7 * s, far)):
+        for i in range(2):
+            total += jnp.dot(dense[first + i], pair[i], preferred_element_type=F32)
     out[0:ROWS, :] = total.astype(BF16)
     out[ROWS:, :] = jnp.broadcast_to(bias[...], (16, WIDTH))
 
 
-def gather_rows(dense, pairs, bias):
+def gather_rows(side, dense, blocks, bias):
     return pl.pallas_call(
         gather_kernel,
-        in_specs=[VMEM] * 7,
+        in_specs=[SMEM] + [VMEM] * 7,
         out_specs=VMEM,
         out_shape=jax.ShapeDtypeStruct((PACK_ROWS, WIDTH), BF16),
         compiler_params=params(),
         cost_estimate=pl.CostEstimate(
-            flops=2 * WINDOW * ROWS * ROWS * WIDTH, bytes_accessed=8 << 20, transcendentals=0
+            flops=2 * OFFSETS * ROWS * ROWS * WIDTH, bytes_accessed=8 << 20, transcendentals=0
         ),
         name="aggregate_features",
-    )(dense, *pairs, bias)
-
-
-def middle_kernel(column, mixed, cots, weight, dense, act, part, ta, tb, tc, td, te, act_all, grad_all, feats):
-    mine = pl.multiple_of(column[0] * WIDTH, WIDTH)
+    )(side, dense, *blocks, bias)
+
+
+def middle_kernel(
+    place, mixed, cots, weight, dense,
+    act, part, before, own, after, far, lone,
+    act_all, grad_all, feats,
+):
+    side = place[0]
+    mine = pl.multiple_of(place[1] * WIDTH, WIDTH)
     bias = jnp.concatenate([mixed[c, ROWS:, :] for c in range(COLS)], axis=1)[0:1].astype(F32)
     step = 128
     for i in range(ROWS // step):
         span = slice(i * step, (i + 1) * step)
-        own = jnp.concatenate([mixed[c, span, :] for c in range(COLS)], axis=1)
-        feats[span, :] = own
-        preact = jnp.dot(own, weight[...], preferred_element_type=F32) + bias
+        rows = jnp.concatenate([mixed[c, span, :] for c in range(COLS)], axis=1)
+        feats[span, :] = rows
+        preact = jnp.dot(rows, weight[...], preferred_element_type=F32) + bias
         sig = 1.0 / (1.0 + jnp.exp(-preact))
         act_all[span, :] = (preact * sig).astype(BF16)
         cot = jnp.concatenate([cots[c, span, :] for c in range(COLS)], axis=1)
@@ -116,13 +126,16 @@
         (((1,), (1,)), ((), ())),
         preferred_element_type=F32,
     ).astype(BF16)
-    for k, pair in enumerate((ta, tb, tc, td, te)):
-        for s in range(2):
-            pair[s] = jnp.dot(back, dense[2 * k + s], preferred_element_type=F32).astype(BF16)
-
-
-def middle(column, mixed, cots, weight, dense):
-    term = jax.ShapeDtypeStruct((2, WIDTH, ROWS), BF16)
+    for first, pair in (
+        (2 - side, before), (4 - side, own), (6 - side, after), (7 * side, far)
+    ):
+        for i in range(2):
+            pair[i] = jnp.dot(back, dense[first + i], preferred_element_type=F32).astype(BF16)
+    lone[...] = jnp.dot(back, dense[8 - 8 * side], preferred_element_type=F32).astype(BF16)
+
+
+def middle(place, mixed, cots, weight, dense):
+    pair = jax.ShapeDtypeStruct((2, WIDTH, ROWS), BF16)
     return pl.pallas_call(
         middle_kernel,
         in_specs=[SMEM] + [VMEM] * 4,
@@ -131,14 +144,15 @@
             jax.ShapeDtypeStruct((ROWS, WIDTH), BF16),
             jax.ShapeDtypeStruct((RING * SHARE, WIDTH), F32),
         ]
-        + [term] * 5,
+        + [pair] * 4
+        + [jax.ShapeDtypeStruct((WIDTH, ROWS), BF16)],
         scratch_shapes=[pltpu.VMEM((ROWS, HIDDEN), BF16)] * 3,
         compiler_params=params(),
         cost_estimate=pl.CostEstimate(
-            flops=2 * (WINDOW + 9) * ROWS * ROWS * WIDTH, bytes_accessed=10 << 20, transcendentals=ROWS * HIDDEN
+            flops=2 * (OFFSETS + 9) * ROWS * ROWS * WIDTH, bytes_accessed=10 << 20, transcendentals=ROWS * HIDDEN
         ),
         name="activation_and_terms",
-    )(column, mixed, cots, weight, dense)
+    )(place, mixed, cots, weight, dense)
 
 
 def share_kernel(scale, shares, *rest):
@@ -159,16 +173,16 @@
     )(shares, *behind)
 
 
-def split_kernel(side, own, ta, tb, td, te, first, keep, send):
+def split_kernel(side, own, before, after, far, lone, first, keep, send):
     del first
     for s in range(2):
         total = own[s].astype(F32)
-        for arrived in (ta, tb, td, te):
+        for arrived in (before, after, far):
             total += arrived[s].astype(F32)
 
         @pl.when(side[0] == s)
         def _():
-            keep[...] = total
+            keep[...] = total + lone[...].astype(F32)
 
         @pl.when(side[0] != s)
         def _():
@@ -226,10 +240,12 @@
     )(whole)
 
 
-def from_pair(block, hops):
-    route = [
-        (2 * ((p + hops) % PAIRS) + s, 2 * p + s) for p in range(PAIRS) for s in range(2)
-    ]
+def routed(block, source):
+    route = []
+    for p in range(PAIRS):
+        for s in range(2):
+            pair, other = source(p, s)
+            route.append((2 * (pair % PAIRS) + other, 2 * p + s))
     return lax.ppermute(block, BLK, route)
 
 
@@ -241,28 +257,35 @@
     codes = tile_row[0] * BLOCKS + tile_col[0] + BLOCKS * BLOCKS * dead.astype(jnp.int32)
 
     with jax.named_scope("feature_halo"):
+        lone = routed(node_feats, lambda p, s: (p + 2 - 4 * s, s))
         pair = lax.all_gather(node_feats, "xl", axis=0, tiled=False)
-        pairs = [pair if k == 0 else from_pair(pair, k) for k in (-2, -1, 0, 1, 2)]
+        far = routed(pair, lambda p, s: (p - 2 + 4 * s, s))
+        before = routed(pair, lambda p, s: (p - 1, s))
+        after = routed(pair, lambda p, s: (p + 1, s))
     with jax.named_scope("column_gather"):
         cots = lax.all_gather(cotangent, COL, axis=0, tiled=False)
-    dense = make_dense(side, codes, adj_tiles, cots)
-    mine = gather_rows(dense, pairs, layer_bias.reshape(1, WIDTH))
+    dense = make_dense(codes, adj_tiles)
+    mine = gather_rows(side, dense, (before, pair, after, far, lone), layer_bias.reshape(1, WIDTH))
     with jax.named_scope("column_gather"):
         mixed = lax.all_gather(mine, COL, axis=0, tiled=False)
-    act, part, ta, tb, tc, td, te = middle(column, mixed, cots, weight, dense)
+    act, part, before, own, after, far, lone = middle(
+        jnp.concatenate([side, column]), mixed, cots, weight, dense
+    )
 
     ring = ("z", "xl")
     with jax.named_scope("weight_scatter"):
         shares = lax.all_to_all(part.reshape(RING, SHARE, WIDTH), ring, 0, 0, tiled=True)
     with jax.named_scope("term_halo"):
-        arrived = [from_pair(t, -k) for k, t in ((-2, ta), (-1, tb), (1, td), (2, te))]
-    spread = spread_sum(shares, arrived[1:3], N_Y, 1.0, F32)
-    keep, send = split_terms(side, tc, arrived, spread)
+        before = routed(before, lambda p, s: (p + 1, s))
+        after = routed(after, lambda p, s: (p - 1, s))
+        far = routed(far, lambda p, s: (p + 2 - 4 * s, s))
+        lone = routed(lone, lambda p, s: (p - 2 + 4 * s, s))
+    spread = spread_sum(shares, [before], N_Y, 1.0, F32)
+    keep, send = split_terms(side, own, (before, after, far, lone), spread)
     with jax.named_scope("weight_rows"):
         shares = lax.all_to_all(spread, "y", 0, 0, tiled=True)
     with jax.named_scope("term_exchange"):
-        swap = [(b ^ 1, b) for b in range(2 * PAIRS)]
-        other = lax.ppermute(send, BLK, swap)
+        other = routed(send, lambda p, s: (p, 1 - s))
     spread = spread_sum(shares, [keep], RING, float(NODES) ** -0.5, BF16)
     grad_nodes = last_sum(keep, other, spread)
     with jax.named_scope("weight_gather"):

time: 123 us -> 126 us (1.024)
  waiting for transfers between devices: 23.8 us -> 20 us
  blocking collectives: 29.7 us -> 33.2 us
  starting transfers between devices: 55.9 us -> 59.4 us
  local copies, waits for them, and re-layouts: 2.35 us -> 0.01 us
  Pallas kernels: 9.43 us -> 10.7 us
    all_to_all x1, waiting for transfers between devices: 4.26 us -> 0.01 us  [on_device(): shares = lax.all_to_all(spread, 'y', 0, 0, tiled=True)]
    all_gather x1, blocking collectives: 13.4 us -> 16.1 us  [on_device(): pair = lax.all_gather(node_feats, 'xl', axis=0, tiled=False)]
    unnamed x6 -> x4, local copies, waits for them, and re-layouts: 2.35 us -> 0.01 us
    all_to_all x1, starting transfers between devices: 5.78 us -> 8.09 us  [on_device(): lax.all_to_all(part.reshape(RING, SHARE, WIDTH), ring, 0, 0, tiled=True)]
  transfers between devices with their start and end apart: 12 -> 12, of which waited for: 7 -> 5; matrix products, arithmetic and copies ran while one was open for 1% -> 1% of each run, Pallas kernels for 3% -> 4%
where the time goes in v5:
time: 126 us; the launch traced here: 125 us
  starting transfers between devices  59.4 us (47%)
  blocking collectives  33.2 us (26%)
  waiting for transfers between devices  20 us (16%)
  Pallas kernels  10.7 us (8%)
    ppermute x9, starting transfers between devices, routed(): return lax.ppermute(block, BLK, route)  36.8 us
    ppermute x9, waiting for transfers between devices, routed(): return lax.ppermute(block, BLK, route)  16.2 us
    all_gather x1, blocking collectives, on_device(): pair = lax.all_gather(node_feats, 'xl', axis=0, tiled=False)  16.1 us
    all_to_all x1, starting transfers between devices, on_device(): lax.all_to_all(spread, ring, 0, 0, tiled=True).reshape(RING * SHARE, WIDTH)  9.82 us
    all_gather x1, blocking collectives, on_device(): mixed = lax.all_gather(mine, COL, axis=0, tiled=False)  8.89 us
    all_gather x1, blocking collectives, on_device(): cots = lax.all_gather(cotangent, COL, axis=0, tiled=False)  8.21 us
    all_to_all x1, starting transfers between devices, on_device(): lax.all_to_all(part.reshape(RING, SHARE, WIDTH), ring, 0, 0, tiled=True)  8.09 us
    all_to_all x1, starting transfers between devices, on_device(): shares = lax.all_to_all(spread, 'y', 0, 0, tiled=True)  4.68 us
  transfers between devices with their start and end apart: 12, of which 5 were waited for; matrix products, arithmetic and copies ran while one was open for 1% of the time, Pallas kernels for 4%

profile of v5, /device:TPU:2, one launch (start us, length us, event | category | flops | bytes accessed | tf_op | source)
XLA Modules:
  0.0 125.0 jit_solution(16857425833709182636)
XLA Ops:
  0.6 6.1 %collective-permute-start.3 = (bf16[512,128]{1,0:T(8,128)(2,1)}, bf16[512,128]{1,0:T(8,128)(2,1)S(1)}, u32[]{:S(2)}, u32[]{:S(2)}) collective-permute-start(bf16[512,128]{1,0:T(8,128)(2,1)} %param.8), channel_id=1, source_target_pairs={{16,0},{756,4},{24,8},{764,12},{32,16},{4,20},{40,24},{12,28},{48,... | collective-permute-start | bytes 393224 | tf_op jit(solution)/shard_map/feature_halo/ppermute | solution.py:249
  6.7 16.1 %all-gather = bf16[1024,128]{1,0:T(8,128)(2,1)S(1)} all-gather(bf16[512,128]{1,0:T(8,128)(2,1)} %param.8), channel_id=2, replica_groups=mesh['y'=8,'z'=12,'xl'=2,'xh'=2,'core'=2] {'xl'}, dimensions={0}, use_global_device_ids=true | all-gather | bytes 393216 | tf_op jit(solution)/shard_map/feature_halo/all_gather | solution.py:261
  22.8 3.4 %collective-permute-start.2 = (bf16[2,512,128]{2,1,0:T(8,128)(2,1)S(1)}, bf16[2,512,128]{2,1,0:T(8,128)(2,1)S(1)}, u32[]{:S(2)}, u32[]{:S(2)}) collective-permute-start(bf16[2,512,128]{2,1,0:T(8,128)(2,1)S(1)} %bitcast.14), channel_id=1, source_target_pairs={{752,0},{20,4},{760,8},{28,12},{0,16},{36,20},{8,24},{44,28},{16,3... | collective-permute-start | bytes 786440 | tf_op jit(solution)/shard_map/feature_halo/ppermute | solution.py:249
  26.2 4.6 %collective-permute-start.1 = (bf16[2,512,128]{2,1,0:T(8,128)(2,1)S(1)}, bf16[2,512,128]{2,1,0:T(8,128)(2,1)S(1)}, u32[]{:S(2)}, u32[]{:S(2)}) collective-permute-start(bf16[2,512,128]{2,1,0:T(8,128)(2,1)S(1)} %bitcast.15), channel_id=1, source_target_pairs={{8,0},{12,4},{16,8},{20,12},{24,16},{28,20},{32,24},{36,28},{40,32... | collective-permute-start | bytes 786440 | tf_op jit(solution)/shard_map/feature_halo/ppermute | solution.py:249
  30.7 1.9 %collective-permute-start = (bf16[2,512,128]{2,1,0:T(8,128)(2,1)S(1)}, bf16[2,512,128]{2,1,0:T(8,128)(2,1)S(1)}, u32[]{:S(2)}, u32[]{:S(2)}) collective-permute-start(bf16[2,512,128]{2,1,0:T(8,128)(2,1)S(1)} %bitcast.16), channel_id=1, source_target_pairs={{760,0},{764,4},{0,8},{4,12},{8,16},{12,20},{16,24},{20,28},{24,32... | collective-permute-start | bytes 786440 | tf_op jit(solution)/shard_map/feature_halo/ppermute | solution.py:249
  32.7 0.8 bitcast_add_fusion.codes
  33.4 8.2 %all-gather.2 = bf16[2048,128]{1,0:T(8,128)(2,1)S(1)} all-gather(bf16[512,128]{1,0:T(8,128)(2,1)} %param.11), channel_id=4, replica_groups=mesh['y'=8,'z'=12,'xl'=2,'xh'=2,'core'=2] {'xh','core'}, dimensions={0}, use_global_device_ids=true | all-gather | bytes 655360 | tf_op jit(solution)/shard_map/column_gather/all_gather | solution.py:266
  41.7 0.0 copy-start.1
  41.7 3.2 %dense_tiles.1.dense = bf16[9,512,512]{2,1,0:T(8,128)(2,1)S(1)} custom-call(s32[9,16]{1,0:T(8,128)S(1)} %bitcast_add_fusion.codes, bf16[1,9,16,128,128]{4,3,2,1,0:T(8,128)(2,1)} %slab.1), custom_call_target="tpu_custom_call" | custom-call | bytes 10485760 | tf_op jit(solution)/shard_map/dense_tiles/pallas_call | solution.py:56
  44.8 0.0 copy-start
  44.9 0.1 pad_add_fusion.place
  44.9 0.0 collective-permute-done.3.lone
  44.9 0.0 collective-permute-done.2.far
  44.9 0.0 collective-permute-done.1.after
  45.0 0.0 collective-permute-done.before
  45.0 0.0 copy-done.1
  45.0 1.4 %aggregate_features.1 = bf16[528,128]{1,0:T(8,128)(2,1)S(1)} custom-call(s32[1]{0:T(128)} %bitcast.side, bf16[9,512,512]{2,1,0:T(8,128)(2,1)S(1)} %dense_tiles.1.dense, bf16[2,512,128]{2,1,0:T(8,128)(2,1)S(1)} %collective-permute-done.before, bf16[2,512,128]{2,1,0:T(8,128)(2,1)S(1)} %bitcast.17, bf16[2,512,128]{2,1,0:T(8,128)(2,1)S(1)} %collective-permute-done.1.after, ...), custom_call_target="tpu_custom_call" | custom-call | flops 603979776 | bytes 8388608 | tf_op jit(solution)/shard_map/aggregate_features/pallas_call | solution.py:82
  46.4 8.9 %all-gather.1 = bf16[2112,128]{1,0:T(8,128)(2,1)S(1)} all-gather(bf16[528,128]{1,0:T(8,128)(2,1)S(1)} %aggregate_features.1), channel_id=3, replica_groups=mesh['y'=8,'z'=12,'xl'=2,'xh'=2,'core'=2] {'xh','core'}, dimensions={0}, use_global_device_ids=true | all-gather | bytes 675840 | tf_op jit(solution)/shard_map/column_gather/all_gather | solution.py:270
  55.3 0.0 copy-done
  55.3 3.1 %activation_and_terms.1 = (bf16[512,128]{1,0:T(8,128)(2,1)}, f32[576,128]{1,0:T(8,128)}, bf16[2,128,512]{2,1,0:T(8,128)(2,1)S(1)}, bf16[2,128,512]{2,1,0:T(8,128...) custom-call(s32[2]{0:T(128)S(1)} %pad_add_fusion.place, ...), custom_call_target="tpu_custom_call" | custom-call | flops 1207959552 | bytes 10485760 | tf_op jit(solution)/shard_map/activation_and_terms/pallas_call | solution.py:139
  58.4 8.1 %all-to-all-start = ((f32[24,24,128]{2,1,0:T(8,128)}), f32[24,24,128]{2,1,0:T(8,128)S(1)}, u32[]{:S(2)}, u32[]{:S(2)}) async-start(f32[24,24,128]{2,1,0:T(8,128)} %bitcast.8), calls=%async_computation | async-start | bytes 589824 | tf_op jit(solution)/shard_map/weight_scatter/all_to_all | solution.py:277
  66.5 7.7 %collective-permute-start.4 = (bf16[2,128,512]{2,1,0:T(8,128)(2,1)S(1)}, bf16[2,128,512]{2,1,0:T(8,128)(2,1)S(1)}, u32[]{:S(2)}, u32[]{:S(2)}) collective-permute-start(bf16[2,128,512]{2,1,0:T(8,128)(2,1)S(1)} %get-tuple-element.17), channel_id=1, source_target_pairs={{8,0},{12,4},{16,8},{20,12},{24,16},{28,20},{32,24},{36,28},{40,32... | collective-permute-start | bytes 786440 | tf_op jit(solution)/shard_map/term_halo/ppermute | solution.py:249
  74.2 1.9 %collective-permute-start.5 = (bf16[2,128,512]{2,1,0:T(8,128)(2,1)S(1)}, bf16[2,128,512]{2,1,0:T(8,128)(2,1)S(1)}, u32[]{:S(2)}, u32[]{:S(2)}) collective-permute-start(bf16[2,128,512]{2,1,0:T(8,128)(2,1)S(1)} %get-tuple-element.18), channel_id=1, source_target_pairs={{760,0},{764,4},{0,8},{4,12},{8,16},{12,20},{16,24},{20,28},{24,32... | collective-permute-start | bytes 786440 | tf_op jit(solution)/shard_map/term_halo/ppermute | solution.py:249
  76.2 1.9 %collective-permute-start.6 = (bf16[2,128,512]{2,1,0:T(8,128)(2,1)S(1)}, bf16[2,128,512]{2,1,0:T(8,128)(2,1)S(1)}, u32[]{:S(2)}, u32[]{:S(2)}) collective-permute-start(bf16[2,128,512]{2,1,0:T(8,128)(2,1)S(1)} %get-tuple-element.19), channel_id=1, source_target_pairs={{16,0},{756,4},{24,8},{764,12},{32,16},{4,20},{40,24},{12,28},{48,... | collective-permute-start | bytes 786440 | tf_op jit(solution)/shard_map/term_halo/ppermute | solution.py:249
  78.1 6.0 %collective-permute-done.4.refs_1_.before = bf16[2,128,512]{2,1,0:T(8,128)(2,1)S(1)} collective-permute-done((bf16[2,128,512]{2,1,0:T(8,128)(2,1)S(1)}, bf16[2,128,512]{2,1,0:T(8,128)(2,1)S(1)}, u32[]{:S(2)}, u32[]{:S(2)}) %collective-permute-start.4) | collective-permute-done | bytes 262176 | tf_op jit(solution)/shard_map/term_halo/ppermute | solution.py:249
  84.1 0.2 all-to-all-done.refs_0_
  84.3 0.7 spread_sum.2.first
  85.0 4.7 %all-to-all-start.1 = ((f32[8,24,128]{2,1,0:T(8,128)}), f32[8,24,128]{2,1,0:T(8,128)S(1)}, u32[]{:S(2)}, u32[]{:S(2)}) async-start(f32[8,24,128]{2,1,0:T(8,128)} %spread_sum.2.first), calls=%async_computation.1 | async-start | bytes 196608 | tf_op jit(solution)/shard_map/weight_rows/all_to_all | solution.py:286
  89.7 7.2 %collective-permute-start.7 = (bf16[128,512]{1,0:T(8,128)(2,1)S(1)}, bf16[128,512]{1,0:T(8,128)(2,1)S(1)}, u32[]{:S(2)}, u32[]{:S(2)}) collective-permute-start(bf16[128,512]{1,0:T(8,128)(2,1)S(1)} %get-tuple-element.20), channel_id=1, source_target_pairs={{752,0},{20,4},{760,8},{28,12},{0,16},{36,20},{8,24},{44,28},{16,3... | collective-permute-start | bytes 393224 | tf_op jit(solution)/shard_map/term_halo/ppermute | solution.py:249
  96.9 5.0 %collective-permute-done.7.lone = bf16[128,512]{1,0:T(8,128)(2,1)S(1)} collective-permute-done((bf16[128,512]{1,0:T(8,128)(2,1)S(1)}, bf16[128,512]{1,0:T(8,128)(2,1)S(1)}, u32[]{:S(2)}, u32[]{:S(2)}) %collective-permute-start.7) | collective-permute-done | bytes 131104 | tf_op jit(solution)/shard_map/term_halo/ppermute | solution.py:249
  101.8 0.0 collective-permute-done.5.after
  101.8 0.0 collective-permute-done.6.far
  101.9 0.2 pair_sums.1
  102.1 0.0 all-to-all-done.1.refs_0_
  102.1 0.7 spread_sum.3.first
  102.8 9.8 %all-to-all-start.2 = ((bf16[24,24,128]{2,1,0:T(8,128)(2,1)}), bf16[24,24,128]{2,1,0:T(8,128)(2,1)S(1)}, u32[]{:S(2)}, u32[]{:S(2)}) async-start(bf16[24,24,128]{2,1,0:T(8,128)(2,1)} %spread_sum.3.first), calls=%async_computation.2 | async-start | bytes 294912 | tf_op jit(solution)/shard_map/weight_gather/all_to_all | solution.py:292
  112.6 2.1 %collective-permute-start.8 = (bf16[128,512]{1,0:T(8,128)(2,1)S(1)}, bf16[128,512]{1,0:T(8,128)(2,1)S(1)}, u32[]{:S(2)}, u32[]{:S(2)}) collective-permute-start(bf16[128,512]{1,0:T(8,128)(2,1)S(1)} %get-tuple-element.23), channel_id=1, source_target_pairs={{4,0},{0,4},{12,8},{8,12},{20,16},{16,20},{28,24},{24,28},{36,32},... | collective-permute-start | bytes 393224 | tf_op jit(solution)/shard_map/term_exchange/ppermute | solution.py:249
  114.7 5.2 %collective-permute-done.8.arrived = bf16[128,512]{1,0:T(8,128)(2,1)S(1)} collective-permute-done((bf16[128,512]{1,0:T(8,128)(2,1)S(1)}, bf16[128,512]{1,0:T(8,128)(2,1)S(1)}, u32[]{:S(2)}, u32[]{:S(2)}) %collective-permute-start.8) | collective-permute-done | bytes 131104 | tf_op jit(solution)/shard_map/term_exchange/ppermute | solution.py:249
  119.8 0.8 node_gradient.1
  120.6 3.6 %all-to-all-done.2 = bf16[24,24,128]{2,1,0:T(8,128)(2,1)S(1)} async-done(((bf16[24,24,128]{2,1,0:T(8,128)(2,1)}), bf16[24,24,128]{2,1,0:T(8,128)(2,1)S(1)}, u32[]{:S(2)}, u32[]{:S(2)}) %all-to-all-start.2) | async-done | bytes 147488 | tf_op jit(solution)/shard_map/weight_gather/all_to_all | solution.py:292
  124.2 0.7 weight_gradient.1
Async XLA Ops:
  0.6 44.3 %collective-permute-start.3 = (bf16[512,128]{1,0:T(8,128)(2,1)}, bf16[512,128]{1,0:T(8,128)(2,1)S(1)}, u32[]{:S(2)}, u32[]{:S(2)}) collective-permute-start(bf16[512,128]{1,0:T(8,128)(2,1)} %param.8), channel_id=1, source_target_pairs={{16,0},{756,4},{24,8},{764,12},{32,16},{4,20},{40,24},{12,28},{48,... | collective-permute-start | bytes 393224 | tf_op jit(solution)/shard_map/feature_halo/ppermute | solution.py:249
  22.8 22.1 %collective-permute-start.2 = (bf16[2,512,128]{2,1,0:T(8,128)(2,1)S(1)}, bf16[2,512,128]{2,1,0:T(8,128)(2,1)S(1)}, u32[]{:S(2)}, u32[]{:S(2)}) collective-permute-start(bf16[2,512,128]{2,1,0:T(8,128)(2,1)S(1)} %bitcast.14), channel_id=1, source_target_pairs={{752,0},{20,4},{760,8},{28,12},{0,16},{36,20},{8,24},{44,28},{16,3... | collective-permute-start | bytes 786440 | tf_op jit(solution)/shard_map/feature_halo/ppermute | solution.py:249
  26.2 18.8 %collective-permute-start.1 = (bf16[2,512,128]{2,1,0:T(8,128)(2,1)S(1)}, bf16[2,512,128]{2,1,0:T(8,128)(2,1)S(1)}, u32[]{:S(2)}, u32[]{:S(2)}) collective-permute-start(bf16[2,512,128]{2,1,0:T(8,128)(2,1)S(1)} %bitcast.15), channel_id=1, source_target_pairs={{8,0},{12,4},{16,8},{20,12},{24,16},{28,20},{32,24},{36,28},{40,32... | collective-permute-start | bytes 786440 | tf_op jit(solution)/shard_map/feature_halo/ppermute | solution.py:249
  30.7 14.2 %collective-permute-start = (bf16[2,512,128]{2,1,0:T(8,128)(2,1)S(1)}, bf16[2,512,128]{2,1,0:T(8,128)(2,1)S(1)}, u32[]{:S(2)}, u32[]{:S(2)}) collective-permute-start(bf16[2,512,128]{2,1,0:T(8,128)(2,1)S(1)} %bitcast.16), channel_id=1, source_target_pairs={{760,0},{764,4},{0,8},{4,12},{8,16},{12,20},{16,24},{20,28},{24,32... | collective-permute-start | bytes 786440 | tf_op jit(solution)/shard_map/feature_halo/ppermute | solution.py:249
  41.7 3.3 %copy-start.1 = (bf16[128]{0:T(256)(128)(2,1)S(1)}, bf16[128]{0:T(256)(128)(2,1)}, u32[]{:S(2)}) copy-start(bf16[128]{0:T(256)(128)(2,1)} %param.10) | copy-start | bytes 772
  44.8 10.4 %copy-start = (bf16[512,512]{1,0:T(8,128)(2,1)S(1)}, bf16[512,512]{1,0:T(8,128)(2,1)}, u32[]{:S(2)}) copy-start(bf16[512,512]{1,0:T(8,128)(2,1)} %weight.1) | copy-start | bytes 1572868
  58.4 26.0 %all-to-all-start = ((f32[24,24,128]{2,1,0:T(8,128)}), f32[24,24,128]{2,1,0:T(8,128)S(1)}, u32[]{:S(2)}, u32[]{:S(2)}) async-start(f32[24,24,128]{2,1,0:T(8,128)} %bitcast.8), calls=%async_computation | async-start | bytes 589824 | tf_op jit(solution)/shard_map/weight_scatter/all_to_all | solution.py:277
  66.5 17.6 %collective-permute-start.4 = (bf16[2,128,512]{2,1,0:T(8,128)(2,1)S(1)}, bf16[2,128,512]{2,1,0:T(8,128)(2,1)S(1)}, u32[]{:S(2)}, u32[]{:S(2)}) collective-permute-start(bf16[2,128,512]{2,1,0:T(8,128)(2,1)S(1)} %get-tuple-element.17), channel_id=1, source_target_pairs={{8,0},{12,4},{16,8},{20,12},{24,16},{28,20},{32,24},{36,28},{40,32... | collective-permute-start | bytes 786440 | tf_op jit(solution)/shard_map/term_halo/ppermute | solution.py:249
  74.2 27.6 %collective-permute-start.5 = (bf16[2,128,512]{2,1,0:T(8,128)(2,1)S(1)}, bf16[2,128,512]{2,1,0:T(8,128)(2,1)S(1)}, u32[]{:S(2)}, u32[]{:S(2)}) collective-permute-start(bf16[2,128,512]{2,1,0:T(8,128)(2,1)S(1)} %get-tuple-element.18), channel_id=1, source_target_pairs={{760,0},{764,4},{0,8},{4,12},{8,16},{12,20},{16,24},{20,28},{24,32... | collective-permute-start | bytes 786440 | tf_op jit(solution)/shard_map/term_halo/ppermute | solution.py:249
  76.2 25.7 %collective-permute-start.6 = (bf16[2,128,512]{2,1,0:T(8,128)(2,1)S(1)}, bf16[2,128,512]{2,1,0:T(8,128)(2,1)S(1)}, u32[]{:S(2)}, u32[]{:S(2)}) collective-permute-start(bf16[2,128,512]{2,1,0:T(8,128)(2,1)S(1)} %get-tuple-element.19), channel_id=1, source_target_pairs={{16,0},{756,4},{24,8},{764,12},{32,16},{4,20},{40,24},{12,28},{48,... | collective-permute-start | bytes 786440 | tf_op jit(solution)/shard_map/term_halo/ppermute | solution.py:249
  85.0 17.0 %all-to-all-start.1 = ((f32[8,24,128]{2,1,0:T(8,128)}), f32[8,24,128]{2,1,0:T(8,128)S(1)}, u32[]{:S(2)}, u32[]{:S(2)}) async-start(f32[8,24,128]{2,1,0:T(8,128)} %spread_sum.2.first), calls=%async_computation.1 | async-start | bytes 196608 | tf_op jit(solution)/shard_map/weight_rows/all_to_all | solution.py:286
  89.7 12.1 %collective-permute-start.7 = (bf16[128,512]{1,0:T(8,128)(2,1)S(1)}, bf16[128,512]{1,0:T(8,128)(2,1)S(1)}, u32[]{:S(2)}, u32[]{:S(2)}) collective-permute-start(bf16[128,512]{1,0:T(8,128)(2,1)S(1)} %get-tuple-element.20), channel_id=1, source_target_pairs={{752,0},{20,4},{760,8},{28,12},{0,16},{36,20},{8,24},{44,28},{16,3... | collective-permute-start | bytes 393224 | tf_op jit(solution)/shard_map/term_halo/ppermute | solution.py:249
  102.8 21.5 %all-to-all-start.2 = ((bf16[24,24,128]{2,1,0:T(8,128)(2,1)}), bf16[24,24,128]{2,1,0:T(8,128)(2,1)S(1)}, u32[]{:S(2)}, u32[]{:S(2)}) async-start(bf16[24,24,128]{2,1,0:T(8,128)(2,1)} %spread_sum.3.first), calls=%async_computation.2 | async-start | bytes 294912 | tf_op jit(solution)/shard_map/weight_gather/all_to_all | solution.py:292
  112.6 7.3 %collective-permute-start.8 = (bf16[128,512]{1,0:T(8,128)(2,1)S(1)}, bf16[128,512]{1,0:T(8,128)(2,1)S(1)}, u32[]{:S(2)}, u32[]{:S(2)}) collective-permute-start(bf16[128,512]{1,0:T(8,128)(2,1)S(1)} %get-tuple-element.23), channel_id=1, source_target_pairs={{4,0},{0,4},{12,8},{8,12},{20,16},{16,20},{28,24},{24,28},{36,32},... | collective-permute-start | bytes 393224 | tf_op jit(solution)/shard_map/term_exchange/ppermute | solution.py:249

commit v6 on v5

--- a/solution.py
+++ b/solution.py
@@ -18,11 +18,13 @@
 SLOTS = 16
 REACH = 4
 N_Y, N_Z, N_XL = 8, 12, 2
+GROUP = 4
 PAIRS = N_Y * N_Z
 PACK_ROWS = ROWS + 16
 RING = N_Z * N_XL
 SHARE = 24
-BLK = ("y", "z", "xl")
+BLK = ("y", "zq", "zp", "xl")
+FOUR = ("zp", "xl")
 COL = ("xh", "core")
 BF16 = jnp.bfloat16
 F32 = jnp.float32
@@ -40,6 +42,8 @@
     ]
     for copy in copies:
         copy.start()
+    dense[0] = jnp.zeros((ROWS, ROWS), BF16)
+    dense[OFFSETS + 1] = jnp.zeros((ROWS, ROWS), BF16)
     for offset, copy in enumerate(copies):
         copy.wait()
         for slot in range(SLOTS):
@@ -47,7 +51,7 @@
             row = pl.multiple_of(((code >> 2) & 3) * TILE, TILE)
             col = pl.multiple_of((code & 3) * TILE, TILE)
             tile = held[offset, slot]
-            dense[offset, pl.ds(row, TILE), pl.ds(col, TILE)] = jnp.where(
+            dense[offset + 1, pl.ds(row, TILE), pl.ds(col, TILE)] = jnp.where(
                 code < BLOCKS * BLOCKS, tile, jnp.zeros_like(tile)
             )
 
@@ -57,7 +61,7 @@
         dense_kernel,
         in_specs=[SMEM, pl.BlockSpec(memory_space=pltpu.HBM)],
         out_specs=VMEM,
-        out_shape=jax.ShapeDtypeStruct((OFFSETS, ROWS, ROWS), BF16),
+        out_shape=jax.ShapeDtypeStruct((OFFSETS + 2, ROWS, ROWS), BF16),
         scratch_shapes=[
             pltpu.VMEM((OFFSETS, SLOTS, TILE, TILE), BF16),
             pltpu.SemaphoreType.DMA((OFFSETS,)),
@@ -68,20 +72,24 @@
     )(codes, pltpu.with_memory_space_constraint(slab, pltpu.HBM))
 
 
-def gather_kernel(side, dense, before, own, after, far, lone, bias, out):
-    s = side[0]
-    total = jnp.dot(dense[8 - 8 * s], lone[...], preferred_element_type=F32)
-    for first, pair in ((2 - s, before), (4 - s, own), (6 - s, after), (7 * s, far)):
-        for i in range(2):
-            total += jnp.dot(dense[first + i], pair[i], preferred_element_type=F32)
+def starts(member):
+    upper = member // 2
+    return 5 - member, 1 + 8 * upper - member, 9 - 6 * upper - member
+
+
+def gather_kernel(member, dense, own, beside, beyond, bias, out):
+    total = jnp.zeros((ROWS, WIDTH), F32)
+    for first, blocks in zip(starts(member[0]), (own, beside, beyond)):
+        for i in range(blocks.shape[0]):
+            total += jnp.dot(dense[first + i], blocks[i], preferred_element_type=F32)
     out[0:ROWS, :] = total.astype(BF16)
     out[ROWS:, :] = jnp.broadcast_to(bias[...], (16, WIDTH))
 
 
-def gather_rows(side, dense, blocks, bias):
+def gather_rows(member, dense, blocks, bias):
     return pl.pallas_call(
         gather_kernel,
-        in_specs=[SMEM] + [VMEM] * 7,
+        in_specs=[SMEM] + [VMEM] * 5,
         out_specs=VMEM,
         out_shape=jax.ShapeDtypeStruct((PACK_ROWS, WIDTH), BF16),
         compiler_params=params(),
@@ -89,15 +97,14 @@
             flops=2 * OFFSETS * ROWS * ROWS * WIDTH, bytes_accessed=8 << 20, transcendentals=0
         ),
         name="aggregate_features",
-    )(side, dense, *blocks, bias)
+    )(member, dense, *blocks, bias)
 
 
 def middle_kernel(
     place, mixed, cots, weight, dense,
-    act, part, before, own, after, far, lone,
+    act, part, own, beside, beyond,
     act_all, grad_all, feats,
 ):
-    side = place[0]
     mine = pl.multiple_of(place[1] * WIDTH, WIDTH)
     bias = jnp.concatenate([mixed[c, ROWS:, :] for c in range(COLS)], axis=1)[0:1].astype(F32)
     step = 128
@@ -126,26 +133,21 @@
         (((1,), (1,)), ((), ())),
         preferred_element_type=F32,
     ).astype(BF16)
-    for first, pair in (
-        (2 - side, before), (4 - side, own), (6 - side, after), (7 * side, far)
-    ):
-        for i in range(2):
-            pair[i] = jnp.dot(back, dense[first + i], preferred_element_type=F32).astype(BF16)
-    lone[...] = jnp.dot(back, dense[8 - 8 * side], preferred_element_type=F32).astype(BF16)
+    for first, terms in zip(starts(place[0]), (own, beside, beyond)):
+        for i in range(terms.shape[0]):
+            terms[i] = jnp.dot(back, dense[first + i], preferred_element_type=F32).astype(BF16)
 
 
 def middle(place, mixed, cots, weight, dense):
-    pair = jax.ShapeDtypeStruct((2, WIDTH, ROWS), BF16)
     return pl.pallas_call(
         middle_kernel,
         in_specs=[SMEM] + [VMEM] * 4,
-        out_specs=[VMEM] * 7,
+        out_specs=[VMEM] * 5,
         out_shape=[
             jax.ShapeDtypeStruct((ROWS, WIDTH), BF16),
             jax.ShapeDtypeStruct((RING * SHARE, WIDTH), F32),
         ]
-        + [pair] * 4
-        + [jax.ShapeDtypeStruct((WIDTH, ROWS), BF16)],
+        + [jax.ShapeDtypeStruct((n, WIDTH, ROWS), BF16) for n in (GROUP, GROUP, 2)],
         scratch_shapes=[pltpu.VMEM((ROWS, HIDDEN), BF16)] * 3,
         compiler_params=params(),
         cost_estimate=pl.CostEstimate(
@@ -173,35 +175,56 @@
     )(shares, *behind)
 
 
-def split_kernel(side, own, before, after, far, lone, first, keep, send):
+def split_kernel(member, own, beside, beyond, first, keep, send):
     del first
-    for s in range(2):
-        total = own[s].astype(F32)
-        for arrived in (before, after, far):
-            total += arrived[s].astype(F32)
-
-        @pl.when(side[0] == s)
+    side, upper = member[0] % 2, member[0] // 2
+    for i in range(GROUP):
+        total = own[i].astype(F32) + beside[i].astype(F32)
+        total += jnp.where(upper == i // 2, beyond[i % 2].astype(F32), 0.0)
+
+        @pl.when(side == i % 2)
         def _():
-            keep[...] = total + lone[...].astype(F32)
-
-        @pl.when(side[0] != s)
+            keep[i // 2] = total
+
+        @pl.when(side != i % 2)
         def _():
-            send[...] = total.astype(BF16)
-
-
-def split_terms(side, own, arrived, first):
+            send[i // 2] = total.astype(BF16)
+
+
+def split_terms(member, own, arrived, first):
     return pl.pallas_call(
         split_kernel,
-        in_specs=[SMEM] + [VMEM] * 5 + [pl.BlockSpec(memory_space=pl.ANY)],
+        in_specs=[SMEM] + [VMEM] * 3 + [pl.BlockSpec(memory_space=pl.ANY)],
+        out_specs=[VMEM] * 2,
+        out_shape=[
+            jax.ShapeDtypeStruct((2, WIDTH, ROWS), F32),
+            jax.ShapeDtypeStruct((2, WIDTH, ROWS), BF16),
+        ],
+        compiler_params=params(),
+        cost_estimate=pl.CostEstimate(flops=1 << 20, bytes_accessed=2 << 20, transcendentals=0),
+        name="group_sums",
+    )(member, own, *arrived, first)
+
+
+def halve_kernel(member, mine, arrived, keep, send):
+    upper = member[0] // 2
+    keep[...] = mine[upper] + arrived[upper].astype(F32)
+    send[...] = (mine[1 - upper] + arrived[1 - upper].astype(F32)).astype(BF16)
+
+
+def halve_terms(member, mine, arrived):
+    return pl.pallas_call(
+        halve_kernel,
+        in_specs=[SMEM] + [VMEM] * 2,
         out_specs=[VMEM] * 2,
         out_shape=[
             jax.ShapeDtypeStruct((WIDTH, ROWS), F32),
             jax.ShapeDtypeStruct((WIDTH, ROWS), BF16),
         ],
         compiler_params=params(),
-        cost_estimate=pl.CostEstimate(flops=1 << 20, bytes_accessed=2 << 20, transcendentals=0),
-        name="pair_sums",
-    )(side, own, *arrived, first)
+        cost_estimate=pl.CostEstimate(flops=1 << 18, bytes_accessed=1 << 20, transcendentals=0),
+        name="side_sums",
+    )(member, mine, arrived)
 
 
 def last_kernel(keep, arrived, first, out):
@@ -250,43 +273,44 @@
 
 
 def on_device(node_feats, weight, layer_bias, cotangent, adj_tiles, tile_row, tile_col, tile_count):
-    side = lax.axis_index("xl").astype(jnp.int32).reshape(1)
+    member = lax.axis_index(FOUR).astype(jnp.int32).reshape(1)
     column = lax.axis_index(COL).astype(jnp.int32).reshape(1)
     slots = jnp.arange(SLOTS, dtype=jnp.int32)[None, :]
     dead = slots >= tile_count[0][:, None]
     codes = tile_row[0] * BLOCKS + tile_col[0] + BLOCKS * BLOCKS * dead.astype(jnp.int32)
 
+    def one_away(block):
+        return routed(block, lambda p, s: (p - 1 + 2 * (p % 2), s))
+
     with jax.named_scope("feature_halo"):
-        lone = routed(node_feats, lambda p, s: (p + 2 - 4 * s, s))
-        pair = lax.all_gather(node_feats, "xl", axis=0, tiled=False)
-        far = routed(pair, lambda p, s: (p - 2 + 4 * s, s))
-        before = routed(pair, lambda p, s: (p - 1, s))
-        after = routed(pair, lambda p, s: (p + 1, s))
+        four = lax.all_gather(node_feats, FOUR, axis=0, tiled=False)
+        beside = one_away(four)
+        pair = lax.dynamic_slice_in_dim(four, 2 * lax.axis_index("zp"), 2, 0)
+        beyond = routed(pair, lambda p, s: (p + 2 - 4 * (p % 2), s))
     with jax.named_scope("column_gather"):
         cots = lax.all_gather(cotangent, COL, axis=0, tiled=False)
     dense = make_dense(codes, adj_tiles)
-    mine = gather_rows(side, dense, (before, pair, after, far, lone), layer_bias.reshape(1, WIDTH))
+    mine = gather_rows(member, dense, (four, beside, beyond), layer_bias.reshape(1, WIDTH))
     with jax.named_scope("column_gather"):
         mixed = lax.all_gather(mine, COL, axis=0, tiled=False)
-    act, part, before, own, after, far, lone = middle(
-        jnp.concatenate([side, column]), mixed, cots, weight, dense
-    )
-
-    ring = ("z", "xl")
+    act, part, own, beside, beyond = middle(
+        jnp.concatenate([member, column]), mixed, cots, weight, dense
+    )
+
+    ring = ("zq", "zp", "xl")
     with jax.named_scope("weight_scatter"):
         shares = lax.all_to_all(part.reshape(RING, SHARE, WIDTH), ring, 0, 0, tiled=True)
     with jax.named_scope("term_halo"):
-        before = routed(before, lambda p, s: (p + 1, s))
-        after = routed(after, lambda p, s: (p - 1, s))
-        far = routed(far, lambda p, s: (p + 2 - 4 * s, s))
-        lone = routed(lone, lambda p, s: (p - 2 + 4 * s, s))
-    spread = spread_sum(shares, [before], N_Y, 1.0, F32)
-    keep, send = split_terms(side, own, (before, after, far, lone), spread)
+        beside = one_away(beside)
+        beyond = routed(beyond, lambda p, s: (p - 2 + 4 * (p % 2), s))
+    spread = spread_sum(shares, [beside], N_Y, 1.0, F32)
+    keep, send = split_terms(member, own, (beside, beyond), spread)
     with jax.named_scope("weight_rows"):
         shares = lax.all_to_all(spread, "y", 0, 0, tiled=True)
+    spread = spread_sum(shares, [keep], RING, float(NODES) ** -0.5, BF16)
     with jax.named_scope("term_exchange"):
-        other = routed(send, lambda p, s: (p, 1 - s))
-    spread = spread_sum(shares, [keep], RING, float(NODES) ** -0.5, BF16)
+        keep, send = halve_terms(member, keep, routed(send, lambda p, s: (p, 1 - s)))
+        other = routed(send, lambda p, s: (p + 1 - 2 * (p % 2), s))
     grad_nodes = last_sum(keep, other, spread)
     with jax.named_scope("weight_gather"):
         whole = lax.all_to_all(spread, ring, 0, 0, tiled=True).reshape(RING * SHARE, WIDTH)
@@ -296,7 +320,7 @@
 
 def solution(mesh):
     fine = Mesh(
-        np.asarray(mesh.devices).reshape(N_Y, N_Z, N_XL, 2, 2), ("y", "z", "xl", "xh", "core")
+        np.asarray(mesh.devices).reshape(N_Y, N_Z // 2, 2, N_XL, 2, 2), BLK + COL
     )
     placed = (
         P(BLK, COL),

time: 126 us -> 140 us (1.11)
  waiting for transfers between devices: 20 us -> 42.3 us
  starting transfers between devices: 59.4 us -> 47.2 us
  blocking collectives: 33.2 us -> 36.6 us
    ppermute x9 -> x6, waiting for transfers between devices: 16.2 us -> 33.9 us  [routed(): return lax.ppermute(block, BLK, route)]
    all_to_all x1, waiting for transfers between devices: 0.01 us -> 8.39 us  [on_device(): shares = lax.all_to_all(spread, 'y', 0, 0, tiled=True)]
    ppermute x9 -> x6, starting transfers between devices: 36.8 us -> 30.3 us  [routed(): return lax.ppermute(block, BLK, route)]
    all_gather x1, blocking collectives: 16.1 us -> 19.9 us  [on_device(): four = lax.all_gather(node_feats, FOUR, axis=0, tiled=False)]
    all_to_all x1, waiting for transfers between devices: 3.63 us -> 0.01 us  [on_device(): lax.all_to_all(spread, ring, 0, 0, tiled=True).reshape(RING * SHARE, WIDTH)]
    all_to_all x1, starting transfers between devices: 8.09 us -> 5.19 us  [on_device(): lax.all_to_all(part.reshape(RING, SHARE, WIDTH), ring, 0, 0, tiled=True)]
    all_to_all x1, starting transfers between devices: 9.82 us -> 7.61 us  [on_device(): lax.all_to_all(spread, ring, 0, 0, tiled=True).reshape(RING * SHARE, WIDTH)]
  transfers between devices with their start and end apart: 12 -> 9, of which waited for: 5 -> 5; matrix products, arithmetic and copies ran while one was open for 1% -> 1% of each run, Pallas kernels for 4% -> 4%
where the time goes in v6:
time: 140 us; the launch traced here: 139 us
  starting transfers between devices  47.2 us (34%)
  waiting for transfers between devices  42.3 us (30%)
  blocking collectives  36.6 us (26%)
  Pallas kernels  11.1 us (8%)
    ppermute x6, waiting for transfers between devices, routed(): return lax.ppermute(block, BLK, route)  33.9 us
    ppermute x6, starting transfers between devices, routed(): return lax.ppermute(block, BLK, route)  30.3 us
    all_gather x1, blocking collectives, on_device(): four = lax.all_gather(node_feats, FOUR, axis=0, tiled=False)  19.9 us
    all_gather x1, blocking collectives, on_device(): mixed = lax.all_gather(mine, COL, axis=0, tiled=False)  8.58 us
    all_to_all x1, waiting for transfers between devices, on_device(): shares = lax.all_to_all(spread, 'y', 0, 0, tiled=True)  8.39 us
    all_gather x1, blocking collectives, on_device(): cots = lax.all_gather(cotangent, COL, axis=0, tiled=False)  8.13 us
    all_to_all x1, starting transfers between devices, on_device(): lax.all_to_all(spread, ring, 0, 0, tiled=True).reshape(RING * SHARE, WIDTH)  7.61 us
    all_to_all x1, starting transfers between devices, on_device(): lax.all_to_all(part.reshape(RING, SHARE, WIDTH), ring, 0, 0, tiled=True)  5.19 us
  transfers between devices with their start and end apart: 9, of which 5 were waited for; matrix products, arithmetic and copies ran while one was open for 1% of the time, Pallas kernels for 4%

profile of v6, /device:TPU:2, one launch (start us, length us, event | category | flops | bytes accessed | tf_op | source)
XLA Modules:
  0.0 139.0 jit_solution(10127708285003852658)
XLA Ops:
  0.6 0.0 copy-start.2
  0.6 19.9 %all-gather = bf16[2048,128]{1,0:T(8,128)(2,1)S(1)} all-gather(bf16[512,128]{1,0:T(8,128)(2,1)} %param.8), channel_id=2, replica_groups=mesh['y'=8,'zq'=6,'zp'=2,'xl'=2,'xh'=2,'core'=2] {'zp','xl'}, dimensions={0}, use_global_device_ids=true | all-gather | bytes 655360 | tf_op jit(solution)/shard_map/feature_halo/all_gather | solution.py:286
  20.5 12.0 %collective-permute-start = (bf16[4,512,128]{2,1,0:T(8,128)(2,1)S(1)}, bf16[4,512,128]{2,1,0:T(8,128)(2,1)S(1)}, u32[]{:S(2)}, u32[]{:S(2)}) collective-permute-start(bf16[4,512,128]{2,1,0:T(8,128)(2,1)S(1)} %bitcast.12), channel_id=1, source_target_pairs={{760,0},{764,4},{16,8},{20,12},{8,16},{12,20},{32,24},{36,28},{24,... | collective-permute-start | bytes 1572872 | tf_op jit(solution)/shard_map/feature_halo/ppermute | solution.py:272
  32.6 0.0 copy-start.1
  32.7 2.5 %collective-permute-start.1 = (bf16[2,512,128]{2,1,0:T(8,128)(2,1)S(1)}, bf16[2,512,128]{2,1,0:T(8,128)(2,1)S(1)}, u32[]{:S(2)}, u32[]{:S(2)}) collective-permute-start(bf16[2,512,128]{2,1,0:T(8,128)(2,1)S(1)} %constant_dynamic-slice_fusion), channel_id=1, source_target_pairs={{16,0},{20,4},{760,8},{764,12},{32,16},{36,20},{8,24},{12,28},{48,... | collective-permute-start | bytes 786440 | tf_op jit(solution)/shard_map/feature_halo/ppermute | solution.py:272
  35.1 0.8 bitcast_add_fusion.codes
  35.9 3.2 %dense_tiles.1.dense = bf16[11,512,512]{2,1,0:T(8,128)(2,1)S(1)} custom-call(s32[9,16]{1,0:T(8,128)S(1)} %bitcast_add_fusion.codes, bf16[1,9,16,128,128]{4,3,2,1,0:T(8,128)(2,1)} %slab.1), custom_call_target="tpu_custom_call" | custom-call | bytes 10485760 | tf_op jit(solution)/shard_map/dense_tiles/pallas_call | solution.py:60
  39.1 0.0 copy-start
  39.1 0.1 pad_add_fusion.place
  39.2 0.0 copy-done.2
  39.2 8.1 %all-gather.2 = bf16[2048,128]{1,0:T(8,128)(2,1)S(1)} all-gather(bf16[512,128]{1,0:T(8,128)(2,1)S(1)} %copy-done.2), channel_id=4, replica_groups=mesh['y'=8,'zq'=6,'zp'=2,'xl'=2,'xh'=2,'core'=2] {'xh','core'}, dimensions={0}, use_global_device_ids=true | all-gather | bytes 655360 | tf_op jit(solution)/shard_map/column_gather/all_gather | solution.py:291
  47.3 0.3 collective-permute-done.1.beyond
  47.6 0.0 collective-permute-done.beside
  47.6 0.0 copy-done.1
  47.6 1.5 %aggregate_features.1 = bf16[528,128]{1,0:T(8,128)(2,1)S(1)} custom-call(s32[1]{0:T(128)} %bitcast.member, bf16[11,512,512]{2,1,0:T(8,128)(2,1)S(1)} %dense_tiles.1.dense, bf16[4,512,128]{2,1,0:T(8,128)(2,1)S(1)} %bitcast.14, bf16[4,512,128]{2,1,0:T(8,128)(2,1)S(1)} %collective-permute-done.beside, bf16[2,512,128]{2,1,0:T(8,128)(2,1)S(1)} %collective-permute-done.1.beyond, ...), custom_call_target="tpu_custom_call" | custom-call | flops 603979776 | bytes 8388608 | tf_op jit(solution)/shard_map/aggregate_features/pallas_call | solution.py:90
  49.2 8.6 %all-gather.1 = bf16[2112,128]{1,0:T(8,128)(2,1)S(1)} all-gather(bf16[528,128]{1,0:T(8,128)(2,1)S(1)} %aggregate_features.1), channel_id=3, replica_groups=mesh['y'=8,'zq'=6,'zp'=2,'xl'=2,'xh'=2,'core'=2] {'xh','core'}, dimensions={0}, use_global_device_ids=true | all-gather | bytes 675840 | tf_op jit(solution)/shard_map/column_gather/all_gather | solution.py:295
  57.8 0.0 copy-done
  57.8 3.2 %activation_and_terms.1 = (bf16[512,128]{1,0:T(8,128)(2,1)}, f32[576,128]{1,0:T(8,128)}, bf16[4,128,512]{2,1,0:T(8,128)(2,1)S(1)}, bf16[4,128,512]{2,1,0:T(8,128)(2,1)S(1)}, bf16[2,128,512]{2,1,0:T(8,128)(2,1)S(1)}) custom-call(s32[2]{0:T(128)S(1)} %pad_add_fusion.place, bf16[4,528,128]{2,1,0:T(8,128)(2,1)S(1)} %bitcast.15, ...), custom_call_target="tpu_custom_call" | custom-call | flops 1207959552 | bytes 10485760 | tf_op jit(solution)/shard_map/activation_and_terms/pallas_call | solution.py:142
  60.9 5.2 %all-to-all-start = ((f32[24,24,128]{2,1,0:T(8,128)}), f32[24,24,128]{2,1,0:T(8,128)S(1)}, u32[]{:S(2)}, u32[]{:S(2)}) async-start(f32[24,24,128]{2,1,0:T(8,128)} %bitcast.8), calls=%async_computation | async-start | bytes 589824 | tf_op jit(solution)/shard_map/weight_scatter/all_to_all | solution.py:302
  66.1 8.4 %collective-permute-start.2 = (bf16[4,128,512]{2,1,0:T(8,128)(2,1)S(1)}, bf16[4,128,512]{2,1,0:T(8,128)(2,1)S(1)}, u32[]{:S(2)}, u32[]{:S(2)}) collective-permute-start(bf16[4,128,512]{2,1,0:T(8,128)(2,1)S(1)} %get-tuple-element.17), channel_id=1, source_target_pairs={{760,0},{764,4},{16,8},{20,12},{8,16},{12,20},{32,24},{36,28},{24,... | collective-permute-start | bytes 1572872 | tf_op jit(solution)/shard_map/term_halo/ppermute | solution.py:272
  74.6 1.9 %collective-permute-start.3 = (bf16[2,128,512]{2,1,0:T(8,128)(2,1)S(1)}, bf16[2,128,512]{2,1,0:T(8,128)(2,1)S(1)}, u32[]{:S(2)}, u32[]{:S(2)}) collective-permute-start(bf16[2,128,512]{2,1,0:T(8,128)(2,1)S(1)} %get-tuple-element.18), channel_id=1, source_target_pairs={{752,0},{756,4},{24,8},{28,12},{0,16},{4,20},{40,24},{44,28},{16,3... | collective-permute-start | bytes 786440 | tf_op jit(solution)/shard_map/term_halo/ppermute | solution.py:272
  76.5 23.3 %collective-permute-done.2.refs_1_.beside = bf16[4,128,512]{2,1,0:T(8,128)(2,1)S(1)} collective-permute-done((bf16[4,128,512]{2,1,0:T(8,128)(2,1)S(1)}, bf16[4,128,512]{2,1,0:T(8,128)(2,1)S(1)}, u32[]{:S(2)}, u32[]{:S(2)}) %collective-permute-start.2) | collective-permute-done | bytes 524320 | tf_op jit(solution)/shard_map/term_halo/ppermute | solution.py:272
  99.8 0.0 all-to-all-done.refs_0_
  99.8 0.7 spread_sum.2.first
  100.5 4.1 %all-to-all-start.1 = ((f32[8,24,128]{2,1,0:T(8,128)}), f32[8,24,128]{2,1,0:T(8,128)S(1)}, u32[]{:S(2)}, u32[]{:S(2)}) async-start(f32[8,24,128]{2,1,0:T(8,128)} %spread_sum.2.first), calls=%async_computation.1 | async-start | bytes 196608 | tf_op jit(solution)/shard_map/weight_rows/all_to_all | solution.py:309
  104.5 0.0 collective-permute-done.3.beyond
  104.5 0.3 group_sums.1
  104.9 8.4 %all-to-all-done.1.refs_0_ = f32[8,24,128]{2,1,0:T(8,128)S(1)} async-done(((f32[8,24,128]{2,1,0:T(8,128)}), f32[8,24,128]{2,1,0:T(8,128)S(1)}, u32[]{:S(2)}, u32[]{:S(2)}) %all-to-all-start.1) | async-done | bytes 98336 | tf_op jit(solution)/shard_map/weight_rows/all_to_all | solution.py:309
  113.3 0.7 spread_sum.3.first
  113.9 7.6 %all-to-all-start.2 = ((bf16[24,24,128]{2,1,0:T(8,128)(2,1)}), bf16[24,24,128]{2,1,0:T(8,128)(2,1)S(1)}, u32[]{:S(2)}, u32[]{:S(2)}) async-start(bf16[24,24,128]{2,1,0:T(8,128)(2,1)} %spread_sum.3.first), calls=%async_computation.2 | async-start | bytes 294912 | tf_op jit(solution)/shard_map/weight_gather/all_to_all | solution.py:316
  121.6 2.1 %collective-permute-start.4 = (bf16[2,128,512]{2,1,0:T(8,128)(2,1)S(1)}, bf16[2,128,512]{2,1,0:T(8,128)(2,1)S(1)}, u32[]{:S(2)}, u32[]{:S(2)}) collective-permute-start(bf16[2,128,512]{2,1,0:T(8,128)(2,1)S(1)} %get-tuple-element.21), channel_id=1, source_target_pairs={{4,0},{0,4},{12,8},{8,12},{20,16},{16,20},{28,24},{24,28},{36,32},... | collective-permute-start | bytes 786440 | tf_op jit(solution)/shard_map/term_exchange/ppermute | solution.py:272
  123.7 6.9 %collective-permute-done.4.arrived = bf16[2,128,512]{2,1,0:T(8,128)(2,1)S(1)} collective-permute-done((bf16[2,128,512]{2,1,0:T(8,128)(2,1)S(1)}, bf16[2,128,512]{2,1,0:T(8,128)(2,1)S(1)}, u32[]{:S(2)}, u32[]{:S(2)}) %collective-permute-start.4) | collective-permute-done | bytes 262176 | tf_op jit(solution)/shard_map/term_exchange/ppermute | solution.py:272
  130.6 3.4 %collective-permute-start.5 = (bf16[128,512]{1,0:T(8,128)(2,1)S(1)}, bf16[128,512]{1,0:T(8,128)(2,1)S(1)}, u32[]{:S(2)}, u32[]{:S(2)}) collective-permute-start(bf16[128,512]{1,0:T(8,128)(2,1)S(1)} %get-tuple-element.23), channel_id=1, source_target_pairs={{8,0},{12,4},{0,8},{4,12},{24,16},{28,20},{16,24},{20,28},{40,32},... | collective-permute-start | bytes 393224 | tf_op jit(solution)/shard_map/term_exchange/ppermute | solution.py:272
  134.0 3.4 %collective-permute-done.5.arrived = bf16[128,512]{1,0:T(8,128)(2,1)S(1)} collective-permute-done((bf16[128,512]{1,0:T(8,128)(2,1)S(1)}, bf16[128,512]{1,0:T(8,128)(2,1)S(1)}, u32[]{:S(2)}, u32[]{:S(2)}) %collective-permute-start.5) | collective-permute-done | bytes 131104 | tf_op jit(solution)/shard_map/term_exchange/ppermute | solution.py:272
  137.5 0.8 node_gradient.1
  138.2 0.0 all-to-all-done.2
  138.2 0.7 weight_gradient.1
  (2 shorter events, 0.1 us)
Async XLA Ops:
  0.6 38.6 %copy-start.2 = (bf16[512,128]{1,0:T(8,128)(2,1)S(1)}, bf16[512,128]{1,0:T(8,128)(2,1)}, u32[]{:S(2)}) copy-start(bf16[512,128]{1,0:T(8,128)(2,1)} %param.11) | copy-start | bytes 393220
  20.5 27.1 %collective-permute-start = (bf16[4,512,128]{2,1,0:T(8,128)(2,1)S(1)}, bf16[4,512,128]{2,1,0:T(8,128)(2,1)S(1)}, u32[]{:S(2)}, u32[]{:S(2)}) collective-permute-start(bf16[4,512,128]{2,1,0:T(8,128)(2,1)S(1)} %bitcast.12), channel_id=1, source_target_pairs={{760,0},{764,4},{16,8},{20,12},{8,16},{12,20},{32,24},{36,28},{24,... | collective-permute-start | bytes 1572872 | tf_op jit(solution)/shard_map/feature_halo/ppermute | solution.py:272
  32.6 15.0 %copy-start.1 = (bf16[128]{0:T(256)(128)(2,1)S(1)}, bf16[128]{0:T(256)(128)(2,1)}, u32[]{:S(2)}) copy-start(bf16[128]{0:T(256)(128)(2,1)} %param.10) | copy-start | bytes 772
  32.7 15.0 %collective-permute-start.1 = (bf16[2,512,128]{2,1,0:T(8,128)(2,1)S(1)}, bf16[2,512,128]{2,1,0:T(8,128)(2,1)S(1)}, u32[]{:S(2)}, u32[]{:S(2)}) collective-permute-start(bf16[2,512,128]{2,1,0:T(8,128)(2,1)S(1)} %constant_dynamic-slice_fusion), channel_id=1, source_target_pairs={{16,0},{20,4},{760,8},{764,12},{32,16},{36,20},{8,24},{12,28},{48,... | collective-permute-start | bytes 786440 | tf_op jit(solution)/shard_map/feature_halo/ppermute | solution.py:272
  39.1 18.7 %copy-start = (bf16[512,512]{1,0:T(8,128)(2,1)S(1)}, bf16[512,512]{1,0:T(8,128)(2,1)}, u32[]{:S(2)}) copy-start(bf16[512,512]{1,0:T(8,128)(2,1)} %weight.1) | copy-start | bytes 1572868
  60.9 38.8 %all-to-all-start = ((f32[24,24,128]{2,1,0:T(8,128)}), f32[24,24,128]{2,1,0:T(8,128)S(1)}, u32[]{:S(2)}, u32[]{:S(2)}) async-start(f32[24,24,128]{2,1,0:T(8,128)} %bitcast.8), calls=%async_computation | async-start | bytes 589824 | tf_op jit(solution)/shard_map/weight_scatter/all_to_all | solution.py:302
  66.1 33.6 %collective-permute-start.2 = (bf16[4,128,512]{2,1,0:T(8,128)(2,1)S(1)}, bf16[4,128,512]{2,1,0:T(8,128)(2,1)S(1)}, u32[]{:S(2)}, u32[]{:S(2)}) collective-permute-start(bf16[4,128,512]{2,1,0:T(8,128)(2,1)S(1)} %get-tuple-element.17), channel_id=1, source_target_pairs={{760,0},{764,4},{16,8},{20,12},{8,16},{12,20},{32,24},{36,28},{24,... | collective-permute-start | bytes 1572872 | tf_op jit(solution)/shard_map/term_halo/ppermute | solution.py:272
  74.6 30.0 %collective-permute-start.3 = (bf16[2,128,512]{2,1,0:T(8,128)(2,1)S(1)}, bf16[2,128,512]{2,1,0:T(8,128)(2,1)S(1)}, u32[]{:S(2)}, u32[]{:S(2)}) collective-permute-start(bf16[2,128,512]{2,1,0:T(8,128)(2,1)S(1)} %get-tuple-element.18), channel_id=1, source_target_pairs={{752,0},{756,4},{24,8},{28,12},{0,16},{4,20},{40,24},{44,28},{16,3... | collective-permute-start | bytes 786440 | tf_op jit(solution)/shard_map/term_halo/ppermute | solution.py:272
  100.5 12.8 %all-to-all-start.1 = ((f32[8,24,128]{2,1,0:T(8,128)}), f32[8,24,128]{2,1,0:T(8,128)S(1)}, u32[]{:S(2)}, u32[]{:S(2)}) async-start(f32[8,24,128]{2,1,0:T(8,128)} %spread_sum.2.first), calls=%async_computation.1 | async-start | bytes 196608 | tf_op jit(solution)/shard_map/weight_rows/all_to_all | solution.py:309
  113.9 24.3 %all-to-all-start.2 = ((bf16[24,24,128]{2,1,0:T(8,128)(2,1)}), bf16[24,24,128]{2,1,0:T(8,128)(2,1)S(1)}, u32[]{:S(2)}, u32[]{:S(2)}) async-start(bf16[24,24,128]{2,1,0:T(8,128)(2,1)} %spread_sum.3.first), calls=%async_computation.2 | async-start | bytes 294912 | tf_op jit(solution)/shard_map/weight_gather/all_to_all | solution.py:316
  121.6 9.0 %collective-permute-start.4 = (bf16[2,128,512]{2,1,0:T(8,128)(2,1)S(1)}, bf16[2,128,512]{2,1,0:T(8,128)(2,1)S(1)}, u32[]{:S(2)}, u32[]{:S(2)}) collective-permute-start(bf16[2,128,512]{2,1,0:T(8,128)(2,1)S(1)} %get-tuple-element.21), channel_id=1, source_target_pairs={{4,0},{0,4},{12,8},{8,12},{20,16},{16,20},{28,24},{24,28},{36,32},... | collective-permute-start | bytes 786440 | tf_op jit(solution)/shard_map/term_exchange/ppermute | solution.py:272
  130.6 6.9 %collective-permute-start.5 = (bf16[128,512]{1,0:T(8,128)(2,1)S(1)}, bf16[128,512]{1,0:T(8,128)(2,1)S(1)}, u32[]{:S(2)}, u32[]{:S(2)}) collective-permute-start(bf16[128,512]{1,0:T(8,128)(2,1)S(1)} %get-tuple-element.23), channel_id=1, source_target_pairs={{8,0},{12,4},{0,8},{4,12},{24,16},{28,20},{16,24},{20,28},{40,32},... | collective-permute-start | bytes 393224 | tf_op jit(solution)/shard_map/term_exchange/ppermute | solution.py:272

commit v7 on v6

--- a/solution.py
+++ b/solution.py
@@ -18,7 +18,6 @@
 SLOTS = 16
 REACH = 4
 N_Y, N_Z, N_XL = 8, 12, 2
-GROUP = 4
 PAIRS = N_Y * N_Z
 PACK_ROWS = ROWS + 16
 RING = N_Z * N_XL
@@ -72,14 +71,13 @@
     )(codes, pltpu.with_memory_space_constraint(slab, pltpu.HBM))
 
 
-def starts(member):
-    upper = member // 2
-    return 5 - member, 1 + 8 * upper - member, 9 - 6 * upper - member
-
-
 def gather_kernel(member, dense, own, beside, beyond, bias, out):
     total = jnp.zeros((ROWS, WIDTH), F32)
-    for first, blocks in zip(starts(member[0]), (own, beside, beyond)):
+    e = member[0]
+    upper = e // 2
+    for first, blocks in (
+        (5 - e, own), (1 + 8 * upper - e, beside), (9 - 6 * upper - e, beyond)
+    ):
         for i in range(blocks.shape[0]):
             total += jnp.dot(dense[first + i], blocks[i], preferred_element_type=F32)
     out[0:ROWS, :] = total.astype(BF16)
@@ -102,7 +100,7 @@
 
 def middle_kernel(
     place, mixed, cots, weight, dense,
-    act, part, own, beside, beyond,
+    act, part, ta, tb, tc, td, te,
     act_all, grad_all, feats,
 ):
     mine = pl.multiple_of(place[1] * WIDTH, WIDTH)
@@ -133,21 +131,24 @@
         (((1,), (1,)), ((), ())),
         preferred_element_type=F32,
     ).astype(BF16)
-    for first, terms in zip(starts(place[0]), (own, beside, beyond)):
-        for i in range(terms.shape[0]):
-            terms[i] = jnp.dot(back, dense[first + i], preferred_element_type=F32).astype(BF16)
+    side = place[0] % 2
+    for k, pair in enumerate((ta, tb, tc, td, te)):
+        for s in range(2):
+            pair[s] = jnp.dot(
+                back, dense[2 * k + 1 + s - side], preferred_element_type=F32
+            ).astype(BF16)
 
 
 def middle(place, mixed, cots, weight, dense):
     return pl.pallas_call(
         middle_kernel,
         in_specs=[SMEM] + [VMEM] * 4,
-        out_specs=[VMEM] * 5,
+        out_specs=[VMEM] * 7,
         out_shape=[
             jax.ShapeDtypeStruct((ROWS, WIDTH), BF16),
             jax.ShapeDtypeStruct((RING * SHARE, WIDTH), F32),
         ]
-        + [jax.ShapeDtypeStruct((n, WIDTH, ROWS), BF16) for n in (GROUP, GROUP, 2)],
+        + [jax.ShapeDtypeStruct((2, WIDTH, ROWS), BF16)] * 5,
         scratch_shapes=[pltpu.VMEM((ROWS, HIDDEN), BF16)] * 3,
         compiler_params=params(),
         cost_estimate=pl.CostEstimate(
@@ -175,56 +176,35 @@
     )(shares, *behind)
 
 
-def split_kernel(member, own, beside, beyond, first, keep, send):
+def split_kernel(side, own, ta, tb, td, te, first, keep, send):
     del first
-    side, upper = member[0] % 2, member[0] // 2
-    for i in range(GROUP):
-        total = own[i].astype(F32) + beside[i].astype(F32)
-        total += jnp.where(upper == i // 2, beyond[i % 2].astype(F32), 0.0)
-
-        @pl.when(side == i % 2)
+    for s in range(2):
+        total = own[s].astype(F32)
+        for arrived in (ta, tb, td, te):
+            total += arrived[s].astype(F32)
+
+        @pl.when(side[0] == s)
         def _():
-            keep[i // 2] = total
-
-        @pl.when(side != i % 2)
+            keep[...] = total
+
+        @pl.when(side[0] != s)
         def _():
-            send[i // 2] = total.astype(BF16)
-
-
-def split_terms(member, own, arrived, first):
+            send[...] = total.astype(BF16)
+
+
+def split_terms(side, own, arrived, first):
     return pl.pallas_call(
         split_kernel,
-        in_specs=[SMEM] + [VMEM] * 3 + [pl.BlockSpec(memory_space=pl.ANY)],
-        out_specs=[VMEM] * 2,
-        out_shape=[
-            jax.ShapeDtypeStruct((2, WIDTH, ROWS), F32),
-            jax.ShapeDtypeStruct((2, WIDTH, ROWS), BF16),
-        ],
-        compiler_params=params(),
-        cost_estimate=pl.CostEstimate(flops=1 << 20, bytes_accessed=2 << 20, transcendentals=0),
-        name="group_sums",
-    )(member, own, *arrived, first)
-
-
-def halve_kernel(member, mine, arrived, keep, send):
-    upper = member[0] // 2
-    keep[...] = mine[upper] + arrived[upper].astype(F32)
-    send[...] = (mine[1 - upper] + arrived[1 - upper].astype(F32)).astype(BF16)
-
-
-def halve_terms(member, mine, arrived):
-    return pl.pallas_call(
-        halve_kernel,
-        in_specs=[SMEM] + [VMEM] * 2,
+        in_specs=[SMEM] + [VMEM] * 5 + [pl.BlockSpec(memory_space=pl.ANY)],
         out_specs=[VMEM] * 2,
         out_shape=[
             jax.ShapeDtypeStruct((WIDTH, ROWS), F32),
             jax.ShapeDtypeStruct((WIDTH, ROWS), BF16),
         ],
         compiler_params=params(),
-        cost_estimate=pl.CostEstimate(flops=1 << 18, bytes_accessed=1 << 20, transcendentals=0),
-        name="side_sums",
-    )(member, mine, arrived)
+        cost_estimate=pl.CostEstimate(flops=1 << 20, bytes_accessed=2 << 20, transcendentals=0),
+        name="pair_sums",
+    )(side, own, *arrived, first)
 
 
 def last_kernel(keep, arrived, first, out):
@@ -293,7 +273,7 @@
     mine = gather_rows(member, dense, (four, beside, beyond), layer_bias.reshape(1, WIDTH))
     with jax.named_scope("column_gather"):
         mixed = lax.all_gather(mine, COL, axis=0, tiled=False)
-    act, part, own, beside, beyond = middle(
+    act, part, ta, tb, tc, td, te = middle(
         jnp.concatenate([member, column]), mixed, cots, weight, dense
     )
 
@@ -301,16 +281,16 @@
     with jax.named_scope("weight_scatter"):
         shares = lax.all_to_all(part.reshape(RING, SHARE, WIDTH), ring, 0, 0, tiled=True)
     with jax.named_scope("term_halo"):
-        beside = one_away(beside)
-        beyond = routed(beyond, lambda p, s: (p - 2 + 4 * (p % 2), s))
-    spread = spread_sum(shares, [beside], N_Y, 1.0, F32)
-    keep, send = split_terms(member, own, (beside, beyond), spread)
+        ra, rb, rd, re = (
+            routed(t, lambda p, s, k=k: (p - k, s)) for k, t in ((-2, ta), (-1, tb), (1, td), (2, te))
+        )
+    spread = spread_sum(shares, [rb], N_Y, 1.0, F32)
     with jax.named_scope("weight_rows"):
         shares = lax.all_to_all(spread, "y", 0, 0, tiled=True)
+    keep, send = split_terms(lax.axis_index("xl").astype(jnp.int32).reshape(1), tc, (ra, rb, rd, re), spread)
     spread = spread_sum(shares, [keep], RING, float(NODES) ** -0.5, BF16)
     with jax.named_scope("term_exchange"):
-        keep, send = halve_terms(member, keep, routed(send, lambda p, s: (p, 1 - s)))
-        other = routed(send, lambda p, s: (p + 1 - 2 * (p % 2), s))
+        other = routed(send, lambda p, s: (p, 1 - s))
     grad_nodes = last_sum(keep, other, spread)
     with jax.named_scope("weight_gather"):
         whole = lax.all_to_all(spread, ring, 0, 0, tiled=True).reshape(RING * SHARE, WIDTH)

time: 140 us -> 124 us (0.89)
  waiting for transfers between devices: 42.3 us -> 18 us
  starting transfers between devices: 47.2 us -> 55.8 us
    ppermute x6 -> x7, waiting for transfers between devices: 33.9 us -> 13.5 us  [routed(): return lax.ppermute(block, BLK, route)]
    all_to_all x1, waiting for transfers between devices: 8.39 us -> 1.54 us  [on_device(): shares = lax.all_to_all(spread, 'y', 0, 0, tiled=True)]
    ppermute x6 -> x7, starting transfers between devices: 30.3 us -> 33.7 us  [routed(): return lax.ppermute(block, BLK, route)]
    all_to_all x1, starting transfers between devices: 4.08 us -> 7.05 us  [on_device(): shares = lax.all_to_all(spread, 'y', 0, 0, tiled=True)]
    all_to_all x1, waiting for transfers between devices: 0.01 us -> 2.91 us  [on_device(): lax.all_to_all(spread, ring, 0, 0, tiled=True).reshape(RING * SHARE, WIDTH)]
    all_to_all x1, starting transfers between devices: 7.61 us -> 9.88 us  [on_device(): lax.all_to_all(spread, ring, 0, 0, tiled=True).reshape(RING * SHARE, WIDTH)]
  transfers between devices with their start and end apart: 9 -> 10, of which waited for: 5 -> 7; matrix products, arithmetic and copies ran while one was open for 1% -> 1% of each run, Pallas kernels for 4% -> 4%
where the time goes in v7:
time: 124 us; the launch traced here: 123 us
  starting transfers between devices  55.8 us (45%)
  blocking collectives  36.6 us (30%)
  waiting for transfers between devices  18 us (15%)
  Pallas kernels  11 us (9%)
    ppermute x7, starting transfers between devices, routed(): return lax.ppermute(block, BLK, route)  33.7 us
    all_gather x1, blocking collectives, on_device(): four = lax.all_gather(node_feats, FOUR, axis=0, tiled=False)  19.9 us
    ppermute x7, waiting for transfers between devices, routed(): return lax.ppermute(block, BLK, route)  13.5 us
    all_to_all x1, starting transfers between devices, on_device(): lax.all_to_all(spread, ring, 0, 0, tiled=True).reshape(RING * SHARE, WIDTH)  9.88 us
    all_gather x1, blocking collectives, on_device(): mixed = lax.all_gather(mine, COL, axis=0, tiled=False)  8.58 us
    all_gather x1, blocking collectives, on_device(): cots = lax.all_gather(cotangent, COL, axis=0, tiled=False)  8.13 us
    all_to_all x1, starting transfers between devices, on_device(): shares = lax.all_to_all(spread, 'y', 0, 0, tiled=True)  7.05 us
    all_to_all x1, starting transfers between devices, on_device(): lax.all_to_all(part.reshape(RING, SHARE, WIDTH), ring, 0, 0, tiled=True)  5.19 us
  transfers between devices with their start and end apart: 10, of which 7 were waited for; matrix products, arithmetic and copies ran while one was open for 1% of the time, Pallas kernels for 4%

profile of v7, /device:TPU:2, one launch (start us, length us, event | category | flops | bytes accessed | tf_op | source)
XLA Modules:
  0.0 123.0 jit_solution(6493628384354716695)
XLA Ops:
  0.6 0.0 copy-start.2
  0.6 19.9 %all-gather = bf16[2048,128]{1,0:T(8,128)(2,1)S(1)} all-gather(bf16[512,128]{1,0:T(8,128)(2,1)} %param.8), channel_id=2, replica_groups=mesh['y'=8,'zq'=6,'zp'=2,'xl'=2,'xh'=2,'core'=2] {'zp','xl'}, dimensions={0}, use_global_device_ids=true | all-gather | bytes 655360 | tf_op jit(solution)/shard_map/feature_halo/all_gather | solution.py:266
  20.5 12.0 %collective-permute-start = (bf16[4,512,128]{2,1,0:T(8,128)(2,1)S(1)}, bf16[4,512,128]{2,1,0:T(8,128)(2,1)S(1)}, u32[]{:S(2)}, u32[]{:S(2)}) collective-permute-start(bf16[4,512,128]{2,1,0:T(8,128)(2,1)S(1)} %bitcast.13), channel_id=1, source_target_pairs={{760,0},{764,4},{16,8},{20,12},{8,16},{12,20},{32,24},{36,28},{24,... | collective-permute-start | bytes 1572872 | tf_op jit(solution)/shard_map/feature_halo/ppermute | solution.py:252
  32.6 0.0 copy-start.1
  32.7 2.5 %collective-permute-start.1 = (bf16[2,512,128]{2,1,0:T(8,128)(2,1)S(1)}, bf16[2,512,128]{2,1,0:T(8,128)(2,1)S(1)}, u32[]{:S(2)}, u32[]{:S(2)}) collective-permute-start(bf16[2,512,128]{2,1,0:T(8,128)(2,1)S(1)} %constant_dynamic-slice_fusion), channel_id=1, source_target_pairs={{16,0},{20,4},{760,8},{764,12},{32,16},{36,20},{8,24},{12,28},{48,... | collective-permute-start | bytes 786440 | tf_op jit(solution)/shard_map/feature_halo/ppermute | solution.py:252
  35.1 0.8 bitcast_add_fusion.codes
  35.9 3.2 %dense_tiles.1.dense = bf16[11,512,512]{2,1,0:T(8,128)(2,1)S(1)} custom-call(s32[9,16]{1,0:T(8,128)S(1)} %bitcast_add_fusion.codes, bf16[1,9,16,128,128]{4,3,2,1,0:T(8,128)(2,1)} %slab.1), custom_call_target="tpu_custom_call" | custom-call | bytes 10485760 | tf_op jit(solution)/shard_map/dense_tiles/pallas_call | solution.py:59
  39.1 0.0 copy-start
  39.1 0.1 pad_add_fusion.place
  39.2 0.0 copy-done.2
  39.2 8.1 %all-gather.2 = bf16[2048,128]{1,0:T(8,128)(2,1)S(1)} all-gather(bf16[512,128]{1,0:T(8,128)(2,1)S(1)} %copy-done.2), channel_id=4, replica_groups=mesh['y'=8,'zq'=6,'zp'=2,'xl'=2,'xh'=2,'core'=2] {'xh','core'}, dimensions={0}, use_global_device_ids=true | all-gather | bytes 655360 | tf_op jit(solution)/shard_map/column_gather/all_gather | solution.py:271
  47.3 0.3 collective-permute-done.1.beyond
  47.6 0.0 collective-permute-done.beside
  47.6 0.0 copy-done.1
  47.6 1.5 %aggregate_features.1 = bf16[528,128]{1,0:T(8,128)(2,1)S(1)} custom-call(s32[1]{0:T(128)} %bitcast.member, bf16[11,512,512]{2,1,0:T(8,128)(2,1)S(1)} %dense_tiles.1.dense, bf16[4,512,128]{2,1,0:T(8,128)(2,1)S(1)} %bitcast.15, bf16[4,512,128]{2,1,0:T(8,128)(2,1)S(1)} %collective-permute-done.beside, bf16[2,512,128]{2,1,0:T(8,128)(2,1)S(1)} %collective-permute-done.1.beyond, ...), custom_call_target="tpu_custom_call" | custom-call | flops 603979776 | bytes 8388608 | tf_op jit(solution)/shard_map/aggregate_features/pallas_call | solution.py:88
  49.2 8.6 %all-gather.1 = bf16[2112,128]{1,0:T(8,128)(2,1)S(1)} all-gather(bf16[528,128]{1,0:T(8,128)(2,1)S(1)} %aggregate_features.1), channel_id=3, replica_groups=mesh['y'=8,'zq'=6,'zp'=2,'xl'=2,'xh'=2,'core'=2] {'xh','core'}, dimensions={0}, use_global_device_ids=true | all-gather | bytes 675840 | tf_op jit(solution)/shard_map/column_gather/all_gather | solution.py:275
  57.8 0.0 copy-done
  57.8 3.2 %activation_and_terms.1 = (bf16[512,128]{1,0:T(8,128)(2,1)}, f32[576,128]{1,0:T(8,128)}, bf16[2,128,512]{2,1,0:T(8,128)(2,1)S(1)}, bf16[2,128,512]{2,1,0:T(8,128...) custom-call(s32[2]{0:T(128)S(1)} %pad_add_fusion.place, ...), custom_call_target="tpu_custom_call" | custom-call | flops 1207959552 | bytes 10485760 | tf_op jit(solution)/shard_map/activation_and_terms/pallas_call | solution.py:143
  60.9 5.2 %all-to-all-start = ((f32[24,24,128]{2,1,0:T(8,128)}), f32[24,24,128]{2,1,0:T(8,128)S(1)}, u32[]{:S(2)}, u32[]{:S(2)}) async-start(f32[24,24,128]{2,1,0:T(8,128)} %bitcast.9), calls=%async_computation | async-start | bytes 589824 | tf_op jit(solution)/shard_map/weight_scatter/all_to_all | solution.py:282
  66.1 8.4 %collective-permute-start.3 = (bf16[2,128,512]{2,1,0:T(8,128)(2,1)S(1)}, bf16[2,128,512]{2,1,0:T(8,128)(2,1)S(1)}, u32[]{:S(2)}, u32[]{:S(2)}) collective-permute-start(bf16[2,128,512]{2,1,0:T(8,128)(2,1)S(1)} %get-tuple-element.18), channel_id=1, source_target_pairs={{8,0},{12,4},{16,8},{20,12},{24,16},{28,20},{32,24},{36,28},{40,32... | collective-permute-start | bytes 786440 | tf_op jit(solution)/shard_map/term_halo/ppermute | solution.py:252
  74.6 4.2 %collective-permute-start.2 = (bf16[2,128,512]{2,1,0:T(8,128)(2,1)S(1)}, bf16[2,128,512]{2,1,0:T(8,128)(2,1)S(1)}, u32[]{:S(2)}, u32[]{:S(2)}) collective-permute-start(bf16[2,128,512]{2,1,0:T(8,128)(2,1)S(1)} %get-tuple-element.17), channel_id=1, source_target_pairs={{16,0},{20,4},{24,8},{28,12},{32,16},{36,20},{40,24},{44,28},{48,3... | collective-permute-start | bytes 786440 | tf_op jit(solution)/shard_map/term_halo/ppermute | solution.py:252
  78.8 2.5 %collective-permute-start.4 = (bf16[2,128,512]{2,1,0:T(8,128)(2,1)S(1)}, bf16[2,128,512]{2,1,0:T(8,128)(2,1)S(1)}, u32[]{:S(2)}, u32[]{:S(2)}) collective-permute-start(bf16[2,128,512]{2,1,0:T(8,128)(2,1)S(1)} %get-tuple-element.19), channel_id=1, source_target_pairs={{760,0},{764,4},{0,8},{4,12},{8,16},{12,20},{16,24},{20,28},{24,32... | collective-permute-start | bytes 786440 | tf_op jit(solution)/shard_map/term_halo/ppermute | solution.py:252
  81.3 1.9 %collective-permute-start.5 = (bf16[2,128,512]{2,1,0:T(8,128)(2,1)S(1)}, bf16[2,128,512]{2,1,0:T(8,128)(2,1)S(1)}, u32[]{:S(2)}, u32[]{:S(2)}) collective-permute-start(bf16[2,128,512]{2,1,0:T(8,128)(2,1)S(1)} %get-tuple-element.20), channel_id=1, source_target_pairs={{752,0},{756,4},{760,8},{764,12},{0,16},{4,20},{8,24},{12,28},{16,... | collective-permute-start | bytes 786440 | tf_op jit(solution)/shard_map/term_halo/ppermute | solution.py:252
  83.2 1.7 %collective-permute-done.3.refs_1_.tb = bf16[2,128,512]{2,1,0:T(8,128)(2,1)S(1)} collective-permute-done((bf16[2,128,512]{2,1,0:T(8,128)(2,1)S(1)}, bf16[2,128,512]{2,1,0:T(8,128)(2,1)S(1)}, u32[]{:S(2)}, u32[]{:S(2)}) %collective-permute-start.3) | collective-permute-done | bytes 262176 | tf_op jit(solution)/shard_map/term_halo/ppermute | solution.py:252
  85.0 0.0 all-to-all-done.refs_0_
  85.0 0.7 spread_sum.2.first
  85.6 7.0 %all-to-all-start.1 = ((f32[8,24,128]{2,1,0:T(8,128)}), f32[8,24,128]{2,1,0:T(8,128)S(1)}, u32[]{:S(2)}, u32[]{:S(2)}) async-start(f32[8,24,128]{2,1,0:T(8,128)} %spread_sum.2.first), calls=%async_computation.1 | async-start | bytes 196608 | tf_op jit(solution)/shard_map/weight_rows/all_to_all | solution.py:289
  92.7 2.9 %collective-permute-done.2.ta = bf16[2,128,512]{2,1,0:T(8,128)(2,1)S(1)} collective-permute-done((bf16[2,128,512]{2,1,0:T(8,128)(2,1)S(1)}, bf16[2,128,512]{2,1,0:T(8,128)(2,1)S(1)}, u32[]{:S(2)}, u32[]{:S(2)}) %collective-permute-start.2) | collective-permute-done | bytes 262176 | tf_op jit(solution)/shard_map/term_halo/ppermute | solution.py:252
  95.6 3.5 %collective-permute-done.4.td = bf16[2,128,512]{2,1,0:T(8,128)(2,1)S(1)} collective-permute-done((bf16[2,128,512]{2,1,0:T(8,128)(2,1)S(1)}, bf16[2,128,512]{2,1,0:T(8,128)(2,1)S(1)}, u32[]{:S(2)}, u32[]{:S(2)}) %collective-permute-start.4) | collective-permute-done | bytes 262176 | tf_op jit(solution)/shard_map/term_halo/ppermute | solution.py:252
  99.1 0.0 collective-permute-done.5.te
  99.1 0.2 pair_sums.1
  99.4 1.5 %all-to-all-done.1.refs_0_ = f32[8,24,128]{2,1,0:T(8,128)S(1)} async-done(((f32[8,24,128]{2,1,0:T(8,128)}), f32[8,24,128]{2,1,0:T(8,128)S(1)}, u32[]{:S(2)}, u32[]{:S(2)}) %all-to-all-start.1) | async-done | bytes 98336 | tf_op jit(solution)/shard_map/weight_rows/all_to_all | solution.py:289
  100.9 0.7 spread_sum.3.first
  101.6 9.9 %all-to-all-start.2 = ((bf16[24,24,128]{2,1,0:T(8,128)(2,1)}), bf16[24,24,128]{2,1,0:T(8,128)(2,1)S(1)}, u32[]{:S(2)}, u32[]{:S(2)}) async-start(bf16[24,24,128]{2,1,0:T(8,128)(2,1)} %spread_sum.3.first), calls=%async_computation.2 | async-start | bytes 294912 | tf_op jit(solution)/shard_map/weight_gather/all_to_all | solution.py:296
  111.5 2.1 %collective-permute-start.6 = (bf16[128,512]{1,0:T(8,128)(2,1)S(1)}, bf16[128,512]{1,0:T(8,128)(2,1)S(1)}, u32[]{:S(2)}, u32[]{:S(2)}) collective-permute-start(bf16[128,512]{1,0:T(8,128)(2,1)S(1)} %get-tuple-element.23), channel_id=1, source_target_pairs={{4,0},{0,4},{12,8},{8,12},{20,16},{16,20},{28,24},{24,28},{36,32},... | collective-permute-start | bytes 393224 | tf_op jit(solution)/shard_map/term_exchange/ppermute | solution.py:252
  113.6 5.0 %collective-permute-done.6.arrived = bf16[128,512]{1,0:T(8,128)(2,1)S(1)} collective-permute-done((bf16[128,512]{1,0:T(8,128)(2,1)S(1)}, bf16[128,512]{1,0:T(8,128)(2,1)S(1)}, u32[]{:S(2)}, u32[]{:S(2)}) %collective-permute-start.6) | collective-permute-done | bytes 131104 | tf_op jit(solution)/shard_map/term_exchange/ppermute | solution.py:252
  118.6 0.8 node_gradient.1
  119.4 2.9 %all-to-all-done.2 = bf16[24,24,128]{2,1,0:T(8,128)(2,1)S(1)} async-done(((bf16[24,24,128]{2,1,0:T(8,128)(2,1)}), bf16[24,24,128]{2,1,0:T(8,128)(2,1)S(1)}, u32[]{:S(2)}, u32[]{:S(2)}) %all-to-all-start.2) | async-done | bytes 147488 | tf_op jit(solution)/shard_map/weight_gather/all_to_all | solution.py:296
  122.3 0.7 weight_gradient.1
  (1 shorter events, 0.0 us)
Async XLA Ops:
  0.6 38.6 %copy-start.2 = (bf16[512,128]{1,0:T(8,128)(2,1)S(1)}, bf16[512,128]{1,0:T(8,128)(2,1)}, u32[]{:S(2)}) copy-start(bf16[512,128]{1,0:T(8,128)(2,1)} %param.11) | copy-start | bytes 393220
  20.5 27.1 %collective-permute-start = (bf16[4,512,128]{2,1,0:T(8,128)(2,1)S(1)}, bf16[4,512,128]{2,1,0:T(8,128)(2,1)S(1)}, u32[]{:S(2)}, u32[]{:S(2)}) collective-permute-start(bf16[4,512,128]{2,1,0:T(8,128)(2,1)S(1)} %bitcast.13), channel_id=1, source_target_pairs={{760,0},{764,4},{16,8},{20,12},{8,16},{12,20},{32,24},{36,28},{24,... | collective-permute-start | bytes 1572872 | tf_op jit(solution)/shard_map/feature_halo/ppermute | solution.py:252
  32.6 15.0 %copy-start.1 = (bf16[128]{0:T(256)(128)(2,1)S(1)}, bf16[128]{0:T(256)(128)(2,1)}, u32[]{:S(2)}) copy-start(bf16[128]{0:T(256)(128)(2,1)} %param.10) | copy-start | bytes 772
  32.7 15.0 %collective-permute-start.1 = (bf16[2,512,128]{2,1,0:T(8,128)(2,1)S(1)}, bf16[2,512,128]{2,1,0:T(8,128)(2,1)S(1)}, u32[]{:S(2)}, u32[]{:S(2)}) collective-permute-start(bf16[2,512,128]{2,1,0:T(8,128)(2,1)S(1)} %constant_dynamic-slice_fusion), channel_id=1, source_target_pairs={{16,0},{20,4},{760,8},{764,12},{32,16},{36,20},{8,24},{12,28},{48,... | collective-permute-start | bytes 786440 | tf_op jit(solution)/shard_map/feature_halo/ppermute | solution.py:252
  39.1 18.7 %copy-start = (bf16[512,512]{1,0:T(8,128)(2,1)S(1)}, bf16[512,512]{1,0:T(8,128)(2,1)}, u32[]{:S(2)}) copy-start(bf16[512,512]{1,0:T(8,128)(2,1)} %weight.1) | copy-start | bytes 1572868
  60.9 24.0 %all-to-all-start = ((f32[24,24,128]{2,1,0:T(8,128)}), f32[24,24,128]{2,1,0:T(8,128)S(1)}, u32[]{:S(2)}, u32[]{:S(2)}) async-start(f32[24,24,128]{2,1,0:T(8,128)} %bitcast.9), calls=%async_computation | async-start | bytes 589824 | tf_op jit(solution)/shard_map/weight_scatter/all_to_all | solution.py:282
  66.1 18.8 %collective-permute-start.3 = (bf16[2,128,512]{2,1,0:T(8,128)(2,1)S(1)}, bf16[2,128,512]{2,1,0:T(8,128)(2,1)S(1)}, u32[]{:S(2)}, u32[]{:S(2)}) collective-permute-start(bf16[2,128,512]{2,1,0:T(8,128)(2,1)S(1)} %get-tuple-element.18), channel_id=1, source_target_pairs={{8,0},{12,4},{16,8},{20,12},{24,16},{28,20},{32,24},{36,28},{40,32... | collective-permute-start | bytes 786440 | tf_op jit(solution)/shard_map/term_halo/ppermute | solution.py:252
  74.6 21.1 %collective-permute-start.2 = (bf16[2,128,512]{2,1,0:T(8,128)(2,1)S(1)}, bf16[2,128,512]{2,1,0:T(8,128)(2,1)S(1)}, u32[]{:S(2)}, u32[]{:S(2)}) collective-permute-start(bf16[2,128,512]{2,1,0:T(8,128)(2,1)S(1)} %get-tuple-element.17), channel_id=1, source_target_pairs={{16,0},{20,4},{24,8},{28,12},{32,16},{36,20},{40,24},{44,28},{48,3... | collective-permute-start | bytes 786440 | tf_op jit(solution)/shard_map/term_halo/ppermute | solution.py:252
  78.8 20.3 %collective-permute-start.4 = (bf16[2,128,512]{2,1,0:T(8,128)(2,1)S(1)}, bf16[2,128,512]{2,1,0:T(8,128)(2,1)S(1)}, u32[]{:S(2)}, u32[]{:S(2)}) collective-permute-start(bf16[2,128,512]{2,1,0:T(8,128)(2,1)S(1)} %get-tuple-element.19), channel_id=1, source_target_pairs={{760,0},{764,4},{0,8},{4,12},{8,16},{12,20},{16,24},{20,28},{24,32... | collective-permute-start | bytes 786440 | tf_op jit(solution)/shard_map/term_halo/ppermute | solution.py:252
  81.3 17.8 %collective-permute-start.5 = (bf16[2,128,512]{2,1,0:T(8,128)(2,1)S(1)}, bf16[2,128,512]{2,1,0:T(8,128)(2,1)S(1)}, u32[]{:S(2)}, u32[]{:S(2)}) collective-permute-start(bf16[2,128,512]{2,1,0:T(8,128)(2,1)S(1)} %get-tuple-element.20), channel_id=1, source_target_pairs={{752,0},{756,4},{760,8},{764,12},{0,16},{4,20},{8,24},{12,28},{16,... | collective-permute-start | bytes 786440 | tf_op jit(solution)/shard_map/term_halo/ppermute | solution.py:252
  85.6 15.3 %all-to-all-start.1 = ((f32[8,24,128]{2,1,0:T(8,128)}), f32[8,24,128]{2,1,0:T(8,128)S(1)}, u32[]{:S(2)}, u32[]{:S(2)}) async-start(f32[8,24,128]{2,1,0:T(8,128)} %spread_sum.2.first), calls=%async_computation.1 | async-start | bytes 196608 | tf_op jit(solution)/shard_map/weight_rows/all_to_all | solution.py:289
  101.6 20.7 %all-to-all-start.2 = ((bf16[24,24,128]{2,1,0:T(8,128)(2,1)}), bf16[24,24,128]{2,1,0:T(8,128)(2,1)S(1)}, u32[]{:S(2)}, u32[]{:S(2)}) async-start(bf16[24,24,128]{2,1,0:T(8,128)(2,1)} %spread_sum.3.first), calls=%async_computation.2 | async-start | bytes 294912 | tf_op jit(solution)/shard_map/weight_gather/all_to_all | solution.py:296
  111.5 7.1 %collective-permute-start.6 = (bf16[128,512]{1,0:T(8,128)(2,1)S(1)}, bf16[128,512]{1,0:T(8,128)(2,1)S(1)}, u32[]{:S(2)}, u32[]{:S(2)}) collective-permute-start(bf16[128,512]{1,0:T(8,128)(2,1)S(1)} %get-tuple-element.23), channel_id=1, source_target_pairs={{4,0},{0,4},{12,8},{8,12},{20,16},{16,20},{28,24},{24,28},{36,32},... | collective-permute-start | bytes 393224 | tf_op jit(solution)/shard_map/term_exchange/ppermute | solution.py:252

commit v8 on v7

--- a/solution.py
+++ b/solution.py
@@ -22,8 +22,7 @@
 PACK_ROWS = ROWS + 16
 RING = N_Z * N_XL
 SHARE = 24
-BLK = ("y", "zq", "zp", "xl")
-FOUR = ("zp", "xl")
+BLK = ("y", "z", "xl")
 COL = ("xh", "core")
 BF16 = jnp.bfloat16
 F32 = jnp.float32
@@ -71,23 +70,22 @@
     )(codes, pltpu.with_memory_space_constraint(slab, pltpu.HBM))
 
 
-def gather_kernel(member, dense, own, beside, beyond, bias, out):
-    total = jnp.zeros((ROWS, WIDTH), F32)
-    e = member[0]
-    upper = e // 2
-    for first, blocks in (
-        (5 - e, own), (1 + 8 * upper - e, beside), (9 - 6 * upper - e, beyond)
-    ):
-        for i in range(blocks.shape[0]):
-            total += jnp.dot(dense[first + i], blocks[i], preferred_element_type=F32)
+def gather_kernel(side, dense, far_before, before, own, after, far_after, cross, bias, out):
+    s = side[0]
+    total = jnp.dot(dense[1], far_before[...], preferred_element_type=F32)
+    total += jnp.dot(dense[9], far_after[...], preferred_element_type=F32)
+    total += jnp.dot(dense[2 + 6 * s], cross[...], preferred_element_type=F32)
+    for first, pair in ((3 - s, before), (5 - s, own), (7 - s, after)):
+        for i in range(2):
+            total += jnp.dot(dense[first + i], pair[i], preferred_element_type=F32)
     out[0:ROWS, :] = total.astype(BF16)
     out[ROWS:, :] = jnp.broadcast_to(bias[...], (16, WIDTH))
 
 
-def gather_rows(member, dense, blocks, bias):
+def gather_rows(side, dense, blocks, bias):
     return pl.pallas_call(
         gather_kernel,
-        in_specs=[SMEM] + [VMEM] * 5,
+        in_specs=[SMEM] + [VMEM] * 8,
         out_specs=VMEM,
         out_shape=jax.ShapeDtypeStruct((PACK_ROWS, WIDTH), BF16),
         compiler_params=params(),
@@ -95,7 +93,7 @@
             flops=2 * OFFSETS * ROWS * ROWS * WIDTH, bytes_accessed=8 << 20, transcendentals=0
         ),
         name="aggregate_features",
-    )(member, dense, *blocks, bias)
+    )(side, dense, *blocks, bias)
 
 
 def middle_kernel(
@@ -131,7 +129,7 @@
         (((1,), (1,)), ((), ())),
         preferred_element_type=F32,
     ).astype(BF16)
-    side = place[0] % 2
+    side = place[0]
     for k, pair in enumerate((ta, tb, tc, td, te)):
         for s in range(2):
             pair[s] = jnp.dot(
@@ -253,31 +251,31 @@
 
 
 def on_device(node_feats, weight, layer_bias, cotangent, adj_tiles, tile_row, tile_col, tile_count):
-    member = lax.axis_index(FOUR).astype(jnp.int32).reshape(1)
+    side = lax.axis_index("xl").astype(jnp.int32).reshape(1)
     column = lax.axis_index(COL).astype(jnp.int32).reshape(1)
     slots = jnp.arange(SLOTS, dtype=jnp.int32)[None, :]
     dead = slots >= tile_count[0][:, None]
     codes = tile_row[0] * BLOCKS + tile_col[0] + BLOCKS * BLOCKS * dead.astype(jnp.int32)
 
-    def one_away(block):
-        return routed(block, lambda p, s: (p - 1 + 2 * (p % 2), s))
-
     with jax.named_scope("feature_halo"):
-        four = lax.all_gather(node_feats, FOUR, axis=0, tiled=False)
-        beside = one_away(four)
-        pair = lax.dynamic_slice_in_dim(four, 2 * lax.axis_index("zp"), 2, 0)
-        beyond = routed(pair, lambda p, s: (p + 2 - 4 * (p % 2), s))
+        x = node_feats
+        far_before, far_after = (routed(x, lambda p, s, k=k: (p + k, s)) for k in (-2, 2))
+        pair = lax.all_gather(x, "xl", axis=0, tiled=False)
+        before, after = (routed(pair, lambda p, s, k=k: (p + k, s)) for k in (-1, 1))
+        cross = jnp.where(side[0] == 1, far_before, far_after)
+        cross = routed(cross, lambda p, s: (p, 1 - s))
     with jax.named_scope("column_gather"):
         cots = lax.all_gather(cotangent, COL, axis=0, tiled=False)
     dense = make_dense(codes, adj_tiles)
-    mine = gather_rows(member, dense, (four, beside, beyond), layer_bias.reshape(1, WIDTH))
+    blocks = (far_before, before, pair, after, far_after, cross)
+    mine = gather_rows(side, dense, blocks, layer_bias.reshape(1, WIDTH))
     with jax.named_scope("column_gather"):
         mixed = lax.all_gather(mine, COL, axis=0, tiled=False)
     act, part, ta, tb, tc, td, te = middle(
-        jnp.concatenate([member, column]), mixed, cots, weight, dense
-    )
-
-    ring = ("zq", "zp", "xl")
+        jnp.concatenate([side, column]), mixed, cots, weight, dense
+    )
+
+    ring = ("z", "xl")
     with jax.named_scope("weight_scatter"):
         shares = lax.all_to_all(part.reshape(RING, SHARE, WIDTH), ring, 0, 0, tiled=True)
     with jax.named_scope("term_halo"):
@@ -287,7 +285,7 @@
     spread = spread_sum(shares, [rb], N_Y, 1.0, F32)
     with jax.named_scope("weight_rows"):
         shares = lax.all_to_all(spread, "y", 0, 0, tiled=True)
-    keep, send = split_terms(lax.axis_index("xl").astype(jnp.int32).reshape(1), tc, (ra, rb, rd, re), spread)
+    keep, send = split_terms(side, tc, (ra, rb, rd, re), spread)
     spread = spread_sum(shares, [keep], RING, float(NODES) ** -0.5, BF16)
     with jax.named_scope("term_exchange"):
         other = routed(send, lambda p, s: (p, 1 - s))
@@ -300,7 +298,7 @@
 
 def solution(mesh):
     fine = Mesh(
-        np.asarray(mesh.devices).reshape(N_Y, N_Z // 2, 2, N_XL, 2, 2), BLK + COL
+        np.asarray(mesh.devices).reshape(N_Y, N_Z, N_XL, 2, 2), BLK + COL
     )
     placed = (
         P(BLK, COL),

time: 124 us -> 124 us (level)
  starting transfers between devices: 55.8 us -> 69.1 us
  blocking collectives: 36.6 us -> 23.8 us
    all_gather x1, blocking collectives: 19.9 us -> 5.86 us  [on_device(): pair = lax.all_gather(x, 'xl', axis=0, tiled=False)]
    ppermute x7 -> x10, starting transfers between devices: 33.7 us -> 47.1 us  [routed(): return lax.ppermute(block, BLK, route)]
    ppermute x7 -> x10, waiting for transfers between devices: 13.5 us -> 13.4 us  [routed(): return lax.ppermute(block, BLK, route)]
  transfers between devices with their start and end apart: 10 -> 13, of which waited for: 7 -> 6; matrix products, arithmetic and copies ran while one was open for 1% -> 1% of each run, Pallas kernels for 4% -> 4%
where the time goes in v8:
time: 124 us; the launch traced here: 123 us
  starting transfers between devices  69.1 us (56%)
  blocking collectives  23.8 us (19%)
  waiting for transfers between devices  17.9 us (14%)
  Pallas kernels  10.8 us (9%)
    ppermute x10, starting transfers between devices, routed(): return lax.ppermute(block, BLK, route)  47.1 us
    ppermute x10, waiting for transfers between devices, routed(): return lax.ppermute(block, BLK, route)  13.4 us
    all_to_all x1, starting transfers between devices, on_device(): lax.all_to_all(spread, ring, 0, 0, tiled=True).reshape(RING * SHARE, WIDTH)  9.89 us
    all_gather x1, blocking collectives, on_device(): cots = lax.all_gather(cotangent, COL, axis=0, tiled=False)  9.01 us
    all_gather x1, blocking collectives, on_device(): mixed = lax.all_gather(mine, COL, axis=0, tiled=False)  8.89 us
    all_to_all x1, starting transfers between devices, on_device(): shares = lax.all_to_all(spread, 'y', 0, 0, tiled=True)  6.79 us
    all_gather x1, blocking collectives, on_device(): pair = lax.all_gather(x, 'xl', axis=0, tiled=False)  5.86 us
    all_to_all x1, starting transfers between devices, on_device(): lax.all_to_all(part.reshape(RING, SHARE, WIDTH), ring, 0, 0, tiled=True)  5.35 us
  transfers between devices with their start and end apart: 13, of which 6 were waited for; matrix products, arithmetic and copies ran while one was open for 1% of the time, Pallas kernels for 4%

profile of v8, /device:TPU:2, one launch (start us, length us, event | category | flops | bytes accessed | tf_op | source)
XLA Modules:
  0.0 123.3 jit_solution(6541301422843124795)
XLA Ops:
  0.6 6.1 %collective-permute-start = (bf16[512,128]{1,0:T(8,128)(2,1)}, bf16[512,128]{1,0:T(8,128)(2,1)S(1)}, u32[]{:S(2)}, u32[]{:S(2)}) collective-permute-start(bf16[512,128]{1,0:T(8,128)(2,1)} %param.8), channel_id=1, source_target_pairs={{752,0},{756,4},{760,8},{764,12},{0,16},{4,20},{8,24},{12,28},{16,... | collective-permute-start | bytes 393224 | tf_op jit(solution)/shard_map/feature_halo/ppermute | solution.py:250
  6.7 13.3 %collective-permute-start.3 = (bf16[512,128]{1,0:T(8,128)(2,1)}, bf16[512,128]{1,0:T(8,128)(2,1)S(1)}, u32[]{:S(2)}, u32[]{:S(2)}) collective-permute-start(bf16[512,128]{1,0:T(8,128)(2,1)} %param.8), channel_id=1, source_target_pairs={{16,0},{20,4},{24,8},{28,12},{32,16},{36,20},{40,24},{44,28},{48,3... | collective-permute-start | bytes 393224 | tf_op jit(solution)/shard_map/feature_halo/ppermute | solution.py:250
  20.0 5.9 %all-gather = bf16[1024,128]{1,0:T(8,128)(2,1)S(1)} all-gather(bf16[512,128]{1,0:T(8,128)(2,1)} %param.8), channel_id=2, replica_groups=mesh['y'=8,'z'=12,'xl'=2,'xh'=2,'core'=2] {'xl'}, dimensions={0}, use_global_device_ids=true | all-gather | bytes 393216 | tf_op jit(solution)/shard_map/feature_halo/all_gather | solution.py:263
  25.9 4.8 %collective-permute-start.2 = (bf16[2,512,128]{2,1,0:T(8,128)(2,1)S(1)}, bf16[2,512,128]{2,1,0:T(8,128)(2,1)S(1)}, u32[]{:S(2)}, u32[]{:S(2)}) collective-permute-start(bf16[2,512,128]{2,1,0:T(8,128)(2,1)S(1)} %bitcast.14), channel_id=1, source_target_pairs={{8,0},{12,4},{16,8},{20,12},{24,16},{28,20},{32,24},{36,28},{40,32... | collective-permute-start | bytes 786440 | tf_op jit(solution)/shard_map/feature_halo/ppermute | solution.py:250
  30.7 1.9 %collective-permute-start.1 = (bf16[2,512,128]{2,1,0:T(8,128)(2,1)S(1)}, bf16[2,512,128]{2,1,0:T(8,128)(2,1)S(1)}, u32[]{:S(2)}, u32[]{:S(2)}) collective-permute-start(bf16[2,512,128]{2,1,0:T(8,128)(2,1)S(1)} %bitcast.15), channel_id=1, source_target_pairs={{760,0},{764,4},{0,8},{4,12},{8,16},{12,20},{16,24},{20,28},{24,32... | collective-permute-start | bytes 786440 | tf_op jit(solution)/shard_map/feature_halo/ppermute | solution.py:250
  32.7 0.8 bitcast_add_fusion.codes
  33.4 0.0 copy-start.1
  33.4 0.0 collective-permute-done.far_before
  33.5 0.0 collective-permute-done.3.far_after
  33.5 2.4 %collective-permute-start.4 = (bf16[512,128]{1,0:T(8,128)(2,1)S(1)}, bf16[512,128]{1,0:T(8,128)(2,1)S(1)}, u32[]{:S(2)}, u32[]{:S(2)}) collective-permute-start(bf16[512,128]{1,0:T(8,128)(2,1)S(1)} %broadcast_select_fusion), channel_id=1, source_target_pairs={{4,0},{0,4},{12,8},{8,12},{20,16},{16,20},{28,24},{24,28},{36,32},... | collective-permute-start | bytes 393224 | tf_op jit(solution)/shard_map/feature_halo/ppermute | solution.py:250
  35.9 9.0 %all-gather.2 = bf16[2048,128]{1,0:T(8,128)(2,1)S(1)} all-gather(bf16[512,128]{1,0:T(8,128)(2,1)} %param.11), channel_id=4, replica_groups=mesh['y'=8,'z'=12,'xl'=2,'xh'=2,'core'=2] {'xh','core'}, dimensions={0}, use_global_device_ids=true | all-gather | bytes 655360 | tf_op jit(solution)/shard_map/column_gather/all_gather | solution.py:268
  45.0 3.2 %dense_tiles.1.dense = bf16[11,512,512]{2,1,0:T(8,128)(2,1)S(1)} custom-call(s32[9,16]{1,0:T(8,128)S(1)} %bitcast_add_fusion.codes, bf16[1,9,16,128,128]{4,3,2,1,0:T(8,128)(2,1)} %slab.1), custom_call_target="tpu_custom_call" | custom-call | bytes 10485760 | tf_op jit(solution)/shard_map/dense_tiles/pallas_call | solution.py:58
  48.1 0.0 copy-start
  48.2 0.1 pad_add_fusion.place
  48.2 0.0 collective-permute-done.4.cross
  48.2 0.0 collective-permute-done.2.after
  48.2 0.0 collective-permute-done.1.before
  48.2 0.0 copy-done.1
  48.3 1.4 %aggregate_features.1 = bf16[528,128]{1,0:T(8,128)(2,1)S(1)} custom-call(s32[1]{0:T(128)} %bitcast.side, bf16[11,512,512]{2,1,0:T(8,128)(2,1)S(1)} %dense_tiles.1.dense, bf16[512,128]{1,0:T(8,128)(2,1)S(1)} %collective-permute-done.far_before, bf16[2,512,128]{2,1,0:T(8,128)(2,1)S(1)} %collective-permute-done.1.before, bf16[2,512,128]{2,1,0:T(8,128)(2,1)S(1)} %bitcast.16, ...), custom_call_target="tpu_custom_call" | custom-call | flops 603979776 | bytes 8388608 | tf_op jit(solution)/shard_map/aggregate_features/pallas_call | solution.py:86
  49.7 8.9 %all-gather.1 = bf16[2112,128]{1,0:T(8,128)(2,1)S(1)} all-gather(bf16[528,128]{1,0:T(8,128)(2,1)S(1)} %aggregate_features.1), channel_id=3, replica_groups=mesh['y'=8,'z'=12,'xl'=2,'xh'=2,'core'=2] {'xh','core'}, dimensions={0}, use_global_device_ids=true | all-gather | bytes 675840 | tf_op jit(solution)/shard_map/column_gather/all_gather | solution.py:273
  58.5 0.0 copy-done
  58.5 3.2 %activation_and_terms.1 = (bf16[512,128]{1,0:T(8,128)(2,1)}, f32[576,128]{1,0:T(8,128)}, bf16[2,128,512]{2,1,0:T(8,128)(2,1)S(1)}, bf16[2,128,512]{2,1,0:T(8,128...) custom-call(s32[2]{0:T(128)S(1)} %pad_add_fusion.place, ...), custom_call_target="tpu_custom_call" | custom-call | flops 1207959552 | bytes 10485760 | tf_op jit(solution)/shard_map/activation_and_terms/pallas_call | solution.py:141
  61.7 5.3 %all-to-all-start = ((f32[24,24,128]{2,1,0:T(8,128)}), f32[24,24,128]{2,1,0:T(8,128)S(1)}, u32[]{:S(2)}, u32[]{:S(2)}) async-start(f32[24,24,128]{2,1,0:T(8,128)} %bitcast.8), calls=%async_computation | async-start | bytes 589824 | tf_op jit(solution)/shard_map/weight_scatter/all_to_all | solution.py:280
  67.1 7.7 %collective-permute-start.6 = (bf16[2,128,512]{2,1,0:T(8,128)(2,1)S(1)}, bf16[2,128,512]{2,1,0:T(8,128)(2,1)S(1)}, u32[]{:S(2)}, u32[]{:S(2)}) collective-permute-start(bf16[2,128,512]{2,1,0:T(8,128)(2,1)S(1)} %get-tuple-element.18), channel_id=1, source_target_pairs={{8,0},{12,4},{16,8},{20,12},{24,16},{28,20},{32,24},{36,28},{40,32... | collective-permute-start | bytes 786440 | tf_op jit(solution)/shard_map/term_halo/ppermute | solution.py:250
  74.8 4.2 %collective-permute-start.5 = (bf16[2,128,512]{2,1,0:T(8,128)(2,1)S(1)}, bf16[2,128,512]{2,1,0:T(8,128)(2,1)S(1)}, u32[]{:S(2)}, u32[]{:S(2)}) collective-permute-start(bf16[2,128,512]{2,1,0:T(8,128)(2,1)S(1)} %get-tuple-element.17), channel_id=1, source_target_pairs={{16,0},{20,4},{24,8},{28,12},{32,16},{36,20},{40,24},{44,28},{48,3... | collective-permute-start | bytes 786440 | tf_op jit(solution)/shard_map/term_halo/ppermute | solution.py:250
  79.1 2.5 %collective-permute-start.7 = (bf16[2,128,512]{2,1,0:T(8,128)(2,1)S(1)}, bf16[2,128,512]{2,1,0:T(8,128)(2,1)S(1)}, u32[]{:S(2)}, u32[]{:S(2)}) collective-permute-start(bf16[2,128,512]{2,1,0:T(8,128)(2,1)S(1)} %get-tuple-element.19), channel_id=1, source_target_pairs={{760,0},{764,4},{0,8},{4,12},{8,16},{12,20},{16,24},{20,28},{24,32... | collective-permute-start | bytes 786440 | tf_op jit(solution)/shard_map/term_halo/ppermute | solution.py:250
  81.6 1.9 %collective-permute-start.8 = (bf16[2,128,512]{2,1,0:T(8,128)(2,1)S(1)}, bf16[2,128,512]{2,1,0:T(8,128)(2,1)S(1)}, u32[]{:S(2)}, u32[]{:S(2)}) collective-permute-start(bf16[2,128,512]{2,1,0:T(8,128)(2,1)S(1)} %get-tuple-element.20), channel_id=1, source_target_pairs={{752,0},{756,4},{760,8},{764,12},{0,16},{4,20},{8,24},{12,28},{16,... | collective-permute-start | bytes 786440 | tf_op jit(solution)/shard_map/term_halo/ppermute | solution.py:250
  83.5 2.0 %collective-permute-done.6.refs_1_.tb = bf16[2,128,512]{2,1,0:T(8,128)(2,1)S(1)} collective-permute-done((bf16[2,128,512]{2,1,0:T(8,128)(2,1)S(1)}, bf16[2,128,512]{2,1,0:T(8,128)(2,1)S(1)}, u32[]{:S(2)}, u32[]{:S(2)}) %collective-permute-start.6) | collective-permute-done | bytes 262176 | tf_op jit(solution)/shard_map/term_halo/ppermute | solution.py:250
  85.5 0.0 all-to-all-done.refs_0_
  85.5 0.7 spread_sum.2.first
  86.2 6.8 %all-to-all-start.1 = ((f32[8,24,128]{2,1,0:T(8,128)}), f32[8,24,128]{2,1,0:T(8,128)S(1)}, u32[]{:S(2)}, u32[]{:S(2)}) async-start(f32[8,24,128]{2,1,0:T(8,128)} %spread_sum.2.first), calls=%async_computation.1 | async-start | bytes 196608 | tf_op jit(solution)/shard_map/weight_rows/all_to_all | solution.py:287
  93.0 3.9 %collective-permute-done.5.ta = bf16[2,128,512]{2,1,0:T(8,128)(2,1)S(1)} collective-permute-done((bf16[2,128,512]{2,1,0:T(8,128)(2,1)S(1)}, bf16[2,128,512]{2,1,0:T(8,128)(2,1)S(1)}, u32[]{:S(2)}, u32[]{:S(2)}) %collective-permute-start.5) | collective-permute-done | bytes 262176 | tf_op jit(solution)/shard_map/term_halo/ppermute | solution.py:250
  96.9 2.5 %collective-permute-done.7.td = bf16[2,128,512]{2,1,0:T(8,128)(2,1)S(1)} collective-permute-done((bf16[2,128,512]{2,1,0:T(8,128)(2,1)S(1)}, bf16[2,128,512]{2,1,0:T(8,128)(2,1)S(1)}, u32[]{:S(2)}, u32[]{:S(2)}) %collective-permute-start.7) | collective-permute-done | bytes 262176 | tf_op jit(solution)/shard_map/term_halo/ppermute | solution.py:250
  99.4 0.0 collective-permute-done.8.te
  99.4 0.2 pair_sums.1
  99.6 1.5 %all-to-all-done.1.refs_0_ = f32[8,24,128]{2,1,0:T(8,128)S(1)} async-done(((f32[8,24,128]{2,1,0:T(8,128)}), f32[8,24,128]{2,1,0:T(8,128)S(1)}, u32[]{:S(2)}, u32[]{:S(2)}) %all-to-all-start.1) | async-done | bytes 98336 | tf_op jit(solution)/shard_map/weight_rows/all_to_all | solution.py:287
  101.2 0.7 spread_sum.3.first
  101.9 9.9 %all-to-all-start.2 = ((bf16[24,24,128]{2,1,0:T(8,128)(2,1)}), bf16[24,24,128]{2,1,0:T(8,128)(2,1)S(1)}, u32[]{:S(2)}, u32[]{:S(2)}) async-start(bf16[24,24,128]{2,1,0:T(8,128)(2,1)} %spread_sum.3.first), calls=%async_computation.2 | async-start | bytes 294912 | tf_op jit(solution)/shard_map/weight_gather/all_to_all | solution.py:294
  111.8 2.1 %collective-permute-start.9 = (bf16[128,512]{1,0:T(8,128)(2,1)S(1)}, bf16[128,512]{1,0:T(8,128)(2,1)S(1)}, u32[]{:S(2)}, u32[]{:S(2)}) collective-permute-start(bf16[128,512]{1,0:T(8,128)(2,1)S(1)} %get-tuple-element.23), channel_id=1, source_target_pairs={{4,0},{0,4},{12,8},{8,12},{20,16},{16,20},{28,24},{24,28},{36,32},... | collective-permute-start | bytes 393224 | tf_op jit(solution)/shard_map/term_exchange/ppermute | solution.py:250
  113.9 5.0 %collective-permute-done.9.arrived = bf16[128,512]{1,0:T(8,128)(2,1)S(1)} collective-permute-done((bf16[128,512]{1,0:T(8,128)(2,1)S(1)}, bf16[128,512]{1,0:T(8,128)(2,1)S(1)}, u32[]{:S(2)}, u32[]{:S(2)}) %collective-permute-start.9) | collective-permute-done | bytes 131104 | tf_op jit(solution)/shard_map/term_exchange/ppermute | solution.py:250
  118.9 0.8 node_gradient.1
  119.6 2.9 %all-to-all-done.2 = bf16[24,24,128]{2,1,0:T(8,128)(2,1)S(1)} async-done(((bf16[24,24,128]{2,1,0:T(8,128)(2,1)}), bf16[24,24,128]{2,1,0:T(8,128)(2,1)S(1)}, u32[]{:S(2)}, u32[]{:S(2)}) %all-to-all-start.2) | async-done | bytes 147488 | tf_op jit(solution)/shard_map/weight_gather/all_to_all | solution.py:294
  122.6 0.7 weight_gradient.1
  (1 shorter events, 0.0 us)
Async XLA Ops:
  0.6 32.8 %collective-permute-start = (bf16[512,128]{1,0:T(8,128)(2,1)}, bf16[512,128]{1,0:T(8,128)(2,1)S(1)}, u32[]{:S(2)}, u32[]{:S(2)}) collective-permute-start(bf16[512,128]{1,0:T(8,128)(2,1)} %param.8), channel_id=1, source_target_pairs={{752,0},{756,4},{760,8},{764,12},{0,16},{4,20},{8,24},{12,28},{16,... | collective-permute-start | bytes 393224 | tf_op jit(solution)/shard_map/feature_halo/ppermute | solution.py:250
  6.7 26.7 %collective-permute-start.3 = (bf16[512,128]{1,0:T(8,128)(2,1)}, bf16[512,128]{1,0:T(8,128)(2,1)S(1)}, u32[]{:S(2)}, u32[]{:S(2)}) collective-permute-start(bf16[512,128]{1,0:T(8,128)(2,1)} %param.8), channel_id=1, source_target_pairs={{16,0},{20,4},{24,8},{28,12},{32,16},{36,20},{40,24},{44,28},{48,3... | collective-permute-start | bytes 393224 | tf_op jit(solution)/shard_map/feature_halo/ppermute | solution.py:250
  25.9 22.3 %collective-permute-start.2 = (bf16[2,512,128]{2,1,0:T(8,128)(2,1)S(1)}, bf16[2,512,128]{2,1,0:T(8,128)(2,1)S(1)}, u32[]{:S(2)}, u32[]{:S(2)}) collective-permute-start(bf16[2,512,128]{2,1,0:T(8,128)(2,1)S(1)} %bitcast.14), channel_id=1, source_target_pairs={{8,0},{12,4},{16,8},{20,12},{24,16},{28,20},{32,24},{36,28},{40,32... | collective-permute-start | bytes 786440 | tf_op jit(solution)/shard_map/feature_halo/ppermute | solution.py:250
  30.7 17.5 %collective-permute-start.1 = (bf16[2,512,128]{2,1,0:T(8,128)(2,1)S(1)}, bf16[2,512,128]{2,1,0:T(8,128)(2,1)S(1)}, u32[]{:S(2)}, u32[]{:S(2)}) collective-permute-start(bf16[2,512,128]{2,1,0:T(8,128)(2,1)S(1)} %bitcast.15), channel_id=1, source_target_pairs={{760,0},{764,4},{0,8},{4,12},{8,16},{12,20},{16,24},{20,28},{24,32... | collective-permute-start | bytes 786440 | tf_op jit(solution)/shard_map/feature_halo/ppermute | solution.py:250
  33.4 14.8 %copy-start.1 = (bf16[128]{0:T(256)(128)(2,1)S(1)}, bf16[128]{0:T(256)(128)(2,1)}, u32[]{:S(2)}) copy-start(bf16[128]{0:T(256)(128)(2,1)} %param.10) | copy-start | bytes 772
  33.5 14.7 %collective-permute-start.4 = (bf16[512,128]{1,0:T(8,128)(2,1)S(1)}, bf16[512,128]{1,0:T(8,128)(2,1)S(1)}, u32[]{:S(2)}, u32[]{:S(2)}) collective-permute-start(bf16[512,128]{1,0:T(8,128)(2,1)S(1)} %broadcast_select_fusion), channel_id=1, source_target_pairs={{4,0},{0,4},{12,8},{8,12},{20,16},{16,20},{28,24},{24,28},{36,32},... | collective-permute-start | bytes 393224 | tf_op jit(solution)/shard_map/feature_halo/ppermute | solution.py:250
  48.1 10.4 %copy-start = (bf16[512,512]{1,0:T(8,128)(2,1)S(1)}, bf16[512,512]{1,0:T(8,128)(2,1)}, u32[]{:S(2)}) copy-start(bf16[512,512]{1,0:T(8,128)(2,1)} %weight.1) | copy-start | bytes 1572868
  61.7 23.8 %all-to-all-start = ((f32[24,24,128]{2,1,0:T(8,128)}), f32[24,24,128]{2,1,0:T(8,128)S(1)}, u32[]{:S(2)}, u32[]{:S(2)}) async-start(f32[24,24,128]{2,1,0:T(8,128)} %bitcast.8), calls=%async_computation | async-start | bytes 589824 | tf_op jit(solution)/shard_map/weight_scatter/all_to_all | solution.py:280
  67.1 18.4 %collective-permute-start.6 = (bf16[2,128,512]{2,1,0:T(8,128)(2,1)S(1)}, bf16[2,128,512]{2,1,0:T(8,128)(2,1)S(1)}, u32[]{:S(2)}, u32[]{:S(2)}) collective-permute-start(bf16[2,128,512]{2,1,0:T(8,128)(2,1)S(1)} %get-tuple-element.18), channel_id=1, source_target_pairs={{8,0},{12,4},{16,8},{20,12},{24,16},{28,20},{32,24},{36,28},{40,32... | collective-permute-start | bytes 786440 | tf_op jit(solution)/shard_map/term_halo/ppermute | solution.py:250
  74.8 22.0 %collective-permute-start.5 = (bf16[2,128,512]{2,1,0:T(8,128)(2,1)S(1)}, bf16[2,128,512]{2,1,0:T(8,128)(2,1)S(1)}, u32[]{:S(2)}, u32[]{:S(2)}) collective-permute-start(bf16[2,128,512]{2,1,0:T(8,128)(2,1)S(1)} %get-tuple-element.17), channel_id=1, source_target_pairs={{16,0},{20,4},{24,8},{28,12},{32,16},{36,20},{40,24},{44,28},{48,3... | collective-permute-start | bytes 786440 | tf_op jit(solution)/shard_map/term_halo/ppermute | solution.py:250
  79.1 20.3 %collective-permute-start.7 = (bf16[2,128,512]{2,1,0:T(8,128)(2,1)S(1)}, bf16[2,128,512]{2,1,0:T(8,128)(2,1)S(1)}, u32[]{:S(2)}, u32[]{:S(2)}) collective-permute-start(bf16[2,128,512]{2,1,0:T(8,128)(2,1)S(1)} %get-tuple-element.19), channel_id=1, source_target_pairs={{760,0},{764,4},{0,8},{4,12},{8,16},{12,20},{16,24},{20,28},{24,32... | collective-permute-start | bytes 786440 | tf_op jit(solution)/shard_map/term_halo/ppermute | solution.py:250
  81.6 17.8 %collective-permute-start.8 = (bf16[2,128,512]{2,1,0:T(8,128)(2,1)S(1)}, bf16[2,128,512]{2,1,0:T(8,128)(2,1)S(1)}, u32[]{:S(2)}, u32[]{:S(2)}) collective-permute-start(bf16[2,128,512]{2,1,0:T(8,128)(2,1)S(1)} %get-tuple-element.20), channel_id=1, source_target_pairs={{752,0},{756,4},{760,8},{764,12},{0,16},{4,20},{8,24},{12,28},{16,... | collective-permute-start | bytes 786440 | tf_op jit(solution)/shard_map/term_halo/ppermute | solution.py:250
  86.2 15.0 %all-to-all-start.1 = ((f32[8,24,128]{2,1,0:T(8,128)}), f32[8,24,128]{2,1,0:T(8,128)S(1)}, u32[]{:S(2)}, u32[]{:S(2)}) async-start(f32[8,24,128]{2,1,0:T(8,128)} %spread_sum.2.first), calls=%async_computation.1 | async-start | bytes 196608 | tf_op jit(solution)/shard_map/weight_rows/all_to_all | solution.py:287
  101.9 20.7 %all-to-all-start.2 = ((bf16[24,24,128]{2,1,0:T(8,128)(2,1)}), bf16[24,24,128]{2,1,0:T(8,128)(2,1)S(1)}, u32[]{:S(2)}, u32[]{:S(2)}) async-start(bf16[24,24,128]{2,1,0:T(8,128)(2,1)} %spread_sum.3.first), calls=%async_computation.2 | async-start | bytes 294912 | tf_op jit(solution)/shard_map/weight_gather/all_to_all | solution.py:294
  111.8 7.1 %collective-permute-start.9 = (bf16[128,512]{1,0:T(8,128)(2,1)S(1)}, bf16[128,512]{1,0:T(8,128)(2,1)S(1)}, u32[]{:S(2)}, u32[]{:S(2)}) collective-permute-start(bf16[128,512]{1,0:T(8,128)(2,1)S(1)} %get-tuple-element.23), channel_id=1, source_target_pairs={{4,0},{0,4},{12,8},{8,12},{20,16},{16,20},{28,24},{24,28},{36,32},... | collective-permute-start | bytes 393224 | tf_op jit(solution)/shard_map/term_exchange/ppermute | solution.py:250

commit v9 on v8

--- a/solution.py
+++ b/solution.py
@@ -19,7 +19,6 @@
 REACH = 4
 N_Y, N_Z, N_XL = 8, 12, 2
 PAIRS = N_Y * N_Z
-PACK_ROWS = ROWS + 16
 RING = N_Z * N_XL
 SHARE = 24
 BLK = ("y", "z", "xl")
@@ -70,7 +69,7 @@
     )(codes, pltpu.with_memory_space_constraint(slab, pltpu.HBM))
 
 
-def gather_kernel(side, dense, far_before, before, own, after, far_after, cross, bias, out):
+def gather_kernel(side, dense, far_before, before, own, after, far_after, cross, out):
     s = side[0]
     total = jnp.dot(dense[1], far_before[...], preferred_element_type=F32)
     total += jnp.dot(dense[9], far_after[...], preferred_element_type=F32)
@@ -78,57 +77,47 @@
     for first, pair in ((3 - s, before), (5 - s, own), (7 - s, after)):
         for i in range(2):
             total += jnp.dot(dense[first + i], pair[i], preferred_element_type=F32)
-    out[0:ROWS, :] = total.astype(BF16)
-    out[ROWS:, :] = jnp.broadcast_to(bias[...], (16, WIDTH))
-
-
-def gather_rows(side, dense, blocks, bias):
+    out[...] = total.astype(BF16)
+
+
+def gather_rows(side, dense, blocks):
     return pl.pallas_call(
         gather_kernel,
-        in_specs=[SMEM] + [VMEM] * 8,
-        out_specs=VMEM,
-        out_shape=jax.ShapeDtypeStruct((PACK_ROWS, WIDTH), BF16),
+        in_specs=[SMEM] + [VMEM] * 7,
+        out_specs=VMEM,
+        out_shape=jax.ShapeDtypeStruct((ROWS, WIDTH), BF16),
         compiler_params=params(),
         cost_estimate=pl.CostEstimate(
             flops=2 * OFFSETS * ROWS * ROWS * WIDTH, bytes_accessed=8 << 20, transcendentals=0
         ),
         name="aggregate_features",
-    )(side, dense, *blocks, bias)
+    )(side, dense, *blocks)
 
 
 def middle_kernel(
-    place, mixed, cots, weight, dense,
+    place, mixed, cot, bias, weight, dense,
     act, part, ta, tb, tc, td, te,
-    act_all, grad_all, feats,
+    grad, feats,
 ):
     mine = pl.multiple_of(place[1] * WIDTH, WIDTH)
-    bias = jnp.concatenate([mixed[c, ROWS:, :] for c in range(COLS)], axis=1)[0:1].astype(F32)
+    columns = weight[:, pl.ds(mine, WIDTH)]
     step = 128
     for i in range(ROWS // step):
         span = slice(i * step, (i + 1) * step)
         rows = jnp.concatenate([mixed[c, span, :] for c in range(COLS)], axis=1)
         feats[span, :] = rows
-        preact = jnp.dot(rows, weight[...], preferred_element_type=F32) + bias
+        preact = jnp.dot(rows, columns, preferred_element_type=F32) + bias[...].astype(F32)
         sig = 1.0 / (1.0 + jnp.exp(-preact))
-        act_all[span, :] = (preact * sig).astype(BF16)
-        cot = jnp.concatenate([cots[c, span, :] for c in range(COLS)], axis=1)
-        grad_all[span, :] = (
-            cot.astype(F32) * sig * (1.0 + preact * (1.0 - sig))
+        act[span, :] = (preact * sig).astype(BF16)
+        grad[span, :] = (
+            cot[span, :].astype(F32) * sig * (1.0 + preact * (1.0 - sig))
         ).astype(BF16)
-    act[...] = act_all[:, pl.ds(mine, WIDTH)]
-    grad_mine = grad_all[:, pl.ds(mine, WIDTH)].astype(F32)
-    weight_grad = jnp.dot(
-        grad_mine.T.astype(BF16), feats[...], preferred_element_type=F32
-    )
+    grad_mine = grad[...].astype(F32)
+    back = grad_mine.T.astype(BF16)
+    weight_grad = jnp.dot(back, feats[...], preferred_element_type=F32)
     part[0:ROWS, :] = weight_grad.T
     first = lax.broadcasted_iota(jnp.int32, (RING * SHARE - HIDDEN, WIDTH), 0) == 0
     part[ROWS:, :] = jnp.where(first, jnp.sum(grad_mine, axis=0, keepdims=True), 0.0)
-    back = lax.dot_general(
-        weight[pl.ds(mine, WIDTH), :],
-        grad_all[...],
-        (((1,), (1,)), ((), ())),
-        preferred_element_type=F32,
-    ).astype(BF16)
     side = place[0]
     for k, pair in enumerate((ta, tb, tc, td, te)):
         for s in range(2):
@@ -137,23 +126,23 @@
             ).astype(BF16)
 
 
-def middle(place, mixed, cots, weight, dense):
+def middle(place, mixed, cot, bias, weight, dense):
     return pl.pallas_call(
         middle_kernel,
-        in_specs=[SMEM] + [VMEM] * 4,
+        in_specs=[SMEM] + [VMEM] * 5,
         out_specs=[VMEM] * 7,
         out_shape=[
             jax.ShapeDtypeStruct((ROWS, WIDTH), BF16),
             jax.ShapeDtypeStruct((RING * SHARE, WIDTH), F32),
         ]
         + [jax.ShapeDtypeStruct((2, WIDTH, ROWS), BF16)] * 5,
-        scratch_shapes=[pltpu.VMEM((ROWS, HIDDEN), BF16)] * 3,
+        scratch_shapes=[pltpu.VMEM((ROWS, WIDTH), BF16), pltpu.VMEM((ROWS, HIDDEN), BF16)],
         compiler_params=params(),
         cost_estimate=pl.CostEstimate(
-            flops=2 * (OFFSETS + 9) * ROWS * ROWS * WIDTH, bytes_accessed=10 << 20, transcendentals=ROWS * HIDDEN
+            flops=2 * (OFFSETS + 9) * ROWS * ROWS * WIDTH, bytes_accessed=10 << 20, transcendentals=ROWS * WIDTH
         ),
         name="activation_and_terms",
-    )(place, mixed, cots, weight, dense)
+    )(place, mixed, cot, bias, weight, dense)
 
 
 def share_kernel(scale, shares, *rest):
@@ -218,8 +207,33 @@
         out_shape=jax.ShapeDtypeStruct((ROWS, WIDTH), BF16),
         compiler_params=params(),
         cost_estimate=pl.CostEstimate(flops=1 << 17, bytes_accessed=1 << 19, transcendentals=0),
+        name="projected_gradient",
+    )(keep, arrived, first)
+
+
+def node_kernel(column, grads, weight, out):
+    mine = pl.multiple_of(column[0] * WIDTH, WIDTH)
+    rows = jnp.concatenate([grads[c] for c in range(COLS)], axis=1)
+    out[...] = lax.dot_general(
+        rows,
+        weight[pl.ds(mine, WIDTH), :],
+        (((1,), (1,)), ((), ())),
+        preferred_element_type=F32,
+    ).astype(BF16)
+
+
+def node_gradient(column, grads, weight):
+    return pl.pallas_call(
+        node_kernel,
+        in_specs=[SMEM] + [VMEM] * 2,
+        out_specs=VMEM,
+        out_shape=jax.ShapeDtypeStruct((ROWS, WIDTH), BF16),
+        compiler_params=params(),
+        cost_estimate=pl.CostEstimate(
+            flops=2 * ROWS * HIDDEN * WIDTH, bytes_accessed=2 << 20, transcendentals=0
+        ),
         name="node_gradient",
-    )(keep, arrived, first)
+    )(column, grads, weight)
 
 
 def widen_kernel(whole, weight_grad, bias_grad):
@@ -264,15 +278,13 @@
         before, after = (routed(pair, lambda p, s, k=k: (p + k, s)) for k in (-1, 1))
         cross = jnp.where(side[0] == 1, far_before, far_after)
         cross = routed(cross, lambda p, s: (p, 1 - s))
-    with jax.named_scope("column_gather"):
-        cots = lax.all_gather(cotangent, COL, axis=0, tiled=False)
     dense = make_dense(codes, adj_tiles)
     blocks = (far_before, before, pair, after, far_after, cross)
-    mine = gather_rows(side, dense, blocks, layer_bias.reshape(1, WIDTH))
+    mine = gather_rows(side, dense, blocks)
     with jax.named_scope("column_gather"):
         mixed = lax.all_gather(mine, COL, axis=0, tiled=False)
     act, part, ta, tb, tc, td, te = middle(
-        jnp.concatenate([side, column]), mixed, cots, weight, dense
+        jnp.concatenate([side, column]), mixed, cotangent, layer_bias.reshape(1, WIDTH), weight, dense
     )
 
     ring = ("z", "xl")
@@ -286,10 +298,13 @@
     with jax.named_scope("weight_rows"):
         shares = lax.all_to_all(spread, "y", 0, 0, tiled=True)
     keep, send = split_terms(side, tc, (ra, rb, rd, re), spread)
-    spread = spread_sum(shares, [keep], RING, float(NODES) ** -0.5, BF16)
     with jax.named_scope("term_exchange"):
         other = routed(send, lambda p, s: (p, 1 - s))
-    grad_nodes = last_sum(keep, other, spread)
+    spread = spread_sum(shares, [other], RING, float(NODES) ** -0.5, BF16)
+    grad_proj = last_sum(keep, other, spread)
+    with jax.named_scope("column_gather"):
+        grads = lax.all_gather(grad_proj, COL, axis=0, tiled=False)
+    grad_nodes = node_gradient(column, grads, weight)
     with jax.named_scope("weight_gather"):
         whole = lax.all_to_all(spread, ring, 0, 0, tiled=True).reshape(RING * SHARE, WIDTH)
     weight_grad, bias_grad = widen(whole)

time: 124 us -> 119 us (0.960)
  starting transfers between devices: 69.1 us -> 63.5 us
  waiting for transfers between devices: 17.9 us -> 20.8 us
  blocking collectives: 23.8 us -> 22.3 us
    ppermute x10, waiting for transfers between devices: 13.4 us -> 18.6 us  [routed(): return lax.ppermute(block, BLK, route)]
    all_to_all x1, starting transfers between devices: 6.79 us -> 4.07 us  [on_device(): shares = lax.all_to_all(spread, 'y', 0, 0, tiled=True)]
    ppermute x10, starting transfers between devices: 47.1 us -> 45 us  [routed(): return lax.ppermute(block, BLK, route)]
    all_to_all x1, waiting for transfers between devices: 1.54 us -> 0.01 us  [on_device(): shares = lax.all_to_all(spread, 'y', 0, 0, tiled=True)]
    pallas_call x2 -> x3, Pallas kernels: 4.58 us -> 4.78 us  [the longest x1 2.45 us: middle(): pl.pallas_call(middle_kernel, in_specs=[SMEM] + [VMEM] * 5, out_specs=[VM...]
  transfers between devices with their start and end apart: 13 -> 13, of which waited for: 6 -> 7; matrix products, arithmetic and copies ran while one was open for 1% -> 1% of each run, Pallas kernels for 4% -> 4%
where the time goes in v9:
time: 119 us
  starting transfers between devices  63.5 us (53%)
  blocking collectives  22.3 us (19%)
  waiting for transfers between devices  20.8 us (17%)
  Pallas kernels  10.4 us (9%)
    ppermute x10, starting transfers between devices, routed(): return lax.ppermute(block, BLK, route)  45 us
    ppermute x10, waiting for transfers between devices, routed(): return lax.ppermute(block, BLK, route)  18.6 us
    all_to_all x1, starting transfers between devices, on_device(): lax.all_to_all(spread, ring, 0, 0, tiled=True).reshape(RING * SHARE, WIDTH)  9.69 us
    all_gather x1, blocking collectives, on_device(): grads = lax.all_gather(grad_proj, COL, axis=0, tiled=False)  8.41 us
    all_gather x1, blocking collectives, on_device(): mixed = lax.all_gather(mine, COL, axis=0, tiled=False)  8.02 us
    all_gather x1, blocking collectives, on_device(): pair = lax.all_gather(x, 'xl', axis=0, tiled=False)  5.86 us
    all_to_all x1, starting transfers between devices, on_device(): lax.all_to_all(part.reshape(RING, SHARE, WIDTH), ring, 0, 0, tiled=True)  4.78 us
    all_to_all x1, starting transfers between devices, on_device(): shares = lax.all_to_all(spread, 'y', 0, 0, tiled=True)  4.07 us
  transfers between devices with their start and end apart: 13, of which 7 were waited for; matrix products, arithmetic and copies ran while one was open for 1% of the time, Pallas kernels for 4%

profile of v9, /device:TPU:2, one launch (start us, length us, event | category | flops | bytes accessed | tf_op | source)
XLA Modules:
  0.0 118.7 jit_solution(12268494193737158835)
XLA Ops:
  0.6 6.1 %collective-permute-start = (bf16[512,128]{1,0:T(8,128)(2,1)}, bf16[512,128]{1,0:T(8,128)(2,1)S(1)}, u32[]{:S(2)}, u32[]{:S(2)}) collective-permute-start(bf16[512,128]{1,0:T(8,128)(2,1)} %param.8), channel_id=1, source_target_pairs={{752,0},{756,4},{760,8},{764,12},{0,16},{4,20},{8,24},{12,28},{16,... | collective-permute-start | bytes 393224 | tf_op jit(solution)/shard_map/feature_halo/ppermute | solution.py:264
  6.7 13.3 %collective-permute-start.3 = (bf16[512,128]{1,0:T(8,128)(2,1)}, bf16[512,128]{1,0:T(8,128)(2,1)S(1)}, u32[]{:S(2)}, u32[]{:S(2)}) collective-permute-start(bf16[512,128]{1,0:T(8,128)(2,1)} %param.8), channel_id=1, source_target_pairs={{16,0},{20,4},{24,8},{28,12},{32,16},{36,20},{40,24},{44,28},{48,3... | collective-permute-start | bytes 393224 | tf_op jit(solution)/shard_map/feature_halo/ppermute | solution.py:264
  20.0 5.9 %all-gather = bf16[1024,128]{1,0:T(8,128)(2,1)S(1)} all-gather(bf16[512,128]{1,0:T(8,128)(2,1)} %param.8), channel_id=2, replica_groups=mesh['y'=8,'z'=12,'xl'=2,'xh'=2,'core'=2] {'xl'}, dimensions={0}, use_global_device_ids=true | all-gather | bytes 393216 | tf_op jit(solution)/shard_map/feature_halo/all_gather | solution.py:277
  25.9 4.8 %collective-permute-start.2 = (bf16[2,512,128]{2,1,0:T(8,128)(2,1)S(1)}, bf16[2,512,128]{2,1,0:T(8,128)(2,1)S(1)}, u32[]{:S(2)}, u32[]{:S(2)}) collective-permute-start(bf16[2,512,128]{2,1,0:T(8,128)(2,1)S(1)} %bitcast.14), channel_id=1, source_target_pairs={{8,0},{12,4},{16,8},{20,12},{24,16},{28,20},{32,24},{36,28},{40,32... | collective-permute-start | bytes 786440 | tf_op jit(solution)/shard_map/feature_halo/ppermute | solution.py:264
  30.7 1.9 %collective-permute-start.1 = (bf16[2,512,128]{2,1,0:T(8,128)(2,1)S(1)}, bf16[2,512,128]{2,1,0:T(8,128)(2,1)S(1)}, u32[]{:S(2)}, u32[]{:S(2)}) collective-permute-start(bf16[2,512,128]{2,1,0:T(8,128)(2,1)S(1)} %bitcast.15), channel_id=1, source_target_pairs={{760,0},{764,4},{0,8},{4,12},{8,16},{12,20},{16,24},{20,28},{24,32... | collective-permute-start | bytes 786440 | tf_op jit(solution)/shard_map/feature_halo/ppermute | solution.py:264
  32.7 0.0 collective-permute-done.far_before
  32.7 0.0 collective-permute-done.3.far_after
  32.7 2.4 %collective-permute-start.4 = (bf16[512,128]{1,0:T(8,128)(2,1)S(1)}, bf16[512,128]{1,0:T(8,128)(2,1)S(1)}, u32[]{:S(2)}, u32[]{:S(2)}) collective-permute-start(bf16[512,128]{1,0:T(8,128)(2,1)S(1)} %broadcast_select_fusion), channel_id=1, source_target_pairs={{4,0},{0,4},{12,8},{8,12},{20,16},{16,20},{28,24},{24,28},{36,32},... | collective-permute-start | bytes 393224 | tf_op jit(solution)/shard_map/feature_halo/ppermute | solution.py:264
  35.2 0.8 bitcast_add_fusion.codes
  35.9 3.2 %dense_tiles.1.dense = bf16[11,512,512]{2,1,0:T(8,128)(2,1)S(1)} custom-call(s32[9,16]{1,0:T(8,128)S(1)} %bitcast_add_fusion.codes, bf16[1,9,16,128,128]{4,3,2,1,0:T(8,128)(2,1)} %slab.1), custom_call_target="tpu_custom_call" | custom-call | bytes 10485760 | tf_op jit(solution)/shard_map/dense_tiles/pallas_call | solution.py:57
  39.1 0.0 copy-start
  39.1 0.0 copy-start.1
  39.2 0.0 copy-start.2
  39.2 0.1 pad_add_fusion.place
  39.2 0.3 collective-permute-done.4.cross
  39.6 0.0 collective-permute-done.2.after
  39.6 2.7 %collective-permute-done.1.before = bf16[2,512,128]{2,1,0:T(8,128)(2,1)S(1)} collective-permute-done((bf16[2,512,128]{2,1,0:T(8,128)(2,1)S(1)}, bf16[2,512,128]{2,1,0:T(8,128)(2,1)S(1)}, u32[]{:S(2)}, u32[]{:S(2)}) %collective-permute-start.1) | collective-permute-done | bytes 262176 | tf_op jit(solution)/shard_map/feature_halo/ppermute | solution.py:264
  42.3 1.4 %aggregate_features.1 = bf16[512,128]{1,0:T(8,128)(2,1)S(1)} custom-call(s32[1]{0:T(128)} %bitcast.side, bf16[11,512,512]{2,1,0:T(8,128)(2,1)S(1)} %dense_tiles.1.dense, bf16[512,128]{1,0:T(8,128)(2,1)S(1)} %collective-permute-done.far_before, bf16[2,512,128]{2,1,0:T(8,128)(2,1)S(1)} %collective-permute-done.1.before, bf16[2,512,128]{2,1,0:T(8,128)(2,1)S(1)} %bitcast.16, ...), custom_call_target="tpu_custom_call" | custom-call | flops 603979776 | bytes 8388608 | tf_op jit(solution)/shard_map/aggregate_features/pallas_call | solution.py:84
  43.7 8.0 %all-gather.1 = bf16[2048,128]{1,0:T(8,128)(2,1)S(1)} all-gather(bf16[512,128]{1,0:T(8,128)(2,1)S(1)} %aggregate_features.1), channel_id=3, replica_groups=mesh['y'=8,'z'=12,'xl'=2,'xh'=2,'core'=2] {'xh','core'}, dimensions={0}, use_global_device_ids=true | all-gather | bytes 655360 | tf_op jit(solution)/shard_map/column_gather/all_gather | solution.py:285
  51.7 0.0 copy-done
  51.7 0.0 copy-done.1
  51.7 0.0 copy-done.2
  51.7 2.4 %activation_and_terms.1 = (bf16[512,128]{1,0:T(8,128)(2,1)}, f32[576,128]{1,0:T(8,128)}, bf16[2,128,512]{2,1,0:T(8,128)(2,1)S(1)}, bf16[2,128,512]{2,1,0:T(8,128...) custom-call(s32[2]{0:T(128)S(1)} %pad_add_fusion.place, ...), custom_call_target="tpu_custom_call" | custom-call | flops 1207959552 | bytes 10485760 | tf_op jit(solution)/shard_map/activation_and_terms/pallas_call | solution.py:130
  54.2 4.8 %all-to-all-start = ((f32[24,24,128]{2,1,0:T(8,128)}), f32[24,24,128]{2,1,0:T(8,128)S(1)}, u32[]{:S(2)}, u32[]{:S(2)}) async-start(f32[24,24,128]{2,1,0:T(8,128)} %bitcast.7), calls=%async_computation | async-start | bytes 589824 | tf_op jit(solution)/shard_map/weight_scatter/all_to_all | solution.py:292
  59.0 5.4 %collective-permute-start.6 = (bf16[2,128,512]{2,1,0:T(8,128)(2,1)S(1)}, bf16[2,128,512]{2,1,0:T(8,128)(2,1)S(1)}, u32[]{:S(2)}, u32[]{:S(2)}) collective-permute-start(bf16[2,128,512]{2,1,0:T(8,128)(2,1)S(1)} %get-tuple-element.18), channel_id=1, source_target_pairs={{8,0},{12,4},{16,8},{20,12},{24,16},{28,20},{32,24},{36,28},{40,32... | collective-permute-start | bytes 786440 | tf_op jit(solution)/shard_map/term_halo/ppermute | solution.py:264
  64.3 4.2 %collective-permute-start.5 = (bf16[2,128,512]{2,1,0:T(8,128)(2,1)S(1)}, bf16[2,128,512]{2,1,0:T(8,128)(2,1)S(1)}, u32[]{:S(2)}, u32[]{:S(2)}) collective-permute-start(bf16[2,128,512]{2,1,0:T(8,128)(2,1)S(1)} %get-tuple-element.17), channel_id=1, source_target_pairs={{16,0},{20,4},{24,8},{28,12},{32,16},{36,20},{40,24},{44,28},{48,3... | collective-permute-start | bytes 786440 | tf_op jit(solution)/shard_map/term_halo/ppermute | solution.py:264
  68.6 2.5 %collective-permute-start.7 = (bf16[2,128,512]{2,1,0:T(8,128)(2,1)S(1)}, bf16[2,128,512]{2,1,0:T(8,128)(2,1)S(1)}, u32[]{:S(2)}, u32[]{:S(2)}) collective-permute-start(bf16[2,128,512]{2,1,0:T(8,128)(2,1)S(1)} %get-tuple-element.19), channel_id=1, source_target_pairs={{760,0},{764,4},{0,8},{4,12},{8,16},{12,20},{16,24},{20,28},{24,32... | collective-permute-start | bytes 786440 | tf_op jit(solution)/shard_map/term_halo/ppermute | solution.py:264
  71.1 1.9 %collective-permute-start.8 = (bf16[2,128,512]{2,1,0:T(8,128)(2,1)S(1)}, bf16[2,128,512]{2,1,0:T(8,128)(2,1)S(1)}, u32[]{:S(2)}, u32[]{:S(2)}) collective-permute-start(bf16[2,128,512]{2,1,0:T(8,128)(2,1)S(1)} %get-tuple-element.20), channel_id=1, source_target_pairs={{752,0},{756,4},{760,8},{764,12},{0,16},{4,20},{8,24},{12,28},{16,... | collective-permute-start | bytes 786440 | tf_op jit(solution)/shard_map/term_halo/ppermute | solution.py:264
  73.0 4.4 %collective-permute-done.6.refs_1_.tb = bf16[2,128,512]{2,1,0:T(8,128)(2,1)S(1)} collective-permute-done((bf16[2,128,512]{2,1,0:T(8,128)(2,1)S(1)}, bf16[2,128,512]{2,1,0:T(8,128)(2,1)S(1)}, u32[]{:S(2)}, u32[]{:S(2)}) %collective-permute-start.6) | collective-permute-done | bytes 262176 | tf_op jit(solution)/shard_map/term_halo/ppermute | solution.py:264
  77.4 0.0 all-to-all-done.refs_0_
  77.4 0.7 spread_sum.2.first
  78.1 4.1 %all-to-all-start.1 = ((f32[8,24,128]{2,1,0:T(8,128)}), f32[8,24,128]{2,1,0:T(8,128)S(1)}, u32[]{:S(2)}, u32[]{:S(2)}) async-start(f32[8,24,128]{2,1,0:T(8,128)} %spread_sum.2.first), calls=%async_computation.1 | async-start | bytes 196608 | tf_op jit(solution)/shard_map/weight_rows/all_to_all | solution.py:299
  82.1 6.6 %collective-permute-done.5.ta = bf16[2,128,512]{2,1,0:T(8,128)(2,1)S(1)} collective-permute-done((bf16[2,128,512]{2,1,0:T(8,128)(2,1)S(1)}, bf16[2,128,512]{2,1,0:T(8,128)(2,1)S(1)}, u32[]{:S(2)}, u32[]{:S(2)}) %collective-permute-start.5) | collective-permute-done | bytes 262176 | tf_op jit(solution)/shard_map/term_halo/ppermute | solution.py:264
  88.8 0.1 collective-permute-done.7.td
  88.9 0.0 collective-permute-done.8.te
  88.9 0.2 pair_sums.1
  89.1 2.4 %collective-permute-start.9 = (bf16[128,512]{1,0:T(8,128)(2,1)S(1)}, bf16[128,512]{1,0:T(8,128)(2,1)S(1)}, u32[]{:S(2)}, u32[]{:S(2)}) collective-permute-start(bf16[128,512]{1,0:T(8,128)(2,1)S(1)} %get-tuple-element.23), channel_id=1, source_target_pairs={{4,0},{0,4},{12,8},{8,12},{20,16},{16,20},{28,24},{24,28},{36,32},... | collective-permute-start | bytes 393224 | tf_op jit(solution)/shard_map/term_exchange/ppermute | solution.py:264
  91.5 4.5 %collective-permute-done.9.refs_1_.arrived = bf16[128,512]{1,0:T(8,128)(2,1)S(1)} collective-permute-done((bf16[128,512]{1,0:T(8,128)(2,1)S(1)}, bf16[128,512]{1,0:T(8,128)(2,1)S(1)}, u32[]{:S(2)}, u32[]{:S(2)}) %collective-permute-start.9) | collective-permute-done | bytes 131104 | tf_op jit(solution)/shard_map/term_exchange/ppermute | solution.py:264
  96.0 0.0 all-to-all-done.1.refs_0_
  96.0 0.7 spread_sum.3.first
  96.6 9.7 %all-to-all-start.2 = ((bf16[24,24,128]{2,1,0:T(8,128)(2,1)}), bf16[24,24,128]{2,1,0:T(8,128)(2,1)S(1)}, u32[]{:S(2)}, u32[]{:S(2)}) async-start(bf16[24,24,128]{2,1,0:T(8,128)(2,1)} %spread_sum.3.first), calls=%async_computation.2 | async-start | bytes 294912 | tf_op jit(solution)/shard_map/weight_gather/all_to_all | solution.py:309
  106.3 0.1 projected_gradient.1
  106.5 8.4 %all-gather.2 = bf16[2048,128]{1,0:T(8,128)(2,1)S(1)} all-gather(bf16[512,128]{1,0:T(8,128)(2,1)S(1)} %projected_gradient.1), channel_id=4, replica_groups=mesh['y'=8,'z'=12,'xl'=2,'xh'=2,'core'=2] {'xh','core'}, dimensions={0}, use_global_device_ids=true | all-gather | bytes 655360 | tf_op jit(solution)/shard_map/column_gather/all_gather | solution.py:306
  114.9 1.0 node_gradient.1
  115.8 2.2 %all-to-all-done.2 = bf16[24,24,128]{2,1,0:T(8,128)(2,1)S(1)} async-done(((bf16[24,24,128]{2,1,0:T(8,128)(2,1)}), bf16[24,24,128]{2,1,0:T(8,128)(2,1)S(1)}, u32[]{:S(2)}, u32[]{:S(2)}) %all-to-all-start.2) | async-done | bytes 147488 | tf_op jit(solution)/shard_map/weight_gather/all_to_all | solution.py:309
  118.0 0.7 weight_gradient.1
  (1 shorter events, 0.0 us)
Async XLA Ops:
  0.6 32.0 %collective-permute-start = (bf16[512,128]{1,0:T(8,128)(2,1)}, bf16[512,128]{1,0:T(8,128)(2,1)S(1)}, u32[]{:S(2)}, u32[]{:S(2)}) collective-permute-start(bf16[512,128]{1,0:T(8,128)(2,1)} %param.8), channel_id=1, source_target_pairs={{752,0},{756,4},{760,8},{764,12},{0,16},{4,20},{8,24},{12,28},{16,... | collective-permute-start | bytes 393224 | tf_op jit(solution)/shard_map/feature_halo/ppermute | solution.py:264
  6.7 26.0 %collective-permute-start.3 = (bf16[512,128]{1,0:T(8,128)(2,1)}, bf16[512,128]{1,0:T(8,128)(2,1)S(1)}, u32[]{:S(2)}, u32[]{:S(2)}) collective-permute-start(bf16[512,128]{1,0:T(8,128)(2,1)} %param.8), channel_id=1, source_target_pairs={{16,0},{20,4},{24,8},{28,12},{32,16},{36,20},{40,24},{44,28},{48,3... | collective-permute-start | bytes 393224 | tf_op jit(solution)/shard_map/feature_halo/ppermute | solution.py:264
  25.9 13.7 %collective-permute-start.2 = (bf16[2,512,128]{2,1,0:T(8,128)(2,1)S(1)}, bf16[2,512,128]{2,1,0:T(8,128)(2,1)S(1)}, u32[]{:S(2)}, u32[]{:S(2)}) collective-permute-start(bf16[2,512,128]{2,1,0:T(8,128)(2,1)S(1)} %bitcast.14), channel_id=1, source_target_pairs={{8,0},{12,4},{16,8},{20,12},{24,16},{28,20},{32,24},{36,28},{40,32... | collective-permute-start | bytes 786440 | tf_op jit(solution)/shard_map/feature_halo/ppermute | solution.py:264
  30.7 11.6 %collective-permute-start.1 = (bf16[2,512,128]{2,1,0:T(8,128)(2,1)S(1)}, bf16[2,512,128]{2,1,0:T(8,128)(2,1)S(1)}, u32[]{:S(2)}, u32[]{:S(2)}) collective-permute-start(bf16[2,512,128]{2,1,0:T(8,128)(2,1)S(1)} %bitcast.15), channel_id=1, source_target_pairs={{760,0},{764,4},{0,8},{4,12},{8,16},{12,20},{16,24},{20,28},{24,32... | collective-permute-start | bytes 786440 | tf_op jit(solution)/shard_map/feature_halo/ppermute | solution.py:264
  32.7 6.9 %collective-permute-start.4 = (bf16[512,128]{1,0:T(8,128)(2,1)S(1)}, bf16[512,128]{1,0:T(8,128)(2,1)S(1)}, u32[]{:S(2)}, u32[]{:S(2)}) collective-permute-start(bf16[512,128]{1,0:T(8,128)(2,1)S(1)} %broadcast_select_fusion), channel_id=1, source_target_pairs={{4,0},{0,4},{12,8},{8,12},{20,16},{16,20},{28,24},{24,28},{36,32},... | collective-permute-start | bytes 393224 | tf_op jit(solution)/shard_map/feature_halo/ppermute | solution.py:264
  39.1 12.6 %copy-start = (bf16[512,512]{1,0:T(8,128)(2,1)S(1)}, bf16[512,512]{1,0:T(8,128)(2,1)}, u32[]{:S(2)}) copy-start(bf16[512,512]{1,0:T(8,128)(2,1)} %weight.3) | copy-start | bytes 1572868
  39.1 12.6 %copy-start.1 = (bf16[512,128]{1,0:T(8,128)(2,1)S(1)}, bf16[512,128]{1,0:T(8,128)(2,1)}, u32[]{:S(2)}) copy-start(bf16[512,128]{1,0:T(8,128)(2,1)} %cot.1) | copy-start | bytes 393220
  39.2 12.6 %copy-start.2 = (bf16[128]{0:T(256)(128)(2,1)S(1)}, bf16[128]{0:T(256)(128)(2,1)}, u32[]{:S(2)}) copy-start(bf16[128]{0:T(256)(128)(2,1)} %param.10) | copy-start | bytes 772
  54.2 23.2 %all-to-all-start = ((f32[24,24,128]{2,1,0:T(8,128)}), f32[24,24,128]{2,1,0:T(8,128)S(1)}, u32[]{:S(2)}, u32[]{:S(2)}) async-start(f32[24,24,128]{2,1,0:T(8,128)} %bitcast.7), calls=%async_computation | async-start | bytes 589824 | tf_op jit(solution)/shard_map/weight_scatter/all_to_all | solution.py:292
  59.0 18.4 %collective-permute-start.6 = (bf16[2,128,512]{2,1,0:T(8,128)(2,1)S(1)}, bf16[2,128,512]{2,1,0:T(8,128)(2,1)S(1)}, u32[]{:S(2)}, u32[]{:S(2)}) collective-permute-start(bf16[2,128,512]{2,1,0:T(8,128)(2,1)S(1)} %get-tuple-element.18), channel_id=1, source_target_pairs={{8,0},{12,4},{16,8},{20,12},{24,16},{28,20},{32,24},{36,28},{40,32... | collective-permute-start | bytes 786440 | tf_op jit(solution)/shard_map/term_halo/ppermute | solution.py:264
  64.3 24.4 %collective-permute-start.5 = (bf16[2,128,512]{2,1,0:T(8,128)(2,1)S(1)}, bf16[2,128,512]{2,1,0:T(8,128)(2,1)S(1)}, u32[]{:S(2)}, u32[]{:S(2)}) collective-permute-start(bf16[2,128,512]{2,1,0:T(8,128)(2,1)S(1)} %get-tuple-element.17), channel_id=1, source_target_pairs={{16,0},{20,4},{24,8},{28,12},{32,16},{36,20},{40,24},{44,28},{48,3... | collective-permute-start | bytes 786440 | tf_op jit(solution)/shard_map/term_halo/ppermute | solution.py:264
  68.6 20.3 %collective-permute-start.7 = (bf16[2,128,512]{2,1,0:T(8,128)(2,1)S(1)}, bf16[2,128,512]{2,1,0:T(8,128)(2,1)S(1)}, u32[]{:S(2)}, u32[]{:S(2)}) collective-permute-start(bf16[2,128,512]{2,1,0:T(8,128)(2,1)S(1)} %get-tuple-element.19), channel_id=1, source_target_pairs={{760,0},{764,4},{0,8},{4,12},{8,16},{12,20},{16,24},{20,28},{24,32... | collective-permute-start | bytes 786440 | tf_op jit(solution)/shard_map/term_halo/ppermute | solution.py:264
  71.1 17.8 %collective-permute-start.8 = (bf16[2,128,512]{2,1,0:T(8,128)(2,1)S(1)}, bf16[2,128,512]{2,1,0:T(8,128)(2,1)S(1)}, u32[]{:S(2)}, u32[]{:S(2)}) collective-permute-start(bf16[2,128,512]{2,1,0:T(8,128)(2,1)S(1)} %get-tuple-element.20), channel_id=1, source_target_pairs={{752,0},{756,4},{760,8},{764,12},{0,16},{4,20},{8,24},{12,28},{16,... | collective-permute-start | bytes 786440 | tf_op jit(solution)/shard_map/term_halo/ppermute | solution.py:264
  78.1 17.9 %all-to-all-start.1 = ((f32[8,24,128]{2,1,0:T(8,128)}), f32[8,24,128]{2,1,0:T(8,128)S(1)}, u32[]{:S(2)}, u32[]{:S(2)}) async-start(f32[8,24,128]{2,1,0:T(8,128)} %spread_sum.2.first), calls=%async_computation.1 | async-start | bytes 196608 | tf_op jit(solution)/shard_map/weight_rows/all_to_all | solution.py:299
  89.1 6.9 %collective-permute-start.9 = (bf16[128,512]{1,0:T(8,128)(2,1)S(1)}, bf16[128,512]{1,0:T(8,128)(2,1)S(1)}, u32[]{:S(2)}, u32[]{:S(2)}) collective-permute-start(bf16[128,512]{1,0:T(8,128)(2,1)S(1)} %get-tuple-element.23), channel_id=1, source_target_pairs={{4,0},{0,4},{12,8},{8,12},{20,16},{16,20},{28,24},{24,28},{36,32},... | collective-permute-start | bytes 393224 | tf_op jit(solution)/shard_map/term_exchange/ppermute | solution.py:264
  96.6 21.4 %all-to-all-start.2 = ((bf16[24,24,128]{2,1,0:T(8,128)(2,1)}), bf16[24,24,128]{2,1,0:T(8,128)(2,1)S(1)}, u32[]{:S(2)}, u32[]{:S(2)}) async-start(bf16[24,24,128]{2,1,0:T(8,128)(2,1)} %spread_sum.3.first), calls=%async_computation.2 | async-start | bytes 294912 | tf_op jit(solution)/shard_map/weight_gather/all_to_all | solution.py:309

commit v10 on v9

--- a/solution.py
+++ b/solution.py
@@ -39,8 +39,6 @@
     ]
     for copy in copies:
         copy.start()
-    dense[0] = jnp.zeros((ROWS, ROWS), BF16)
-    dense[OFFSETS + 1] = jnp.zeros((ROWS, ROWS), BF16)
     for offset, copy in enumerate(copies):
         copy.wait()
         for slot in range(SLOTS):
@@ -48,7 +46,7 @@
             row = pl.multiple_of(((code >> 2) & 3) * TILE, TILE)
             col = pl.multiple_of((code & 3) * TILE, TILE)
             tile = held[offset, slot]
-            dense[offset + 1, pl.ds(row, TILE), pl.ds(col, TILE)] = jnp.where(
+            dense[offset, pl.ds(row, TILE), pl.ds(col, TILE)] = jnp.where(
                 code < BLOCKS * BLOCKS, tile, jnp.zeros_like(tile)
             )
 
@@ -58,7 +56,7 @@
         dense_kernel,
         in_specs=[SMEM, pl.BlockSpec(memory_space=pltpu.HBM)],
         out_specs=VMEM,
-        out_shape=jax.ShapeDtypeStruct((OFFSETS + 2, ROWS, ROWS), BF16),
+        out_shape=jax.ShapeDtypeStruct((OFFSETS, ROWS, ROWS), BF16),
         scratch_shapes=[
             pltpu.VMEM((OFFSETS, SLOTS, TILE, TILE), BF16),
             pltpu.SemaphoreType.DMA((OFFSETS,)),
@@ -71,10 +69,10 @@
 
 def gather_kernel(side, dense, far_before, before, own, after, far_after, cross, out):
     s = side[0]
-    total = jnp.dot(dense[1], far_before[...], preferred_element_type=F32)
-    total += jnp.dot(dense[9], far_after[...], preferred_element_type=F32)
-    total += jnp.dot(dense[2 + 6 * s], cross[...], preferred_element_type=F32)
-    for first, pair in ((3 - s, before), (5 - s, own), (7 - s, after)):
+    total = jnp.dot(dense[0], far_before[...], preferred_element_type=F32)
+    total += jnp.dot(dense[8], far_after[...], preferred_element_type=F32)
+    total += jnp.dot(dense[1 + 6 * s], cross[...], preferred_element_type=F32)
+    for first, pair in ((2 - s, before), (4 - s, own), (6 - s, after)):
         for i in range(2):
             total += jnp.dot(dense[first + i], pair[i], preferred_element_type=F32)
     out[...] = total.astype(BF16)
@@ -96,7 +94,7 @@
 
 def middle_kernel(
     place, mixed, cot, bias, weight, dense,
-    act, part, ta, tb, tc, td, te,
+    act, part, cross, tb, tc, td, ta, te,
     grad, feats,
 ):
     mine = pl.multiple_of(place[1] * WIDTH, WIDTH)
@@ -119,23 +117,25 @@
     first = lax.broadcasted_iota(jnp.int32, (RING * SHARE - HIDDEN, WIDTH), 0) == 0
     part[ROWS:, :] = jnp.where(first, jnp.sum(grad_mine, axis=0, keepdims=True), 0.0)
     side = place[0]
-    for k, pair in enumerate((ta, tb, tc, td, te)):
-        for s in range(2):
-            pair[s] = jnp.dot(
-                back, dense[2 * k + 1 + s - side], preferred_element_type=F32
-            ).astype(BF16)
+    for k, term in ((1 + 6 * side, cross), (0, ta), (8, te)):
+        term[...] = jnp.dot(back, dense[k], preferred_element_type=F32).astype(BF16)
+    for first, pair in ((2 - side, tb), (4 - side, tc), (6 - side, td)):
+        for i in range(2):
+            pair[i] = jnp.dot(back, dense[first + i], preferred_element_type=F32).astype(BF16)
 
 
 def middle(place, mixed, cot, bias, weight, dense):
     return pl.pallas_call(
         middle_kernel,
         in_specs=[SMEM] + [VMEM] * 5,
-        out_specs=[VMEM] * 7,
+        out_specs=[VMEM] * 8,
         out_shape=[
             jax.ShapeDtypeStruct((ROWS, WIDTH), BF16),
             jax.ShapeDtypeStruct((RING * SHARE, WIDTH), F32),
         ]
-        + [jax.ShapeDtypeStruct((2, WIDTH, ROWS), BF16)] * 5,
+        + [jax.ShapeDtypeStruct((WIDTH, ROWS), BF16)]
+        + [jax.ShapeDtypeStruct((2, WIDTH, ROWS), BF16)] * 3
+        + [jax.ShapeDtypeStruct((WIDTH, ROWS), BF16)] * 2,
         scratch_shapes=[pltpu.VMEM((ROWS, WIDTH), BF16), pltpu.VMEM((ROWS, HIDDEN), BF16)],
         compiler_params=params(),
         cost_estimate=pl.CostEstimate(
@@ -163,16 +163,32 @@
     )(shares, *behind)
 
 
-def split_kernel(side, own, ta, tb, td, te, first, keep, send):
+def far_kernel(side, ta, te, cross, out_a, out_e):
+    r = cross[...].astype(F32)
+    out_a[...] = (ta[...].astype(F32) + jnp.where(side[0] == 1, r, 0.0)).astype(BF16)
+    out_e[...] = (te[...].astype(F32) + jnp.where(side[0] == 0, r, 0.0)).astype(BF16)
+
+
+def far_sums(side, ta, te, cross):
+    return pl.pallas_call(
+        far_kernel,
+        in_specs=[SMEM] + [VMEM] * 3,
+        out_specs=[VMEM] * 2,
+        out_shape=[jax.ShapeDtypeStruct((WIDTH, ROWS), BF16)] * 2,
+        compiler_params=params(),
+        cost_estimate=pl.CostEstimate(flops=1 << 18, bytes_accessed=1 << 20, transcendentals=0),
+        name="far_sums",
+    )(side, ta, te, cross)
+
+
+def split_kernel(side, own, tb, td, ta, te, first, keep, send):
     del first
     for s in range(2):
-        total = own[s].astype(F32)
-        for arrived in (ta, tb, td, te):
-            total += arrived[s].astype(F32)
+        total = own[s].astype(F32) + tb[s].astype(F32) + td[s].astype(F32)
 
         @pl.when(side[0] == s)
         def _():
-            keep[...] = total
+            keep[...] = total + ta[...].astype(F32) + te[...].astype(F32)
 
         @pl.when(side[0] != s)
         def _():
@@ -283,7 +299,7 @@
     mine = gather_rows(side, dense, blocks)
     with jax.named_scope("column_gather"):
         mixed = lax.all_gather(mine, COL, axis=0, tiled=False)
-    act, part, ta, tb, tc, td, te = middle(
+    act, part, cross, tb, tc, td, ta, te = middle(
         jnp.concatenate([side, column]), mixed, cotangent, layer_bias.reshape(1, WIDTH), weight, dense
     )
 
@@ -291,13 +307,14 @@
     with jax.named_scope("weight_scatter"):
         shares = lax.all_to_all(part.reshape(RING, SHARE, WIDTH), ring, 0, 0, tiled=True)
     with jax.named_scope("term_halo"):
-        ra, rb, rd, re = (
-            routed(t, lambda p, s, k=k: (p - k, s)) for k, t in ((-2, ta), (-1, tb), (1, td), (2, te))
-        )
-    spread = spread_sum(shares, [rb], N_Y, 1.0, F32)
+        cross = routed(cross, lambda p, s: (p, 1 - s))
+        rb, rd = (routed(t, lambda p, s, k=k: (p - k, s)) for k, t in ((-1, tb), (1, td)))
+        ta, te = far_sums(side, ta, te, cross)
+        ra, re = (routed(t, lambda p, s, k=k: (p - k, s)) for k, t in ((-2, ta), (2, te)))
+    spread = spread_sum(shares, [ta], N_Y, 1.0, F32)
     with jax.named_scope("weight_rows"):
         shares = lax.all_to_all(spread, "y", 0, 0, tiled=True)
-    keep, send = split_terms(side, tc, (ra, rb, rd, re), spread)
+    keep, send = split_terms(side, tc, (rb, rd, ra, re), spread)
     with jax.named_scope("term_exchange"):
         other = routed(send, lambda p, s: (p, 1 - s))
     spread = spread_sum(shares, [other], RING, float(NODES) ** -0.5, BF16)

time: 119 us -> 114 us (0.958)
  waiting for transfers between devices: 20.8 us -> 11 us
  starting transfers between devices: 63.5 us -> 67.9 us
    ppermute x10 -> x11, waiting for transfers between devices: 18.6 us -> 8.52 us  [routed(): return lax.ppermute(block, BLK, route)]
    ppermute x10 -> x11, starting transfers between devices: 45 us -> 50.9 us  [routed(): return lax.ppermute(block, BLK, route)]
    all_to_all x1, starting transfers between devices: 9.69 us -> 8.11 us  [on_device(): lax.all_to_all(spread, ring, 0, 0, tiled=True).reshape(RING * SHARE, WIDTH)]
  transfers between devices with their start and end apart: 13 -> 14, of which waited for: 7 -> 6; matrix products, arithmetic and copies ran while one was open for 1% -> 1% of each run, Pallas kernels for 4% -> 5%
where the time goes in v10:
time: 114 us; the launch traced here: 113 us
  starting transfers between devices  67.9 us (60%)
  blocking collectives  22.3 us (20%)
  waiting for transfers between devices  11 us (10%)
  Pallas kernels  10.3 us (9%)
    ppermute x11, starting transfers between devices, routed(): return lax.ppermute(block, BLK, route)  50.9 us
    ppermute x11, waiting for transfers between devices, routed(): return lax.ppermute(block, BLK, route)  8.52 us
    all_gather x1, blocking collectives, on_device(): grads = lax.all_gather(grad_proj, COL, axis=0, tiled=False)  8.41 us
    all_to_all x1, starting transfers between devices, on_device(): lax.all_to_all(spread, ring, 0, 0, tiled=True).reshape(RING * SHARE, WIDTH)  8.11 us
    all_gather x1, blocking collectives, on_device(): mixed = lax.all_gather(mine, COL, axis=0, tiled=False)  8.02 us
    all_gather x1, blocking collectives, on_device(): pair = lax.all_gather(x, 'xl', axis=0, tiled=False)  5.86 us
    all_to_all x1, starting transfers between devices, on_device(): lax.all_to_all(part.reshape(RING, SHARE, WIDTH), ring, 0, 0, tiled=True)  4.78 us
    all_to_all x1, starting transfers between devices, on_device(): shares = lax.all_to_all(spread, 'y', 0, 0, tiled=True)  4.1 us
  transfers between devices with their start and end apart: 14, of which 6 were waited for; matrix products, arithmetic and copies ran while one was open for 1% of the time, Pallas kernels for 5%

profile of v10, /device:TPU:2, one launch (start us, length us, event | category | flops | bytes accessed | tf_op | source)
XLA Modules:
  0.0 113.3 jit_solution(9187844737362601817)
XLA Ops:
  0.6 6.1 %collective-permute-start = (bf16[512,128]{1,0:T(8,128)(2,1)}, bf16[512,128]{1,0:T(8,128)(2,1)S(1)}, u32[]{:S(2)}, u32[]{:S(2)}) collective-permute-start(bf16[512,128]{1,0:T(8,128)(2,1)} %param.8), channel_id=1, source_target_pairs={{752,0},{756,4},{760,8},{764,12},{0,16},{4,20},{8,24},{12,28},{16,... | collective-permute-start | bytes 393224 | tf_op jit(solution)/shard_map/feature_halo/ppermute | solution.py:280
  6.7 13.3 %collective-permute-start.3 = (bf16[512,128]{1,0:T(8,128)(2,1)}, bf16[512,128]{1,0:T(8,128)(2,1)S(1)}, u32[]{:S(2)}, u32[]{:S(2)}) collective-permute-start(bf16[512,128]{1,0:T(8,128)(2,1)} %param.8), channel_id=1, source_target_pairs={{16,0},{20,4},{24,8},{28,12},{32,16},{36,20},{40,24},{44,28},{48,3... | collective-permute-start | bytes 393224 | tf_op jit(solution)/shard_map/feature_halo/ppermute | solution.py:280
  20.0 5.9 %all-gather = bf16[1024,128]{1,0:T(8,128)(2,1)S(1)} all-gather(bf16[512,128]{1,0:T(8,128)(2,1)} %param.8), channel_id=2, replica_groups=mesh['y'=8,'z'=12,'xl'=2,'xh'=2,'core'=2] {'xl'}, dimensions={0}, use_global_device_ids=true | all-gather | bytes 393216 | tf_op jit(solution)/shard_map/feature_halo/all_gather | solution.py:293
  25.9 4.8 %collective-permute-start.2 = (bf16[2,512,128]{2,1,0:T(8,128)(2,1)S(1)}, bf16[2,512,128]{2,1,0:T(8,128)(2,1)S(1)}, u32[]{:S(2)}, u32[]{:S(2)}) collective-permute-start(bf16[2,512,128]{2,1,0:T(8,128)(2,1)S(1)} %bitcast.14), channel_id=1, source_target_pairs={{8,0},{12,4},{16,8},{20,12},{24,16},{28,20},{32,24},{36,28},{40,32... | collective-permute-start | bytes 786440 | tf_op jit(solution)/shard_map/feature_halo/ppermute | solution.py:280
  30.7 1.9 %collective-permute-start.1 = (bf16[2,512,128]{2,1,0:T(8,128)(2,1)S(1)}, bf16[2,512,128]{2,1,0:T(8,128)(2,1)S(1)}, u32[]{:S(2)}, u32[]{:S(2)}) collective-permute-start(bf16[2,512,128]{2,1,0:T(8,128)(2,1)S(1)} %bitcast.15), channel_id=1, source_target_pairs={{760,0},{764,4},{0,8},{4,12},{8,16},{12,20},{16,24},{20,28},{24,32... | collective-permute-start | bytes 786440 | tf_op jit(solution)/shard_map/feature_halo/ppermute | solution.py:280
  32.7 0.0 collective-permute-done.far_before
  32.7 0.0 collective-permute-done.3.far_after
  32.7 2.4 %collective-permute-start.4 = (bf16[512,128]{1,0:T(8,128)(2,1)S(1)}, bf16[512,128]{1,0:T(8,128)(2,1)S(1)}, u32[]{:S(2)}, u32[]{:S(2)}) collective-permute-start(bf16[512,128]{1,0:T(8,128)(2,1)S(1)} %broadcast_select_fusion), channel_id=1, source_target_pairs={{4,0},{0,4},{12,8},{8,12},{20,16},{16,20},{28,24},{24,28},{36,32},... | collective-permute-start | bytes 393224 | tf_op jit(solution)/shard_map/feature_halo/ppermute | solution.py:280
  35.2 0.8 bitcast_add_fusion.codes
  35.9 3.2 %dense_tiles.1.dense = bf16[9,512,512]{2,1,0:T(8,128)(2,1)S(1)} custom-call(s32[9,16]{1,0:T(8,128)S(1)} %bitcast_add_fusion.codes, bf16[1,9,16,128,128]{4,3,2,1,0:T(8,128)(2,1)} %slab.1), custom_call_target="tpu_custom_call" | custom-call | bytes 10485760 | tf_op jit(solution)/shard_map/dense_tiles/pallas_call | solution.py:55
  39.1 0.0 copy-start
  39.1 0.0 copy-start.1
  39.2 0.0 copy-start.2
  39.2 0.1 pad_add_fusion.place
  39.2 0.3 collective-permute-done.4.cross
  39.6 0.0 collective-permute-done.2.after
  39.6 2.7 %collective-permute-done.1.before = bf16[2,512,128]{2,1,0:T(8,128)(2,1)S(1)} collective-permute-done((bf16[2,512,128]{2,1,0:T(8,128)(2,1)S(1)}, bf16[2,512,128]{2,1,0:T(8,128)(2,1)S(1)}, u32[]{:S(2)}, u32[]{:S(2)}) %collective-permute-start.1) | collective-permute-done | bytes 262176 | tf_op jit(solution)/shard_map/feature_halo/ppermute | solution.py:280
  42.3 1.4 %aggregate_features.1 = bf16[512,128]{1,0:T(8,128)(2,1)S(1)} custom-call(s32[1]{0:T(128)} %bitcast.side, bf16[9,512,512]{2,1,0:T(8,128)(2,1)S(1)} %dense_tiles.1.dense, bf16[512,128]{1,0:T(8,128)(2,1)S(1)} %collective-permute-done.far_before, bf16[2,512,128]{2,1,0:T(8,128)(2,1)S(1)} %collective-permute-done.1.before, bf16[2,512,128]{2,1,0:T(8,128)(2,1)S(1)} %bitcast.16, ...), custom_call_target="tpu_custom_call" | custom-call | flops 603979776 | bytes 8388608 | tf_op jit(solution)/shard_map/aggregate_features/pallas_call | solution.py:82
  43.7 8.0 %all-gather.1 = bf16[2048,128]{1,0:T(8,128)(2,1)S(1)} all-gather(bf16[512,128]{1,0:T(8,128)(2,1)S(1)} %aggregate_features.1), channel_id=3, replica_groups=mesh['y'=8,'z'=12,'xl'=2,'xh'=2,'core'=2] {'xh','core'}, dimensions={0}, use_global_device_ids=true | all-gather | bytes 655360 | tf_op jit(solution)/shard_map/column_gather/all_gather | solution.py:301
  51.7 0.0 copy-done
  51.7 0.0 copy-done.1
  51.7 0.0 copy-done.2
  51.7 2.4 %activation_and_terms.1 = (bf16[512,128]{1,0:T(8,128)(2,1)}, f32[576,128]{1,0:T(8,128)}, bf16[128,512]{1,0:T(8,128)(2,1)S(1)}, bf16[2,128,512]{2,1,0:T(8,128)(2,...) custom-call(s32[2]{0:T(128)S(1)} %pad_add_fusion.place, ...), custom_call_target="tpu_custom_call" | custom-call | flops 1207959552 | bytes 10485760 | tf_op jit(solution)/shard_map/activation_and_terms/pallas_call | solution.py:128
  54.1 4.8 %all-to-all-start = ((f32[24,24,128]{2,1,0:T(8,128)}), f32[24,24,128]{2,1,0:T(8,128)S(1)}, u32[]{:S(2)}, u32[]{:S(2)}) async-start(f32[24,24,128]{2,1,0:T(8,128)} %bitcast.7), calls=%async_computation | async-start | bytes 589824 | tf_op jit(solution)/shard_map/weight_scatter/all_to_all | solution.py:308
  58.9 2.2 %collective-permute-start.7 = (bf16[128,512]{1,0:T(8,128)(2,1)S(1)}, bf16[128,512]{1,0:T(8,128)(2,1)S(1)}, u32[]{:S(2)}, u32[]{:S(2)}) collective-permute-start(bf16[128,512]{1,0:T(8,128)(2,1)S(1)} %get-tuple-element.24), channel_id=1, source_target_pairs={{4,0},{0,4},{12,8},{8,12},{20,16},{16,20},{28,24},{24,28},{36,32},... | collective-permute-start | bytes 393224 | tf_op jit(solution)/shard_map/term_halo/ppermute | solution.py:280
  61.1 5.6 %collective-permute-start.5 = (bf16[2,128,512]{2,1,0:T(8,128)(2,1)S(1)}, bf16[2,128,512]{2,1,0:T(8,128)(2,1)S(1)}, u32[]{:S(2)}, u32[]{:S(2)}) collective-permute-start(bf16[2,128,512]{2,1,0:T(8,128)(2,1)S(1)} %get-tuple-element.20), channel_id=1, source_target_pairs={{8,0},{12,4},{16,8},{20,12},{24,16},{28,20},{32,24},{36,28},{40,32... | collective-permute-start | bytes 786440 | tf_op jit(solution)/shard_map/term_halo/ppermute | solution.py:280
  66.7 1.9 %collective-permute-start.6 = (bf16[2,128,512]{2,1,0:T(8,128)(2,1)S(1)}, bf16[2,128,512]{2,1,0:T(8,128)(2,1)S(1)}, u32[]{:S(2)}, u32[]{:S(2)}) collective-permute-start(bf16[2,128,512]{2,1,0:T(8,128)(2,1)S(1)} %get-tuple-element.21), channel_id=1, source_target_pairs={{760,0},{764,4},{0,8},{4,12},{8,16},{12,20},{16,24},{20,28},{24,32... | collective-permute-start | bytes 786440 | tf_op jit(solution)/shard_map/term_halo/ppermute | solution.py:280
  68.7 0.0 collective-permute-done.7.cross
  68.7 0.1 far_sums.1
  68.8 3.3 %collective-permute-start.9 = (bf16[128,512]{1,0:T(8,128)(2,1)S(1)}, bf16[128,512]{1,0:T(8,128)(2,1)S(1)}, u32[]{:S(2)}, u32[]{:S(2)}) collective-permute-start(bf16[128,512]{1,0:T(8,128)(2,1)S(1)} %get-tuple-element.26), channel_id=1, source_target_pairs={{752,0},{756,4},{760,8},{764,12},{0,16},{4,20},{8,24},{12,28},{16,... | collective-permute-start | bytes 393224 | tf_op jit(solution)/shard_map/term_halo/ppermute | solution.py:280
  72.1 6.7 %collective-permute-start.8 = (bf16[128,512]{1,0:T(8,128)(2,1)S(1)}, bf16[128,512]{1,0:T(8,128)(2,1)S(1)}, u32[]{:S(2)}, u32[]{:S(2)}) collective-permute-start(bf16[128,512]{1,0:T(8,128)(2,1)S(1)} %get-tuple-element.25.refs_1_), channel_id=1, source_target_pairs={{16,0},{20,4},{24,8},{28,12},{32,16},{36,20},{40,24},{44,28},{48,3... | collective-permute-start | bytes 393224 | tf_op jit(solution)/shard_map/term_halo/ppermute | solution.py:280
  78.8 0.0 all-to-all-done.refs_0_
  78.8 0.7 spread_sum.2.first
  79.5 4.1 %all-to-all-start.1 = ((f32[8,24,128]{2,1,0:T(8,128)}), f32[8,24,128]{2,1,0:T(8,128)S(1)}, u32[]{:S(2)}, u32[]{:S(2)}) async-start(f32[8,24,128]{2,1,0:T(8,128)} %spread_sum.2.first), calls=%async_computation.1 | async-start | bytes 196608 | tf_op jit(solution)/shard_map/weight_rows/all_to_all | solution.py:316
  83.6 1.1 collective-permute-done.9.te
  84.7 0.0 collective-permute-done.8.ta
  84.7 0.0 collective-permute-done.5.tb
  84.7 0.0 collective-permute-done.6.td
  84.8 0.2 pair_sums.1
  84.9 2.5 %collective-permute-start.10 = (bf16[128,512]{1,0:T(8,128)(2,1)S(1)}, bf16[128,512]{1,0:T(8,128)(2,1)S(1)}, u32[]{:S(2)}, u32[]{:S(2)}) collective-permute-start(bf16[128,512]{1,0:T(8,128)(2,1)S(1)} %get-tuple-element.29), channel_id=1, source_target_pairs={{4,0},{0,4},{12,8},{8,12},{20,16},{16,20},{28,24},{24,28},{36,32},... | collective-permute-start | bytes 393224 | tf_op jit(solution)/shard_map/term_exchange/ppermute | solution.py:280
  87.5 4.3 %collective-permute-done.10.refs_1_.arrived = bf16[128,512]{1,0:T(8,128)(2,1)S(1)} collective-permute-done((bf16[128,512]{1,0:T(8,128)(2,1)S(1)}, bf16[128,512]{1,0:T(8,128)(2,1)S(1)}, u32[]{:S(2)}, u32[]{:S(2)}) %collective-permute-start.10) | collective-permute-done | bytes 131104 | tf_op jit(solution)/shard_map/term_exchange/ppermute | solution.py:280
  91.8 0.5 all-to-all-done.1.refs_0_
  92.4 0.7 spread_sum.3.first
  93.0 8.1 %all-to-all-start.2 = ((bf16[24,24,128]{2,1,0:T(8,128)(2,1)}), bf16[24,24,128]{2,1,0:T(8,128)(2,1)S(1)}, u32[]{:S(2)}, u32[]{:S(2)}) async-start(bf16[24,24,128]{2,1,0:T(8,128)(2,1)} %spread_sum.3.first), calls=%async_computation.2 | async-start | bytes 294912 | tf_op jit(solution)/shard_map/weight_gather/all_to_all | solution.py:326
  101.1 0.1 projected_gradient.1
  101.3 8.4 %all-gather.2 = bf16[2048,128]{1,0:T(8,128)(2,1)S(1)} all-gather(bf16[512,128]{1,0:T(8,128)(2,1)S(1)} %projected_gradient.1), channel_id=4, replica_groups=mesh['y'=8,'z'=12,'xl'=2,'xh'=2,'core'=2] {'xh','core'}, dimensions={0}, use_global_device_ids=true | all-gather | bytes 655360 | tf_op jit(solution)/shard_map/column_gather/all_gather | solution.py:323
  109.7 1.0 node_gradient.1
  110.6 2.0 %all-to-all-done.2 = bf16[24,24,128]{2,1,0:T(8,128)(2,1)S(1)} async-done(((bf16[24,24,128]{2,1,0:T(8,128)(2,1)}), bf16[24,24,128]{2,1,0:T(8,128)(2,1)S(1)}, u32[]{:S(2)}, u32[]{:S(2)}) %all-to-all-start.2) | async-done | bytes 147488 | tf_op jit(solution)/shard_map/weight_gather/all_to_all | solution.py:326
  112.6 0.7 weight_gradient.1
  (1 shorter events, 0.0 us)
Async XLA Ops:
  0.6 32.0 %collective-permute-start = (bf16[512,128]{1,0:T(8,128)(2,1)}, bf16[512,128]{1,0:T(8,128)(2,1)S(1)}, u32[]{:S(2)}, u32[]{:S(2)}) collective-permute-start(bf16[512,128]{1,0:T(8,128)(2,1)} %param.8), channel_id=1, source_target_pairs={{752,0},{756,4},{760,8},{764,12},{0,16},{4,20},{8,24},{12,28},{16,... | collective-permute-start | bytes 393224 | tf_op jit(solution)/shard_map/feature_halo/ppermute | solution.py:280
  6.7 26.0 %collective-permute-start.3 = (bf16[512,128]{1,0:T(8,128)(2,1)}, bf16[512,128]{1,0:T(8,128)(2,1)S(1)}, u32[]{:S(2)}, u32[]{:S(2)}) collective-permute-start(bf16[512,128]{1,0:T(8,128)(2,1)} %param.8), channel_id=1, source_target_pairs={{16,0},{20,4},{24,8},{28,12},{32,16},{36,20},{40,24},{44,28},{48,3... | collective-permute-start | bytes 393224 | tf_op jit(solution)/shard_map/feature_halo/ppermute | solution.py:280
  25.9 13.7 %collective-permute-start.2 = (bf16[2,512,128]{2,1,0:T(8,128)(2,1)S(1)}, bf16[2,512,128]{2,1,0:T(8,128)(2,1)S(1)}, u32[]{:S(2)}, u32[]{:S(2)}) collective-permute-start(bf16[2,512,128]{2,1,0:T(8,128)(2,1)S(1)} %bitcast.14), channel_id=1, source_target_pairs={{8,0},{12,4},{16,8},{20,12},{24,16},{28,20},{32,24},{36,28},{40,32... | collective-permute-start | bytes 786440 | tf_op jit(solution)/shard_map/feature_halo/ppermute | solution.py:280
  30.7 11.6 %collective-permute-start.1 = (bf16[2,512,128]{2,1,0:T(8,128)(2,1)S(1)}, bf16[2,512,128]{2,1,0:T(8,128)(2,1)S(1)}, u32[]{:S(2)}, u32[]{:S(2)}) collective-permute-start(bf16[2,512,128]{2,1,0:T(8,128)(2,1)S(1)} %bitcast.15), channel_id=1, source_target_pairs={{760,0},{764,4},{0,8},{4,12},{8,16},{12,20},{16,24},{20,28},{24,32... | collective-permute-start | bytes 786440 | tf_op jit(solution)/shard_map/feature_halo/ppermute | solution.py:280
  32.7 6.9 %collective-permute-start.4 = (bf16[512,128]{1,0:T(8,128)(2,1)S(1)}, bf16[512,128]{1,0:T(8,128)(2,1)S(1)}, u32[]{:S(2)}, u32[]{:S(2)}) collective-permute-start(bf16[512,128]{1,0:T(8,128)(2,1)S(1)} %broadcast_select_fusion), channel_id=1, source_target_pairs={{4,0},{0,4},{12,8},{8,12},{20,16},{16,20},{28,24},{24,28},{36,32},... | collective-permute-start | bytes 393224 | tf_op jit(solution)/shard_map/feature_halo/ppermute | solution.py:280
  39.1 12.6 %copy-start = (bf16[512,512]{1,0:T(8,128)(2,1)S(1)}, bf16[512,512]{1,0:T(8,128)(2,1)}, u32[]{:S(2)}) copy-start(bf16[512,512]{1,0:T(8,128)(2,1)} %weight.3) | copy-start | bytes 1572868
  39.1 12.6 %copy-start.1 = (bf16[512,128]{1,0:T(8,128)(2,1)S(1)}, bf16[512,128]{1,0:T(8,128)(2,1)}, u32[]{:S(2)}) copy-start(bf16[512,128]{1,0:T(8,128)(2,1)} %cot.1) | copy-start | bytes 393220
  39.2 12.6 %copy-start.2 = (bf16[128]{0:T(256)(128)(2,1)S(1)}, bf16[128]{0:T(256)(128)(2,1)}, u32[]{:S(2)}) copy-start(bf16[128]{0:T(256)(128)(2,1)} %param.10) | copy-start | bytes 772
  54.1 24.7 %all-to-all-start = ((f32[24,24,128]{2,1,0:T(8,128)}), f32[24,24,128]{2,1,0:T(8,128)S(1)}, u32[]{:S(2)}, u32[]{:S(2)}) async-start(f32[24,24,128]{2,1,0:T(8,128)} %bitcast.7), calls=%async_computation | async-start | bytes 589824 | tf_op jit(solution)/shard_map/weight_scatter/all_to_all | solution.py:308
  58.9 9.8 %collective-permute-start.7 = (bf16[128,512]{1,0:T(8,128)(2,1)S(1)}, bf16[128,512]{1,0:T(8,128)(2,1)S(1)}, u32[]{:S(2)}, u32[]{:S(2)}) collective-permute-start(bf16[128,512]{1,0:T(8,128)(2,1)S(1)} %get-tuple-element.24), channel_id=1, source_target_pairs={{4,0},{0,4},{12,8},{8,12},{20,16},{16,20},{28,24},{24,28},{36,32},... | collective-permute-start | bytes 393224 | tf_op jit(solution)/shard_map/term_halo/ppermute | solution.py:280
  61.1 23.6 %collective-permute-start.5 = (bf16[2,128,512]{2,1,0:T(8,128)(2,1)S(1)}, bf16[2,128,512]{2,1,0:T(8,128)(2,1)S(1)}, u32[]{:S(2)}, u32[]{:S(2)}) collective-permute-start(bf16[2,128,512]{2,1,0:T(8,128)(2,1)S(1)} %get-tuple-element.20), channel_id=1, source_target_pairs={{8,0},{12,4},{16,8},{20,12},{24,16},{28,20},{32,24},{36,28},{40,32... | collective-permute-start | bytes 786440 | tf_op jit(solution)/shard_map/term_halo/ppermute | solution.py:280
  66.7 18.0 %collective-permute-start.6 = (bf16[2,128,512]{2,1,0:T(8,128)(2,1)S(1)}, bf16[2,128,512]{2,1,0:T(8,128)(2,1)S(1)}, u32[]{:S(2)}, u32[]{:S(2)}) collective-permute-start(bf16[2,128,512]{2,1,0:T(8,128)(2,1)S(1)} %get-tuple-element.21), channel_id=1, source_target_pairs={{760,0},{764,4},{0,8},{4,12},{8,16},{12,20},{16,24},{20,28},{24,32... | collective-permute-start | bytes 786440 | tf_op jit(solution)/shard_map/term_halo/ppermute | solution.py:280
  68.8 16.0 %collective-permute-start.9 = (bf16[128,512]{1,0:T(8,128)(2,1)S(1)}, bf16[128,512]{1,0:T(8,128)(2,1)S(1)}, u32[]{:S(2)}, u32[]{:S(2)}) collective-permute-start(bf16[128,512]{1,0:T(8,128)(2,1)S(1)} %get-tuple-element.26), channel_id=1, source_target_pairs={{752,0},{756,4},{760,8},{764,12},{0,16},{4,20},{8,24},{12,28},{16,... | collective-permute-start | bytes 393224 | tf_op jit(solution)/shard_map/term_halo/ppermute | solution.py:280
  72.1 12.6 %collective-permute-start.8 = (bf16[128,512]{1,0:T(8,128)(2,1)S(1)}, bf16[128,512]{1,0:T(8,128)(2,1)S(1)}, u32[]{:S(2)}, u32[]{:S(2)}) collective-permute-start(bf16[128,512]{1,0:T(8,128)(2,1)S(1)} %get-tuple-element.25.refs_1_), channel_id=1, source_target_pairs={{16,0},{20,4},{24,8},{28,12},{32,16},{36,20},{40,24},{44,28},{48,3... | collective-permute-start | bytes 393224 | tf_op jit(solution)/shard_map/term_halo/ppermute | solution.py:280
  79.5 12.8 %all-to-all-start.1 = ((f32[8,24,128]{2,1,0:T(8,128)}), f32[8,24,128]{2,1,0:T(8,128)S(1)}, u32[]{:S(2)}, u32[]{:S(2)}) async-start(f32[8,24,128]{2,1,0:T(8,128)} %spread_sum.2.first), calls=%async_computation.1 | async-start | bytes 196608 | tf_op jit(solution)/shard_map/weight_rows/all_to_all | solution.py:316
  84.9 6.9 %collective-permute-start.10 = (bf16[128,512]{1,0:T(8,128)(2,1)S(1)}, bf16[128,512]{1,0:T(8,128)(2,1)S(1)}, u32[]{:S(2)}, u32[]{:S(2)}) collective-permute-start(bf16[128,512]{1,0:T(8,128)(2,1)S(1)} %get-tuple-element.29), channel_id=1, source_target_pairs={{4,0},{0,4},{12,8},{8,12},{20,16},{16,20},{28,24},{24,28},{36,32},... | collective-permute-start | bytes 393224 | tf_op jit(solution)/shard_map/term_exchange/ppermute | solution.py:280
  93.0 19.6 %all-to-all-start.2 = ((bf16[24,24,128]{2,1,0:T(8,128)(2,1)}), bf16[24,24,128]{2,1,0:T(8,128)(2,1)S(1)}, u32[]{:S(2)}, u32[]{:S(2)}) async-start(bf16[24,24,128]{2,1,0:T(8,128)(2,1)} %spread_sum.3.first), calls=%async_computation.2 | async-start | bytes 294912 | tf_op jit(solution)/shard_map/weight_gather/all_to_all | solution.py:326

commit v11 on v10

--- a/solution.py
+++ b/solution.py
@@ -65,6 +65,23 @@
         cost_estimate=pl.CostEstimate(flops=0, bytes_accessed=10 << 20, transcendentals=0),
         name="dense_tiles",
     )(codes, pltpu.with_memory_space_constraint(slab, pltpu.HBM))
+
+
+def pair_kernel(side, x, other, out):
+    out[side[0]] = x[...]
+    out[1 - side[0]] = other[...]
+
+
+def make_pair(side, x, other):
+    return pl.pallas_call(
+        pair_kernel,
+        in_specs=[SMEM] + [VMEM] * 2,
+        out_specs=VMEM,
+        out_shape=jax.ShapeDtypeStruct((2, ROWS, WIDTH), BF16),
+        compiler_params=params(),
+        cost_estimate=pl.CostEstimate(flops=0, bytes_accessed=1 << 19, transcendentals=0),
+        name="pair_blocks",
+    )(side, x, other)
 
 
 def gather_kernel(side, dense, far_before, before, own, after, far_after, cross, out):
@@ -210,65 +227,55 @@
     )(side, own, *arrived, first)
 
 
-def last_kernel(keep, arrived, first, out):
-    del first
+def last_kernel(keep, arrived, shares, out, spread):
     out[...] = (keep[...] + arrived[...].astype(F32)).T.astype(BF16)
-
-
-def last_sum(keep, arrived, first):
+    share_kernel(float(NODES) ** -0.5, shares, spread)
+
+
+def last_sum(keep, arrived, shares):
     return pl.pallas_call(
         last_kernel,
-        in_specs=[VMEM] * 2 + [pl.BlockSpec(memory_space=pl.ANY)],
-        out_specs=VMEM,
-        out_shape=jax.ShapeDtypeStruct((ROWS, WIDTH), BF16),
+        in_specs=[VMEM] * 3,
+        out_specs=[VMEM] * 2,
+        out_shape=[
+            jax.ShapeDtypeStruct((ROWS, WIDTH), BF16),
+            jax.ShapeDtypeStruct((RING, SHARE, WIDTH), BF16),
+        ],
         compiler_params=params(),
         cost_estimate=pl.CostEstimate(flops=1 << 17, bytes_accessed=1 << 19, transcendentals=0),
         name="projected_gradient",
-    )(keep, arrived, first)
-
-
-def node_kernel(column, grads, weight, out):
+    )(keep, arrived, shares)
+
+
+def final_kernel(column, grads, weight, whole, nodes, weight_grad, bias_grad):
     mine = pl.multiple_of(column[0] * WIDTH, WIDTH)
     rows = jnp.concatenate([grads[c] for c in range(COLS)], axis=1)
-    out[...] = lax.dot_general(
+    nodes[...] = lax.dot_general(
         rows,
         weight[pl.ds(mine, WIDTH), :],
         (((1,), (1,)), ((), ())),
         preferred_element_type=F32,
     ).astype(BF16)
-
-
-def node_gradient(column, grads, weight):
-    return pl.pallas_call(
-        node_kernel,
-        in_specs=[SMEM] + [VMEM] * 2,
-        out_specs=VMEM,
-        out_shape=jax.ShapeDtypeStruct((ROWS, WIDTH), BF16),
+    weight_grad[...] = whole[0:HIDDEN, :].astype(F32)
+    bias_grad[...] = whole[HIDDEN : HIDDEN + 16, :].astype(F32)[0:1]
+
+
+def final(column, grads, weight, whole):
+    return pl.pallas_call(
+        final_kernel,
+        in_specs=[SMEM] + [VMEM] * 3,
+        out_specs=[VMEM] * 3,
+        out_shape=[
+            jax.ShapeDtypeStruct((ROWS, WIDTH), BF16),
+            jax.ShapeDtypeStruct((HIDDEN, WIDTH), F32),
+            jax.ShapeDtypeStruct((1, WIDTH), F32),
+        ],
         compiler_params=params(),
         cost_estimate=pl.CostEstimate(
             flops=2 * ROWS * HIDDEN * WIDTH, bytes_accessed=2 << 20, transcendentals=0
         ),
-        name="node_gradient",
-    )(column, grads, weight)
-
-
-def widen_kernel(whole, weight_grad, bias_grad):
-    weight_grad[...] = whole[0:HIDDEN, :].astype(F32)
-    bias_grad[...] = whole[HIDDEN : HIDDEN + 16, :].astype(F32)[0:1]
-
-
-def widen(whole):
-    return pl.pallas_call(
-        widen_kernel,
-        in_specs=[VMEM],
-        out_specs=[VMEM] * 2,
-        out_shape=[
-            jax.ShapeDtypeStruct((HIDDEN, WIDTH), F32),
-            jax.ShapeDtypeStruct((1, WIDTH), F32),
-        ],
-        compiler_params=params(),
-        name="weight_gradient",
-    )(whole)
+        name="gradients",
+    )(column, grads, weight, whole)
 
 
 def routed(block, source):
@@ -290,7 +297,7 @@
     with jax.named_scope("feature_halo"):
         x = node_feats
         far_before, far_after = (routed(x, lambda p, s, k=k: (p + k, s)) for k in (-2, 2))
-        pair = lax.all_gather(x, "xl", axis=0, tiled=False)
+        pair = make_pair(side, x, routed(x, lambda p, s: (p, 1 - s)))
         before, after = (routed(pair, lambda p, s, k=k: (p + k, s)) for k in (-1, 1))
         cross = jnp.where(side[0] == 1, far_before, far_after)
         cross = routed(cross, lambda p, s: (p, 1 - s))
@@ -317,14 +324,12 @@
     keep, send = split_terms(side, tc, (rb, rd, ra, re), spread)
     with jax.named_scope("term_exchange"):
         other = routed(send, lambda p, s: (p, 1 - s))
-    spread = spread_sum(shares, [other], RING, float(NODES) ** -0.5, BF16)
-    grad_proj = last_sum(keep, other, spread)
+    grad_proj, spread = last_sum(keep, other, shares)
+    with jax.named_scope("weight_gather"):
+        whole = lax.all_to_all(spread, ring, 0, 0, tiled=True).reshape(RING * SHARE, WIDTH)
     with jax.named_scope("column_gather"):
         grads = lax.all_gather(grad_proj, COL, axis=0, tiled=False)
-    grad_nodes = node_gradient(column, grads, weight)
-    with jax.named_scope("weight_gather"):
-        whole = lax.all_to_all(spread, ring, 0, 0, tiled=True).reshape(RING * SHARE, WIDTH)
-    weight_grad, bias_grad = widen(whole)
+    grad_nodes, weight_grad, bias_grad = final(column, grads, weight, whole)
     return act, grad_nodes, weight_grad, bias_grad.reshape(WIDTH)
 
 

time: 114 us -> 113 us (level)
  blocking collectives: 22.3 us -> 16.6 us
  starting transfers between devices: 67.9 us -> 71.9 us
    all_gather x1 -> x0, blocking collectives: 5.86 us -> none  [on_device(): pair = lax.all_gather(x, 'xl', axis=0, tiled=False)]
    ppermute x11 -> x12, starting transfers between devices: 50.9 us -> 54.9 us  [routed(): return lax.ppermute(block, BLK, route)]
    ppermute x11 -> x12, waiting for transfers between devices: 8.52 us -> 8.54 us  [routed(): return lax.ppermute(block, BLK, route)]
  transfers between devices with their start and end apart: 14 -> 15, of which waited for: 6 -> 5; matrix products, arithmetic and copies ran while one was open for 1% -> 1% of each run, Pallas kernels for 5% -> 4%
where the time goes in v11:
time: 113 us; the launch traced here: 112 us
  starting transfers between devices  71.9 us (64%)
  blocking collectives  16.6 us (15%)
  waiting for transfers between devices  11.7 us (10%)
  Pallas kernels  9.58 us (8%)
    ppermute x12, starting transfers between devices, routed(): return lax.ppermute(block, BLK, route)  54.9 us
    ppermute x12, waiting for transfers between devices, routed(): return lax.ppermute(block, BLK, route)  8.54 us
    all_gather x1, blocking collectives, on_device(): grads = lax.all_gather(grad_proj, COL, axis=0, tiled=False)  8.48 us
    all_gather x1, blocking collectives, on_device(): mixed = lax.all_gather(mine, COL, axis=0, tiled=False)  8.1 us
    all_to_all x1, starting transfers between devices, on_device(): lax.all_to_all(spread, ring, 0, 0, tiled=True).reshape(RING * SHARE, WIDTH)  7.95 us
    all_to_all x1, starting transfers between devices, on_device(): lax.all_to_all(part.reshape(RING, SHARE, WIDTH), ring, 0, 0, tiled=True)  5.37 us
    all_to_all x1, starting transfers between devices, on_device(): shares = lax.all_to_all(spread, 'y', 0, 0, tiled=True)  3.68 us
    pallas_call x1, Pallas kernels, make_dense(): pl.pallas_call(dense_kernel, in_specs=[SMEM, pl.BlockSpec(memory_space=pl...  3.18 us
  transfers between devices with their start and end apart: 15, of which 5 were waited for; matrix products, arithmetic and copies ran while one was open for 1% of the time, Pallas kernels for 4%

profile of v11, /device:TPU:2, one launch (start us, length us, event | category | flops | bytes accessed | tf_op | source)
XLA Modules:
  0.0 112.4 jit_solution(13874197515061789313)
XLA Ops:
  0.6 11.5 %collective-permute-start.1 = (bf16[512,128]{1,0:T(8,128)(2,1)}, bf16[512,128]{1,0:T(8,128)(2,1)S(1)}, u32[]{:S(2)}, u32[]{:S(2)}) collective-permute-start(bf16[512,128]{1,0:T(8,128)(2,1)} %x.1), channel_id=1, source_target_pairs={{4,0},{0,4},{12,8},{8,12},{20,16},{16,20},{28,24},{24,28},{36,32},... | collective-permute-start | bytes 393224 | tf_op jit(solution)/shard_map/feature_halo/ppermute | solution.py:287
  12.1 1.9 %collective-permute-start = (bf16[512,128]{1,0:T(8,128)(2,1)}, bf16[512,128]{1,0:T(8,128)(2,1)S(1)}, u32[]{:S(2)}, u32[]{:S(2)}) collective-permute-start(bf16[512,128]{1,0:T(8,128)(2,1)} %x.1), channel_id=1, source_target_pairs={{752,0},{756,4},{760,8},{764,12},{0,16},{4,20},{8,24},{12,28},{16,... | collective-permute-start | bytes 393224 | tf_op jit(solution)/shard_map/feature_halo/ppermute | solution.py:287
  14.0 8.5 %collective-permute-start.4 = (bf16[512,128]{1,0:T(8,128)(2,1)}, bf16[512,128]{1,0:T(8,128)(2,1)S(1)}, u32[]{:S(2)}, u32[]{:S(2)}) collective-permute-start(bf16[512,128]{1,0:T(8,128)(2,1)} %x.1), channel_id=1, source_target_pairs={{16,0},{20,4},{24,8},{28,12},{32,16},{36,20},{40,24},{44,28},{48,3... | collective-permute-start | bytes 393224 | tf_op jit(solution)/shard_map/feature_halo/ppermute | solution.py:287
  22.5 0.0 collective-permute-done.1.other
  22.5 0.0 copy-start.1
  22.5 0.9 copy-done.1
  23.5 4.8 %collective-permute-start.3 = (bf16[2,512,128]{2,1,0:T(8,128)(2,1)S(1)}, bf16[2,512,128]{2,1,0:T(8,128)(2,1)S(1)}, u32[]{:S(2)}, u32[]{:S(2)}) collective-permute-start(bf16[2,512,128]{2,1,0:T(8,128)(2,1)S(1)} %pair_blocks.1.own), channel_id=1, source_target_pairs={{8,0},{12,4},{16,8},{20,12},{24,16},{28,20},{32,24},{36,28},{40,32... | collective-permute-start | bytes 786440 | tf_op jit(solution)/shard_map/feature_halo/ppermute | solution.py:287
  28.3 1.9 %collective-permute-start.2 = (bf16[2,512,128]{2,1,0:T(8,128)(2,1)S(1)}, bf16[2,512,128]{2,1,0:T(8,128)(2,1)S(1)}, u32[]{:S(2)}, u32[]{:S(2)}) collective-permute-start(bf16[2,512,128]{2,1,0:T(8,128)(2,1)S(1)} %pair_blocks.1.own), channel_id=1, source_target_pairs={{760,0},{764,4},{0,8},{4,12},{8,16},{12,20},{16,24},{20,28},{24,32... | collective-permute-start | bytes 786440 | tf_op jit(solution)/shard_map/feature_halo/ppermute | solution.py:287
  30.2 0.0 collective-permute-done.far_before
  30.3 0.0 collective-permute-done.4.far_after
  30.3 3.4 %collective-permute-start.5 = (bf16[512,128]{1,0:T(8,128)(2,1)S(1)}, bf16[512,128]{1,0:T(8,128)(2,1)S(1)}, u32[]{:S(2)}, u32[]{:S(2)}) collective-permute-start(bf16[512,128]{1,0:T(8,128)(2,1)S(1)} %broadcast_select_fusion), channel_id=1, source_target_pairs={{4,0},{0,4},{12,8},{8,12},{20,16},{16,20},{28,24},{24,28},{36,32},... | collective-permute-start | bytes 393224 | tf_op jit(solution)/shard_map/feature_halo/ppermute | solution.py:287
  33.7 0.8 bitcast_add_fusion.codes
  34.5 3.2 %dense_tiles.1.dense = bf16[9,512,512]{2,1,0:T(8,128)(2,1)S(1)} custom-call(s32[9,16]{1,0:T(8,128)S(1)} %bitcast_add_fusion.codes, bf16[1,9,16,128,128]{4,3,2,1,0:T(8,128)(2,1)} %slab.1), custom_call_target="tpu_custom_call" | custom-call | bytes 10485760 | tf_op jit(solution)/shard_map/dense_tiles/pallas_call | solution.py:55
  37.7 0.0 copy-start
  37.7 0.0 copy-start.2
  37.7 0.0 copy-start.3
  37.7 0.1 pad_add_fusion.place
  37.8 0.0 collective-permute-done.5.cross
  37.8 0.0 collective-permute-done.3.after
  37.8 2.7 %collective-permute-done.2.before = bf16[2,512,128]{2,1,0:T(8,128)(2,1)S(1)} collective-permute-done((bf16[2,512,128]{2,1,0:T(8,128)(2,1)S(1)}, bf16[2,512,128]{2,1,0:T(8,128)(2,1)S(1)}, u32[]{:S(2)}, u32[]{:S(2)}) %collective-permute-start.2) | collective-permute-done | bytes 262176 | tf_op jit(solution)/shard_map/feature_halo/ppermute | solution.py:287
  40.5 1.4 %aggregate_features.1 = bf16[512,128]{1,0:T(8,128)(2,1)S(1)} custom-call(s32[1]{0:T(128)} %bitcast.side, bf16[9,512,512]{2,1,0:T(8,128)(2,1)S(1)} %dense_tiles.1.dense, bf16[512,128]{1,0:T(8,128)(2,1)S(1)} %collective-permute-done.far_before, bf16[2,512,128]{2,1,0:T(8,128)(2,1)S(1)} %collective-permute-done.2.before, ...), custom_call_target="tpu_custom_call" | custom-call | flops 603979776 | bytes 8388608 | tf_op jit(solution)/shard_map/aggregate_features/pallas_call | solution.py:99
  41.8 8.1 %all-gather = bf16[2048,128]{1,0:T(8,128)(2,1)S(1)} all-gather(bf16[512,128]{1,0:T(8,128)(2,1)S(1)} %aggregate_features.1), channel_id=2, replica_groups=mesh['y'=8,'z'=12,'xl'=2,'xh'=2,'core'=2] {'xh','core'}, dimensions={0}, use_global_device_ids=true | all-gather | bytes 655360 | tf_op jit(solution)/shard_map/column_gather/all_gather | solution.py:308
  49.9 0.0 copy-done
  49.9 0.0 copy-done.2
  49.9 0.0 copy-done.3
  49.9 2.4 %activation_and_terms.1 = (bf16[512,128]{1,0:T(8,128)(2,1)}, f32[576,128]{1,0:T(8,128)}, bf16[128,512]{1,0:T(8,128)(2,1)S(1)}, bf16[2,128,512]{2,1,0:T(8,128)(2,...) custom-call(s32[2]{0:T(128)S(1)} %pad_add_fusion.place, ...), custom_call_target="tpu_custom_call" | custom-call | flops 1207959552 | bytes 10485760 | tf_op jit(solution)/shard_map/activation_and_terms/pallas_call | solution.py:145
  52.3 5.4 %all-to-all-start = ((f32[24,24,128]{2,1,0:T(8,128)}), f32[24,24,128]{2,1,0:T(8,128)S(1)}, u32[]{:S(2)}, u32[]{:S(2)}) async-start(f32[24,24,128]{2,1,0:T(8,128)} %bitcast.6), calls=%async_computation | async-start | bytes 589824 | tf_op jit(solution)/shard_map/weight_scatter/all_to_all | solution.py:315
  57.7 2.2 %collective-permute-start.8 = (bf16[128,512]{1,0:T(8,128)(2,1)S(1)}, bf16[128,512]{1,0:T(8,128)(2,1)S(1)}, u32[]{:S(2)}, u32[]{:S(2)}) collective-permute-start(bf16[128,512]{1,0:T(8,128)(2,1)S(1)} %get-tuple-element.27), channel_id=1, source_target_pairs={{4,0},{0,4},{12,8},{8,12},{20,16},{16,20},{28,24},{24,28},{36,32},... | collective-permute-start | bytes 393224 | tf_op jit(solution)/shard_map/term_halo/ppermute | solution.py:287
  59.9 6.2 %collective-permute-start.6 = (bf16[2,128,512]{2,1,0:T(8,128)(2,1)S(1)}, bf16[2,128,512]{2,1,0:T(8,128)(2,1)S(1)}, u32[]{:S(2)}, u32[]{:S(2)}) collective-permute-start(bf16[2,128,512]{2,1,0:T(8,128)(2,1)S(1)} %get-tuple-element.23), channel_id=1, source_target_pairs={{8,0},{12,4},{16,8},{20,12},{24,16},{28,20},{32,24},{36,28},{40,32... | collective-permute-start | bytes 786440 | tf_op jit(solution)/shard_map/term_halo/ppermute | solution.py:287
  66.1 1.9 %collective-permute-start.7 = (bf16[2,128,512]{2,1,0:T(8,128)(2,1)S(1)}, bf16[2,128,512]{2,1,0:T(8,128)(2,1)S(1)}, u32[]{:S(2)}, u32[]{:S(2)}) collective-permute-start(bf16[2,128,512]{2,1,0:T(8,128)(2,1)S(1)} %get-tuple-element.24), channel_id=1, source_target_pairs={{760,0},{764,4},{0,8},{4,12},{8,16},{12,20},{16,24},{20,28},{24,32... | collective-permute-start | bytes 786440 | tf_op jit(solution)/shard_map/term_halo/ppermute | solution.py:287
  68.0 0.0 collective-permute-done.8.cross
  68.0 0.1 far_sums.1
  68.1 2.8 %collective-permute-start.10 = (bf16[128,512]{1,0:T(8,128)(2,1)S(1)}, bf16[128,512]{1,0:T(8,128)(2,1)S(1)}, u32[]{:S(2)}, u32[]{:S(2)}) collective-permute-start(bf16[128,512]{1,0:T(8,128)(2,1)S(1)} %get-tuple-element.29), channel_id=1, source_target_pairs={{752,0},{756,4},{760,8},{764,12},{0,16},{4,20},{8,24},{12,28},{16,... | collective-permute-start | bytes 393224 | tf_op jit(solution)/shard_map/term_halo/ppermute | solution.py:287
  70.9 7.3 %collective-permute-start.9 = (bf16[128,512]{1,0:T(8,128)(2,1)S(1)}, bf16[128,512]{1,0:T(8,128)(2,1)S(1)}, u32[]{:S(2)}, u32[]{:S(2)}) collective-permute-start(bf16[128,512]{1,0:T(8,128)(2,1)S(1)} %get-tuple-element.28.refs_1_), channel_id=1, source_target_pairs={{16,0},{20,4},{24,8},{28,12},{32,16},{36,20},{40,24},{44,28},{48,3... | collective-permute-start | bytes 393224 | tf_op jit(solution)/shard_map/term_halo/ppermute | solution.py:287
  78.2 0.0 all-to-all-done.refs_0_
  78.2 0.7 spread_sum.1.first
  78.9 3.7 %all-to-all-start.1 = ((f32[8,24,128]{2,1,0:T(8,128)}), f32[8,24,128]{2,1,0:T(8,128)S(1)}, u32[]{:S(2)}, u32[]{:S(2)}) async-start(f32[8,24,128]{2,1,0:T(8,128)} %spread_sum.1.first), calls=%async_computation.1 | async-start | bytes 196608 | tf_op jit(solution)/shard_map/weight_rows/all_to_all | solution.py:323
  82.6 1.5 %collective-permute-done.10.te = bf16[128,512]{1,0:T(8,128)(2,1)S(1)} collective-permute-done((bf16[128,512]{1,0:T(8,128)(2,1)S(1)}, bf16[128,512]{1,0:T(8,128)(2,1)S(1)}, u32[]{:S(2)}, u32[]{:S(2)}) %collective-permute-start.10) | collective-permute-done | bytes 131104 | tf_op jit(solution)/shard_map/term_halo/ppermute | solution.py:287
  84.1 0.0 collective-permute-done.9.ta
  84.1 0.0 collective-permute-done.6.tb
  84.1 0.0 collective-permute-done.7.td
  84.1 0.2 pair_sums.1
  84.3 2.5 %collective-permute-start.11 = (bf16[128,512]{1,0:T(8,128)(2,1)S(1)}, bf16[128,512]{1,0:T(8,128)(2,1)S(1)}, u32[]{:S(2)}, u32[]{:S(2)}) collective-permute-start(bf16[128,512]{1,0:T(8,128)(2,1)S(1)} %get-tuple-element.32), channel_id=1, source_target_pairs={{4,0},{0,4},{12,8},{8,12},{20,16},{16,20},{28,24},{24,28},{36,32},... | collective-permute-start | bytes 393224 | tf_op jit(solution)/shard_map/term_exchange/ppermute | solution.py:287
  86.9 4.3 %collective-permute-done.11.arrived = bf16[128,512]{1,0:T(8,128)(2,1)S(1)} collective-permute-done((bf16[128,512]{1,0:T(8,128)(2,1)S(1)}, bf16[128,512]{1,0:T(8,128)(2,1)S(1)}, u32[]{:S(2)}, u32[]{:S(2)}) %collective-permute-start.11) | collective-permute-done | bytes 131104 | tf_op jit(solution)/shard_map/term_exchange/ppermute | solution.py:287
  91.2 0.1 all-to-all-done.1.shares
  91.3 0.7 projected_gradient.1
  92.0 7.9 %all-to-all-start.2 = ((bf16[24,24,128]{2,1,0:T(8,128)(2,1)}), bf16[24,24,128]{2,1,0:T(8,128)(2,1)S(1)}, u32[]{:S(2)}, u32[]{:S(2)}) async-start(bf16[24,24,128]{2,1,0:T(8,128)(2,1)} %get-tuple-element.34), calls=%async_computation.2 | async-start | bytes 294912 | tf_op jit(solution)/shard_map/weight_gather/all_to_all | solution.py:329
  100.0 8.5 %all-gather.1 = bf16[2048,128]{1,0:T(8,128)(2,1)S(1)} all-gather(bf16[512,128]{1,0:T(8,128)(2,1)S(1)} %get-tuple-element.33), channel_id=3, replica_groups=mesh['y'=8,'z'=12,'xl'=2,'xh'=2,'core'=2] {'xh','core'}, dimensions={0}, use_global_device_ids=true | all-gather | bytes 655360 | tf_op jit(solution)/shard_map/column_gather/all_gather | solution.py:331
  108.4 3.0 %all-to-all-done.2 = bf16[24,24,128]{2,1,0:T(8,128)(2,1)S(1)} async-done(((bf16[24,24,128]{2,1,0:T(8,128)(2,1)}), bf16[24,24,128]{2,1,0:T(8,128)(2,1)S(1)}, u32[]{:S(2)}, u32[]{:S(2)}) %all-to-all-start.2) | async-done | bytes 147488 | tf_op jit(solution)/shard_map/weight_gather/all_to_all | solution.py:329
  111.4 1.0 gradients.1
  (2 shorter events, 0.0 us)
Async XLA Ops:
  0.6 21.9 %collective-permute-start.1 = (bf16[512,128]{1,0:T(8,128)(2,1)}, bf16[512,128]{1,0:T(8,128)(2,1)S(1)}, u32[]{:S(2)}, u32[]{:S(2)}) collective-permute-start(bf16[512,128]{1,0:T(8,128)(2,1)} %x.1), channel_id=1, source_target_pairs={{4,0},{0,4},{12,8},{8,12},{20,16},{16,20},{28,24},{24,28},{36,32},... | collective-permute-start | bytes 393224 | tf_op jit(solution)/shard_map/feature_halo/ppermute | solution.py:287
  12.1 18.2 %collective-permute-start = (bf16[512,128]{1,0:T(8,128)(2,1)}, bf16[512,128]{1,0:T(8,128)(2,1)S(1)}, u32[]{:S(2)}, u32[]{:S(2)}) collective-permute-start(bf16[512,128]{1,0:T(8,128)(2,1)} %x.1), channel_id=1, source_target_pairs={{752,0},{756,4},{760,8},{764,12},{0,16},{4,20},{8,24},{12,28},{16,... | collective-permute-start | bytes 393224 | tf_op jit(solution)/shard_map/feature_halo/ppermute | solution.py:287
  14.0 16.2 %collective-permute-start.4 = (bf16[512,128]{1,0:T(8,128)(2,1)}, bf16[512,128]{1,0:T(8,128)(2,1)S(1)}, u32[]{:S(2)}, u32[]{:S(2)}) collective-permute-start(bf16[512,128]{1,0:T(8,128)(2,1)} %x.1), channel_id=1, source_target_pairs={{16,0},{20,4},{24,8},{28,12},{32,16},{36,20},{40,24},{44,28},{48,3... | collective-permute-start | bytes 393224 | tf_op jit(solution)/shard_map/feature_halo/ppermute | solution.py:287
  22.5 0.9 copy-start.1
  23.5 14.3 %collective-permute-start.3 = (bf16[2,512,128]{2,1,0:T(8,128)(2,1)S(1)}, bf16[2,512,128]{2,1,0:T(8,128)(2,1)S(1)}, u32[]{:S(2)}, u32[]{:S(2)}) collective-permute-start(bf16[2,512,128]{2,1,0:T(8,128)(2,1)S(1)} %pair_blocks.1.own), channel_id=1, source_target_pairs={{8,0},{12,4},{16,8},{20,12},{24,16},{28,20},{32,24},{36,28},{40,32... | collective-permute-start | bytes 786440 | tf_op jit(solution)/shard_map/feature_halo/ppermute | solution.py:287
  28.3 12.1 %collective-permute-start.2 = (bf16[2,512,128]{2,1,0:T(8,128)(2,1)S(1)}, bf16[2,512,128]{2,1,0:T(8,128)(2,1)S(1)}, u32[]{:S(2)}, u32[]{:S(2)}) collective-permute-start(bf16[2,512,128]{2,1,0:T(8,128)(2,1)S(1)} %pair_blocks.1.own), channel_id=1, source_target_pairs={{760,0},{764,4},{0,8},{4,12},{8,16},{12,20},{16,24},{20,28},{24,32... | collective-permute-start | bytes 786440 | tf_op jit(solution)/shard_map/feature_halo/ppermute | solution.py:287
  30.3 7.5 %collective-permute-start.5 = (bf16[512,128]{1,0:T(8,128)(2,1)S(1)}, bf16[512,128]{1,0:T(8,128)(2,1)S(1)}, u32[]{:S(2)}, u32[]{:S(2)}) collective-permute-start(bf16[512,128]{1,0:T(8,128)(2,1)S(1)} %broadcast_select_fusion), channel_id=1, source_target_pairs={{4,0},{0,4},{12,8},{8,12},{20,16},{16,20},{28,24},{24,28},{36,32},... | collective-permute-start | bytes 393224 | tf_op jit(solution)/shard_map/feature_halo/ppermute | solution.py:287
  37.7 12.3 %copy-start = (bf16[512,512]{1,0:T(8,128)(2,1)S(1)}, bf16[512,512]{1,0:T(8,128)(2,1)}, u32[]{:S(2)}) copy-start(bf16[512,512]{1,0:T(8,128)(2,1)} %weight.3) | copy-start | bytes 1572868
  37.7 12.3 %copy-start.2 = (bf16[512,128]{1,0:T(8,128)(2,1)S(1)}, bf16[512,128]{1,0:T(8,128)(2,1)}, u32[]{:S(2)}) copy-start(bf16[512,128]{1,0:T(8,128)(2,1)} %cot.1) | copy-start | bytes 393220
  37.7 12.3 %copy-start.3 = (bf16[128]{0:T(256)(128)(2,1)S(1)}, bf16[128]{0:T(256)(128)(2,1)}, u32[]{:S(2)}) copy-start(bf16[128]{0:T(256)(128)(2,1)} %param.10) | copy-start | bytes 772
  52.3 25.9 %all-to-all-start = ((f32[24,24,128]{2,1,0:T(8,128)}), f32[24,24,128]{2,1,0:T(8,128)S(1)}, u32[]{:S(2)}, u32[]{:S(2)}) async-start(f32[24,24,128]{2,1,0:T(8,128)} %bitcast.6), calls=%async_computation | async-start | bytes 589824 | tf_op jit(solution)/shard_map/weight_scatter/all_to_all | solution.py:315
  57.7 10.3 %collective-permute-start.8 = (bf16[128,512]{1,0:T(8,128)(2,1)S(1)}, bf16[128,512]{1,0:T(8,128)(2,1)S(1)}, u32[]{:S(2)}, u32[]{:S(2)}) collective-permute-start(bf16[128,512]{1,0:T(8,128)(2,1)S(1)} %get-tuple-element.27), channel_id=1, source_target_pairs={{4,0},{0,4},{12,8},{8,12},{20,16},{16,20},{28,24},{24,28},{36,32},... | collective-permute-start | bytes 393224 | tf_op jit(solution)/shard_map/term_halo/ppermute | solution.py:287
  59.9 24.2 %collective-permute-start.6 = (bf16[2,128,512]{2,1,0:T(8,128)(2,1)S(1)}, bf16[2,128,512]{2,1,0:T(8,128)(2,1)S(1)}, u32[]{:S(2)}, u32[]{:S(2)}) collective-permute-start(bf16[2,128,512]{2,1,0:T(8,128)(2,1)S(1)} %get-tuple-element.23), channel_id=1, source_target_pairs={{8,0},{12,4},{16,8},{20,12},{24,16},{28,20},{32,24},{36,28},{40,32... | collective-permute-start | bytes 786440 | tf_op jit(solution)/shard_map/term_halo/ppermute | solution.py:287
  66.1 18.0 %collective-permute-start.7 = (bf16[2,128,512]{2,1,0:T(8,128)(2,1)S(1)}, bf16[2,128,512]{2,1,0:T(8,128)(2,1)S(1)}, u32[]{:S(2)}, u32[]{:S(2)}) collective-permute-start(bf16[2,128,512]{2,1,0:T(8,128)(2,1)S(1)} %get-tuple-element.24), channel_id=1, source_target_pairs={{760,0},{764,4},{0,8},{4,12},{8,16},{12,20},{16,24},{20,28},{24,32... | collective-permute-start | bytes 786440 | tf_op jit(solution)/shard_map/term_halo/ppermute | solution.py:287
  68.1 16.0 %collective-permute-start.10 = (bf16[128,512]{1,0:T(8,128)(2,1)S(1)}, bf16[128,512]{1,0:T(8,128)(2,1)S(1)}, u32[]{:S(2)}, u32[]{:S(2)}) collective-permute-start(bf16[128,512]{1,0:T(8,128)(2,1)S(1)} %get-tuple-element.29), channel_id=1, source_target_pairs={{752,0},{756,4},{760,8},{764,12},{0,16},{4,20},{8,24},{12,28},{16,... | collective-permute-start | bytes 393224 | tf_op jit(solution)/shard_map/term_halo/ppermute | solution.py:287
  70.9 13.2 %collective-permute-start.9 = (bf16[128,512]{1,0:T(8,128)(2,1)S(1)}, bf16[128,512]{1,0:T(8,128)(2,1)S(1)}, u32[]{:S(2)}, u32[]{:S(2)}) collective-permute-start(bf16[128,512]{1,0:T(8,128)(2,1)S(1)} %get-tuple-element.28.refs_1_), channel_id=1, source_target_pairs={{16,0},{20,4},{24,8},{28,12},{32,16},{36,20},{40,24},{44,28},{48,3... | collective-permute-start | bytes 393224 | tf_op jit(solution)/shard_map/term_halo/ppermute | solution.py:287
  78.9 12.4 %all-to-all-start.1 = ((f32[8,24,128]{2,1,0:T(8,128)}), f32[8,24,128]{2,1,0:T(8,128)S(1)}, u32[]{:S(2)}, u32[]{:S(2)}) async-start(f32[8,24,128]{2,1,0:T(8,128)} %spread_sum.1.first), calls=%async_computation.1 | async-start | bytes 196608 | tf_op jit(solution)/shard_map/weight_rows/all_to_all | solution.py:323
  84.3 6.9 %collective-permute-start.11 = (bf16[128,512]{1,0:T(8,128)(2,1)S(1)}, bf16[128,512]{1,0:T(8,128)(2,1)S(1)}, u32[]{:S(2)}, u32[]{:S(2)}) collective-permute-start(bf16[128,512]{1,0:T(8,128)(2,1)S(1)} %get-tuple-element.32), channel_id=1, source_target_pairs={{4,0},{0,4},{12,8},{8,12},{20,16},{16,20},{28,24},{24,28},{36,32},... | collective-permute-start | bytes 393224 | tf_op jit(solution)/shard_map/term_exchange/ppermute | solution.py:287
  92.0 19.4 %all-to-all-start.2 = ((bf16[24,24,128]{2,1,0:T(8,128)(2,1)}), bf16[24,24,128]{2,1,0:T(8,128)(2,1)S(1)}, u32[]{:S(2)}, u32[]{:S(2)}) async-start(bf16[24,24,128]{2,1,0:T(8,128)(2,1)} %get-tuple-element.34), calls=%async_computation.2 | async-start | bytes 294912 | tf_op jit(solution)/shard_map/weight_gather/all_to_all | solution.py:329

commit v12 on v11

--- a/solution.py
+++ b/solution.py
@@ -67,21 +67,24 @@
     )(codes, pltpu.with_memory_space_constraint(slab, pltpu.HBM))
 
 
-def pair_kernel(side, x, other, out):
-    out[side[0]] = x[...]
+def pair_kernel(side, x, other, out, sem):
+    copy = pltpu.make_async_copy(x, out.at[side[0]], sem)
+    copy.start()
     out[1 - side[0]] = other[...]
+    copy.wait()
 
 
 def make_pair(side, x, other):
     return pl.pallas_call(
         pair_kernel,
-        in_specs=[SMEM] + [VMEM] * 2,
+        in_specs=[SMEM, pl.BlockSpec(memory_space=pltpu.HBM), VMEM],
         out_specs=VMEM,
         out_shape=jax.ShapeDtypeStruct((2, ROWS, WIDTH), BF16),
+        scratch_shapes=[pltpu.SemaphoreType.DMA],
         compiler_params=params(),
         cost_estimate=pl.CostEstimate(flops=0, bytes_accessed=1 << 19, transcendentals=0),
         name="pair_blocks",
-    )(side, x, other)
+    )(side, pltpu.with_memory_space_constraint(x, pltpu.HBM), other)
 
 
 def gather_kernel(side, dense, far_before, before, own, after, far_after, cross, out):

time: 113 us -> 113 us (level)
  transfers between devices with their start and end apart: 15 -> 15, of which waited for: 5 -> 5; matrix products, arithmetic and copies ran while one was open for 1% -> 1% of each run, Pallas kernels for 4% -> 5%
where the time goes in v12:
time: 113 us; the launch traced here: 112 us
  starting transfers between devices  71.9 us (64%)
  blocking collectives  16.6 us (15%)
  waiting for transfers between devices  11.7 us (10%)
  Pallas kernels  10.5 us (9%)
    ppermute x12, starting transfers between devices, routed(): return lax.ppermute(block, BLK, route)  54.9 us
    ppermute x12, waiting for transfers between devices, routed(): return lax.ppermute(block, BLK, route)  8.55 us
    all_gather x1, blocking collectives, on_device(): grads = lax.all_gather(grad_proj, COL, axis=0, tiled=False)  8.48 us
    all_gather x1, blocking collectives, on_device(): mixed = lax.all_gather(mine, COL, axis=0, tiled=False)  8.1 us
    all_to_all x1, starting transfers between devices, on_device(): lax.all_to_all(spread, ring, 0, 0, tiled=True).reshape(RING * SHARE, WIDTH)  7.95 us
    all_to_all x1, starting transfers between devices, on_device(): lax.all_to_all(part.reshape(RING, SHARE, WIDTH), ring, 0, 0, tiled=True)  5.35 us
    all_to_all x1, starting transfers between devices, on_device(): shares = lax.all_to_all(spread, 'y', 0, 0, tiled=True)  3.67 us
    pallas_call x1, Pallas kernels, make_dense(): pl.pallas_call(dense_kernel, in_specs=[SMEM, pl.BlockSpec(memory_space=pl...  3.18 us
  transfers between devices with their start and end apart: 15, of which 5 were waited for; matrix products, arithmetic and copies ran while one was open for 1% of the time, Pallas kernels for 5%

profile of v12, /device:TPU:2, one launch (start us, length us, event | category | flops | bytes accessed | tf_op | source)
XLA Modules:
  0.0 112.4 jit_solution(2425768284858806938)
XLA Ops:
  0.6 11.5 %collective-permute-start.1 = (bf16[512,128]{1,0:T(8,128)(2,1)}, bf16[512,128]{1,0:T(8,128)(2,1)S(1)}, u32[]{:S(2)}, u32[]{:S(2)}) collective-permute-start(bf16[512,128]{1,0:T(8,128)(2,1)} %x.1), channel_id=1, source_target_pairs={{4,0},{0,4},{12,8},{8,12},{20,16},{16,20},{28,24},{24,28},{36,32},... | collective-permute-start | bytes 393224 | tf_op jit(solution)/shard_map/feature_halo/ppermute | solution.py:290
  12.1 1.9 %collective-permute-start = (bf16[512,128]{1,0:T(8,128)(2,1)}, bf16[512,128]{1,0:T(8,128)(2,1)S(1)}, u32[]{:S(2)}, u32[]{:S(2)}) collective-permute-start(bf16[512,128]{1,0:T(8,128)(2,1)} %x.1), channel_id=1, source_target_pairs={{752,0},{756,4},{760,8},{764,12},{0,16},{4,20},{8,24},{12,28},{16,... | collective-permute-start | bytes 393224 | tf_op jit(solution)/shard_map/feature_halo/ppermute | solution.py:290
  14.0 8.5 %collective-permute-start.4 = (bf16[512,128]{1,0:T(8,128)(2,1)}, bf16[512,128]{1,0:T(8,128)(2,1)S(1)}, u32[]{:S(2)}, u32[]{:S(2)}) collective-permute-start(bf16[512,128]{1,0:T(8,128)(2,1)} %x.1), channel_id=1, source_target_pairs={{16,0},{20,4},{24,8},{28,12},{32,16},{36,20},{40,24},{44,28},{48,3... | collective-permute-start | bytes 393224 | tf_op jit(solution)/shard_map/feature_halo/ppermute | solution.py:290
  22.5 0.0 collective-permute-done.1.other
  22.5 0.9 pair_blocks.1.own
  23.5 4.8 %collective-permute-start.3 = (bf16[2,512,128]{2,1,0:T(8,128)(2,1)S(1)}, bf16[2,512,128]{2,1,0:T(8,128)(2,1)S(1)}, u32[]{:S(2)}, u32[]{:S(2)}) collective-permute-start(bf16[2,512,128]{2,1,0:T(8,128)(2,1)S(1)} %pair_blocks.1.own), channel_id=1, source_target_pairs={{8,0},{12,4},{16,8},{20,12},{24,16},{28,20},{32,24},{36,28},{40,32... | collective-permute-start | bytes 786440 | tf_op jit(solution)/shard_map/feature_halo/ppermute | solution.py:290
  28.3 1.9 %collective-permute-start.2 = (bf16[2,512,128]{2,1,0:T(8,128)(2,1)S(1)}, bf16[2,512,128]{2,1,0:T(8,128)(2,1)S(1)}, u32[]{:S(2)}, u32[]{:S(2)}) collective-permute-start(bf16[2,512,128]{2,1,0:T(8,128)(2,1)S(1)} %pair_blocks.1.own), channel_id=1, source_target_pairs={{760,0},{764,4},{0,8},{4,12},{8,16},{12,20},{16,24},{20,28},{24,32... | collective-permute-start | bytes 786440 | tf_op jit(solution)/shard_map/feature_halo/ppermute | solution.py:290
  30.2 0.0 collective-permute-done.far_before
  30.2 0.0 collective-permute-done.4.far_after
  30.3 3.4 %collective-permute-start.5 = (bf16[512,128]{1,0:T(8,128)(2,1)S(1)}, bf16[512,128]{1,0:T(8,128)(2,1)S(1)}, u32[]{:S(2)}, u32[]{:S(2)}) collective-permute-start(bf16[512,128]{1,0:T(8,128)(2,1)S(1)} %broadcast_select_fusion), channel_id=1, source_target_pairs={{4,0},{0,4},{12,8},{8,12},{20,16},{16,20},{28,24},{24,28},{36,32},... | collective-permute-start | bytes 393224 | tf_op jit(solution)/shard_map/feature_halo/ppermute | solution.py:290
  33.7 0.8 bitcast_add_fusion.codes
  34.5 3.2 %dense_tiles.1.dense = bf16[9,512,512]{2,1,0:T(8,128)(2,1)S(1)} custom-call(s32[9,16]{1,0:T(8,128)S(1)} %bitcast_add_fusion.codes, bf16[1,9,16,128,128]{4,3,2,1,0:T(8,128)(2,1)} %slab.1), custom_call_target="tpu_custom_call" | custom-call | bytes 10485760 | tf_op jit(solution)/shard_map/dense_tiles/pallas_call | solution.py:55
  37.7 0.0 copy-start
  37.7 0.0 copy-start.1
  37.7 0.0 copy-start.2
  37.7 0.1 pad_add_fusion.place
  37.8 0.0 collective-permute-done.5.cross
  37.8 0.0 collective-permute-done.3.after
  37.8 2.7 %collective-permute-done.2.before = bf16[2,512,128]{2,1,0:T(8,128)(2,1)S(1)} collective-permute-done((bf16[2,512,128]{2,1,0:T(8,128)(2,1)S(1)}, bf16[2,512,128]{2,1,0:T(8,128)(2,1)S(1)}, u32[]{:S(2)}, u32[]{:S(2)}) %collective-permute-start.2) | collective-permute-done | bytes 262176 | tf_op jit(solution)/shard_map/feature_halo/ppermute | solution.py:290
  40.4 1.4 %aggregate_features.1 = bf16[512,128]{1,0:T(8,128)(2,1)S(1)} custom-call(s32[1]{0:T(128)} %bitcast.side, bf16[9,512,512]{2,1,0:T(8,128)(2,1)S(1)} %dense_tiles.1.dense, bf16[512,128]{1,0:T(8,128)(2,1)S(1)} %collective-permute-done.far_before, bf16[2,512,128]{2,1,0:T(8,128)(2,1)S(1)} %collective-permute-done.2.before, ...), custom_call_target="tpu_custom_call" | custom-call | flops 603979776 | bytes 8388608 | tf_op jit(solution)/shard_map/aggregate_features/pallas_call | solution.py:102
  41.8 8.1 %all-gather = bf16[2048,128]{1,0:T(8,128)(2,1)S(1)} all-gather(bf16[512,128]{1,0:T(8,128)(2,1)S(1)} %aggregate_features.1), channel_id=2, replica_groups=mesh['y'=8,'z'=12,'xl'=2,'xh'=2,'core'=2] {'xh','core'}, dimensions={0}, use_global_device_ids=true | all-gather | bytes 655360 | tf_op jit(solution)/shard_map/column_gather/all_gather | solution.py:311
  49.9 0.0 copy-done
  49.9 0.0 copy-done.1
  49.9 0.0 copy-done.2
  49.9 2.4 %activation_and_terms.1 = (bf16[512,128]{1,0:T(8,128)(2,1)}, f32[576,128]{1,0:T(8,128)}, bf16[128,512]{1,0:T(8,128)(2,1)S(1)}, bf16[2,128,512]{2,1,0:T(8,128)(2,...) custom-call(s32[2]{0:T(128)S(1)} %pad_add_fusion.place, ...), custom_call_target="tpu_custom_call" | custom-call | flops 1207959552 | bytes 10485760 | tf_op jit(solution)/shard_map/activation_and_terms/pallas_call | solution.py:148
  52.3 5.3 %all-to-all-start = ((f32[24,24,128]{2,1,0:T(8,128)}), f32[24,24,128]{2,1,0:T(8,128)S(1)}, u32[]{:S(2)}, u32[]{:S(2)}) async-start(f32[24,24,128]{2,1,0:T(8,128)} %bitcast.6), calls=%async_computation | async-start | bytes 589824 | tf_op jit(solution)/shard_map/weight_scatter/all_to_all | solution.py:318
  57.7 2.2 %collective-permute-start.8 = (bf16[128,512]{1,0:T(8,128)(2,1)S(1)}, bf16[128,512]{1,0:T(8,128)(2,1)S(1)}, u32[]{:S(2)}, u32[]{:S(2)}) collective-permute-start(bf16[128,512]{1,0:T(8,128)(2,1)S(1)} %get-tuple-element.27), channel_id=1, source_target_pairs={{4,0},{0,4},{12,8},{8,12},{20,16},{16,20},{28,24},{24,28},{36,32},... | collective-permute-start | bytes 393224 | tf_op jit(solution)/shard_map/term_halo/ppermute | solution.py:290
  59.9 6.2 %collective-permute-start.6 = (bf16[2,128,512]{2,1,0:T(8,128)(2,1)S(1)}, bf16[2,128,512]{2,1,0:T(8,128)(2,1)S(1)}, u32[]{:S(2)}, u32[]{:S(2)}) collective-permute-start(bf16[2,128,512]{2,1,0:T(8,128)(2,1)S(1)} %get-tuple-element.23), channel_id=1, source_target_pairs={{8,0},{12,4},{16,8},{20,12},{24,16},{28,20},{32,24},{36,28},{40,32... | collective-permute-start | bytes 786440 | tf_op jit(solution)/shard_map/term_halo/ppermute | solution.py:290
  66.1 1.9 %collective-permute-start.7 = (bf16[2,128,512]{2,1,0:T(8,128)(2,1)S(1)}, bf16[2,128,512]{2,1,0:T(8,128)(2,1)S(1)}, u32[]{:S(2)}, u32[]{:S(2)}) collective-permute-start(bf16[2,128,512]{2,1,0:T(8,128)(2,1)S(1)} %get-tuple-element.24), channel_id=1, source_target_pairs={{760,0},{764,4},{0,8},{4,12},{8,16},{12,20},{16,24},{20,28},{24,32... | collective-permute-start | bytes 786440 | tf_op jit(solution)/shard_map/term_halo/ppermute | solution.py:290
  68.0 0.0 collective-permute-done.8.cross
  68.0 0.1 far_sums.1
  68.1 2.7 %collective-permute-start.10 = (bf16[128,512]{1,0:T(8,128)(2,1)S(1)}, bf16[128,512]{1,0:T(8,128)(2,1)S(1)}, u32[]{:S(2)}, u32[]{:S(2)}) collective-permute-start(bf16[128,512]{1,0:T(8,128)(2,1)S(1)} %get-tuple-element.29), channel_id=1, source_target_pairs={{752,0},{756,4},{760,8},{764,12},{0,16},{4,20},{8,24},{12,28},{16,... | collective-permute-start | bytes 393224 | tf_op jit(solution)/shard_map/term_halo/ppermute | solution.py:290
  70.9 7.3 %collective-permute-start.9 = (bf16[128,512]{1,0:T(8,128)(2,1)S(1)}, bf16[128,512]{1,0:T(8,128)(2,1)S(1)}, u32[]{:S(2)}, u32[]{:S(2)}) collective-permute-start(bf16[128,512]{1,0:T(8,128)(2,1)S(1)} %get-tuple-element.28.refs_1_), channel_id=1, source_target_pairs={{16,0},{20,4},{24,8},{28,12},{32,16},{36,20},{40,24},{44,28},{48,3... | collective-permute-start | bytes 393224 | tf_op jit(solution)/shard_map/term_halo/ppermute | solution.py:290
  78.2 0.0 all-to-all-done.refs_0_
  78.2 0.7 spread_sum.1.first
  78.9 3.7 %all-to-all-start.1 = ((f32[8,24,128]{2,1,0:T(8,128)}), f32[8,24,128]{2,1,0:T(8,128)S(1)}, u32[]{:S(2)}, u32[]{:S(2)}) async-start(f32[8,24,128]{2,1,0:T(8,128)} %spread_sum.1.first), calls=%async_computation.1 | async-start | bytes 196608 | tf_op jit(solution)/shard_map/weight_rows/all_to_all | solution.py:326
  82.6 1.5 %collective-permute-done.10.te = bf16[128,512]{1,0:T(8,128)(2,1)S(1)} collective-permute-done((bf16[128,512]{1,0:T(8,128)(2,1)S(1)}, bf16[128,512]{1,0:T(8,128)(2,1)S(1)}, u32[]{:S(2)}, u32[]{:S(2)}) %collective-permute-start.10) | collective-permute-done | bytes 131104 | tf_op jit(solution)/shard_map/term_halo/ppermute | solution.py:290
  84.1 0.0 collective-permute-done.9.ta
  84.1 0.0 collective-permute-done.6.tb
  84.1 0.0 collective-permute-done.7.td
  84.1 0.2 pair_sums.1
  84.3 2.5 %collective-permute-start.11 = (bf16[128,512]{1,0:T(8,128)(2,1)S(1)}, bf16[128,512]{1,0:T(8,128)(2,1)S(1)}, u32[]{:S(2)}, u32[]{:S(2)}) collective-permute-start(bf16[128,512]{1,0:T(8,128)(2,1)S(1)} %get-tuple-element.32), channel_id=1, source_target_pairs={{4,0},{0,4},{12,8},{8,12},{20,16},{16,20},{28,24},{24,28},{36,32},... | collective-permute-start | bytes 393224 | tf_op jit(solution)/shard_map/term_exchange/ppermute | solution.py:290
  86.9 4.3 %collective-permute-done.11.arrived = bf16[128,512]{1,0:T(8,128)(2,1)S(1)} collective-permute-done((bf16[128,512]{1,0:T(8,128)(2,1)S(1)}, bf16[128,512]{1,0:T(8,128)(2,1)S(1)}, u32[]{:S(2)}, u32[]{:S(2)}) %collective-permute-start.11) | collective-permute-done | bytes 131104 | tf_op jit(solution)/shard_map/term_exchange/ppermute | solution.py:290
  91.2 0.1 all-to-all-done.1.shares
  91.3 0.7 projected_gradient.1
  92.0 7.9 %all-to-all-start.2 = ((bf16[24,24,128]{2,1,0:T(8,128)(2,1)}), bf16[24,24,128]{2,1,0:T(8,128)(2,1)S(1)}, u32[]{:S(2)}, u32[]{:S(2)}) async-start(bf16[24,24,128]{2,1,0:T(8,128)(2,1)} %get-tuple-element.34), calls=%async_computation.2 | async-start | bytes 294912 | tf_op jit(solution)/shard_map/weight_gather/all_to_all | solution.py:332
  100.0 8.5 %all-gather.1 = bf16[2048,128]{1,0:T(8,128)(2,1)S(1)} all-gather(bf16[512,128]{1,0:T(8,128)(2,1)S(1)} %get-tuple-element.33), channel_id=3, replica_groups=mesh['y'=8,'z'=12,'xl'=2,'xh'=2,'core'=2] {'xh','core'}, dimensions={0}, use_global_device_ids=true | all-gather | bytes 655360 | tf_op jit(solution)/shard_map/column_gather/all_gather | solution.py:334
  108.4 3.0 %all-to-all-done.2 = bf16[24,24,128]{2,1,0:T(8,128)(2,1)S(1)} async-done(((bf16[24,24,128]{2,1,0:T(8,128)(2,1)}), bf16[24,24,128]{2,1,0:T(8,128)(2,1)S(1)}, u32[]{:S(2)}, u32[]{:S(2)}) %all-to-all-start.2) | async-done | bytes 147488 | tf_op jit(solution)/shard_map/weight_gather/all_to_all | solution.py:332
  111.4 1.0 gradients.1
  (1 shorter events, 0.0 us)
Async XLA Ops:
  0.6 21.9 %collective-permute-start.1 = (bf16[512,128]{1,0:T(8,128)(2,1)}, bf16[512,128]{1,0:T(8,128)(2,1)S(1)}, u32[]{:S(2)}, u32[]{:S(2)}) collective-permute-start(bf16[512,128]{1,0:T(8,128)(2,1)} %x.1), channel_id=1, source_target_pairs={{4,0},{0,4},{12,8},{8,12},{20,16},{16,20},{28,24},{24,28},{36,32},... | collective-permute-start | bytes 393224 | tf_op jit(solution)/shard_map/feature_halo/ppermute | solution.py:290
  12.1 18.1 %collective-permute-start = (bf16[512,128]{1,0:T(8,128)(2,1)}, bf16[512,128]{1,0:T(8,128)(2,1)S(1)}, u32[]{:S(2)}, u32[]{:S(2)}) collective-permute-start(bf16[512,128]{1,0:T(8,128)(2,1)} %x.1), channel_id=1, source_target_pairs={{752,0},{756,4},{760,8},{764,12},{0,16},{4,20},{8,24},{12,28},{16,... | collective-permute-start | bytes 393224 | tf_op jit(solution)/shard_map/feature_halo/ppermute | solution.py:290
  14.0 16.2 %collective-permute-start.4 = (bf16[512,128]{1,0:T(8,128)(2,1)}, bf16[512,128]{1,0:T(8,128)(2,1)S(1)}, u32[]{:S(2)}, u32[]{:S(2)}) collective-permute-start(bf16[512,128]{1,0:T(8,128)(2,1)} %x.1), channel_id=1, source_target_pairs={{16,0},{20,4},{24,8},{28,12},{32,16},{36,20},{40,24},{44,28},{48,3... | collective-permute-start | bytes 393224 | tf_op jit(solution)/shard_map/feature_halo/ppermute | solution.py:290
  23.5 14.3 %collective-permute-start.3 = (bf16[2,512,128]{2,1,0:T(8,128)(2,1)S(1)}, bf16[2,512,128]{2,1,0:T(8,128)(2,1)S(1)}, u32[]{:S(2)}, u32[]{:S(2)}) collective-permute-start(bf16[2,512,128]{2,1,0:T(8,128)(2,1)S(1)} %pair_blocks.1.own), channel_id=1, source_target_pairs={{8,0},{12,4},{16,8},{20,12},{24,16},{28,20},{32,24},{36,28},{40,32... | collective-permute-start | bytes 786440 | tf_op jit(solution)/shard_map/feature_halo/ppermute | solution.py:290
  28.3 12.1 %collective-permute-start.2 = (bf16[2,512,128]{2,1,0:T(8,128)(2,1)S(1)}, bf16[2,512,128]{2,1,0:T(8,128)(2,1)S(1)}, u32[]{:S(2)}, u32[]{:S(2)}) collective-permute-start(bf16[2,512,128]{2,1,0:T(8,128)(2,1)S(1)} %pair_blocks.1.own), channel_id=1, source_target_pairs={{760,0},{764,4},{0,8},{4,12},{8,16},{12,20},{16,24},{20,28},{24,32... | collective-permute-start | bytes 786440 | tf_op jit(solution)/shard_map/feature_halo/ppermute | solution.py:290
  30.3 7.5 %collective-permute-start.5 = (bf16[512,128]{1,0:T(8,128)(2,1)S(1)}, bf16[512,128]{1,0:T(8,128)(2,1)S(1)}, u32[]{:S(2)}, u32[]{:S(2)}) collective-permute-start(bf16[512,128]{1,0:T(8,128)(2,1)S(1)} %broadcast_select_fusion), channel_id=1, source_target_pairs={{4,0},{0,4},{12,8},{8,12},{20,16},{16,20},{28,24},{24,28},{36,32},... | collective-permute-start | bytes 393224 | tf_op jit(solution)/shard_map/feature_halo/ppermute | solution.py:290
  37.7 12.3 %copy-start = (bf16[512,512]{1,0:T(8,128)(2,1)S(1)}, bf16[512,512]{1,0:T(8,128)(2,1)}, u32[]{:S(2)}) copy-start(bf16[512,512]{1,0:T(8,128)(2,1)} %weight.3) | copy-start | bytes 1572868
  37.7 12.3 %copy-start.1 = (bf16[512,128]{1,0:T(8,128)(2,1)S(1)}, bf16[512,128]{1,0:T(8,128)(2,1)}, u32[]{:S(2)}) copy-start(bf16[512,128]{1,0:T(8,128)(2,1)} %cot.1) | copy-start | bytes 393220
  37.7 12.3 %copy-start.2 = (bf16[128]{0:T(256)(128)(2,1)S(1)}, bf16[128]{0:T(256)(128)(2,1)}, u32[]{:S(2)}) copy-start(bf16[128]{0:T(256)(128)(2,1)} %param.10) | copy-start | bytes 772
  52.3 25.9 %all-to-all-start = ((f32[24,24,128]{2,1,0:T(8,128)}), f32[24,24,128]{2,1,0:T(8,128)S(1)}, u32[]{:S(2)}, u32[]{:S(2)}) async-start(f32[24,24,128]{2,1,0:T(8,128)} %bitcast.6), calls=%async_computation | async-start | bytes 589824 | tf_op jit(solution)/shard_map/weight_scatter/all_to_all | solution.py:318
  57.7 10.4 %collective-permute-start.8 = (bf16[128,512]{1,0:T(8,128)(2,1)S(1)}, bf16[128,512]{1,0:T(8,128)(2,1)S(1)}, u32[]{:S(2)}, u32[]{:S(2)}) collective-permute-start(bf16[128,512]{1,0:T(8,128)(2,1)S(1)} %get-tuple-element.27), channel_id=1, source_target_pairs={{4,0},{0,4},{12,8},{8,12},{20,16},{16,20},{28,24},{24,28},{36,32},... | collective-permute-start | bytes 393224 | tf_op jit(solution)/shard_map/term_halo/ppermute | solution.py:290
  59.9 24.2 %collective-permute-start.6 = (bf16[2,128,512]{2,1,0:T(8,128)(2,1)S(1)}, bf16[2,128,512]{2,1,0:T(8,128)(2,1)S(1)}, u32[]{:S(2)}, u32[]{:S(2)}) collective-permute-start(bf16[2,128,512]{2,1,0:T(8,128)(2,1)S(1)} %get-tuple-element.23), channel_id=1, source_target_pairs={{8,0},{12,4},{16,8},{20,12},{24,16},{28,20},{32,24},{36,28},{40,32... | collective-permute-start | bytes 786440 | tf_op jit(solution)/shard_map/term_halo/ppermute | solution.py:290
  66.1 18.0 %collective-permute-start.7 = (bf16[2,128,512]{2,1,0:T(8,128)(2,1)S(1)}, bf16[2,128,512]{2,1,0:T(8,128)(2,1)S(1)}, u32[]{:S(2)}, u32[]{:S(2)}) collective-permute-start(bf16[2,128,512]{2,1,0:T(8,128)(2,1)S(1)} %get-tuple-element.24), channel_id=1, source_target_pairs={{760,0},{764,4},{0,8},{4,12},{8,16},{12,20},{16,24},{20,28},{24,32... | collective-permute-start | bytes 786440 | tf_op jit(solution)/shard_map/term_halo/ppermute | solution.py:290
  68.1 16.0 %collective-permute-start.10 = (bf16[128,512]{1,0:T(8,128)(2,1)S(1)}, bf16[128,512]{1,0:T(8,128)(2,1)S(1)}, u32[]{:S(2)}, u32[]{:S(2)}) collective-permute-start(bf16[128,512]{1,0:T(8,128)(2,1)S(1)} %get-tuple-element.29), channel_id=1, source_target_pairs={{752,0},{756,4},{760,8},{764,12},{0,16},{4,20},{8,24},{12,28},{16,... | collective-permute-start | bytes 393224 | tf_op jit(solution)/shard_map/term_halo/ppermute | solution.py:290
  70.9 13.2 %collective-permute-start.9 = (bf16[128,512]{1,0:T(8,128)(2,1)S(1)}, bf16[128,512]{1,0:T(8,128)(2,1)S(1)}, u32[]{:S(2)}, u32[]{:S(2)}) collective-permute-start(bf16[128,512]{1,0:T(8,128)(2,1)S(1)} %get-tuple-element.28.refs_1_), channel_id=1, source_target_pairs={{16,0},{20,4},{24,8},{28,12},{32,16},{36,20},{40,24},{44,28},{48,3... | collective-permute-start | bytes 393224 | tf_op jit(solution)/shard_map/term_halo/ppermute | solution.py:290
  78.9 12.4 %all-to-all-start.1 = ((f32[8,24,128]{2,1,0:T(8,128)}), f32[8,24,128]{2,1,0:T(8,128)S(1)}, u32[]{:S(2)}, u32[]{:S(2)}) async-start(f32[8,24,128]{2,1,0:T(8,128)} %spread_sum.1.first), calls=%async_computation.1 | async-start | bytes 196608 | tf_op jit(solution)/shard_map/weight_rows/all_to_all | solution.py:326
  84.3 6.9 %collective-permute-start.11 = (bf16[128,512]{1,0:T(8,128)(2,1)S(1)}, bf16[128,512]{1,0:T(8,128)(2,1)S(1)}, u32[]{:S(2)}, u32[]{:S(2)}) collective-permute-start(bf16[128,512]{1,0:T(8,128)(2,1)S(1)} %get-tuple-element.32), channel_id=1, source_target_pairs={{4,0},{0,4},{12,8},{8,12},{20,16},{16,20},{28,24},{24,28},{36,32},... | collective-permute-start | bytes 393224 | tf_op jit(solution)/shard_map/term_exchange/ppermute | solution.py:290
  92.0 19.4 %all-to-all-start.2 = ((bf16[24,24,128]{2,1,0:T(8,128)(2,1)}), bf16[24,24,128]{2,1,0:T(8,128)(2,1)S(1)}, u32[]{:S(2)}, u32[]{:S(2)}) async-start(bf16[24,24,128]{2,1,0:T(8,128)(2,1)} %get-tuple-element.34), calls=%async_computation.2 | async-start | bytes 294912 | tf_op jit(solution)/shard_map/weight_gather/all_to_all | solution.py:332
